TPU v7x, 32 devices: a whole 2x2x4 slice. The times are simulated.
32 devices in a mesh: section: 2 (over core), dp: 4 (over z), tensor: 4 (over y, x).
Axes of the slice: x: 2, y: 2, z: 4, core: 2. Of those that a mesh axis runs over, the one named last changes fastest.
Arguments:
- inputs: bfloat16 [2, 1152, 2048], P(None, 'dp'), may hold values from -6 to 6
- cotangent: bfloat16 [2, 1152, 2048], P(None, 'dp'), may hold values from -6 to 6
- seg_ids: int32 [2, 1152], replicated, may hold values from 0 to 8, as said below
- parents: int32 [2, 9], replicated, may hold values from 0 to 4, as said below
- order: int32 [2], replicated, may hold values from 0 to 1, each once
- attn_gain: bfloat16 [2, 2048], P('section', 'dp'), may hold values from 0.5 to 1.5
- w_query: bfloat16 [2, 2048, 2048], P('section', 'dp', 'tensor'), may hold values from -0.125 to 0.125
- w_key: bfloat16 [2, 2048, 1024], P('section', 'dp', 'tensor'), may hold values from -0.125 to 0.125
- w_value: bfloat16 [2, 2048, 1024], P('section', 'dp', 'tensor'), may hold values from -0.125 to 0.125
- w_out: bfloat16 [2, 2048, 2048], P('section', 'tensor', 'dp'), may hold values from -1.5 to 1.5
- q_gain: bfloat16 [2, 128], P('section'), may hold values from 0.25 to 1.75
- k_gain: bfloat16 [2, 128], P('section'), may hold values from 0.25 to 1.75
- mlp_gain: bfloat16 [2, 2048], P('section', 'dp'), may hold values from 0.5 to 1.5
- w_gate: bfloat16 [2, 2048, 6144], P('section', 'dp', 'tensor'), may hold values from -0.125 to 0.125
- w_up: bfloat16 [2, 2048, 6144], P('section', 'dp', 'tensor'), may hold values from -0.125 to 0.125
- w_down: bfloat16 [2, 6144, 2048], P('section', 'tensor', 'dp'), may hold values from -0.078125 to 0.078125
Outputs:
- layer_out: bfloat16 [2, 2, 1152, 2048], P('section', None, 'dp')
- input_grad: bfloat16 [2, 2, 1152, 2048], P('section', None, 'dp')
- grad_attn_gain: float32 [2, 2048], P('section', 'dp')
- grad_w_query: float32 [2, 2048, 2048], P('section', 'dp', 'tensor')
- grad_w_key: float32 [2, 2048, 1024], P('section', 'dp', 'tensor')
- grad_w_value: float32 [2, 2048, 1024], P('section', 'dp', 'tensor')
- grad_w_out: float32 [2, 2048, 2048], P('section', 'tensor', 'dp')
- grad_q_gain: float32 [2, 128], P('section')
- grad_k_gain: float32 [2, 128], P('section')
- grad_mlp_gain: float32 [2, 2048], P('section', 'dp')
- grad_w_gate: float32 [2, 2048, 6144], P('section', 'dp', 'tensor')
- grad_w_up: float32 [2, 2048, 6144], P('section', 'dp', 'tensor')
- grad_w_down: float32 [2, 6144, 2048], P('section', 'tensor', 'dp')
Inputs may be any that keep to these rules, and one draw needn't show every extreme that they name: `seg_ids`: in each tree the first 512 places hold segment 0, the trunk; the others hold the branch segments 1 to 4 of 96 tokens each and the leaf segments 5 to 8 of 64 tokens each, each segment contiguous, in any order. `parents`: entry s is the parent segment of segment s: 0 for the trunk and every branch, a branch for every leaf.
All inputs are finite; a program needn't handle non-finite values.
Results may differ from a plain program's by a relative error of at most 0.034.
Values may be sent and summed in bfloat16 or wider, within the bound.
A program may use at most 320 MiB of HBM per device.

v0:
```python
from functools import partial

import jax
import jax.numpy as jnp
from jax import lax
from jax.sharding import PartitionSpec as P

HD = 128
TRUNK = 512
BRANCH = 96
NB = 4
TREE = 1152
SEGS = 9


EPSILON = 1e-06
THETA = 1000000.0
MASKED = -1e30


def shifted(array, axis, by):
    size = lax.axis_size(axis)
    pairs = [(i, i + by) for i in range(size) if 0 <= i + by < size]
    return lax.ppermute(array, axis, pairs)


def rms_scale(values, weight_gain):
    mean_sq = jnp.mean(values * values, axis=-1, keepdims=True)
    return values * lax.rsqrt(mean_sq + EPSILON) * weight_gain


def rotate(values, cos_table, sine_table):
    middle_at = values.shape[-1] // 2
    leading = values[..., :middle_at]
    trailing = values[..., middle_at:]
    return jnp.concatenate(
        [leading * cos_table - trailing * sine_table, trailing * cos_table + leading * sine_table],
        axis=-1,
    )


def rope_tables(positions, head_dim):
    half_steps = jnp.arange(head_dim // 2, dtype=jnp.float32)
    inverse = THETA ** (-2.0 * half_steps / head_dim)
    angles = positions.astype(jnp.float32)[:, None] * inverse[None, :]
    return (jnp.cos(angles)[:, None, :], jnp.sin(angles)[:, None, :])


def swiglu(gate_in, up_in):
    return jax.nn.silu(gate_in) * up_in


def tensor_total(partial_sum):
    return lax.psum(partial_sum.astype(jnp.bfloat16), "tensor").astype(jnp.float32)


def embed_heads(q_pre, k_pre, q_scale, k_scale, cos_table, sine_table):
    row_count = q_pre.shape[0]
    queries = rms_scale(q_pre.reshape(row_count, -1, HD), q_scale)
    keys_part = rms_scale(k_pre.reshape(row_count, -1, HD), k_scale)
    return (rotate(queries, cos_table, sine_table), rotate(keys_part, cos_table, sine_table))


def tree_layout(seg_row, parent_row):
    labels = jnp.arange(SEGS, dtype=jnp.int32)
    places = jnp.arange(TREE, dtype=jnp.int32)
    member = seg_row[None, :] == labels[:, None]
    starts = jnp.min(jnp.where(member, places[None, :], TREE), axis=1)
    depth_base = jnp.where(labels == 0, 0, jnp.where(labels <= NB, TRUNK, TRUNK + BRANCH))
    shifts = depth_base - starts
    positions = places + jnp.sum(jnp.where(member, shifts[:, None], 0), axis=0)
    grandparent = jnp.sum(
        jnp.where(parent_row[:, None] == labels[None, :], parent_row[None, :], 0), axis=1
    )
    ancestor = (
        (labels[None, :] == labels[:, None])
        | (labels[None, :] == parent_row[:, None])
        | (labels[None, :] == grandparent[:, None])
    )
    return (positions, member.astype(jnp.float32), ancestor.astype(jnp.float32))


def path_mask(seg_row, parent_row, row_start, row_count):
    positions, member, ancestor = tree_layout(seg_row, parent_row)
    member_rows = lax.dynamic_slice_in_dim(member, row_start, row_count, 1)
    seg_rows = lax.dynamic_slice_in_dim(seg_row, row_start, row_count, 0)
    reach_table = jnp.dot(jnp.dot(member_rows.T, ancestor), member)
    places = jnp.arange(TREE, dtype=jnp.int32)
    row_places = row_start + jnp.arange(row_count, dtype=jnp.int32)
    same_seg = seg_rows[:, None] == seg_row[None, :]
    causal = places[None, :] <= row_places[:, None]
    allowed = (reach_table > 0.5) & (jnp.logical_not(same_seg) | causal)
    row_positions = lax.dynamic_slice_in_dim(positions, row_start, row_count, 0)
    return (allowed, row_positions)


def masked_scores(query_bf, key_all, allowed):
    row_count, local_heads, head_dim = query_bf.shape
    kv_heads = key_all.shape[1] // head_dim
    grouped = query_bf.reshape(row_count, kv_heads, local_heads // kv_heads, head_dim)
    key_heads = key_all.reshape(key_all.shape[0], kv_heads, head_dim)
    raw_scores = jnp.einsum(
        "rkgd,tkd->kgrt", grouped, key_heads, preferred_element_type=jnp.float32
    ) * head_dim ** (-0.5)
    return (jnp.where(allowed[None, None], raw_scores, MASKED), grouped, key_heads)


def layer_forward(hidden_in, weights, q_scale, k_scale, allowed, cos_table, sine_table):
    attn_scale, w_query, w_key, w_value, w_out, mlp_scale, w_gate, w_up, w_down = weights
    residual = hidden_in.astype(jnp.float32)
    normed = rms_scale(residual, attn_scale.astype(jnp.float32)).astype(jnp.bfloat16)
    q_pre = jnp.dot(normed, w_query, preferred_element_type=jnp.float32)
    k_pre = jnp.dot(normed, w_key, preferred_element_type=jnp.float32)
    value_bf = jnp.dot(normed, w_value, preferred_element_type=jnp.float32).astype(jnp.bfloat16)
    queries, keys_rot = embed_heads(q_pre, k_pre, q_scale, k_scale, cos_table, sine_table)
    query_bf = queries.astype(jnp.bfloat16)
    key_bf = keys_rot.reshape(keys_rot.shape[0], -1).astype(jnp.bfloat16)
    key_all, value_all = (
        lax.all_gather(key_bf, "dp", axis=0, tiled=True),
        lax.all_gather(value_bf, "dp", axis=0, tiled=True),
    )
    scores, grouped, key_heads = masked_scores(query_bf, key_all, allowed)
    row_max = jnp.max(scores, axis=-1, keepdims=True)
    exp_scores = jnp.exp(scores - row_max)
    row_total = jnp.sum(exp_scores, axis=-1, keepdims=True)
    prob_bf = (exp_scores / row_total).astype(jnp.bfloat16)
    log_total = row_max + jnp.log(row_total)
    value_heads = value_all.reshape(value_all.shape[0], -1, HD)
    attended = jnp.einsum(
        "kgrt,tkd->rkgd", prob_bf, value_heads, preferred_element_type=jnp.float32
    )
    attended_bf = attended.reshape(attended.shape[0], -1).astype(jnp.bfloat16)
    attn_partial = jnp.dot(attended_bf, w_out, preferred_element_type=jnp.float32)
    kept_attn = tensor_total(attn_partial)
    middle = residual + kept_attn
    mlp_in = rms_scale(middle, mlp_scale.astype(jnp.float32)).astype(jnp.bfloat16)
    gate_pre = jnp.dot(mlp_in, w_gate, preferred_element_type=jnp.float32)
    upward = jnp.dot(mlp_in, w_up, preferred_element_type=jnp.float32)
    hidden_bf = swiglu(gate_pre, upward).astype(jnp.bfloat16)
    mlp_partial = jnp.dot(hidden_bf, w_down, preferred_element_type=jnp.float32)
    output_bf = (middle + tensor_total(mlp_partial)).astype(jnp.bfloat16)
    stored = (
        hidden_in,
        normed,
        q_pre,
        k_pre,
        query_bf,
        key_all,
        value_all,
        log_total,
        attended_bf,
        kept_attn,
        mlp_in,
        gate_pre,
        upward,
        hidden_bf,
    )
    return (output_bf, stored)


def layer_backward(grad_out, stored, weights, q_scale, k_scale, allowed, cos_table, sine_table):
    attn_scale, w_query, w_key, w_value, w_out, mlp_scale, w_gate, w_up, w_down = weights
    (
        hidden_in,
        normed,
        q_pre,
        k_pre,
        query_bf,
        key_all,
        value_all,
        log_total,
        attended_bf,
        kept_attn,
        mlp_in,
        gate_pre,
        upward,
        hidden_bf,
    ) = stored
    outer_dims = (((0,), (0,)), ((), ()))
    inner_dims = (((1,), (1,)), ((), ()))
    grad_mlp = grad_out.astype(jnp.bfloat16)
    grad_down = lax.dot_general(hidden_bf, grad_mlp, outer_dims, preferred_element_type=jnp.float32)
    grad_hidden = lax.dot_general(grad_mlp, w_down, inner_dims, preferred_element_type=jnp.float32)
    _, swiglu_pull = jax.vjp(swiglu, gate_pre, upward)
    grad_gate, grad_upward = swiglu_pull(grad_hidden)
    gate_bf = grad_gate.astype(jnp.bfloat16)
    up_bf = grad_upward.astype(jnp.bfloat16)
    grad_wgate = lax.dot_general(mlp_in, gate_bf, outer_dims, preferred_element_type=jnp.float32)
    grad_wup = lax.dot_general(mlp_in, up_bf, outer_dims, preferred_element_type=jnp.float32)
    mlp_partial = lax.dot_general(
        gate_bf, w_gate, inner_dims, preferred_element_type=jnp.float32
    ) + lax.dot_general(up_bf, w_up, inner_dims, preferred_element_type=jnp.float32)
    residual = hidden_in.astype(jnp.float32)
    middle = residual + kept_attn
    _, mlp_norm_pull = jax.vjp(rms_scale, middle, mlp_scale.astype(jnp.float32))
    grad_middle, feedforward_scale_gradient = mlp_norm_pull(tensor_total(mlp_partial))
    grad_middle = grad_middle + grad_out
    grad_attn = grad_middle.astype(jnp.bfloat16)
    grad_wout = lax.dot_general(
        attended_bf, grad_attn, outer_dims, preferred_element_type=jnp.float32
    )
    grad_attended = lax.dot_general(
        grad_attn, w_out, inner_dims, preferred_element_type=jnp.float32
    ).astype(jnp.bfloat16)
    scores, grouped, key_heads = masked_scores(query_bf, key_all, allowed)
    prob_full = jnp.exp(scores - log_total)
    value_heads = value_all.reshape(value_all.shape[0], -1, HD)
    grad_heads = grad_attended.reshape(grouped.shape)
    grad_prob = jnp.einsum(
        "rkgd,tkd->kgrt", grad_heads, value_heads, preferred_element_type=jnp.float32
    )
    row_dot = jnp.sum(prob_full * grad_prob, axis=-1, keepdims=True)
    grad_scores = (prob_full * (grad_prob - row_dot)).astype(jnp.bfloat16)
    scale_factor = HD ** (-0.5)
    grad_query = (
        jnp.einsum("kgrt,tkd->rkgd", grad_scores, key_heads, preferred_element_type=jnp.float32)
        * scale_factor
    )
    grad_key_all = (
        jnp.einsum("kgrt,rkgd->tkd", grad_scores, grouped, preferred_element_type=jnp.float32)
        * scale_factor
    )
    grad_value_all = jnp.einsum(
        "kgrt,rkgd->tkd",
        prob_full.astype(jnp.bfloat16),
        grad_heads,
        preferred_element_type=jnp.float32,
    )
    grad_key, grad_value = (
        lax.psum_scatter(
            grad_key_all.reshape(grad_key_all.shape[0], -1).astype(jnp.bfloat16),
            "dp",
            scatter_dimension=0,
            tiled=True,
        ).astype(jnp.float32),
        lax.psum_scatter(
            grad_value_all.reshape(grad_value_all.shape[0], -1).astype(jnp.bfloat16),
            "dp",
            scatter_dimension=0,
            tiled=True,
        ).astype(jnp.float32),
    )
    row_count = q_pre.shape[0]
    _, embedding_gradient_pullback = jax.vjp(
        partial(embed_heads, cos_table=cos_table, sine_table=sine_table),
        q_pre,
        k_pre,
        q_scale,
        k_scale,
    )
    query_prenorm_gradient, key_prenorm_gradient, query_scale_gradient, key_scale_gradient = (
        embedding_gradient_pullback(
            (grad_query.reshape(row_count, -1, HD), grad_key.reshape(row_count, -1, HD))
        )
    )
    qpre_bf = query_prenorm_gradient.astype(jnp.bfloat16)
    kpre_bf = key_prenorm_gradient.astype(jnp.bfloat16)
    value_grad_bf = grad_value.astype(jnp.bfloat16)
    grad_wquery = lax.dot_general(normed, qpre_bf, outer_dims, preferred_element_type=jnp.float32)
    grad_wkey = lax.dot_general(normed, kpre_bf, outer_dims, preferred_element_type=jnp.float32)
    grad_wvalue = lax.dot_general(
        normed, value_grad_bf, outer_dims, preferred_element_type=jnp.float32
    )
    attn_partial = (
        lax.dot_general(qpre_bf, w_query, inner_dims, preferred_element_type=jnp.float32)
        + lax.dot_general(kpre_bf, w_key, inner_dims, preferred_element_type=jnp.float32)
        + lax.dot_general(value_grad_bf, w_value, inner_dims, preferred_element_type=jnp.float32)
    )
    _, attn_norm_pull = jax.vjp(rms_scale, residual, attn_scale.astype(jnp.float32))
    grad_residual, attention_scale_gradient = attn_norm_pull(tensor_total(attn_partial))
    incoming_gradient = (grad_residual + grad_middle).astype(jnp.bfloat16)
    weight_pieces = (
        grad_wquery,
        grad_wkey,
        grad_wvalue,
        grad_wout,
        grad_wgate,
        grad_wup,
        grad_down,
    )
    return (
        incoming_gradient,
        weight_pieces,
        (
            query_scale_gradient,
            key_scale_gradient,
            attention_scale_gradient,
            feedforward_scale_gradient,
        ),
    )


def on_device(
    inputs,
    cotangent,
    seg_ids,
    parents,
    order,
    attn_gain,
    w_query,
    w_key,
    w_value,
    w_out,
    q_gain,
    k_gain,
    mlp_gain,
    w_gate,
    w_up,
    w_down,
):
    section_index = lax.axis_index("section")
    data_index = lax.axis_index("dp")
    tensor_index = lax.axis_index("tensor")
    micro_count = inputs.shape[0]
    row_count = inputs.shape[1]
    row_start = data_index * row_count
    first_section = section_index == 0
    gathered = (
        lax.all_gather(attn_gain[0], "dp", axis=0, tiled=True),
        lax.all_gather(w_query[0], "dp", axis=0, tiled=True),
        lax.all_gather(w_key[0], "dp", axis=0, tiled=True),
        lax.all_gather(w_value[0], "dp", axis=0, tiled=True),
        lax.all_gather(w_out[0], "dp", axis=1, tiled=True),
        lax.all_gather(mlp_gain[0], "dp", axis=0, tiled=True),
        lax.all_gather(w_gate[0], "dp", axis=0, tiled=True),
        lax.all_gather(w_up[0], "dp", axis=0, tiled=True),
        lax.all_gather(w_down[0], "dp", axis=1, tiled=True),
    )
    q_scale = q_gain[0].astype(jnp.float32)
    k_scale = k_gain[0].astype(jnp.float32)

    def slot_setup(slot_index):
        tree_id = lax.dynamic_index_in_dim(order, slot_index, 0, keepdims=False)
        seg_row = lax.dynamic_index_in_dim(seg_ids, tree_id, 0, keepdims=False)
        parent_row = lax.dynamic_index_in_dim(parents, tree_id, 0, keepdims=False)
        allowed, row_positions = path_mask(seg_row, parent_row, row_start, row_count)
        cos_table, sine_table = rope_tables(row_positions, HD)
        return (tree_id, allowed, cos_table, sine_table)

    def forward_tick(incoming, tick_index):
        slot_index = jnp.clip(tick_index - section_index, 0, micro_count - 1)
        tree_id, allowed, cos_table, sine_table = slot_setup(slot_index)
        fresh_rows = lax.dynamic_index_in_dim(inputs, tree_id, 0, keepdims=False)
        hidden_in = jnp.where(first_section, fresh_rows, incoming)
        output_bf, stored = layer_forward(
            hidden_in, gathered, q_scale, k_scale, allowed, cos_table, sine_table
        )
        passed = shifted(output_bf, "section", 1)
        return (passed, (output_bf, stored + (allowed, cos_table, sine_table)))

    tick_range = jnp.arange(micro_count + 1, dtype=jnp.int32)
    start_rows = jnp.zeros((row_count, inputs.shape[2]), jnp.bfloat16)
    _, (outputs_all, stored_all) = lax.scan(forward_tick, start_rows, tick_range)
    backward_weights = (
        lax.all_gather(attn_gain[0], "dp", axis=0, tiled=True),
        lax.all_gather(w_query[0], "dp", axis=0, tiled=True),
        lax.all_gather(w_key[0], "dp", axis=0, tiled=True),
        lax.all_gather(w_value[0], "dp", axis=0, tiled=True),
        lax.all_gather(w_out[0], "dp", axis=1, tiled=True),
        lax.all_gather(mlp_gain[0], "dp", axis=0, tiled=True),
        lax.all_gather(w_gate[0], "dp", axis=0, tiled=True),
        lax.all_gather(w_up[0], "dp", axis=0, tiled=True),
        lax.all_gather(w_down[0], "dp", axis=1, tiled=True),
    )
    matrix_zeros = tuple(
        (
            jnp.zeros(weight.shape, jnp.float32)
            for weight in (
                gathered[1],
                gathered[2],
                gathered[3],
                gathered[4],
                gathered[6],
                gathered[7],
                gathered[8],
            )
        )
    )
    gain_zeros = (
        jnp.zeros((HD,), jnp.float32),
        jnp.zeros((HD,), jnp.float32),
        jnp.zeros(gathered[0].shape, jnp.float32),
        jnp.zeros(gathered[5].shape, jnp.float32),
    )

    def backward_tick(carried, step_index):
        incoming, weight_sums, gain_sums = carried
        slot_raw = micro_count - step_index - section_index
        is_valid = (slot_raw >= 0) & (slot_raw < micro_count)
        slot_index = jnp.clip(slot_raw, 0, micro_count - 1)
        tick_index = slot_index + section_index
        stored = jax.tree.map(
            lambda stacked: lax.dynamic_index_in_dim(stacked, tick_index, 0, keepdims=False),
            stored_all,
        )
        allowed, cos_table, sine_table = (stored[-3], stored[-2], stored[-1])
        fresh_rows = lax.dynamic_index_in_dim(cotangent, slot_index, 0, keepdims=False)
        grad_out = jnp.where(first_section, incoming, fresh_rows).astype(jnp.float32)
        incoming_gradient, weight_pieces, gain_parts = layer_backward(
            grad_out,
            stored[:-3],
            backward_weights,
            q_scale,
            k_scale,
            allowed,
            cos_table,
            sine_table,
        )
        weight_sums = tuple(
            (
                running + jnp.where(is_valid, addend, 0.0)
                for running, addend in zip(weight_sums, weight_pieces)
            )
        )
        gain_sums = tuple(
            (
                running + jnp.where(is_valid, addend, 0.0)
                for running, addend in zip(gain_sums, gain_parts)
            )
        )
        passed = shifted(incoming_gradient, "section", -1)
        return ((passed, weight_sums, gain_sums), incoming_gradient)

    (_, weight_sums, gain_sums), grads_all = lax.scan(
        backward_tick, (start_rows, matrix_zeros, gain_zeros), tick_range
    )
    layer_out = lax.dynamic_slice_in_dim(outputs_all, section_index, micro_count, 0)[None]
    input_grad = jnp.flip(
        lax.dynamic_slice_in_dim(grads_all, 1 - section_index, micro_count, 0), axis=0
    )[None]
    summed = (
        lax.psum_scatter(
            weight_sums[0].astype(jnp.bfloat16), "dp", scatter_dimension=0, tiled=True
        ).astype(jnp.float32),
        lax.psum_scatter(
            weight_sums[1].astype(jnp.bfloat16), "dp", scatter_dimension=0, tiled=True
        ).astype(jnp.float32),
        lax.psum_scatter(
            weight_sums[2].astype(jnp.bfloat16), "dp", scatter_dimension=0, tiled=True
        ).astype(jnp.float32),
        lax.psum_scatter(
            weight_sums[3].astype(jnp.bfloat16), "dp", scatter_dimension=1, tiled=True
        ).astype(jnp.float32),
        lax.psum_scatter(
            weight_sums[4].astype(jnp.bfloat16), "dp", scatter_dimension=0, tiled=True
        ).astype(jnp.float32),
        lax.psum_scatter(
            weight_sums[5].astype(jnp.bfloat16), "dp", scatter_dimension=0, tiled=True
        ).astype(jnp.float32),
        lax.psum_scatter(
            weight_sums[6].astype(jnp.bfloat16), "dp", scatter_dimension=1, tiled=True
        ).astype(jnp.float32),
    )
    norm_keep = jnp.where(tensor_index == 0, 1.0, 0.0)
    gain_total = lax.psum(
        (gain_sums[0], gain_sums[1], gain_sums[2] * norm_keep, gain_sums[3] * norm_keep),
        ("dp", "tensor"),
    )
    share_width = attn_gain.shape[1]
    attn_gain_grad = lax.dynamic_slice_in_dim(
        gain_total[2], data_index * share_width, share_width, 0
    )
    mlp_gain_grad = lax.dynamic_slice_in_dim(
        gain_total[3], data_index * share_width, share_width, 0
    )
    return (
        layer_out,
        input_grad,
        attn_gain_grad[None],
        summed[0][None],
        summed[1][None],
        summed[2][None],
        summed[3][None],
        gain_total[0][None],
        gain_total[1][None],
        mlp_gain_grad[None],
        summed[4][None],
        summed[5][None],
        summed[6][None],
    )


def solution(mesh):
    in_specs = (
        P(None, "dp", None),
        P(None, "dp", None),
        P(),
        P(),
        P(),
        P("section", "dp"),
        P("section", "dp", "tensor"),
        P("section", "dp", "tensor"),
        P("section", "dp", "tensor"),
        P("section", "tensor", "dp"),
        P("section", None),
        P("section", None),
        P("section", "dp"),
        P("section", "dp", "tensor"),
        P("section", "dp", "tensor"),
        P("section", "tensor", "dp"),
    )
    out_specs = (
        P("section", None, "dp", None),
        P("section", None, "dp", None),
        P("section", "dp"),
        P("section", "dp", "tensor"),
        P("section", "dp", "tensor"),
        P("section", "dp", "tensor"),
        P("section", "tensor", "dp"),
        P("section", None),
        P("section", None),
        P("section", "dp"),
        P("section", "dp", "tensor"),
        P("section", "dp", "tensor"),
        P("section", "tensor", "dp"),
    )
    return jax.shard_map(
        on_device, mesh=mesh, in_specs=in_specs, out_specs=out_specs, check_vma=False
    )
```

profile of v0, /device:TPU:0, one launch (start us, length us, event | category | flops | bytes accessed | tf_op | source)
XLA Modules:
  0.0 2301.6 jit_solution(312484342322730672)
XLA Ops:
  12.2 13.7 all-gather
  26.5 12.0 all-gather.5
  40.4 29.0 %all-gather.19.cloned.1.call-done = bf16[1,2048,256]{2,1,0:T(8,128)(2,1)} async-done(((bf16[1,512,256]{2,1,0:T(8,128)(2,1)}), bf16[1,2048,256]{2,1,0:T(8,128)(2,1)}) %all-gather.19.cloned.1.call-update) | async-done | bytes 1048592 | tf_op jit(solution)/shard_map/all_gather | solution.py:321
  69.4 47.0 %all-gather.21.cloned.1.call-done = bf16[1,2048,512]{2,1,0:T(8,128)(2,1)} async-done(((bf16[1,512,512]{2,1,0:T(8,128)(2,1)}), bf16[1,2048,512]{2,1,0:T(8,128)(2,1)}) %all-gather.21.cloned.1.call-update) | async-done | bytes 2097168 | tf_op jit(solution)/shard_map/all_gather | solution.py:320
  116.5 46.1 %all-gather.23.cloned.1.call-done = bf16[1,512,2048]{2,1,0:T(8,128)(2,1)} async-done(((bf16[1,512,512]{2,1,0:T(8,128)(2,1)}), bf16[1,512,2048]{2,1,0:T(8,128)(2,1)}) %all-gather.23.cloned.1.call-update) | async-done | bytes 2097168 | tf_op jit(solution)/shard_map/all_gather | solution.py:323
  162.6 115.5 %all-gather.25.cloned.1.call-done = bf16[1,2048,1536]{2,1,0:T(8,128)(2,1)} async-done(((bf16[1,512,1536]{2,1,0:T(8,128)(2,1)}), bf16[1,2048,1536]{2,1,0:T(8,128)(2,1)}) %all-gather.25.cloned.1.call-update) | async-done | bytes 6291472 | tf_op jit(solution)/shard_map/all_gather | solution.py:325
  278.1 115.0 %all-gather.27.cloned.1.call-done = bf16[1,2048,1536]{2,1,0:T(8,128)(2,1)} async-done(((bf16[1,512,1536]{2,1,0:T(8,128)(2,1)}), bf16[1,2048,1536]{2,1,0:T(8,128)(2,1)}) %all-gather.27.cloned.1.call-update) | async-done | bytes 6291472 | tf_op jit(solution)/shard_map/all_gather | solution.py:326
  393.1 115.2 %all-gather.29.cloned.1.call-done = bf16[1,1536,2048]{2,1,0:T(8,128)(2,1)} async-done(((bf16[1,1536,512]{2,1,0:T(8,128)(2,1)}), bf16[1,1536,2048]{2,1,0:T(8,128)(2,1)}) %all-gather.29.cloned.1.call-update) | async-done | bytes 6291472 | tf_op jit(solution)/shard_map/all_gather | solution.py:327
  518.4 617.6 %while.84 = (s32[]{:T(128)}, bf16[288,2048]{1,0:T(8,128)(2,1)}, bf16[3,288,2048]{2,1,0:T(8,128)(2,1)}, bf16[3,288,2048]{2,1,0:T(8,128)(2,1)}, bf16[3,288,2048]{2...) while((s32[]{:T(128)}, bf16[288,2048]{1,0:T(8,128)(2,1)}, ...), condition=%wide.region_12.13_spmd, body=%wide.region_0.12_spmd.sunk | while | flops 7976288256 | bytes 187932592 | solution.py:353
  533.2 16.6 all_gather.61
  558.7 16.4 all_gather.62
  590.5 50.9 %all-reduce.10.cloned.1.call-done = bf16[288,2048]{1,0:T(8,128)(2,1)} async-done(((bf16[288,2048]{1,0:T(8,128)(2,1)}), bf16[288,2048]{1,0:T(8,128)(2,1)}) %all-reduce.10.cloned.1.call-update) | async-done | bytes 1179664 | tf_op jit(solution)/shard_map/while/body/eval_jaxpr/psum | solution.py:54
  661.5 52.3 %all-reduce.12.cloned.1.call-done = bf16[288,2048]{1,0:T(8,128)(2,1)} async-done(((bf16[288,2048]{1,0:T(8,128)(2,1)}), bf16[288,2048]{1,0:T(8,128)(2,1)}) %all-reduce.12.cloned.1.call-update) | async-done | bytes 1179664 | tf_op jit(solution)/shard_map/while/body/eval_jaxpr/psum | solution.py:54
  738.7 15.6 all_gather.61
  763.2 16.3 all_gather.62
  794.9 52.6 %all-reduce.10.cloned.1.call-done = bf16[288,2048]{1,0:T(8,128)(2,1)} async-done(((bf16[288,2048]{1,0:T(8,128)(2,1)}), bf16[288,2048]{1,0:T(8,128)(2,1)}) %all-reduce.10.cloned.1.call-update) | async-done | bytes 1179664 | tf_op jit(solution)/shard_map/while/body/eval_jaxpr/psum | solution.py:54
  867.5 52.3 %all-reduce.12.cloned.1.call-done = bf16[288,2048]{1,0:T(8,128)(2,1)} async-done(((bf16[288,2048]{1,0:T(8,128)(2,1)}), bf16[288,2048]{1,0:T(8,128)(2,1)}) %all-reduce.12.cloned.1.call-update) | async-done | bytes 1179664 | tf_op jit(solution)/shard_map/while/body/eval_jaxpr/psum | solution.py:54
  944.8 15.6 all_gather.61
  969.4 16.3 all_gather.62
  1001.1 52.5 %all-reduce.10.cloned.1.call-done = bf16[288,2048]{1,0:T(8,128)(2,1)} async-done(((bf16[288,2048]{1,0:T(8,128)(2,1)}), bf16[288,2048]{1,0:T(8,128)(2,1)}) %all-reduce.10.cloned.1.call-update) | async-done | bytes 1179664 | tf_op jit(solution)/shard_map/while/body/eval_jaxpr/psum | solution.py:54
  1073.7 52.2 %all-reduce.12.cloned.1.call-done = bf16[288,2048]{1,0:T(8,128)(2,1)} async-done(((bf16[288,2048]{1,0:T(8,128)(2,1)}), bf16[288,2048]{1,0:T(8,128)(2,1)}) %all-reduce.12.cloned.1.call-update) | async-done | bytes 1179664 | tf_op jit(solution)/shard_map/while/body/eval_jaxpr/psum | solution.py:54
  1139.9 658.2 %while.85 = (s32[]{:T(128)}, bf16[288,2048]{1,0:T(8,128)(2,1)}, f32[2048,512]{1,0:T(8,128)}, f32[2048,256]{1,0:T(8,128)}, f32[2048,256]{1,0:T(8,128)}, /*index=5...) while((s32[]{:T(128)}, bf16[288,2048]{1,0:T(8,128)(2,1)}, ...), condition=%wide.region_31.32_spmd.clone, body=%wide.region_13.31_spmd.clone.sunk | while | flops 16286356480 | bytes 461959840 | solution.py:424
  1189.5 9.7 select_add_fusion.16
  1199.2 8.1 select_add_fusion.17
  1216.8 7.8 select_add_fusion.18
  1224.6 9.8 all-reduce.14.cloned.1.call-done
  1287.1 16.5 reduce-scatter.34.cloned.1.call-done
  1316.2 44.2 %all-reduce.16.cloned.1.call-done = bf16[288,2048]{1,0:T(8,128)(2,1)} async-done(((bf16[288,2048]{1,0:T(8,128)(2,1)}), bf16[288,2048]{1,0:T(8,128)(2,1)}) %all-reduce.16.cloned.1.call-update) | async-done | bytes 1179664 | tf_op jit(solution)/shard_map/while/body/eval_jaxpr/psum | solution.py:54
  1398.5 13.5 select_add_fusion.16
  1412.0 9.7 select_add_fusion.17
  1431.2 9.8 select_add_fusion.18
  1484.0 7.6 reduce-scatter.32.cloned.1.call-done
  1497.7 16.4 reduce-scatter.34.cloned.1.call-done
  1529.3 41.6 %all-reduce.16.cloned.1.call-done = bf16[288,2048]{1,0:T(8,128)(2,1)} async-done(((bf16[288,2048]{1,0:T(8,128)(2,1)}), bf16[288,2048]{1,0:T(8,128)(2,1)}) %all-reduce.16.cloned.1.call-update) | async-done | bytes 1179664 | tf_op jit(solution)/shard_map/while/body/eval_jaxpr/psum | solution.py:54
  1609.0 13.5 select_add_fusion.16
  1622.5 9.7 select_add_fusion.17
  1641.7 9.8 select_add_fusion.18
  1694.5 7.6 reduce-scatter.32.cloned.1.call-done
  1708.2 16.5 reduce-scatter.34.cloned.1.call-done
  1739.7 41.6 %all-reduce.16.cloned.1.call-done = bf16[288,2048]{1,0:T(8,128)(2,1)} async-done(((bf16[288,2048]{1,0:T(8,128)(2,1)}), bf16[288,2048]{1,0:T(8,128)(2,1)}) %all-reduce.16.cloned.1.call-update) | async-done | bytes 1179664 | tf_op jit(solution)/shard_map/while/body/eval_jaxpr/psum | solution.py:54
  1810.0 8.0 convert_element_type.301
  1818.0 8.1 convert_element_type.302
  1826.1 8.4 convert_element_type.303
  1835.8 78.7 %all-reduce.4 = (f32[2048]{0:T(1024)}, f32[1,128]{1,0:T(1,128)}, f32[1,128]{1,0:T(1,128)}, f32[2048]{0:T(1024)S(1)}) all-reduce(f32[2048]{0:T(1024)} %broadcast_multiply_fusion.1, f32[1,128]{1,0:T(1,128)} %bitcast.507, f32[1,128]{1,0:T(1,128)} %bitcast.508, ...), channel_id=1, replica_groups=mesh['section'=2,'dp'=4,'tensor'=4] {'dp','tensor'}, use_global_device_ids=true, to_apply=%region_32.33 | all-reduce | flops 4352 | bytes 34816 | tf_op jit(solution)/shard_map/psum | solution.py:455
  1926.9 25.0 %reduce-scatter.24.cloned.1.call-done = bf16[512,512]{1,0:T(8,128)(2,1)} async-done(((bf16[512,2048]{1,0:T(8,128)(2,1)}), bf16[512,512]{1,0:T(8,128)(2,1)}) %reduce-scatter.24.cloned.1.call-update) | async-done | bytes 524304 | tf_op jit(solution)/shard_map/reduce_scatter | solution.py:441
  1954.0 110.1 %reduce-scatter.26.cloned.1.call-done = bf16[512,1536]{1,0:T(8,128)(2,1)} async-done(((bf16[2048,1536]{1,0:T(8,128)(2,1)}), bf16[512,1536]{1,0:T(8,128)(2,1)}) %reduce-scatter.26.cloned.1.call-update) | async-done | bytes 1572880 | tf_op jit(solution)/shard_map/reduce_scatter | solution.py:444
  2067.6 110.1 %reduce-scatter.28.cloned.1.call-done = bf16[512,1536]{1,0:T(8,128)(2,1)} async-done(((bf16[2048,1536]{1,0:T(8,128)(2,1)}), bf16[512,1536]{1,0:T(8,128)(2,1)}) %reduce-scatter.28.cloned.1.call-update) | async-done | bytes 1572880 | tf_op jit(solution)/shard_map/reduce_scatter | solution.py:447
  2181.2 110.1 %reduce-scatter.30.cloned.1.call-done = bf16[1536,512]{1,0:T(8,128)(2,1)} async-done(((bf16[1536,2048]{1,0:T(8,128)(2,1)}), bf16[1536,512]{1,0:T(8,128)(2,1)}) %reduce-scatter.30.cloned.1.call-update) | async-done | bytes 1572880 | tf_op jit(solution)/shard_map/reduce_scatter | solution.py:450
  (1124 shorter events, 590.4 us)
Async XLA Ops:
  7.2 33.3 %all-gather.17.cloned.1.call-start = ((), (), s32[]{:S(2)}) async-start(), calls=%async_computation.16 | async-start | bytes 1310720 | tf_op jit(solution)/shard_map/all_gather | solution.py:322
  7.9 61.5 %all-gather.19.cloned.1.call-start = ((), (), s32[]{:S(2)}) async-start(), calls=%async_computation.17 | async-start | bytes 1310720 | tf_op jit(solution)/shard_map/all_gather | solution.py:321
  8.7 107.8 %all-gather.21.cloned.1.call-start = ((), (), s32[]{:S(2)}) async-start(), calls=%async_computation.18 | async-start | bytes 2621440 | tf_op jit(solution)/shard_map/all_gather | solution.py:320
  9.4 153.2 %all-gather.23.cloned.1.call-start = ((), (), s32[]{:S(2)}) async-start(), calls=%async_computation.19 | async-start | bytes 2621440 | tf_op jit(solution)/shard_map/all_gather | solution.py:323
  10.0 29.1 %copy-start.90 = (bf16[1,128]{1,0:T(2,128)(2,1)S(1)}, bf16[1,128]{1,0:T(2,128)(2,1)}, u32[]{:S(2)}) copy-start(bf16[1,128]{1,0:T(2,128)(2,1)} %param.31) | copy-start | bytes 772
  10.0 29.1 %copy-start.91 = (bf16[1,128]{1,0:T(2,128)(2,1)S(1)}, bf16[1,128]{1,0:T(2,128)(2,1)}, u32[]{:S(2)}) copy-start(bf16[1,128]{1,0:T(2,128)(2,1)} %param.30) | copy-start | bytes 772
  10.0 268.1 %all-gather.25.cloned.1.call-start = ((), (), s32[]{:S(2)}) async-start(), calls=%async_computation.20 | async-start | bytes 7864320 | tf_op jit(solution)/shard_map/all_gather | solution.py:325
  10.6 382.5 %all-gather.27.cloned.1.call-start = ((), (), s32[]{:S(2)}) async-start(), calls=%async_computation.21 | async-start | bytes 7864320 | tf_op jit(solution)/shard_map/all_gather | solution.py:326
  11.2 497.1 %all-gather.29.cloned.1.call-start = ((), (), s32[]{:S(2)}) async-start(), calls=%async_computation.22 | async-start | bytes 7864320 | tf_op jit(solution)/shard_map/all_gather | solution.py:327
  518.4 36.4 %copy-start.76 = (f32[128]{0:T(128)}, f32[128]{0:T(128)S(1)}, u32[]{:S(2)}) copy-start(f32[128]{0:T(128)S(1)} %get-tuple-element.2337) | copy-start | bytes 1540 | tf_op jit(solution)/shard_map/while
  518.4 123.0 %all-reduce.10.cloned.1.call-start = ((), (), s32[]{:S(2)}) async-start(), calls=%async_computation.23 | async-start | bytes 2359296 | tf_op jit(solution)/shard_map/while/body/eval_jaxpr/psum | solution.py:54
  527.5 30.6 %copy-start.71 = (f32[288]{0:T(512)}, f32[288]{0:T(512)S(1)}, u32[]{:S(2)}) copy-start(f32[288]{0:T(512)S(1)} %add_rsqrt_fusion.8) | copy-start | bytes 3460 | tf_op jit(solution)/shard_map/while
  531.7 22.4 copy-start.62
  587.9 125.9 %all-reduce.12.cloned.1.call-start = ((), (), s32[]{:S(2)}) async-start(), calls=%async_computation.24 | async-start | bytes 2359296 | tf_op jit(solution)/shard_map/while/body/eval_jaxpr/psum | solution.py:54
  716.8 7.0 collective-permute-start
  723.9 35.4 %copy-start.76 = (f32[128]{0:T(128)}, f32[128]{0:T(128)S(1)}, u32[]{:S(2)}) copy-start(f32[128]{0:T(128)S(1)} %get-tuple-element.2337) | copy-start | bytes 1540 | tf_op jit(solution)/shard_map/while
  723.9 123.6 %all-reduce.10.cloned.1.call-start = ((), (), s32[]{:S(2)}) async-start(), calls=%async_computation.23 | async-start | bytes 2359296 | tf_op jit(solution)/shard_map/while/body/eval_jaxpr/psum | solution.py:54
  733.0 29.6 %copy-start.71 = (f32[288]{0:T(512)}, f32[288]{0:T(512)S(1)}, u32[]{:S(2)}) copy-start(f32[288]{0:T(512)S(1)} %add_rsqrt_fusion.8) | copy-start | bytes 3460 | tf_op jit(solution)/shard_map/while
  792.3 127.5 %all-reduce.12.cloned.1.call-start = ((), (), s32[]{:S(2)}) async-start(), calls=%async_computation.24 | async-start | bytes 2359296 | tf_op jit(solution)/shard_map/while/body/eval_jaxpr/psum | solution.py:54
  922.8 7.1 collective-permute-start
  929.9 35.4 %copy-start.76 = (f32[128]{0:T(128)}, f32[128]{0:T(128)S(1)}, u32[]{:S(2)}) copy-start(f32[128]{0:T(128)S(1)} %get-tuple-element.2337) | copy-start | bytes 1540 | tf_op jit(solution)/shard_map/while
  930.0 123.6 %all-reduce.10.cloned.1.call-start = ((), (), s32[]{:S(2)}) async-start(), calls=%async_computation.23 | async-start | bytes 2359296 | tf_op jit(solution)/shard_map/while/body/eval_jaxpr/psum | solution.py:54
  939.1 29.6 %copy-start.71 = (f32[288]{0:T(512)}, f32[288]{0:T(512)S(1)}, u32[]{:S(2)}) copy-start(f32[288]{0:T(512)S(1)} %add_rsqrt_fusion.8) | copy-start | bytes 3460 | tf_op jit(solution)/shard_map/while
  998.4 127.6 %all-reduce.12.cloned.1.call-start = ((), (), s32[]{:S(2)}) async-start(), calls=%async_computation.24 | async-start | bytes 2359296 | tf_op jit(solution)/shard_map/while/body/eval_jaxpr/psum | solution.py:54
  1128.9 7.0 collective-permute-start
  1163.5 70.9 %all-reduce.14.cloned.1.call-start = ((), (), s32[]{:S(2)}) async-start(), calls=%async_computation.25 | async-start | bytes 2359296 | tf_op jit(solution)/shard_map/while/body/eval_jaxpr/psum | solution.py:54
  1179.8 101.3 %reduce-scatter.32.cloned.1.call-start = ((), (), s32[]{:S(2)}) async-start(), calls=%async_computation.26 | async-start | bytes 737280 | tf_op jit(solution)/shard_map/while
  1259.0 44.7 %reduce-scatter.34.cloned.1.call-start = ((), (), s32[]{:S(2)}) async-start(), calls=%async_computation.27 | async-start | bytes 737280 | tf_op jit(solution)/shard_map/while
  1273.4 86.9 %all-reduce.16.cloned.1.call-start = ((), (), s32[]{:S(2)}) async-start(), calls=%async_computation.28 | async-start | bytes 2359296 | tf_op jit(solution)/shard_map/while/body/eval_jaxpr/psum | solution.py:54
  1366.4 4.9 collective-permute-start.1
  1372.6 72.3 %all-reduce.14.cloned.1.call-start = ((), (), s32[]{:S(2)}) async-start(), calls=%async_computation.25 | async-start | bytes 2359296 | tf_op jit(solution)/shard_map/while/body/eval_jaxpr/psum | solution.py:54
  1388.9 102.8 %reduce-scatter.32.cloned.1.call-start = ((), (), s32[]{:S(2)}) async-start(), calls=%async_computation.26 | async-start | bytes 737280 | tf_op jit(solution)/shard_map/while
  1469.5 44.6 %reduce-scatter.34.cloned.1.call-start = ((), (), s32[]{:S(2)}) async-start(), calls=%async_computation.27 | async-start | bytes 737280 | tf_op jit(solution)/shard_map/while
  1484.0 86.9 %all-reduce.16.cloned.1.call-start = ((), (), s32[]{:S(2)}) async-start(), calls=%async_computation.28 | async-start | bytes 2359296 | tf_op jit(solution)/shard_map/while/body/eval_jaxpr/psum | solution.py:54
  1576.9 4.9 collective-permute-start.1
  1583.1 72.3 %all-reduce.14.cloned.1.call-start = ((), (), s32[]{:S(2)}) async-start(), calls=%async_computation.25 | async-start | bytes 2359296 | tf_op jit(solution)/shard_map/while/body/eval_jaxpr/psum | solution.py:54
  1599.3 102.8 %reduce-scatter.32.cloned.1.call-start = ((), (), s32[]{:S(2)}) async-start(), calls=%async_computation.26 | async-start | bytes 737280 | tf_op jit(solution)/shard_map/while
  1680.0 44.6 %reduce-scatter.34.cloned.1.call-start = ((), (), s32[]{:S(2)}) async-start(), calls=%async_computation.27 | async-start | bytes 737280 | tf_op jit(solution)/shard_map/while
  1694.4 86.9 %all-reduce.16.cloned.1.call-start = ((), (), s32[]{:S(2)}) async-start(), calls=%async_computation.28 | async-start | bytes 2359296 | tf_op jit(solution)/shard_map/while/body/eval_jaxpr/psum | solution.py:54
  1787.4 4.9 collective-permute-start.1
  1798.1 123.1 %reduce-scatter.20.cloned.1.call-start = ((), (), s32[]{:S(2)}) async-start(), calls=%async_computation.10 | async-start | bytes 1310720 | tf_op jit(solution)/shard_map/reduce_scatter | solution.py:435
  1801.0 122.0 %reduce-scatter.22.cloned.1.call-start = ((), (), s32[]{:S(2)}) async-start(), calls=%async_computation.11 | async-start | bytes 1310720 | tf_op jit(solution)/shard_map/reduce_scatter | solution.py:438
  1802.2 122.6 %reduce-scatter.18.cloned.1.call-start = ((), (), s32[]{:S(2)}) async-start(), calls=%async_computation.9 | async-start | bytes 2621440 | tf_op jit(solution)/shard_map/reduce_scatter | solution.py:432
  1806.0 145.8 %reduce-scatter.24.cloned.1.call-start = ((), (), s32[]{:S(2)}) async-start(), calls=%async_computation.12 | async-start | bytes 2621440 | tf_op jit(solution)/shard_map/reduce_scatter | solution.py:441
  1809.9 254.2 %reduce-scatter.26.cloned.1.call-start = ((), (), s32[]{:S(2)}) async-start(), calls=%async_computation.13 | async-start | bytes 7864320 | tf_op jit(solution)/shard_map/reduce_scatter | solution.py:444
  1818.0 359.8 %reduce-scatter.28.cloned.1.call-start = ((), (), s32[]{:S(2)}) async-start(), calls=%async_computation.14 | async-start | bytes 7864320 | tf_op jit(solution)/shard_map/reduce_scatter | solution.py:447
  1826.1 465.3 %reduce-scatter.30.cloned.1.call-start = ((), (), s32[]{:S(2)}) async-start(), calls=%async_computation.15 | async-start | bytes 7864320 | tf_op jit(solution)/shard_map/reduce_scatter | solution.py:450
  1834.5 82.0 %copy-start.45 = (bf16[3,288,2048]{2,1,0:T(8,128)(2,1)S(1)}, bf16[3,288,2048]{2,1,0:T(8,128)(2,1)}, u32[]{:S(2)}) copy-start(bf16[3,288,2048]{2,1,0:T(8,128)(2,1)} %get-tuple-element.875) | copy-start | bytes 10616836
  (282 other events, 1445.1 us)
Sparse Core Ops, SparseCore 0:
  9.6 30.8 all-gather.16
  42.0 27.3 all-gather.18
  71.0 45.4 all-gather.20
  117.9 44.6 all-gather.22
  164.0 114.0 all-gather.24
  279.5 113.5 all-gather.26
  394.7 113.5 all-gather.28
  588.0 53.4 all-reduce.9
  659.3 54.4 all-reduce.11
  792.4 55.0 all-reduce.9
  865.3 54.4 all-reduce.11
  998.5 55.0 all-reduce.9
  1071.4 54.4 all-reduce.11
  1179.9 54.4 all-reduce.13
  1259.1 21.9 reduce-scatter.31
  1283.3 20.3 reduce-scatter.33
  1307.4 52.9 all-reduce.15
  1389.0 55.8 all-reduce.13
  1469.6 21.9 reduce-scatter.31
  1493.9 20.2 reduce-scatter.33
  1517.9 52.8 all-reduce.15
  1599.5 55.8 all-reduce.13
  1680.1 21.9 reduce-scatter.31
  1704.3 20.2 reduce-scatter.33
  1728.4 52.8 all-reduce.15
  1801.5 28.9 reduce-scatter.19
  1833.3 26.1 reduce-scatter.21
  1862.4 42.9 reduce-scatter.17
  1908.4 43.4 reduce-scatter.23
  1954.0 110.0 reduce-scatter.25
  2066.4 111.2 reduce-scatter.27
  2180.1 111.2 reduce-scatter.29
where the time goes:
time: 2320 us; the launch traced here: 2300 us
  waiting for transfers between devices  1360 us (59%)
  matrix products  314 us (14%)
  other arithmetic  208 us (9%)
  blocking collectives  201 us (9%)
  local copies, waits for them, and re-layouts  150 us (6%)
  loops' own time  42 us (2%)
    psum x12, waiting for transfers between devices, tensor_total(): lax.psum(partial_sum.astype(jnp.bfloat16), 'tensor').astype(jnp.float32)  458 us
    all_gather x1, waiting for transfers between devices, on_device(): lax.all_gather(w_gate[0], 'dp', axis=0, tiled=True)  116 us
    all_gather x1, waiting for transfers between devices, on_device(): lax.all_gather(w_down[0], 'dp', axis=1, tiled=True)  115 us
    all_gather x1, waiting for transfers between devices, on_device(): lax.all_gather(w_up[0], 'dp', axis=0, tiled=True)  115 us
    reduce_scatter x1, waiting for transfers between devices, on_device(): lax.psum_scatter(weight_sums[6].astype(jnp.bfloat16), 'dp', scatter_dimen...  110 us
    reduce_scatter x1, waiting for transfers between devices, on_device(): lax.psum_scatter(weight_sums[5].astype(jnp.bfloat16), 'dp', scatter_dimen...  110 us
    reduce_scatter x1, waiting for transfers between devices, on_device(): lax.psum_scatter(weight_sums[4].astype(jnp.bfloat16), 'dp', scatter_dimen...  110 us
    psum x1, blocking collectives, on_device(): lax.psum((gain_sums[0], gain_sums[1], gain_sums[2] * norm_keep, gain_sums...  78.7 us
  transfers between devices with their start and end apart: 38, of which 29 were waited for; matrix products, arithmetic and copies ran while one was open for 14% of the time, Pallas kernels for 0%

commit v1 on v0

v1 whole, which is shorter than its diff:
```python
from functools import partial

import jax
import jax.numpy as jnp
from jax import lax
from jax.sharding import PartitionSpec as P

HD = 128
TRUNK = 512
BRANCH = 96
NB = 4
TREE = 1152
SEGS = 9


EPSILON = 1e-06
THETA = 1000000.0
MASKED = -1e30
F32 = jnp.float32
BF16 = jnp.bfloat16


def rms_scale(values, weight_gain):
    mean_sq = jnp.mean(values * values, axis=-1, keepdims=True)
    return values * lax.rsqrt(mean_sq + EPSILON) * weight_gain


def rotate(values, cos_table, sine_table):
    middle_at = values.shape[-1] // 2
    leading = values[..., :middle_at]
    trailing = values[..., middle_at:]
    return jnp.concatenate(
        [leading * cos_table - trailing * sine_table, trailing * cos_table + leading * sine_table],
        axis=-1,
    )


def rope_tables(positions, head_dim):
    half_steps = jnp.arange(head_dim // 2, dtype=F32)
    inverse = THETA ** (-2.0 * half_steps / head_dim)
    angles = positions.astype(F32)[:, None] * inverse[None, :]
    return (jnp.cos(angles)[:, None, :], jnp.sin(angles)[:, None, :])


def swiglu(gate_in, up_in):
    return jax.nn.silu(gate_in) * up_in


def embed_heads(q_pre, k_pre, q_scale, k_scale, cos_table, sine_table):
    row_count = q_pre.shape[0]
    queries = rms_scale(q_pre.reshape(row_count, -1, HD), q_scale)
    keys_part = rms_scale(k_pre.reshape(row_count, -1, HD), k_scale)
    return (rotate(queries, cos_table, sine_table), rotate(keys_part, cos_table, sine_table))


def tree_layout(seg_row, parent_row):
    labels = jnp.arange(SEGS, dtype=jnp.int32)
    places = jnp.arange(TREE, dtype=jnp.int32)
    member = seg_row[None, :] == labels[:, None]
    starts = jnp.min(jnp.where(member, places[None, :], TREE), axis=1)
    depth_base = jnp.where(labels == 0, 0, jnp.where(labels <= NB, TRUNK, TRUNK + BRANCH))
    shifts = depth_base - starts
    positions = places + jnp.sum(jnp.where(member, shifts[:, None], 0), axis=0)
    grandparent = jnp.sum(
        jnp.where(parent_row[:, None] == labels[None, :], parent_row[None, :], 0), axis=1
    )
    ancestor = (
        (labels[None, :] == labels[:, None])
        | (labels[None, :] == parent_row[:, None])
        | (labels[None, :] == grandparent[:, None])
    )
    return (positions, member.astype(F32), ancestor.astype(F32))


def path_mask(seg_row, parent_row, row_start, row_count):
    positions, member, ancestor = tree_layout(seg_row, parent_row)
    member_rows = lax.dynamic_slice_in_dim(member, row_start, row_count, 1)
    seg_rows = lax.dynamic_slice_in_dim(seg_row, row_start, row_count, 0)
    reach_table = jnp.dot(jnp.dot(member_rows.T, ancestor), member)
    places = jnp.arange(TREE, dtype=jnp.int32)
    row_places = row_start + jnp.arange(row_count, dtype=jnp.int32)
    same_seg = seg_rows[:, None] == seg_row[None, :]
    causal = places[None, :] <= row_places[:, None]
    allowed = (reach_table > 0.5) & (jnp.logical_not(same_seg) | causal)
    row_positions = lax.dynamic_slice_in_dim(positions, row_start, row_count, 0)
    return (allowed, row_positions)


OUTER = (((0,), (0,)), ((), ()))
INNER = (((1,), (1,)), ((), ()))


def dot(left, right):
    return jnp.dot(left, right, preferred_element_type=F32)


def dot_inner(left, right):
    return lax.dot_general(left, right, INNER, preferred_element_type=F32)


def dot_outer(left, right):
    return lax.dot_general(left, right, OUTER, preferred_element_type=F32)


def exchange(pieces, axis):
    size = lax.axis_size(axis)
    me = lax.axis_index(axis)
    got = jnp.zeros_like(pieces)
    own = lax.dynamic_index_in_dim(pieces, me, 0, keepdims=True)
    got = lax.dynamic_update_slice_in_dim(got, own, me, 0)
    for step in range(1, size):
        other = me ^ step
        piece = lax.dynamic_index_in_dim(pieces, other, 0, keepdims=True)
        arrived = lax.ppermute(piece, axis, [(i, i ^ step) for i in range(size)])
        got = lax.dynamic_update_slice_in_dim(got, arrived, other, 0)
    return got


def masked_scores(query_bf, key_all, allowed):
    row_count = query_bf.shape[0]
    kv_heads = key_all.shape[1] // HD
    grouped = query_bf.reshape(row_count, kv_heads, -1, HD)
    key_heads = key_all.reshape(key_all.shape[0], kv_heads, HD)
    raw_scores = jnp.einsum(
        "rkgd,tkd->kgrt", grouped, key_heads, preferred_element_type=F32
    ) * HD ** (-0.5)
    return (jnp.where(allowed[None, None], raw_scores, MASKED), grouped, key_heads)


def layer_forward(hidden_in, weights, gains, slot):
    attn_scale, q_scale, k_scale, mlp_scale = gains
    w_qkv, w_outt, w_gate, w_up, w_downt, q_width, k_width = weights
    allowed, cos_table, sine_table = slot
    residual = hidden_in.astype(F32)
    normed = rms_scale(residual, attn_scale).astype(BF16)
    qkv = dot(normed, w_qkv)
    q_pre = qkv[:, :q_width]
    k_pre = qkv[:, q_width : q_width + k_width]
    value_bf = qkv[:, q_width + k_width :].astype(BF16)
    queries, keys_rot = embed_heads(q_pre, k_pre, q_scale, k_scale, cos_table, sine_table)
    query_bf = queries.astype(BF16)
    key_bf = keys_rot.reshape(keys_rot.shape[0], -1).astype(BF16)
    kv_all = lax.all_gather(jnp.concatenate([key_bf, value_bf], axis=1), "dp", axis=0, tiled=True)
    key_all = kv_all[:, :k_width]
    value_all = kv_all[:, k_width:]
    scores, grouped, key_heads = masked_scores(query_bf, key_all, allowed)
    row_max = jnp.max(scores, axis=-1, keepdims=True)
    exp_scores = jnp.exp(scores - row_max)
    row_total = jnp.sum(exp_scores, axis=-1, keepdims=True)
    prob_bf = (exp_scores / row_total).astype(BF16)
    log_total = row_max + jnp.log(row_total)
    value_heads = value_all.reshape(value_all.shape[0], -1, HD)
    attended = jnp.einsum("kgrt,tkd->rkgd", prob_bf, value_heads, preferred_element_type=F32)
    attended_bf = attended.reshape(attended.shape[0], -1).astype(BF16)
    attn_partial = dot_inner(attended_bf, w_outt).astype(BF16)
    attn_rows = lax.psum_scatter(attn_partial, "tensor", scatter_dimension=0, tiled=True)
    own_rows = attn_rows.shape[0]
    own_in = lax.dynamic_slice_in_dim(
        hidden_in, lax.axis_index("tensor") * own_rows, own_rows, 0
    ).astype(F32)
    middle = own_in + attn_rows.astype(F32)
    mlp_in = lax.all_gather(
        rms_scale(middle, mlp_scale).astype(BF16), "dp", axis=0, tiled=True
    )
    gate_pre = dot(mlp_in, w_gate)
    upward = dot(mlp_in, w_up)
    hidden_bf = swiglu(gate_pre, upward).astype(BF16)
    mlp_partial = dot_inner(hidden_bf, w_downt).astype(BF16)
    mlp_rows = lax.psum_scatter(mlp_partial, "dp", scatter_dimension=0, tiled=True)
    output_own = (middle + mlp_rows.astype(F32)).astype(BF16)
    output_bf = lax.all_gather(output_own, "tensor", axis=0, tiled=True)
    stored = (
        own_in, normed, q_pre, k_pre, query_bf, key_all, value_all, log_total, attended_bf,
        middle, mlp_in, gate_pre, upward, hidden_bf,
    )
    return (output_bf, stored)


def layer_backward(grad_out, stored, weights, gains, slot):
    attn_scale, q_scale, k_scale, mlp_scale = gains
    w_qkv, w_outt, w_gate, w_up, w_downt, q_width, k_width = weights
    allowed, cos_table, sine_table = slot
    (
        own_in, normed, q_pre, k_pre, query_bf, key_all, value_all, log_total, attended_bf,
        middle, mlp_in, gate_pre, upward, hidden_bf,
    ) = stored
    own_rows = own_in.shape[0]
    own_grad = lax.dynamic_slice_in_dim(
        grad_out, lax.axis_index("tensor") * own_rows, own_rows, 0
    )
    grad_mlp = lax.all_gather(own_grad, "dp", axis=0, tiled=True)
    grad_hidden = dot(grad_mlp, w_downt)
    _, swiglu_pull = jax.vjp(swiglu, gate_pre, upward)
    grad_gate, grad_upward = swiglu_pull(grad_hidden)
    gate_bf = grad_gate.astype(BF16)
    up_bf = grad_upward.astype(BF16)
    mlp_partial = (dot_inner(gate_bf, w_gate) + dot_inner(up_bf, w_up)).astype(BF16)
    mlp_rows = lax.psum_scatter(mlp_partial, "dp", scatter_dimension=0, tiled=True)
    _, mlp_norm_pull = jax.vjp(rms_scale, middle, mlp_scale)
    grad_middle, grad_mlp_scale = mlp_norm_pull(mlp_rows.astype(F32))
    grad_middle = grad_middle + own_grad.astype(F32)
    grad_attn = lax.all_gather(grad_middle.astype(BF16), "tensor", axis=0, tiled=True)
    grad_attended = dot(grad_attn, w_outt).astype(BF16)
    scores, grouped, key_heads = masked_scores(query_bf, key_all, allowed)
    prob_full = jnp.exp(scores - log_total)
    value_heads = value_all.reshape(value_all.shape[0], -1, HD)
    grad_heads = grad_attended.reshape(grouped.shape)
    grad_prob = jnp.einsum(
        "rkgd,tkd->kgrt", grad_heads, value_heads, preferred_element_type=F32
    )
    row_dot = jnp.sum(prob_full * grad_prob, axis=-1, keepdims=True)
    grad_scores = (prob_full * (grad_prob - row_dot)).astype(BF16)
    scale_factor = HD ** (-0.5)
    grad_query = (
        jnp.einsum("kgrt,tkd->rkgd", grad_scores, key_heads, preferred_element_type=F32)
        * scale_factor
    )
    grad_key_all = (
        jnp.einsum("kgrt,rkgd->tkd", grad_scores, grouped, preferred_element_type=F32)
        * scale_factor
    )
    grad_value_all = jnp.einsum(
        "kgrt,rkgd->tkd", prob_full.astype(BF16), grad_heads, preferred_element_type=F32
    )
    tree_rows = grad_key_all.shape[0]
    grad_kv = lax.psum_scatter(
        jnp.concatenate(
            [grad_key_all.reshape(tree_rows, -1), grad_value_all.reshape(tree_rows, -1)], axis=1
        ).astype(BF16),
        "dp",
        scatter_dimension=0,
        tiled=True,
    )
    grad_key = grad_kv[:, :k_width].astype(F32)
    value_grad_bf = grad_kv[:, k_width:]
    row_count = q_pre.shape[0]
    _, embedding_pull = jax.vjp(
        partial(embed_heads, cos_table=cos_table, sine_table=sine_table),
        q_pre, k_pre, q_scale, k_scale,
    )
    grad_q_pre, grad_k_pre, grad_q_scale, grad_k_scale = embedding_pull(
        (grad_query.reshape(row_count, -1, HD), grad_key.reshape(row_count, -1, HD))
    )
    qkv_grad = jnp.concatenate(
        [grad_q_pre.astype(BF16), grad_k_pre.astype(BF16), value_grad_bf], axis=1
    )
    attn_partial = dot_inner(qkv_grad, w_qkv).astype(BF16)
    attn_rows = lax.psum_scatter(attn_partial, "tensor", scatter_dimension=0, tiled=True)
    _, attn_norm_pull = jax.vjp(rms_scale, own_in, attn_scale)
    grad_residual, grad_attn_scale = attn_norm_pull(attn_rows.astype(F32))
    incoming_own = (grad_residual + grad_middle).astype(BF16)
    incoming = lax.all_gather(incoming_own, "tensor", axis=0, tiled=True)
    products = (
        (normed, qkv_grad),
        (grad_attn, attended_bf),
        (mlp_in, gate_bf),
        (mlp_in, up_bf),
        (grad_mlp, hidden_bf),
    )
    return (incoming, products, (grad_q_scale, grad_k_scale, grad_attn_scale, grad_mlp_scale))


def on_device(
    inputs, cotangent, seg_ids, parents, order, attn_gain, w_query, w_key, w_value, w_out,
    q_gain, k_gain, mlp_gain, w_gate, w_up, w_down,
):
    section_index = lax.axis_index("section")
    data_index = lax.axis_index("dp")
    dp_size = lax.axis_size("dp")
    tensor_size = lax.axis_size("tensor")
    micro_count, row_count, depth = inputs.shape
    row_start = data_index * row_count
    first_section = section_index == 0
    q_width = w_query.shape[2]
    k_width = w_key.shape[2]
    own_depth = w_query.shape[1]
    own_units = w_gate.shape[2]
    share = own_units // dp_size

    gains_all = lax.all_gather(
        jnp.concatenate([attn_gain, mlp_gain], axis=0), "dp", axis=1, tiled=True
    ).astype(F32)
    gains = (gains_all[0], q_gain[0].astype(F32), k_gain[0].astype(F32), gains_all[1])

    attn_shard = jnp.concatenate([w_query[0], w_key[0], w_value[0], w_out[0].T], axis=1)
    attn_all = lax.all_gather(attn_shard, "dp", axis=0, tiled=True)
    qkv_width = q_width + 2 * k_width
    w_qkv = attn_all[:, :qkv_width]
    w_outt = attn_all[:, qkv_width:]

    def spread(shard):
        pieces = shard.reshape(own_depth, dp_size, share).transpose(1, 0, 2)
        rows = exchange(pieces, "dp").reshape(depth, share)
        return lax.all_gather(rows, "tensor", axis=1, tiled=True)

    weights = (
        w_qkv, w_outt, spread(w_gate[0]), spread(w_up[0]), spread(w_down[0].T), q_width, k_width,
    )

    def slot_setup(slot_index):
        tree_id = lax.dynamic_index_in_dim(order, slot_index, 0, keepdims=False)
        seg_row = lax.dynamic_index_in_dim(seg_ids, tree_id, 0, keepdims=False)
        parent_row = lax.dynamic_index_in_dim(parents, tree_id, 0, keepdims=False)
        allowed, row_positions = path_mask(seg_row, parent_row, row_start, row_count)
        cos_table, sine_table = rope_tables(row_positions, HD)
        return (tree_id, (allowed, cos_table, sine_table))

    ticks = micro_count + 1
    incoming = jnp.zeros((row_count, depth), BF16)
    outputs, kept, slots = [], [], []
    for tick in range(ticks):
        slot_index = jnp.clip(tick - section_index, 0, micro_count - 1)
        tree_id, slot = slot_setup(slot_index)
        fresh_rows = lax.dynamic_index_in_dim(inputs, tree_id, 0, keepdims=False)
        hidden_in = jnp.where(first_section, fresh_rows, incoming)
        output_bf, stored = layer_forward(hidden_in, weights, gains, slot)
        if tick + 1 < ticks:
            incoming = lax.ppermute(output_bf, "section", [(0, 1)])
        outputs.append(output_bf)
        kept.append(stored)
        slots.append(slot)

    incoming = jnp.zeros((row_count, depth), BF16)
    grads, products, gain_parts = [None] * ticks, [None] * ticks, [None] * ticks
    for step in range(ticks):
        tick = ticks - 1 - step
        slot_index = jnp.clip(tick - section_index, 0, micro_count - 1)
        fresh_rows = lax.dynamic_index_in_dim(cotangent, slot_index, 0, keepdims=False)
        grad_out = jnp.where(first_section, incoming, fresh_rows)
        incoming_out, products[tick], gain_parts[tick] = layer_backward(
            grad_out, kept[tick], weights, gains, slots[tick]
        )
        if tick > 0:
            incoming = lax.ppermute(incoming_out, "section", [(1, 0)])
        grads[tick] = incoming_out

    def of_section(items):
        return [jnp.where(first_section, items[i], items[i + 1]) for i in range(micro_count)]

    layer_out = jnp.stack(of_section(outputs))[None]
    input_grad = jnp.stack(of_section(grads))[None]

    def weight_grad(which):
        left = jnp.concatenate(of_section([p[which][0] for p in products]), axis=0)
        right = jnp.concatenate(of_section([p[which][1] for p in products]), axis=0)
        return dot_outer(left, right).astype(BF16)

    def collect(which):
        whole = weight_grad(which)
        rows = lax.psum_scatter(whole, "tensor", scatter_dimension=1, tiled=True)
        pieces = exchange(rows.reshape(dp_size, own_depth, share), "dp")
        return pieces.transpose(1, 0, 2).reshape(own_depth, own_units).astype(F32)

    grad_down = collect(4).T
    grad_gate = collect(2)
    grad_up = collect(3)
    attn_grad = lax.psum_scatter(
        jnp.concatenate([weight_grad(0), weight_grad(1)], axis=1),
        "dp", scatter_dimension=0, tiled=True,
    ).astype(F32)
    gain_sums = [
        sum(of_section([part[which] for part in gain_parts])) for which in range(4)
    ]
    flat = jnp.concatenate([gain_sums[0], gain_sums[1], gain_sums[2], gain_sums[3]])
    gain_total = lax.psum(flat, ("dp", "tensor"))
    share_width = attn_gain.shape[1]
    attn_gain_grad = lax.dynamic_slice_in_dim(
        gain_total, 2 * HD + data_index * share_width, share_width, 0
    )
    mlp_gain_grad = lax.dynamic_slice_in_dim(
        gain_total, 2 * HD + depth + data_index * share_width, share_width, 0
    )
    return (
        layer_out,
        input_grad,
        attn_gain_grad[None],
        attn_grad[:, :q_width][None],
        attn_grad[:, q_width : q_width + k_width][None],
        attn_grad[:, q_width + k_width : qkv_width][None],
        attn_grad[:, qkv_width:].T[None],
        gain_total[:HD][None],
        gain_total[HD : 2 * HD][None],
        mlp_gain_grad[None],
        grad_gate[None],
        grad_up[None],
        grad_down[None],
    )


def solution(mesh):
    rows = P(None, "dp", None)
    wide = P("section", "dp", "tensor")
    tall = P("section", "tensor", "dp")
    gain = P("section", "dp")
    head_gain = P("section", None)
    slots = P("section", None, "dp", None)
    in_specs = (
        rows, rows, P(), P(), P(), gain, wide, wide, wide, tall, head_gain, head_gain, gain,
        wide, wide, tall,
    )
    out_specs = (
        slots, slots, gain, wide, wide, wide, tall, head_gain, head_gain, gain, wide, wide, tall,
    )
    return jax.shard_map(
        on_device, mesh=mesh, in_specs=in_specs, out_specs=out_specs, check_vma=False
    )
```

time: 2320 us -> 1990 us (0.86)
  blocking collectives: 201 us -> 91.4 us
  matrix products: 314 us -> 221 us
  other arithmetic: 208 us -> 120 us
  waiting for transfers between devices: 1360 us -> 1310 us
  loops' own time: 42 us -> 0 us
  starting transfers between devices: 13.8 us -> 49.6 us
    psum x12 -> x0, waiting for transfers between devices: 458 us -> none  [tensor_total(): lax.psum(partial_sum.astype(jnp.bfloat16), 'tensor').astype(jnp.float32)]
    unnamed x14 -> x53, waiting for transfers between devices: 4.45 us -> 302 us
    all_gather x7 -> x22, waiting for transfers between devices: 469 us -> 638 us  [the longest x3 132 us: spread(): return lax.all_gather(rows, 'tensor', axis=1, tiled=True)]
    ppermute x6 -> x22, waiting for transfers between devices: 0.02 us -> 151 us  [the longest x18 142 us: exchange(): arrived = lax.ppermute(piece, axis, [(i, i ^ step) for i in range(size)])]
    reduce_scatter x7, waiting for transfers between devices: 355 us -> 221 us  [the longest x3 88 us: layer_forward(): lax.psum_scatter(mlp_partial, 'dp', scatter_dimension=0, tiled=True)]
    all_gather x8 -> x1, blocking collectives: 122 us -> 13.7 us  [on_device(): lax.all_gather(jnp.concatenate([attn_gain, mlp_gain], axis=0), 'dp', axis...]
    dot_general x72 -> x41, matrix products: 293 us -> 191 us  [the longest x15 80.9 us: dot(): return jnp.dot(left, right, preferred_element_type=F32)]
    unnamed x20 -> x529, local copies, waits for them, and re-layouts: 1.98 us -> 88.7 us
  transfers between devices with their start and end apart: 38 -> 63, of which waited for: 29 -> 49; matrix products, arithmetic and copies ran while one was open for 14% -> 11% of each run, Pallas kernels for 0% -> 0%
where the time goes in v1:
time: 1990 us; the launch traced here: 1970 us
  waiting for transfers between devices  1310 us (66%)
  matrix products  221 us (11%)
  local copies, waits for them, and re-layouts  154 us (8%)
  other arithmetic  120 us (6%)
  blocking collectives  91.4 us (5%)
  starting transfers between devices  49.6 us (2%)
  between operations  24.9 us (1%)
    unnamed x53, waiting for transfers between devices  302 us
    ppermute x18, waiting for transfers between devices, exchange(): arrived = lax.ppermute(piece, axis, [(i, i ^ step) for i in range(size)])  142 us
    all_gather x3, waiting for transfers between devices, spread(): return lax.all_gather(rows, 'tensor', axis=1, tiled=True)  132 us
    all_gather x1, waiting for transfers between devices, on_device(): attn_all = lax.all_gather(attn_shard, 'dp', axis=0, tiled=True)  91.2 us
    unnamed x529, local copies, waits for them, and re-layouts  88.7 us
    reduce_scatter x3, waiting for transfers between devices, layer_forward(): lax.psum_scatter(mlp_partial, 'dp', scatter_dimension=0, tiled=True)  88 us
    reduce_scatter x3, waiting for transfers between devices, layer_backward(): lax.psum_scatter(mlp_partial, 'dp', scatter_dimension=0, tiled=True)  85.3 us
    dot_general x15, matrix products, dot(): return jnp.dot(left, right, preferred_element_type=F32)  80.9 us
  transfers between devices with their start and end apart: 63, of which 49 were waited for; matrix products, arithmetic and copies ran while one was open for 11% of the time, Pallas kernels for 0%

profile of v1, /device:TPU:0, one launch (start us, length us, event | category | flops | bytes accessed | tf_op | source)
XLA Modules:
  0.0 1972.2 jit_solution(10174188546686897920)
XLA Ops:
  20.5 13.7 all_gather.69
  40.2 91.2 %all-gather.24.cloned.1.call-done = bf16[2048,1536]{0,1:T(8,128)(2,1)} async-done(((bf16[512,1536]{0,1:T(8,128)(2,1)}), bf16[2048,1536]{0,1:T(8,128)(2,1)}) %all-gather.24.cloned.1.call-update) | async-done | bytes 6291472 | tf_op jit(solution)/shard_map/all_gather | solution.py:286
  145.6 23.5 %all-gather.26.cloned.1.call-done = bf16[1152,512]{1,0:T(8,128)(2,1)} async-done(((bf16[288,512]{1,0:T(8,128)(2,1)}), bf16[1152,512]{1,0:T(8,128)(2,1)}) %all-gather.26.cloned.1.call-update) | async-done | bytes 1179664 | tf_op jit(solution)/shard_map/all_gather | solution.py:143
  192.3 12.8 collective-permute-done
  205.2 13.2 collective-permute-done.1
  239.9 11.8 collective-permute-done.3
  251.8 15.2 collective-permute-done.4
  291.0 16.9 collective-permute-done.7
  311.3 20.4 %all-gather.28.cloned.1.call-done = bf16[288,2048]{1,0:T(8,128)(2,1)} async-done(((bf16[72,2048]{1,0:T(8,128)(2,1)}), bf16[288,2048]{1,0:T(8,128)(2,1)}) %all-gather.28.cloned.1.call-update) | async-done | bytes 1179664 | tf_op jit(solution)/shard_map/all_gather | solution.py:162
  338.1 66.1 %all-gather.32.cloned.1.call-done = bf16[2048,1536]{1,0:T(8,128)(2,1)} async-done(((bf16[2048,384]{1,0:T(8,128)(2,1)}), bf16[2048,1536]{1,0:T(8,128)(2,1)}) %all-gather.32.cloned.1.call-update) | async-done | bytes 6291472 | tf_op jit(solution)/shard_map/all_gather | solution.py:294
  410.8 65.9 %all-gather.34.cloned.1.call-done = bf16[2048,1536]{1,0:T(8,128)(2,1)} async-done(((bf16[2048,384]{1,0:T(8,128)(2,1)}), bf16[2048,1536]{1,0:T(8,128)(2,1)}) %all-gather.34.cloned.1.call-update) | async-done | bytes 6291472 | tf_op jit(solution)/shard_map/all_gather | solution.py:294
  482.7 29.3 %reduce-scatter.44.cloned.1.call-done = bf16[72,2048]{1,0:T(8,128)(2,1)} async-done(((bf16[288,2048]{1,0:T(8,128)(2,1)}), bf16[72,2048]{1,0:T(8,128)(2,1)}) %reduce-scatter.44.cloned.1.call-update) | async-done | bytes 294928 | tf_op jit(solution)/shard_map/reduce_scatter | solution.py:169
  513.8 27.0 %all-gather.36.cloned.1.call-done = bf16[288,2048]{1,0:T(8,128)(2,1)} async-done(((bf16[72,2048]{1,0:T(8,128)(2,1)}), bf16[288,2048]{1,0:T(8,128)(2,1)}) %all-gather.36.cloned.1.call-update) | async-done | bytes 1179664 | tf_op jit(solution)/shard_map/all_gather | solution.py:171
  564.8 22.8 %all-gather.38.cloned.1.call-done = bf16[1152,512]{1,0:T(8,128)(2,1)} async-done(((bf16[288,512]{1,0:T(8,128)(2,1)}), bf16[1152,512]{1,0:T(8,128)(2,1)}) %all-gather.38.cloned.1.call-update) | async-done | bytes 1179664 | tf_op jit(solution)/shard_map/all_gather | solution.py:143
  600.3 27.8 %reduce-scatter.72.cloned.1.call-done = bf16[72,2048]{1,0:T(8,128)(2,1)} async-done(((bf16[288,2048]{1,0:T(8,128)(2,1)}), bf16[72,2048]{1,0:T(8,128)(2,1)}) %reduce-scatter.72.cloned.1.call-update) | async-done | bytes 294928
  631.4 30.3 %all-gather.40.cloned.1.call-done = bf16[288,2048]{1,0:T(8,128)(2,1)} async-done(((bf16[72,2048]{1,0:T(8,128)(2,1)}), bf16[288,2048]{1,0:T(8,128)(2,1)}) %all-gather.40.cloned.1.call-update) | async-done | bytes 1179664 | tf_op jit(solution)/shard_map/all_gather | solution.py:162
  678.3 28.4 %reduce-scatter.46.cloned.1.call-done = bf16[72,2048]{1,0:T(8,128)(2,1)} async-done(((bf16[288,2048]{1,0:T(8,128)(2,1)}), bf16[72,2048]{1,0:T(8,128)(2,1)}) %reduce-scatter.46.cloned.1.call-update) | async-done | bytes 294928 | tf_op jit(solution)/shard_map/reduce_scatter | solution.py:169
  708.6 26.9 %all-gather.42.cloned.1.call-done = bf16[288,2048]{1,0:T(8,128)(2,1)} async-done(((bf16[72,2048]{1,0:T(8,128)(2,1)}), bf16[288,2048]{1,0:T(8,128)(2,1)}) %all-gather.42.cloned.1.call-update) | async-done | bytes 1179664 | tf_op jit(solution)/shard_map/all_gather | solution.py:171
  759.5 23.1 %all-gather.44.cloned.1.call-done = bf16[1152,512]{1,0:T(8,128)(2,1)} async-done(((bf16[288,512]{1,0:T(8,128)(2,1)}), bf16[1152,512]{1,0:T(8,128)(2,1)}) %all-gather.44.cloned.1.call-update) | async-done | bytes 1179664 | tf_op jit(solution)/shard_map/all_gather | solution.py:143
  795.2 27.8 %reduce-scatter.74.cloned.1.call-done = bf16[72,2048]{1,0:T(8,128)(2,1)} async-done(((bf16[288,2048]{1,0:T(8,128)(2,1)}), bf16[72,2048]{1,0:T(8,128)(2,1)}) %reduce-scatter.74.cloned.1.call-update) | async-done | bytes 294928
  828.3 28.3 %all-gather.46.cloned.1.call-done = bf16[288,2048]{1,0:T(8,128)(2,1)} async-done(((bf16[72,2048]{1,0:T(8,128)(2,1)}), bf16[288,2048]{1,0:T(8,128)(2,1)}) %all-gather.46.cloned.1.call-update) | async-done | bytes 1179664 | tf_op jit(solution)/shard_map/all_gather | solution.py:162
  870.0 17.5 all-gather.66.cloned.1.call-done
  905.5 28.4 %reduce-scatter.50.cloned.1.call-done = bf16[72,2048]{1,0:T(8,128)(2,1)} async-done(((bf16[288,2048]{1,0:T(8,128)(2,1)}), bf16[72,2048]{1,0:T(8,128)(2,1)}) %reduce-scatter.50.cloned.1.call-update) | async-done | bytes 294928 | tf_op jit(solution)/shard_map/reduce_scatter | solution.py:198
  938.2 26.3 %all-gather.50.cloned.1.call-done = bf16[288,2048]{1,0:T(8,128)(2,1)} async-done(((bf16[72,2048]{1,0:T(8,128)(2,1)}), bf16[288,2048]{1,0:T(8,128)(2,1)}) %all-gather.50.cloned.1.call-update) | async-done | bytes 1179664 | tf_op jit(solution)/shard_map/all_gather | solution.py:202
  986.8 22.2 %reduce-scatter.58.cloned.1.call-done = bf16[288,512]{1,0:T(8,128)(2,1)} async-done(((bf16[1152,512]{1,0:T(8,128)(2,1)}), bf16[288,512]{1,0:T(8,128)(2,1)}) %reduce-scatter.58.cloned.1.call-update) | async-done | bytes 294928
  1024.9 20.8 %reduce-scatter.76.cloned.1.call-done = bf16[72,2048]{1,0:T(8,128)(2,1)} async-done(((bf16[288,2048]{1,0:T(8,128)(2,1)}), bf16[72,2048]{1,0:T(8,128)(2,1)}) %reduce-scatter.76.cloned.1.call-update) | async-done | bytes 294928
  1047.5 30.3 %reduce-scatter.48.cloned.1.call-done = bf16[72,2048]{1,0:T(8,128)(2,1)} async-done(((bf16[288,2048]{1,0:T(8,128)(2,1)}), bf16[72,2048]{1,0:T(8,128)(2,1)}) %reduce-scatter.48.cloned.1.call-update) | async-done | bytes 294928 | tf_op jit(solution)/shard_map/reduce_scatter | solution.py:169
  1080.4 26.5 %all-gather.52.cloned.1.call-done = bf16[288,2048]{1,0:T(8,128)(2,1)} async-done(((bf16[72,2048]{1,0:T(8,128)(2,1)}), bf16[288,2048]{1,0:T(8,128)(2,1)}) %all-gather.52.cloned.1.call-update) | async-done | bytes 1179664 | tf_op jit(solution)/shard_map/all_gather | solution.py:252
  1112.8 30.8 %all-gather.54.cloned.1.call-done = bf16[288,2048]{1,0:T(8,128)(2,1)} async-done(((bf16[72,2048]{1,0:T(8,128)(2,1)}), bf16[288,2048]{1,0:T(8,128)(2,1)}) %all-gather.54.cloned.1.call-update) | async-done | bytes 1179664 | tf_op jit(solution)/shard_map/all_gather | solution.py:191
  1159.9 28.5 %reduce-scatter.52.cloned.1.call-done = bf16[72,2048]{1,0:T(8,128)(2,1)} async-done(((bf16[288,2048]{1,0:T(8,128)(2,1)}), bf16[72,2048]{1,0:T(8,128)(2,1)}) %reduce-scatter.52.cloned.1.call-update) | async-done | bytes 294928 | tf_op jit(solution)/shard_map/reduce_scatter | solution.py:198
  1192.7 26.1 %all-gather.56.cloned.1.call-done = bf16[288,2048]{1,0:T(8,128)(2,1)} async-done(((bf16[72,2048]{1,0:T(8,128)(2,1)}), bf16[288,2048]{1,0:T(8,128)(2,1)}) %all-gather.56.cloned.1.call-update) | async-done | bytes 1179664 | tf_op jit(solution)/shard_map/all_gather | solution.py:202
  1239.8 22.8 %reduce-scatter.60.cloned.1.call-done = bf16[288,512]{1,0:T(8,128)(2,1)} async-done(((bf16[1152,512]{1,0:T(8,128)(2,1)}), bf16[288,512]{1,0:T(8,128)(2,1)}) %reduce-scatter.60.cloned.1.call-update) | async-done | bytes 294928
  1272.9 27.2 %reduce-scatter.78.cloned.1.call-done = bf16[72,2048]{1,0:T(8,128)(2,1)} async-done(((bf16[288,2048]{1,0:T(8,128)(2,1)}), bf16[72,2048]{1,0:T(8,128)(2,1)}) %reduce-scatter.78.cloned.1.call-update) | async-done | bytes 294928
  1304.2 27.8 %all-gather.58.cloned.1.call-done = bf16[288,2048]{1,0:T(8,128)(2,1)} async-done(((bf16[72,2048]{1,0:T(8,128)(2,1)}), bf16[288,2048]{1,0:T(8,128)(2,1)}) %all-gather.58.cloned.1.call-update) | async-done | bytes 1179664 | tf_op jit(solution)/shard_map/all_gather | solution.py:252
  1338.8 30.5 %all-gather.60.cloned.1.call-done = bf16[288,2048]{1,0:T(8,128)(2,1)} async-done(((bf16[72,2048]{1,0:T(8,128)(2,1)}), bf16[288,2048]{1,0:T(8,128)(2,1)}) %all-gather.60.cloned.1.call-update) | async-done | bytes 1179664 | tf_op jit(solution)/shard_map/all_gather | solution.py:191
  1388.4 28.4 %reduce-scatter.54.cloned.1.call-done = bf16[72,2048]{1,0:T(8,128)(2,1)} async-done(((bf16[288,2048]{1,0:T(8,128)(2,1)}), bf16[72,2048]{1,0:T(8,128)(2,1)}) %reduce-scatter.54.cloned.1.call-update) | async-done | bytes 294928 | tf_op jit(solution)/shard_map/reduce_scatter | solution.py:198
  1420.8 26.5 %all-gather.62.cloned.1.call-done = bf16[288,2048]{1,0:T(8,128)(2,1)} async-done(((bf16[72,2048]{1,0:T(8,128)(2,1)}), bf16[288,2048]{1,0:T(8,128)(2,1)}) %all-gather.62.cloned.1.call-update) | async-done | bytes 1179664 | tf_op jit(solution)/shard_map/all_gather | solution.py:202
  1468.4 22.5 %reduce-scatter.62.cloned.1.call-done = bf16[288,512]{1,0:T(8,128)(2,1)} async-done(((bf16[1152,512]{1,0:T(8,128)(2,1)}), bf16[288,512]{1,0:T(8,128)(2,1)}) %reduce-scatter.62.cloned.1.call-update) | async-done | bytes 294928
  1502.3 26.1 %reduce-scatter.80.cloned.1.call-done = bf16[72,2048]{1,0:T(8,128)(2,1)} async-done(((bf16[288,2048]{1,0:T(8,128)(2,1)}), bf16[72,2048]{1,0:T(8,128)(2,1)}) %reduce-scatter.80.cloned.1.call-update) | async-done | bytes 294928
  1541.7 8.7 copy.560
  1561.2 8.7 copy.558
  1580.0 8.7 copy.556
  1607.1 77.7 %psum.7 = f32[4352]{0:T(1024)S(1)} all-reduce(f32[4352]{0:T(1024)S(1)} %pad_maximum_fusion.28), channel_id=1, replica_groups=mesh['section'=2,'dp'=4,'tensor'=4] {'dp','tensor'}, use_global_device_ids=true, to_apply=%region_72.73 | all-reduce | flops 4352 | bytes 34816 | tf_op jit(solution)/shard_map/psum | solution.py:365
  1698.1 38.3 %reduce-scatter.66.cloned.1.call-done = bf16[384,2048]{1,0:T(8,128)(2,1)} async-done(((bf16[1536,2048]{1,0:T(8,128)(2,1)}), bf16[384,2048]{1,0:T(8,128)(2,1)}) %reduce-scatter.66.cloned.1.call-update) | async-done | bytes 1572880
  1744.5 65.1 %reduce-scatter.64.cloned.1.call-done = bf16[384,2048]{1,0:T(8,128)(2,1)} async-done(((bf16[1536,2048]{1,0:T(8,128)(2,1)}), bf16[384,2048]{1,0:T(8,128)(2,1)}) %reduce-scatter.64.cloned.1.call-update) | async-done | bytes 1572880
  1842.5 8.8 collective-permute-done.13
  1853.1 48.3 %collective-permute-done.14 = bf16[1,512,384]{2,1,0:T(8,128)(2,1)} collective-permute-done((bf16[1,512,384]{2,1,0:T(8,128)(2,1)}, bf16[1,512,384]{2,1,0:T(8,128)(2,1)}, u32[]{:S(2)}, u32[]{:S(2)}) %collective-permute-start.14) | collective-permute-done | bytes 393248 | tf_op jit(solution)/shard_map/ppermute | solution.py:114
  1911.6 47.3 %reduce-scatter.56.cloned.1.call-done = bf16[512,1536]{0,1:T(8,128)(2,1)} async-done(((bf16[2048,1536]{0,1:T(8,128)(2,1)}), bf16[512,1536]{0,1:T(8,128)(2,1)}) %reduce-scatter.56.cloned.1.call-update) | async-done | bytes 1572880 | tf_op jit(solution)/shard_map/reduce_scatter | solution.py:357
  (982 shorter events, 544.1 us)
Async XLA Ops:
  7.2 124.3 %all-gather.24.cloned.1.call-start = ((), (), s32[]{:S(2)}) async-start(), calls=%async_computation.19 | async-start | bytes 7864320 | tf_op jit(solution)/shard_map/all_gather | solution.py:286
  13.2 155.9 %all-gather.26.cloned.1.call-start = ((), (), s32[]{:S(2)}) async-start(), calls=%async_computation.20 | async-start | bytes 1474560 | tf_op jit(solution)/shard_map/all_gather | solution.py:143
  140.3 79.5 %reduce-scatter.70.cloned.1.call-start = ((), (), s32[]{:S(2)}) async-start(), calls=%async_computation.54 | async-start | bytes 1474560
  180.9 130.3 %all-gather.30.cloned.1.call-start = ((), (), s32[]{:S(2)}) async-start(), calls=%async_computation.22 | async-start | bytes 7864320 | tf_op jit(solution)/shard_map/all_gather | solution.py:294
  219.7 112.0 %all-gather.28.cloned.1.call-start = ((), (), s32[]{:S(2)}) async-start(), calls=%async_computation.21 | async-start | bytes 1474560 | tf_op jit(solution)/shard_map/all_gather | solution.py:162
  222.8 181.5 %all-gather.32.cloned.1.call-start = ((), (), s32[]{:S(2)}) async-start(), calls=%async_computation.23 | async-start | bytes 7864320 | tf_op jit(solution)/shard_map/all_gather | solution.py:294
  268.3 208.4 %all-gather.34.cloned.1.call-start = ((), (), s32[]{:S(2)}) async-start(), calls=%async_computation.24 | async-start | bytes 7864320 | tf_op jit(solution)/shard_map/all_gather | solution.py:294
  311.2 200.7 %reduce-scatter.44.cloned.1.call-start = ((), (), s32[]{:S(2)}) async-start(), calls=%async_computation.25 | async-start | bytes 1474560 | tf_op jit(solution)/shard_map/reduce_scatter | solution.py:169
  482.6 58.2 %all-gather.36.cloned.1.call-start = ((), (), s32[]{:S(2)}) async-start(), calls=%async_computation.26 | async-start | bytes 1474560 | tf_op jit(solution)/shard_map/all_gather | solution.py:171
  513.8 73.8 %all-gather.38.cloned.1.call-start = ((), (), s32[]{:S(2)}) async-start(), calls=%async_computation.27 | async-start | bytes 1474560 | tf_op jit(solution)/shard_map/all_gather | solution.py:143
  556.9 71.1 %reduce-scatter.72.cloned.1.call-start = ((), (), s32[]{:S(2)}) async-start(), calls=%async_computation.55 | async-start | bytes 1474560
  600.2 61.4 %all-gather.40.cloned.1.call-start = ((), (), s32[]{:S(2)}) async-start(), calls=%async_computation.28 | async-start | bytes 1474560 | tf_op jit(solution)/shard_map/all_gather | solution.py:162
  631.1 75.6 %reduce-scatter.46.cloned.1.call-start = ((), (), s32[]{:S(2)}) async-start(), calls=%async_computation.29 | async-start | bytes 1474560 | tf_op jit(solution)/shard_map/reduce_scatter | solution.py:169
  678.3 57.2 %all-gather.42.cloned.1.call-start = ((), (), s32[]{:S(2)}) async-start(), calls=%async_computation.30 | async-start | bytes 1474560 | tf_op jit(solution)/shard_map/all_gather | solution.py:171
  708.5 74.0 %all-gather.44.cloned.1.call-start = ((), (), s32[]{:S(2)}) async-start(), calls=%async_computation.31 | async-start | bytes 1474560 | tf_op jit(solution)/shard_map/all_gather | solution.py:143
  751.9 71.0 %reduce-scatter.74.cloned.1.call-start = ((), (), s32[]{:S(2)}) async-start(), calls=%async_computation.56 | async-start | bytes 1474560
  795.1 61.4 %all-gather.46.cloned.1.call-start = ((), (), s32[]{:S(2)}) async-start(), calls=%async_computation.32 | async-start | bytes 1474560 | tf_op jit(solution)/shard_map/all_gather | solution.py:162
  825.9 61.6 %all-gather.66.cloned.1.call-start = ((), (), s32[]{:S(2)}) async-start(), calls=%async_computation.47 | async-start | bytes 1474560 | tf_op jit(solution)/shard_map/all_gather | solution.py:191
  827.7 106.2 %reduce-scatter.50.cloned.1.call-start = ((), (), s32[]{:S(2)}) async-start(), calls=%async_computation.35 | async-start | bytes 1474560 | tf_op jit(solution)/shard_map/reduce_scatter | solution.py:198
  905.5 59.0 %all-gather.50.cloned.1.call-start = ((), (), s32[]{:S(2)}) async-start(), calls=%async_computation.36 | async-start | bytes 1474560 | tf_op jit(solution)/shard_map/all_gather | solution.py:202
  937.9 71.1 %reduce-scatter.58.cloned.1.call-start = ((), (), s32[]{:S(2)}) async-start(), calls=%async_computation.48 | async-start | bytes 1474560
  979.6 66.1 %reduce-scatter.76.cloned.1.call-start = ((), (), s32[]{:S(2)}) async-start(), calls=%async_computation.57 | async-start | bytes 1474560
  1018.3 59.5 %reduce-scatter.48.cloned.1.call-start = ((), (), s32[]{:S(2)}) async-start(), calls=%async_computation.33 | async-start | bytes 1474560 | tf_op jit(solution)/shard_map/reduce_scatter | solution.py:169
  1024.8 82.1 %all-gather.52.cloned.1.call-start = ((), (), s32[]{:S(2)}) async-start(), calls=%async_computation.37 | async-start | bytes 1474560 | tf_op jit(solution)/shard_map/all_gather | solution.py:252
  1080.4 63.2 %all-gather.54.cloned.1.call-start = ((), (), s32[]{:S(2)}) async-start(), calls=%async_computation.38 | async-start | bytes 1474560 | tf_op jit(solution)/shard_map/all_gather | solution.py:191
  1112.7 75.7 %reduce-scatter.52.cloned.1.call-start = ((), (), s32[]{:S(2)}) async-start(), calls=%async_computation.39 | async-start | bytes 1474560 | tf_op jit(solution)/shard_map/reduce_scatter | solution.py:198
  1159.8 59.0 %all-gather.56.cloned.1.call-start = ((), (), s32[]{:S(2)}) async-start(), calls=%async_computation.40 | async-start | bytes 1474560 | tf_op jit(solution)/shard_map/all_gather | solution.py:202
  1192.2 70.3 %reduce-scatter.60.cloned.1.call-start = ((), (), s32[]{:S(2)}) async-start(), calls=%async_computation.49 | async-start | bytes 1474560
  1233.2 66.8 %reduce-scatter.78.cloned.1.call-start = ((), (), s32[]{:S(2)}) async-start(), calls=%async_computation.58 | async-start | bytes 1474560
  1272.6 59.4 %all-gather.58.cloned.1.call-start = ((), (), s32[]{:S(2)}) async-start(), calls=%async_computation.41 | async-start | bytes 1474560 | tf_op jit(solution)/shard_map/all_gather | solution.py:252
  1304.1 65.2 %all-gather.60.cloned.1.call-start = ((), (), s32[]{:S(2)}) async-start(), calls=%async_computation.42 | async-start | bytes 1474560 | tf_op jit(solution)/shard_map/all_gather | solution.py:191
  1338.7 78.1 %reduce-scatter.54.cloned.1.call-start = ((), (), s32[]{:S(2)}) async-start(), calls=%async_computation.43 | async-start | bytes 1474560 | tf_op jit(solution)/shard_map/reduce_scatter | solution.py:198
  1388.4 58.9 %all-gather.62.cloned.1.call-start = ((), (), s32[]{:S(2)}) async-start(), calls=%async_computation.44 | async-start | bytes 1474560 | tf_op jit(solution)/shard_map/all_gather | solution.py:202
  1420.7 70.3 %reduce-scatter.62.cloned.1.call-start = ((), (), s32[]{:S(2)}) async-start(), calls=%async_computation.50 | async-start | bytes 1474560
  1461.6 66.8 %reduce-scatter.80.cloned.1.call-start = ((), (), s32[]{:S(2)}) async-start(), calls=%async_computation.59 | async-start | bytes 1474560
  1501.0 102.4 %all-gather.48.cloned.1.call-start = ((), (), s32[]{:S(2)}) async-start(), calls=%async_computation.34 | async-start | bytes 1474560 | tf_op jit(solution)/shard_map/all_gather | solution.py:171
  1501.6 184.4 %all-gather.64.cloned.1.call-start = ((), (), s32[]{:S(2)}) async-start(), calls=%async_computation.45 | async-start | bytes 1474560 | tf_op jit(solution)/shard_map/all_gather | solution.py:252
  1532.5 156.3 %reduce-scatter.68.cloned.1.call-start = ((), (), s32[]{:S(2)}) async-start(), calls=%async_computation.53 | async-start | bytes 7864320
  1550.4 185.9 %reduce-scatter.66.cloned.1.call-start = ((), (), s32[]{:S(2)}) async-start(), calls=%async_computation.52 | async-start | bytes 7864320
  1570.0 239.6 %reduce-scatter.64.cloned.1.call-start = ((), (), s32[]{:S(2)}) async-start(), calls=%async_computation.51 | async-start | bytes 7864320
  1588.7 370.1 %reduce-scatter.56.cloned.1.call-start = ((), (), s32[]{:S(2)}) async-start(), calls=%async_computation.46 | async-start | bytes 7864320 | tf_op jit(solution)/shard_map/reduce_scatter | solution.py:357
  1692.1 120.6 %collective-permute-start.19 = (bf16[1,512,384]{2,1,0:T(8,128)(2,1)}, bf16[1,512,384]{2,1,0:T(8,128)(2,1)}, u32[]{:S(2)}, u32[]{:S(2)}) collective-permute-start(bf16[1,512,384]{2,1,0:T(8,128)(2,1)} %get-tuple-element.169), channel_id=1, source_target_pairs={{0,4},{4,0},{8,12},{12,8},{1,5},{5,1},{9,13},{13,9},{2,6},{6,2},{1... | collective-permute-start | bytes 1179656 | tf_op jit(solution)/shard_map/ppermute | solution.py:114
  1694.7 122.5 %collective-permute-start.20 = (bf16[1,512,384]{2,1,0:T(8,128)(2,1)}, bf16[1,512,384]{2,1,0:T(8,128)(2,1)}, u32[]{:S(2)}, u32[]{:S(2)}) collective-permute-start(bf16[1,512,384]{2,1,0:T(8,128)(2,1)} %get-tuple-element.168), channel_id=1, source_target_pairs={{0,8},{4,12},{8,0},{12,4},{1,9},{5,13},{9,1},{13,5},{2,10},{6,14},... | collective-permute-start | bytes 1179656 | tf_op jit(solution)/shard_map/ppermute | solution.py:114
  1694.7 123.7 %collective-permute-start.21 = (bf16[1,512,384]{2,1,0:T(8,128)(2,1)}, bf16[1,512,384]{2,1,0:T(8,128)(2,1)S(1)}, u32[]{:S(2)}, u32[]{:S(2)}) collective-permute-start(bf16[1,512,384]{2,1,0:T(8,128)(2,1)} %get-tuple-element.167), channel_id=1, source_target_pairs={{0,12},{4,8},{8,4},{12,0},{1,13},{5,9},{9,5},{13,1},{2,14},{6,10},... | collective-permute-start | bytes 1179656 | tf_op jit(solution)/shard_map/ppermute | solution.py:114
  1740.6 79.4 %collective-permute-start.16 = (bf16[1,512,384]{2,1,0:T(8,128)(2,1)}, bf16[1,512,384]{2,1,0:T(8,128)(2,1)}, u32[]{:S(2)}, u32[]{:S(2)}) collective-permute-start(bf16[1,512,384]{2,1,0:T(8,128)(2,1)} %get-tuple-element.173), channel_id=1, source_target_pairs={{0,4},{4,0},{8,12},{12,8},{1,5},{5,1},{9,13},{13,9},{2,6},{6,2},{1... | collective-permute-start | bytes 1179656 | tf_op jit(solution)/shard_map/ppermute | solution.py:114
  1742.1 82.0 %collective-permute-start.17 = (bf16[1,512,384]{2,1,0:T(8,128)(2,1)}, bf16[1,512,384]{2,1,0:T(8,128)(2,1)}, u32[]{:S(2)}, u32[]{:S(2)}) collective-permute-start(bf16[1,512,384]{2,1,0:T(8,128)(2,1)} %get-tuple-element.172), channel_id=1, source_target_pairs={{0,8},{4,12},{8,0},{12,4},{1,9},{5,13},{9,1},{13,5},{2,10},{6,14},... | collective-permute-start | bytes 1179656 | tf_op jit(solution)/shard_map/ppermute | solution.py:114
  1818.4 83.0 %collective-permute-start.14 = (bf16[1,512,384]{2,1,0:T(8,128)(2,1)}, bf16[1,512,384]{2,1,0:T(8,128)(2,1)}, u32[]{:S(2)}, u32[]{:S(2)}) collective-permute-start(bf16[1,512,384]{2,1,0:T(8,128)(2,1)} %get-tuple-element.176), channel_id=1, source_target_pairs={{0,8},{4,12},{8,0},{12,4},{1,9},{5,13},{9,1},{13,5},{2,10},{6,14},... | collective-permute-start | bytes 1179656 | tf_op jit(solution)/shard_map/ppermute | solution.py:114
  1820.0 83.3 %collective-permute-start.15 = (bf16[1,512,384]{2,1,0:T(8,128)(2,1)}, bf16[1,512,384]{2,1,0:T(8,128)(2,1)S(1)}, u32[]{:S(2)}, u32[]{:S(2)}) collective-permute-start(bf16[1,512,384]{2,1,0:T(8,128)(2,1)} %get-tuple-element.175), channel_id=1, source_target_pairs={{0,12},{4,8},{8,4},{12,0},{1,13},{5,9},{9,5},{13,1},{2,14},{6,10},... | collective-permute-start | bytes 1179656 | tf_op jit(solution)/shard_map/ppermute | solution.py:114
  (259 other events, 5186.8 us)
Sparse Core Ops, SparseCore 0:
  13.3 118.0 all-gather.23
  140.4 28.6 all-gather.25
  181.1 27.6 reduce-scatter.69
  219.8 75.6 all-gather.29
  297.5 34.1 all-gather.27
  333.9 70.2 all-gather.31
  406.7 70.0 all-gather.33
  482.7 29.1 reduce-scatter.43
  514.4 26.4 all-gather.35
  557.0 30.4 all-gather.37
  600.4 27.6 reduce-scatter.71
  631.2 30.4 all-gather.39
  678.4 28.2 reduce-scatter.45
  709.0 26.4 all-gather.41
  752.0 30.4 all-gather.43
  795.2 27.6 reduce-scatter.73
  826.1 30.4 all-gather.45
  857.9 29.5 all-gather.65
  905.6 28.3 reduce-scatter.49
  938.0 26.4 all-gather.49
  979.7 29.1 reduce-scatter.57
  1018.5 27.2 reduce-scatter.75
  1048.6 29.1 reduce-scatter.47
  1080.5 26.4 all-gather.51
  1112.8 30.6 all-gather.53
  1160.0 28.3 reduce-scatter.51
  1192.4 26.4 all-gather.55
  1233.4 29.1 reduce-scatter.59
  1272.7 27.2 reduce-scatter.77
  1304.3 27.7 all-gather.57
  1338.9 30.4 all-gather.59
  1388.5 28.2 reduce-scatter.53
  1420.8 26.4 all-gather.61
  1461.7 29.1 reduce-scatter.61
  1501.1 27.2 reduce-scatter.79
  1530.7 27.7 all-gather.47
  1560.7 27.7 all-gather.63
  1591.5 71.6 reduce-scatter.67
  1666.0 70.3 reduce-scatter.65
  1739.3 70.1 reduce-scatter.63
  1811.9 146.9 reduce-scatter.55

commit v2 on v1

v2 whole, which is shorter than its diff:
```python
from functools import partial

import jax
import jax.numpy as jnp
from jax import lax
from jax.sharding import PartitionSpec as P

HD = 128
TRUNK = 512
BRANCH = 96
NB = 4
TREE = 1152
SEGS = 9


EPSILON = 1e-06
THETA = 1000000.0
MASKED = -1e30
F32 = jnp.float32
BF16 = jnp.bfloat16


def rms_scale(values, weight_gain):
    mean_sq = jnp.mean(values * values, axis=-1, keepdims=True)
    return values * lax.rsqrt(mean_sq + EPSILON) * weight_gain


def rotate(values, cos_table, sine_table):
    middle_at = values.shape[-1] // 2
    leading = values[..., :middle_at]
    trailing = values[..., middle_at:]
    return jnp.concatenate(
        [leading * cos_table - trailing * sine_table, trailing * cos_table + leading * sine_table],
        axis=-1,
    )


def rope_tables(positions, head_dim):
    half_steps = jnp.arange(head_dim // 2, dtype=F32)
    inverse = THETA ** (-2.0 * half_steps / head_dim)
    angles = positions.astype(F32)[:, None] * inverse[None, :]
    return (jnp.cos(angles)[:, None, :], jnp.sin(angles)[:, None, :])


def swiglu(gate_in, up_in):
    return jax.nn.silu(gate_in) * up_in


def embed_heads(q_pre, k_pre, q_scale, k_scale, cos_table, sine_table):
    row_count = q_pre.shape[0]
    queries = rms_scale(q_pre.reshape(row_count, -1, HD), q_scale)
    keys_part = rms_scale(k_pre.reshape(row_count, -1, HD), k_scale)
    return (rotate(queries, cos_table, sine_table), rotate(keys_part, cos_table, sine_table))


def tree_layout(seg_row, parent_row):
    labels = jnp.arange(SEGS, dtype=jnp.int32)
    places = jnp.arange(TREE, dtype=jnp.int32)
    member = seg_row[None, :] == labels[:, None]
    starts = jnp.min(jnp.where(member, places[None, :], TREE), axis=1)
    depth_base = jnp.where(labels == 0, 0, jnp.where(labels <= NB, TRUNK, TRUNK + BRANCH))
    shifts = depth_base - starts
    positions = places + jnp.sum(jnp.where(member, shifts[:, None], 0), axis=0)
    grandparent = jnp.sum(
        jnp.where(parent_row[:, None] == labels[None, :], parent_row[None, :], 0), axis=1
    )
    ancestor = (
        (labels[None, :] == labels[:, None])
        | (labels[None, :] == parent_row[:, None])
        | (labels[None, :] == grandparent[:, None])
    )
    return (positions, member.astype(F32), ancestor.astype(F32))


def path_mask(seg_row, parent_row, row_start, row_count):
    positions, member, ancestor = tree_layout(seg_row, parent_row)
    member_rows = lax.dynamic_slice_in_dim(member, row_start, row_count, 1)
    seg_rows = lax.dynamic_slice_in_dim(seg_row, row_start, row_count, 0)
    reach_table = jnp.dot(jnp.dot(member_rows.T, ancestor), member)
    places = jnp.arange(TREE, dtype=jnp.int32)
    row_places = row_start + jnp.arange(row_count, dtype=jnp.int32)
    same_seg = seg_rows[:, None] == seg_row[None, :]
    causal = places[None, :] <= row_places[:, None]
    allowed = (reach_table > 0.5) & (jnp.logical_not(same_seg) | causal)
    row_positions = lax.dynamic_slice_in_dim(positions, row_start, row_count, 0)
    return (allowed, row_positions)


OUTER = (((0,), (0,)), ((), ()))
INNER = (((1,), (1,)), ((), ()))


def dot(left, right):
    return jnp.dot(left, right, preferred_element_type=F32)


def dot_inner(left, right):
    return lax.dot_general(left, right, INNER, preferred_element_type=F32)


def dot_outer(left, right):
    return lax.dot_general(left, right, OUTER, preferred_element_type=F32)


def exchange(pieces, axis):
    size = lax.axis_size(axis)
    me = lax.axis_index(axis)
    got = jnp.zeros_like(pieces)
    own = lax.dynamic_index_in_dim(pieces, me, 0, keepdims=True)
    got = lax.dynamic_update_slice_in_dim(got, own, me, 0)
    for step in range(1, size):
        other = me ^ step
        piece = lax.dynamic_index_in_dim(pieces, other, 0, keepdims=True)
        arrived = lax.ppermute(piece, axis, [(i, i ^ step) for i in range(size)])
        got = lax.dynamic_update_slice_in_dim(got, arrived, other, 0)
    return got


def masked_scores(query_bf, key_all, allowed):
    raw_scores = jnp.einsum(
        "brgd,btd->bgrt", query_bf, key_all, preferred_element_type=F32
    ) * HD ** (-0.5)
    return jnp.where(allowed[:, None], raw_scores, MASKED)


def gather_kv(own):
    return lax.all_gather(own, "dp", axis=1, tiled=True)


def scatter_kv(whole):
    return lax.psum_scatter(whole, "dp", scatter_dimension=1, tiled=True)


def scatter_attn(whole):
    mine = lax.psum_scatter(whole, "section", scatter_dimension=0, tiled=True)
    return lax.psum_scatter(mine, "tensor", scatter_dimension=1, tiled=True)[0]


def gather_rows(own):
    mine = lax.all_gather(own, "tensor", axis=0, tiled=True)
    return lax.all_gather(mine, "section", axis=0)


def gather_mlp(own):
    mine = lax.all_gather(own, "dp", axis=0, tiled=True)
    return lax.all_gather(mine, "section", axis=0, tiled=True)


def scatter_mlp(whole):
    mine = lax.psum_scatter(whole, "section", scatter_dimension=0, tiled=True)
    return lax.psum_scatter(mine, "dp", scatter_dimension=0, tiled=True)


def embed(q_pre, k_pre, q_scale, k_scale, cos_table, sine_table):
    queries = rms_scale(q_pre, q_scale)
    keys = rms_scale(k_pre, k_scale)
    return (
        rotate(queries, cos_table[:, :, None], sine_table[:, :, None]),
        rotate(keys, cos_table, sine_table),
    )


def layer_forward(hidden_in, own_in, weights, gains, slot):
    attn_scale, mlp_scale, q_scale, k_scale = gains
    w_qkv, w_outt, w_gate, w_up, w_down = weights
    allowed, cos_table, sine_table = slot
    trees, row_count, depth = hidden_in.shape
    q_width = w_outt.shape[1]
    normed = rms_scale(hidden_in.astype(F32), attn_scale).astype(BF16).reshape(-1, depth)
    qkv = dot(normed, w_qkv).reshape(trees, row_count, -1)
    q_pre = qkv[:, :, :q_width].reshape(trees, row_count, -1, HD)
    k_pre = qkv[:, :, q_width : q_width + HD]
    value_bf = qkv[:, :, q_width + HD :].astype(BF16)
    queries, keys_rot = embed(q_pre, k_pre, q_scale, k_scale, cos_table, sine_table)
    query_bf = queries.astype(BF16)
    kv_all = gather_kv(jnp.concatenate([keys_rot.astype(BF16), value_bf], axis=2))
    key_all = kv_all[:, :, :HD]
    value_all = kv_all[:, :, HD:]
    scores = masked_scores(query_bf, key_all, allowed)
    row_max = jnp.max(scores, axis=-1, keepdims=True)
    exp_scores = jnp.exp(scores - row_max)
    row_total = jnp.sum(exp_scores, axis=-1, keepdims=True)
    prob_bf = (exp_scores / row_total).astype(BF16)
    log_total = row_max + jnp.log(row_total)
    attended = jnp.einsum("bgrt,btd->brgd", prob_bf, value_all, preferred_element_type=F32)
    attended_bf = attended.reshape(trees * row_count, -1).astype(BF16)
    attn_partial = dot_inner(attended_bf, w_outt).astype(BF16).reshape(trees, row_count, depth)
    middle = own_in + scatter_attn(attn_partial).astype(F32)
    mlp_in = gather_mlp(rms_scale(middle, mlp_scale).astype(BF16))
    gate_pre = dot_inner(mlp_in, w_gate)
    upward = dot_inner(mlp_in, w_up)
    hidden_bf = swiglu(gate_pre, upward).astype(BF16)
    mlp_rows = scatter_mlp(dot(hidden_bf, w_down).astype(BF16))
    output_own = (middle + mlp_rows.astype(F32)).astype(BF16)
    output_bf = gather_rows(output_own)
    stored = (
        own_in, normed, q_pre, k_pre, query_bf, key_all, value_all, log_total, attended_bf,
        middle, mlp_in, gate_pre, upward, hidden_bf,
    )
    return (output_bf, output_own.astype(F32), stored)


def layer_backward(grad_own, stored, weights, gains, slot, shared_kv):
    attn_scale, mlp_scale, q_scale, k_scale = gains
    w_qkv, w_outt, w_gate, w_up, w_down = weights
    allowed, cos_table, sine_table = slot
    (
        own_in, normed, q_pre, k_pre, query_bf, key_all, value_all, log_total, attended_bf,
        middle, mlp_in, gate_pre, upward, hidden_bf,
    ) = stored
    trees, row_count = query_bf.shape[:2]
    depth = normed.shape[1]
    grad_mlp = gather_mlp(grad_own)
    grad_hidden = dot_inner(grad_mlp, w_down)
    _, swiglu_pull = jax.vjp(swiglu, gate_pre, upward)
    grad_gate, grad_upward = swiglu_pull(grad_hidden)
    gate_bf = grad_gate.astype(BF16)
    up_bf = grad_upward.astype(BF16)
    mlp_rows = scatter_mlp((dot(gate_bf, w_gate) + dot(up_bf, w_up)).astype(BF16))
    _, mlp_norm_pull = jax.vjp(rms_scale, middle, mlp_scale)
    grad_middle, grad_mlp_scale = mlp_norm_pull(mlp_rows.astype(F32))
    grad_middle = grad_middle + grad_own.astype(F32)
    grad_attn = gather_rows(grad_middle.astype(BF16)).reshape(-1, depth)
    grad_heads = dot(grad_attn, w_outt).astype(BF16).reshape(query_bf.shape)
    scores = masked_scores(query_bf, key_all, allowed)
    prob_full = jnp.exp(scores - log_total)
    grad_prob = jnp.einsum("brgd,btd->bgrt", grad_heads, value_all, preferred_element_type=F32)
    row_dot = jnp.sum(prob_full * grad_prob, axis=-1, keepdims=True)
    grad_scores = (prob_full * (grad_prob - row_dot)).astype(BF16)
    scale_factor = HD ** (-0.5)
    grad_query = (
        jnp.einsum("bgrt,btd->brgd", grad_scores, key_all, preferred_element_type=F32)
        * scale_factor
    )
    grad_key_all = (
        jnp.einsum("bgrt,brgd->btd", grad_scores, query_bf, preferred_element_type=F32)
        * scale_factor
    )
    grad_value_all = jnp.einsum(
        "bgrt,brgd->btd", prob_full.astype(BF16), grad_heads, preferred_element_type=F32
    )
    grad_kv = scatter_kv(jnp.concatenate([grad_key_all, grad_value_all], axis=2).astype(BF16))
    if shared_kv:
        total = lax.psum(grad_kv, "section")
        grad_kv = jnp.where(lax.axis_index("section") == 0, total, jnp.zeros_like(total))
    _, embedding_pull = jax.vjp(
        partial(embed, cos_table=cos_table, sine_table=sine_table), q_pre, k_pre, q_scale, k_scale
    )
    grad_q_pre, grad_k_pre, grad_q_scale, grad_k_scale = embedding_pull(
        (grad_query, grad_kv[:, :, :HD].astype(F32))
    )
    qkv_grad = jnp.concatenate(
        [
            grad_q_pre.astype(BF16).reshape(trees, row_count, -1),
            grad_k_pre.astype(BF16),
            grad_kv[:, :, HD:],
        ],
        axis=2,
    ).reshape(trees * row_count, -1)
    attn_partial = dot_inner(qkv_grad, w_qkv).astype(BF16).reshape(trees, row_count, depth)
    attn_rows = scatter_attn(attn_partial)
    _, attn_norm_pull = jax.vjp(rms_scale, own_in, attn_scale)
    grad_residual, grad_attn_scale = attn_norm_pull(attn_rows.astype(F32))
    incoming_own = (grad_residual + grad_middle).astype(BF16)
    incoming = gather_rows(incoming_own)
    products = (
        (normed, qkv_grad),
        (grad_attn, attended_bf),
        (gate_bf, mlp_in),
        (up_bf, mlp_in),
        (hidden_bf, grad_mlp),
    )
    gain_grads = jnp.concatenate([grad_attn_scale, grad_mlp_scale, grad_q_scale, grad_k_scale])
    return (incoming, incoming_own, products, gain_grads)


def swap_cores(mine, other):
    core = lax.axis_index("section")
    arrived = lax.ppermute(other, "section", [(0, 1), (1, 0)])
    return (jnp.where(core == 0, mine, arrived), jnp.where(core == 0, arrived, mine))


def on_device(
    inputs, cotangent, seg_ids, parents, order, attn_gain, w_query, w_key, w_value, w_out,
    q_gain, k_gain, mlp_gain, w_gate, w_up, w_down,
):
    core = lax.axis_index("section")
    data_index = lax.axis_index("dp")
    tensor_index = lax.axis_index("tensor")
    dp_size = lax.axis_size("dp")
    tensor_size = lax.axis_size("tensor")
    trees, row_count, depth = inputs.shape
    own_rows = row_count // tensor_size
    row_start = data_index * row_count
    own_depth = w_query.shape[1]
    q_width = w_query.shape[2] // 2
    shared_kv = w_key.shape[2] == HD
    k_width = HD if shared_kv else w_key.shape[2] // 2
    own_units = w_gate.shape[2]
    share = own_units // (2 * dp_size)

    def pick(stacked, index):
        return lax.dynamic_index_in_dim(stacked, index, 0, keepdims=False)

    gains_own = jnp.concatenate([attn_gain[0], mlp_gain[0], q_gain[0], k_gain[0]])
    gains_all = lax.all_gather(gains_own, ("section", "dp")).astype(F32)
    gains_all = gains_all.reshape(2, dp_size, -1)
    gains = [
        (
            gains_all[layer, :, :own_depth].reshape(depth),
            gains_all[layer, :, own_depth : 2 * own_depth].reshape(depth),
            gains_all[layer, 0, 2 * own_depth : 2 * own_depth + HD],
            gains_all[layer, 0, 2 * own_depth + HD :],
        )
        for layer in range(2)
    ]

    def halves(width, array):
        return [array[:, :width], array[:, array.shape[1] - width :]]

    attn_halves = jnp.stack(
        [
            jnp.concatenate(parts, axis=1)
            for parts in zip(
                halves(q_width, w_query[0]),
                halves(k_width, w_key[0]),
                halves(k_width, w_value[0]),
                halves(q_width, w_out[0].T),
            )
        ]
    )
    attn_shards = swap_cores(pick(attn_halves, core), pick(attn_halves, 1 - core))
    unit_blocks = jnp.stack([w_gate[0].T, w_up[0].T, w_down[0]]).reshape(
        3, 2, dp_size, share, own_depth
    )
    unit_blocks = unit_blocks.transpose(1, 2, 0, 3, 4)
    unit_shards = swap_cores(pick(unit_blocks, core), pick(unit_blocks, 1 - core))

    qkv_width = q_width + 2 * k_width
    weights = []
    for layer in range(2):
        attn_all = lax.all_gather(attn_shards[layer], "dp", axis=0, tiled=True)
        pieces = exchange(unit_shards[layer], "dp")
        pieces = pieces.transpose(1, 2, 0, 3).reshape(3, share, depth)
        mats = [lax.all_gather(pieces[i], "tensor", axis=0, tiled=True) for i in range(3)]
        weights.append((attn_all[:, :qkv_width], attn_all[:, qkv_width:], *mats))

    def slot_setup(slot_index):
        tree_id = pick(order, slot_index)
        allowed, row_positions = path_mask(
            pick(seg_ids, tree_id), pick(parents, tree_id), row_start, row_count
        )
        cos_table, sine_table = rope_tables(row_positions, HD)
        return (pick(inputs, tree_id), allowed, cos_table[:, 0], sine_table[:, 0])

    setups = [slot_setup(i) for i in range(trees)]
    hidden, *slot = (jnp.stack(item) for item in zip(*setups))

    def own_part(whole):
        return lax.dynamic_slice_in_dim(
            pick(whole, core), tensor_index * own_rows, own_rows, 0
        )

    own_in = own_part(hidden).astype(F32)
    outputs, kept = [], []
    for layer in range(2):
        hidden, own_in, stored = layer_forward(hidden, own_in, weights[layer], gains[layer], slot)
        outputs.append(hidden)
        kept.append(stored)

    grad_own = own_part(cotangent)
    grads, weight_grads, gain_grads = [None, None], [None, None], [None, None]
    for layer in (1, 0):
        grads[layer], grad_own, products, gain_grads[layer] = layer_backward(
            grad_own, kept[layer], weights[layer], gains[layer], slot, shared_kv
        )
        whole = [dot_outer(left, right).astype(BF16) for left, right in products]
        attn_grad = lax.psum_scatter(
            jnp.concatenate(whole[:2], axis=1), "dp", scatter_dimension=0, tiled=True
        )
        unit_grad = [
            lax.psum_scatter(item, "tensor", scatter_dimension=0, tiled=True) for item in whole[2:]
        ]
        pieces = jnp.stack(unit_grad).reshape(3, share, dp_size, own_depth).transpose(2, 0, 1, 3)
        weight_grads[layer] = (attn_grad, exchange(pieces, "dp"))

    def bring_home(first, second):
        mine, other = jnp.where(core == 0, first, second), jnp.where(core == 0, second, first)
        arrived = lax.ppermute(other, "section", [(0, 1), (1, 0)])
        return (jnp.where(core == 0, mine, arrived), jnp.where(core == 0, arrived, mine))

    attn_home = bring_home(weight_grads[0][0], weight_grads[1][0])
    unit_home = jnp.stack(bring_home(weight_grads[0][1], weight_grads[1][1]))
    unit_home = unit_home.transpose(2, 0, 1, 3, 4).reshape(3, own_units, own_depth)

    def joined(start, width):
        parts = [half[:, start : start + width] for half in attn_home]
        if shared_kv and start in (q_width, q_width + k_width):
            return parts[0].astype(F32)
        return jnp.concatenate(parts, axis=1).astype(F32)

    gain_total = lax.psum(jnp.stack(gain_grads), ("section", "dp", "tensor"))
    gain_own = pick(gain_total, core)
    share_width = attn_gain.shape[1]
    attn_gain_grad = lax.dynamic_slice_in_dim(gain_own, data_index * share_width, share_width, 0)
    mlp_gain_grad = lax.dynamic_slice_in_dim(
        gain_own, depth + data_index * share_width, share_width, 0
    )
    return (
        jnp.where(core == 0, outputs[0], outputs[1])[None],
        jnp.where(core == 0, grads[0], grads[1])[None],
        attn_gain_grad[None],
        joined(0, q_width)[None],
        joined(q_width, k_width)[None],
        joined(q_width + k_width, k_width)[None],
        joined(qkv_width, q_width).T[None],
        gain_own[2 * depth : 2 * depth + HD][None],
        gain_own[2 * depth + HD :][None],
        mlp_gain_grad[None],
        unit_home[0].T.astype(F32)[None],
        unit_home[1].T.astype(F32)[None],
        unit_home[2].astype(F32)[None],
    )


def solution(mesh):
    rows = P(None, "dp", None)
    wide = P("section", "dp", "tensor")
    tall = P("section", "tensor", "dp")
    gain = P("section", "dp")
    head_gain = P("section", None)
    slots = P("section", None, "dp", None)
    in_specs = (
        rows, rows, P(), P(), P(), gain, wide, wide, wide, tall, head_gain, head_gain, gain,
        wide, wide, tall,
    )
    out_specs = (
        slots, slots, gain, wide, wide, wide, tall, head_gain, head_gain, gain, wide, wide, tall,
    )
    return jax.shard_map(
        on_device, mesh=mesh, in_specs=in_specs, out_specs=out_specs, check_vma=False
    )
```

time: 1990 us -> 1960 us (0.985)
  waiting for transfers between devices: 1310 us -> 1480 us
  matrix products: 221 us -> 161 us
  local copies, waits for them, and re-layouts: 154 us -> 99.9 us
  blocking collectives: 91.4 us -> 65.2 us
  starting transfers between devices: 49.6 us -> 23.4 us
  other arithmetic: 120 us -> 97.8 us
    reduce_scatter x7 -> x22, waiting for transfers between devices: 221 us -> 598 us  [the longest x6 235 us: on_device(): lax.psum_scatter(item, 'tensor', scatter_dimension=0, tiled=True)]
    unnamed x53 -> x60, waiting for transfers between devices: 302 us -> 91.9 us
    dot_general x15 -> x10, matrix products: 80.9 us -> 33.3 us  [dot(): return jnp.dot(left, right, preferred_element_type=F32)]
    unnamed x529 -> x372, local copies, waits for them, and re-layouts: 88.7 us -> 47 us
    psum x1, blocking collectives: 77.7 us -> 39.7 us  [on_device(): gain_total = lax.psum(jnp.stack(gain_grads), ('section', 'dp', 'tensor'))]
    dot_general x15 -> x10, matrix products: 69.7 us -> 48.7 us  [dot_inner(): return lax.dot_general(left, right, INNER, preferred_element_type=F32)]
    ppermute x18 -> x12, starting transfers between devices: 38.2 us -> 17.9 us  [exchange(): arrived = lax.ppermute(piece, axis, [(i, i ^ step) for i in range(size)])]
    dot_general x5 -> x10, matrix products: 28.1 us -> 44 us  [dot_outer(): return lax.dot_general(left, right, OUTER, preferred_element_type=F32)]
  transfers between devices with their start and end apart: 63 -> 72, of which waited for: 49 -> 56; matrix products, arithmetic and copies ran while one was open for 11% -> 11% of each run, Pallas kernels for 0% -> 0%
where the time goes in v2:
time: 1960 us; the launch traced here: 1950 us
  waiting for transfers between devices  1480 us (76%)
  matrix products  161 us (8%)
  local copies, waits for them, and re-layouts  99.9 us (5%)
  other arithmetic  97.8 us (5%)
  blocking collectives  65.2 us (3%)
  starting transfers between devices  23.4 us (1%)
  between operations  21.9 us (1%)
    all_gather x6, waiting for transfers between devices, on_device(): lax.all_gather(pieces[i], 'tensor', axis=0, tiled=True)  263 us
    reduce_scatter x6, waiting for transfers between devices, on_device(): lax.psum_scatter(item, 'tensor', scatter_dimension=0, tiled=True)  235 us
    ppermute x12, waiting for transfers between devices, exchange(): arrived = lax.ppermute(piece, axis, [(i, i ^ step) for i in range(size)])  152 us
    reduce_scatter x4, waiting for transfers between devices, scatter_mlp(): return lax.psum_scatter(mine, 'dp', scatter_dimension=0, tiled=True)  127 us
    reduce_scatter x2, waiting for transfers between devices, on_device(): lax.psum_scatter(jnp.concatenate(whole[:2], axis=1), 'dp', scatter_dimens...  120 us
    all_gather x6, waiting for transfers between devices, gather_rows(): mine = lax.all_gather(own, 'tensor', axis=0, tiled=True)  96.6 us
    all_gather x2, waiting for transfers between devices, on_device(): attn_all = lax.all_gather(attn_shards[layer], 'dp', axis=0, tiled=True)  93.2 us
    unnamed x60, waiting for transfers between devices  91.9 us
  transfers between devices with their start and end apart: 72, of which 56 were waited for; matrix products, arithmetic and copies ran while one was open for 11% of the time, Pallas kernels for 0%

profile of v2, /device:TPU:0, one launch (start us, length us, event | category | flops | bytes accessed | tf_op | source)
XLA Modules:
  0.0 1952.0 jit_solution(2116463953616512915)
XLA Ops:
  17.1 25.5 %all-gather.9 = bf16[8,1,1280]{2,1,0:T(2,128)(2,1)S(1)} all-gather(bf16[1,1,1280]{2,1,0:T(2,128)(2,1)S(1)} %reshape.733), channel_id=2, replica_groups=mesh['section'=2,'dp'=4,'tensor'=4] {'section','dp'}, dimensions={0}, use_global_device_ids=true | all-gather | bytes 23040 | tf_op jit(solution)/shard_map/all_gather | solution.py:306
  51.1 29.4 %all-gather.41.cloned.1.call-done = bf16[2048,768]{1,0:T(8,128)(2,1)} async-done(((bf16[512,768]{1,0:T(8,128)(2,1)}), bf16[2048,768]{1,0:T(8,128)(2,1)}) %all-gather.41.cloned.1.call-update) | async-done | bytes 3145744 | tf_op jit(solution)/shard_map/all_gather | solution.py:342
  102.6 12.3 all-gather.43.cloned.1.call-done
  146.0 21.8 %reduce-scatter.83.cloned.1.call-done = bf16[1,72,2048]{2,1,0:T(8,128)(2,1)} async-done(((bf16[1,288,2048]{2,1,0:T(8,128)(2,1)}), bf16[1,72,2048]{2,1,0:T(8,128)(2,1)}) %reduce-scatter.83.cloned.1.call-update) | async-done | bytes 294928
  179.8 40.8 %collective-permute-done.2 = bf16[1,3,192,512]{3,2,0,1:T(8,128)(2,1)S(1)} collective-permute-done((bf16[1,3,192,512]{3,2,0,1:T(8,128)(2,1)S(1)}, bf16[1,3,192,512]{3,2,0,1:T(8,128)(2,1)S(1)}, u32[]{:S(2)}, u32[]{:S(2)}) %collective-permute-start.2) | collective-permute-done | bytes 589856 | tf_op jit(solution)/shard_map/ppermute | solution.py:114
  220.6 17.7 collective-permute-done.3
  245.1 48.7 %all-gather.49.cloned.1.call-done = bf16[768,2048]{1,0:T(8,128)(2,1)} async-done(((bf16[192,2048]{1,0:T(8,128)(2,1)}), bf16[768,2048]{1,0:T(8,128)(2,1)}) %all-gather.49.cloned.1.call-update) | async-done | bytes 3145744 | tf_op jit(solution)/shard_map/all_gather | solution.py:345
  293.8 12.6 all-gather.47.cloned.1.call-done
  312.4 41.8 %all-gather.51.cloned.1.call-done = bf16[768,2048]{1,0:T(8,128)(2,1)} async-done(((bf16[192,2048]{1,0:T(8,128)(2,1)}), bf16[768,2048]{1,0:T(8,128)(2,1)}) %all-gather.51.cloned.1.call-update) | async-done | bytes 3145744 | tf_op jit(solution)/shard_map/all_gather | solution.py:345
  360.1 40.0 %all-gather.53.cloned.1.call-done = bf16[768,2048]{1,0:T(8,128)(2,1)} async-done(((bf16[192,2048]{1,0:T(8,128)(2,1)}), bf16[768,2048]{1,0:T(8,128)(2,1)}) %all-gather.53.cloned.1.call-update) | async-done | bytes 3145744 | tf_op jit(solution)/shard_map/all_gather | solution.py:345
  415.9 32.6 %reduce-scatter.43.cloned.1.call-done = bf16[72,2048]{1,0:T(8,128)(2,1)} async-done(((bf16[288,2048]{1,0:T(8,128)(2,1)}), bf16[72,2048]{1,0:T(8,128)(2,1)}) %reduce-scatter.43.cloned.1.call-update) | async-done | bytes 294928 | tf_op jit(solution)/shard_map/reduce_scatter | solution.py:151
  450.3 26.5 %all-gather.55.cloned.1.call-done = bf16[288,2048]{1,0:T(8,128)(2,1)} async-done(((bf16[72,2048]{1,0:T(8,128)(2,1)}), bf16[288,2048]{1,0:T(8,128)(2,1)}) %all-gather.55.cloned.1.call-update) | async-done | bytes 1179664 | tf_op jit(solution)/shard_map/all_gather | solution.py:140
  477.6 11.9 all-gather.85.cloned.1.call-done
  492.4 63.7 %all-gather.57.cloned.1.call-done = bf16[2048,768]{1,0:T(8,128)(2,1)} async-done(((bf16[512,768]{1,0:T(8,128)(2,1)}), bf16[2048,768]{1,0:T(8,128)(2,1)}) %all-gather.57.cloned.1.call-update) | async-done | bytes 3145744 | tf_op jit(solution)/shard_map/all_gather | solution.py:342
  565.3 25.5 %all-gather.59.cloned.1.call-done = bf16[2,1152,256]{2,1,0:T(8,128)(2,1)} async-done(((bf16[2,288,256]{2,1,0:T(8,128)(2,1)}), bf16[2,1152,256]{2,1,0:T(8,128)(2,1)}) %all-gather.59.cloned.1.call-update) | async-done | bytes 1179664 | tf_op jit(solution)/shard_map/all_gather | solution.py:127
  610.9 32.7 %reduce-scatter.85.cloned.1.call-done = bf16[1,72,2048]{2,1,0:T(8,128)(2,1)} async-done(((bf16[1,288,2048]{2,1,0:T(8,128)(2,1)}), bf16[1,72,2048]{2,1,0:T(8,128)(2,1)}) %reduce-scatter.85.cloned.1.call-update) | async-done | bytes 294928
  653.6 40.4 %collective-permute-done.5 = bf16[1,3,192,512]{3,2,0,1:T(8,128)(2,1)S(1)} collective-permute-done((bf16[1,3,192,512]{3,2,0,1:T(8,128)(2,1)S(1)}, bf16[1,3,192,512]{3,2,0,1:T(8,128)(2,1)S(1)}, u32[]{:S(2)}, u32[]{:S(2)}) %collective-permute-start.5) | collective-permute-done | bytes 589856 | tf_op jit(solution)/shard_map/ppermute | solution.py:114
  694.1 18.1 collective-permute-done.6
  716.8 27.4 %all-gather.89.cloned.1.call-done = bf16[1,288,2048]{2,1,0:T(8,128)(2,1)} async-done(((bf16[1,72,2048]{2,1,0:T(8,128)(2,1)}), bf16[1,288,2048]{2,1,0:T(8,128)(2,1)}) %all-gather.89.cloned.1.call-update) | async-done | bytes 1179664 | tf_op jit(solution)/shard_map/all_gather | solution.py:145
  746.3 43.5 %all-gather.67.cloned.1.call-done = bf16[768,2048]{1,0:T(8,128)(2,1)} async-done(((bf16[192,2048]{1,0:T(8,128)(2,1)}), bf16[768,2048]{1,0:T(8,128)(2,1)}) %all-gather.67.cloned.1.call-update) | async-done | bytes 3145744 | tf_op jit(solution)/shard_map/all_gather | solution.py:345
  789.7 12.6 all-gather.63.cloned.1.call-done
  808.3 41.7 %all-gather.65.cloned.1.call-done = bf16[768,2048]{1,0:T(8,128)(2,1)} async-done(((bf16[192,2048]{1,0:T(8,128)(2,1)}), bf16[768,2048]{1,0:T(8,128)(2,1)}) %all-gather.65.cloned.1.call-update) | async-done | bytes 3145744 | tf_op jit(solution)/shard_map/all_gather | solution.py:345
  862.7 47.0 %all-gather.69.cloned.1.call-done = bf16[768,2048]{1,0:T(8,128)(2,1)} async-done(((bf16[192,2048]{1,0:T(8,128)(2,1)}), bf16[768,2048]{1,0:T(8,128)(2,1)}) %all-gather.69.cloned.1.call-update) | async-done | bytes 3145744 | tf_op jit(solution)/shard_map/all_gather | solution.py:345
  933.2 32.5 %reduce-scatter.53.cloned.1.call-done = bf16[72,2048]{1,0:T(8,128)(2,1)} async-done(((bf16[288,2048]{1,0:T(8,128)(2,1)}), bf16[72,2048]{1,0:T(8,128)(2,1)}) %reduce-scatter.53.cloned.1.call-update) | async-done | bytes 294928 | tf_op jit(solution)/shard_map/reduce_scatter | solution.py:151
  969.7 26.6 %all-gather.73.cloned.1.call-done = bf16[288,2048]{1,0:T(8,128)(2,1)} async-done(((bf16[72,2048]{1,0:T(8,128)(2,1)}), bf16[288,2048]{1,0:T(8,128)(2,1)}) %all-gather.73.cloned.1.call-update) | async-done | bytes 1179664 | tf_op jit(solution)/shard_map/all_gather | solution.py:140
  996.7 12.0 all-gather.93.cloned.1.call-done
  1029.9 24.8 %reduce-scatter.55.cloned.1.call-done = bf16[2,288,256]{2,1,0:T(8,128)(2,1)} async-done(((bf16[2,1152,256]{2,1,0:T(8,128)(2,1)}), bf16[2,288,256]{2,1,0:T(8,128)(2,1)}) %reduce-scatter.55.cloned.1.call-update) | async-done | bytes 294928 | tf_op jit(solution)/shard_map/reduce_scatter | solution.py:131
  1071.1 14.0 reduce-scatter.47.cloned.1.call-done
  1085.4 32.4 %reduce-scatter.87.cloned.1.call-done = bf16[1,72,2048]{2,1,0:T(8,128)(2,1)} async-done(((bf16[1,288,2048]{2,1,0:T(8,128)(2,1)}), bf16[1,72,2048]{2,1,0:T(8,128)(2,1)}) %reduce-scatter.87.cloned.1.call-update) | async-done | bytes 294928
  1119.6 29.6 %reduce-scatter.49.cloned.1.call-done = bf16[72,2048]{1,0:T(8,128)(2,1)} async-done(((bf16[288,2048]{1,0:T(8,128)(2,1)}), bf16[72,2048]{1,0:T(8,128)(2,1)}) %reduce-scatter.49.cloned.1.call-update) | async-done | bytes 294928 | tf_op jit(solution)/shard_map/reduce_scatter | solution.py:151
  1151.8 29.2 %all-gather.75.cloned.1.call-done = bf16[288,2048]{1,0:T(8,128)(2,1)} async-done(((bf16[72,2048]{1,0:T(8,128)(2,1)}), bf16[288,2048]{1,0:T(8,128)(2,1)}) %all-gather.75.cloned.1.call-update) | async-done | bytes 1179664 | tf_op jit(solution)/shard_map/all_gather | solution.py:145
  1215.8 32.6 %reduce-scatter.61.cloned.1.call-done = bf16[72,2048]{1,0:T(8,128)(2,1)} async-done(((bf16[288,2048]{1,0:T(8,128)(2,1)}), bf16[72,2048]{1,0:T(8,128)(2,1)}) %reduce-scatter.61.cloned.1.call-update) | async-done | bytes 294928 | tf_op jit(solution)/shard_map/reduce_scatter | solution.py:151
  1252.3 26.5 %all-gather.79.cloned.1.call-done = bf16[288,2048]{1,0:T(8,128)(2,1)} async-done(((bf16[72,2048]{1,0:T(8,128)(2,1)}), bf16[288,2048]{1,0:T(8,128)(2,1)}) %all-gather.79.cloned.1.call-update) | async-done | bytes 1179664 | tf_op jit(solution)/shard_map/all_gather | solution.py:140
  1279.2 12.1 all-gather.95.cloned.1.call-done
  1311.6 24.9 %reduce-scatter.63.cloned.1.call-done = bf16[2,288,256]{2,1,0:T(8,128)(2,1)} async-done(((bf16[2,1152,256]{2,1,0:T(8,128)(2,1)}), bf16[2,288,256]{2,1,0:T(8,128)(2,1)}) %reduce-scatter.63.cloned.1.call-update) | async-done | bytes 294928 | tf_op jit(solution)/shard_map/reduce_scatter | solution.py:131
  1401.4 28.1 %reduce-scatter.79.cloned.1.call-done = bf16[192,2048]{1,0:T(8,128)(2,1)} async-done(((bf16[768,2048]{1,0:T(8,128)(2,1)}), bf16[192,2048]{1,0:T(8,128)(2,1)}) %reduce-scatter.79.cloned.1.call-update) | async-done | bytes 786448 | tf_op jit(solution)/shard_map/reduce_scatter | solution.py:382
  1432.5 44.6 %reduce-scatter.77.cloned.1.call-done = bf16[192,2048]{1,0:T(8,128)(2,1)} async-done(((bf16[768,2048]{1,0:T(8,128)(2,1)}), bf16[192,2048]{1,0:T(8,128)(2,1)}) %reduce-scatter.77.cloned.1.call-update) | async-done | bytes 786448 | tf_op jit(solution)/shard_map/reduce_scatter | solution.py:382
  1480.1 43.8 %reduce-scatter.81.cloned.1.call-done = bf16[192,2048]{1,0:T(8,128)(2,1)} async-done(((bf16[768,2048]{1,0:T(8,128)(2,1)}), bf16[192,2048]{1,0:T(8,128)(2,1)}) %reduce-scatter.81.cloned.1.call-update) | async-done | bytes 786448 | tf_op jit(solution)/shard_map/reduce_scatter | solution.py:382
  1535.3 35.4 %reduce-scatter.71.cloned.1.call-done = bf16[192,2048]{1,0:T(8,128)(2,1)} async-done(((bf16[768,2048]{1,0:T(8,128)(2,1)}), bf16[192,2048]{1,0:T(8,128)(2,1)}) %reduce-scatter.71.cloned.1.call-update) | async-done | bytes 786448 | tf_op jit(solution)/shard_map/reduce_scatter | solution.py:382
  1573.7 43.8 %reduce-scatter.73.cloned.1.call-done = bf16[192,2048]{1,0:T(8,128)(2,1)} async-done(((bf16[768,2048]{1,0:T(8,128)(2,1)}), bf16[192,2048]{1,0:T(8,128)(2,1)}) %reduce-scatter.73.cloned.1.call-update) | async-done | bytes 786448 | tf_op jit(solution)/shard_map/reduce_scatter | solution.py:382
  1624.8 39.5 %reduce-scatter.75.cloned.1.call-done = bf16[192,2048]{1,0:T(8,128)(2,1)} async-done(((bf16[768,2048]{1,0:T(8,128)(2,1)}), bf16[192,2048]{1,0:T(8,128)(2,1)}) %reduce-scatter.75.cloned.1.call-update) | async-done | bytes 786448 | tf_op jit(solution)/shard_map/reduce_scatter | solution.py:382
  1680.0 17.8 collective-permute-done.9
  1697.8 17.5 collective-permute-done.10
  1725.5 12.1 all-gather.87.cloned.1.call-done
  1746.0 56.9 %reduce-scatter.69.cloned.1.call-done = bf16[512,768]{1,0:T(8,128)(2,1)} async-done(((bf16[2048,768]{1,0:T(8,128)(2,1)}), bf16[512,768]{1,0:T(8,128)(2,1)}) %reduce-scatter.69.cloned.1.call-update) | async-done | bytes 786448 | tf_op jit(solution)/shard_map/reduce_scatter | solution.py:378
  1802.9 63.0 %reduce-scatter.67.cloned.1.call-done = bf16[512,768]{1,0:T(8,128)(2,1)} async-done(((bf16[2048,768]{1,0:T(8,128)(2,1)}), bf16[512,768]{1,0:T(8,128)(2,1)}) %reduce-scatter.67.cloned.1.call-update) | async-done | bytes 786448 | tf_op jit(solution)/shard_map/reduce_scatter | solution.py:378
  1880.3 15.9 all-gather.81.cloned.1.call-done
  1897.8 39.7 %psum.7 = f32[2,4352]{1,0:T(2,128)S(1)} all-reduce(f32[2,4352]{1,0:T(2,128)S(1)} %pad_maximum_fusion.18), channel_id=1, replica_groups=mesh['section'=2,'dp'=4,'tensor'=4] {'section','dp','tensor'}, use_global_device_ids=true, to_apply=%region_56.57 | all-reduce | flops 8704 | bytes 69632 | tf_op jit(solution)/shard_map/psum | solution.py:402
  (760 shorter events, 460.6 us)
Async XLA Ops:
  7.2 73.3 %all-gather.41.cloned.1.call-start = ((), (), s32[]{:S(2)}) async-start(), calls=%async_computation.26 | async-start | bytes 3932160 | tf_op jit(solution)/shard_map/all_gather | solution.py:342
  13.7 101.2 %all-gather.43.cloned.1.call-start = ((), (), s32[]{:S(2)}) async-start(), calls=%async_computation.27 | async-start | bytes 1474560 | tf_op jit(solution)/shard_map/all_gather | solution.py:127
  85.6 49.4 %reduce-scatter.39.cloned.1.call-start = ((), (), s32[]{:S(2)}) async-start(), calls=%async_computation.28 | async-start | bytes 3538944 | tf_op jit(solution)/shard_map/reduce_scatter | solution.py:135
  135.1 105.3 %all-gather.45.cloned.1.call-start = ((), (), s32[]{:S(2)}) async-start(), calls=%async_computation.29 | async-start | bytes 1474560 | tf_op jit(solution)/shard_map/all_gather | solution.py:145
  170.7 123.1 %all-gather.49.cloned.1.call-start = ((), (), s32[]{:S(2)}) async-start(), calls=%async_computation.31 | async-start | bytes 3932160 | tf_op jit(solution)/shard_map/all_gather | solution.py:345
  176.9 61.4 %collective-permute-start.3 = (bf16[1,3,192,512]{3,2,0,1:T(8,128)(2,1)S(1)}, bf16[1,3,192,512]{3,2,0,1:T(8,128)(2,1)S(1)}, u32[]{:S(2)}, u32[]{:S(2)}) collective-permute-start(bf16[1,3,192,512]{3,2,0,1:T(8,128)(2,1)S(1)} %get-tuple-element.146), channel_id=1, source_target_pairs={{0,8},{4,12},{8,0},{12,4},{1,9},{5,13},{9,1},{13,5},{2,10},{6,14},... | collective-permute-start | bytes 1769480 | tf_op jit(solution)/shard_map/ppermute | solution.py:114
  179.3 59.1 %collective-permute-start.4 = (bf16[1,3,192,512]{3,2,0,1:T(8,128)(2,1)S(1)}, bf16[1,3,192,512]{3,2,0,1:T(8,128)(2,1)S(1)}, u32[]{:S(2)}, u32[]{:S(2)}) collective-permute-start(bf16[1,3,192,512]{3,2,0,1:T(8,128)(2,1)S(1)} %get-tuple-element.145), channel_id=1, source_target_pairs={{0,12},{4,8},{8,4},{12,0},{1,13},{5,9},{9,5},{13,1},{2,14},{6,10},... | collective-permute-start | bytes 1769480 | tf_op jit(solution)/shard_map/ppermute | solution.py:114
  240.4 66.0 %all-gather.47.cloned.1.call-start = ((), (), s32[]{:S(2)}) async-start(), calls=%async_computation.30 | async-start | bytes 3538944 | tf_op jit(solution)/shard_map/all_gather | solution.py:146
  241.1 113.0 %all-gather.51.cloned.1.call-start = ((), (), s32[]{:S(2)}) async-start(), calls=%async_computation.32 | async-start | bytes 3932160 | tf_op jit(solution)/shard_map/all_gather | solution.py:345
  243.3 156.9 %all-gather.53.cloned.1.call-start = ((), (), s32[]{:S(2)}) async-start(), calls=%async_computation.33 | async-start | bytes 3932160 | tf_op jit(solution)/shard_map/all_gather | solution.py:345
  245.0 170.8 %reduce-scatter.41.cloned.1.call-start = ((), (), s32[]{:S(2)}) async-start(), calls=%async_computation.34 | async-start | bytes 3538944 | tf_op jit(solution)/shard_map/reduce_scatter | solution.py:150
  415.8 61.1 %all-gather.55.cloned.1.call-start = ((), (), s32[]{:S(2)}) async-start(), calls=%async_computation.36 | async-start | bytes 1474560 | tf_op jit(solution)/shard_map/all_gather | solution.py:140
  476.9 79.2 %all-gather.57.cloned.1.call-start = ((), (), s32[]{:S(2)}) async-start(), calls=%async_computation.37 | async-start | bytes 3932160 | tf_op jit(solution)/shard_map/all_gather | solution.py:342
  477.5 113.3 %all-gather.59.cloned.1.call-start = ((), (), s32[]{:S(2)}) async-start(), calls=%async_computation.38 | async-start | bytes 1474560 | tf_op jit(solution)/shard_map/all_gather | solution.py:127
  610.9 103.4 %all-gather.61.cloned.1.call-start = ((), (), s32[]{:S(2)}) async-start(), calls=%async_computation.40 | async-start | bytes 1474560 | tf_op jit(solution)/shard_map/all_gather | solution.py:145
  646.8 97.4 %all-gather.89.cloned.1.call-start = ((), (), s32[]{:S(2)}) async-start(), calls=%async_computation.72 | async-start | bytes 1474560 | tf_op jit(solution)/shard_map/all_gather | solution.py:145
  648.7 141.1 %all-gather.67.cloned.1.call-start = ((), (), s32[]{:S(2)}) async-start(), calls=%async_computation.43 | async-start | bytes 3932160 | tf_op jit(solution)/shard_map/all_gather | solution.py:345
  650.7 61.4 %collective-permute-start.6 = (bf16[1,3,192,512]{3,2,0,1:T(8,128)(2,1)S(1)}, bf16[1,3,192,512]{3,2,0,1:T(8,128)(2,1)S(1)}, u32[]{:S(2)}, u32[]{:S(2)}) collective-permute-start(bf16[1,3,192,512]{3,2,0,1:T(8,128)(2,1)S(1)} %get-tuple-element.139), channel_id=1, source_target_pairs={{0,8},{4,12},{8,0},{12,4},{1,9},{5,13},{9,1},{13,5},{2,10},{6,14},... | collective-permute-start | bytes 1769480 | tf_op jit(solution)/shard_map/ppermute | solution.py:114
  653.1 59.1 %collective-permute-start.7 = (bf16[1,3,192,512]{3,2,0,1:T(8,128)(2,1)S(1)}, bf16[1,3,192,512]{3,2,0,1:T(8,128)(2,1)S(1)}, u32[]{:S(2)}, u32[]{:S(2)}) collective-permute-start(bf16[1,3,192,512]{3,2,0,1:T(8,128)(2,1)S(1)} %get-tuple-element.138), channel_id=1, source_target_pairs={{0,12},{4,8},{8,4},{12,0},{1,13},{5,9},{9,5},{13,1},{2,14},{6,10},... | collective-permute-start | bytes 1769480 | tf_op jit(solution)/shard_map/ppermute | solution.py:114
  714.2 88.1 %all-gather.63.cloned.1.call-start = ((), (), s32[]{:S(2)}) async-start(), calls=%async_computation.41 | async-start | bytes 3538944 | tf_op jit(solution)/shard_map/all_gather | solution.py:146
  715.0 135.1 %all-gather.65.cloned.1.call-start = ((), (), s32[]{:S(2)}) async-start(), calls=%async_computation.42 | async-start | bytes 3932160 | tf_op jit(solution)/shard_map/all_gather | solution.py:345
  716.7 146.0 %all-gather.91.cloned.1.call-start = ((), (), s32[]{:S(2)}) async-start(), calls=%async_computation.73 | async-start | bytes 3538944 | tf_op jit(solution)/shard_map/all_gather | solution.py:146
  744.2 165.5 %all-gather.69.cloned.1.call-start = ((), (), s32[]{:S(2)}) async-start(), calls=%async_computation.44 | async-start | bytes 3932160 | tf_op jit(solution)/shard_map/all_gather | solution.py:345
  746.0 187.1 %reduce-scatter.51.cloned.1.call-start = ((), (), s32[]{:S(2)}) async-start(), calls=%async_computation.48 | async-start | bytes 3538944 | tf_op jit(solution)/shard_map/reduce_scatter | solution.py:150
  933.1 63.1 %all-gather.73.cloned.1.call-start = ((), (), s32[]{:S(2)}) async-start(), calls=%async_computation.50 | async-start | bytes 1474560 | tf_op jit(solution)/shard_map/all_gather | solution.py:140
  996.2 58.5 %reduce-scatter.55.cloned.1.call-start = ((), (), s32[]{:S(2)}) async-start(), calls=%async_computation.51 | async-start | bytes 1474560 | tf_op jit(solution)/shard_map/reduce_scatter | solution.py:131
  1071.1 78.0 %reduce-scatter.49.cloned.1.call-start = ((), (), s32[]{:S(2)}) async-start(), calls=%async_computation.46 | async-start | bytes 1474560 | tf_op jit(solution)/shard_map/reduce_scatter | solution.py:151
  1085.1 95.9 %all-gather.75.cloned.1.call-start = ((), (), s32[]{:S(2)}) async-start(), calls=%async_computation.53 | async-start | bytes 1474560 | tf_op jit(solution)/shard_map/all_gather | solution.py:145
  1215.8 63.1 %all-gather.79.cloned.1.call-start = ((), (), s32[]{:S(2)}) async-start(), calls=%async_computation.57 | async-start | bytes 1474560 | tf_op jit(solution)/shard_map/all_gather | solution.py:140
  1278.9 57.7 %reduce-scatter.63.cloned.1.call-start = ((), (), s32[]{:S(2)}) async-start(), calls=%async_computation.58 | async-start | bytes 1474560 | tf_op jit(solution)/shard_map/reduce_scatter | solution.py:131
  1306.0 78.6 %reduce-scatter.65.cloned.1.call-start = ((), (), s32[]{:S(2)}) async-start(), calls=%async_computation.59 | async-start | bytes 3538944 | tf_op jit(solution)/shard_map/reduce_scatter | solution.py:135
  1343.9 85.6 %reduce-scatter.79.cloned.1.call-start = ((), (), s32[]{:S(2)}) async-start(), calls=%async_computation.68 | async-start | bytes 3932160 | tf_op jit(solution)/shard_map/reduce_scatter | solution.py:382
  1350.1 127.0 %reduce-scatter.77.cloned.1.call-start = ((), (), s32[]{:S(2)}) async-start(), calls=%async_computation.67 | async-start | bytes 3932160 | tf_op jit(solution)/shard_map/reduce_scatter | solution.py:382
  1357.0 166.9 %reduce-scatter.81.cloned.1.call-start = ((), (), s32[]{:S(2)}) async-start(), calls=%async_computation.69 | async-start | bytes 3932160 | tf_op jit(solution)/shard_map/reduce_scatter | solution.py:382
  1363.9 206.8 %reduce-scatter.71.cloned.1.call-start = ((), (), s32[]{:S(2)}) async-start(), calls=%async_computation.64 | async-start | bytes 3932160 | tf_op jit(solution)/shard_map/reduce_scatter | solution.py:382
  1370.8 246.7 %reduce-scatter.73.cloned.1.call-start = ((), (), s32[]{:S(2)}) async-start(), calls=%async_computation.65 | async-start | bytes 3932160 | tf_op jit(solution)/shard_map/reduce_scatter | solution.py:382
  1377.7 286.6 %reduce-scatter.75.cloned.1.call-start = ((), (), s32[]{:S(2)}) async-start(), calls=%async_computation.66 | async-start | bytes 3932160 | tf_op jit(solution)/shard_map/reduce_scatter | solution.py:382
  1384.5 331.4 %reduce-scatter.89.cloned.1.call-start = ((), (), s32[]{:S(2)}) async-start(), calls=%async_computation.81 | async-start | bytes 1474560
  1385.1 340.1 %all-gather.83.cloned.1.call-start = ((), (), s32[]{:S(2)}) async-start(), calls=%async_computation.61 | async-start | bytes 1474560 | tf_op jit(solution)/shard_map/all_gather | solution.py:140
  1385.9 351.8 %all-gather.87.cloned.1.call-start = ((), (), s32[]{:S(2)}) async-start(), calls=%async_computation.71 | async-start | bytes 3538944 | tf_op jit(solution)/shard_map/all_gather | solution.py:141
  1386.4 416.5 %reduce-scatter.69.cloned.1.call-start = ((), (), s32[]{:S(2)}) async-start(), calls=%async_computation.63 | async-start | bytes 3932160 | tf_op jit(solution)/shard_map/reduce_scatter | solution.py:378
  1393.5 472.5 %reduce-scatter.67.cloned.1.call-start = ((), (), s32[]{:S(2)}) async-start(), calls=%async_computation.62 | async-start | bytes 3932160 | tf_op jit(solution)/shard_map/reduce_scatter | solution.py:378
  1401.2 494.9 %all-gather.81.cloned.1.call-start = ((), (), s32[]{:S(2)}) async-start(), calls=%async_computation.60 | async-start | bytes 1474560 | tf_op jit(solution)/shard_map/all_gather | solution.py:140
  1530.9 144.3 %collective-permute-start.12 = (bf16[1,3,192,512]{3,2,0,1:T(8,128)(2,1)}, bf16[1,3,192,512]{3,2,0,1:T(8,128)(2,1)}, u32[]{:S(2)}, u32[]{:S(2)}) collective-permute-start(bf16[1,3,192,512]{3,2,0,1:T(8,128)(2,1)} %get-tuple-element.132), channel_id=1, source_target_pairs={{0,4},{4,0},{8,12},{12,8},{1,5},{5,1},{9,13},{13,9},{2,6},{6,2},{1... | collective-permute-start | bytes 1769480 | tf_op jit(solution)/shard_map/ppermute | solution.py:114
  1532.4 144.5 %collective-permute-start.13 = (bf16[1,3,192,512]{3,2,0,1:T(8,128)(2,1)}, bf16[1,3,192,512]{3,2,0,1:T(8,128)(2,1)}, u32[]{:S(2)}, u32[]{:S(2)}) collective-permute-start(bf16[1,3,192,512]{3,2,0,1:T(8,128)(2,1)} %get-tuple-element.131), channel_id=1, source_target_pairs={{0,8},{4,12},{8,0},{12,4},{1,9},{5,13},{9,1},{13,5},{2,10},{6,14},... | collective-permute-start | bytes 1769480 | tf_op jit(solution)/shard_map/ppermute | solution.py:114
  1534.8 143.3 %collective-permute-start.14 = (bf16[1,3,192,512]{3,2,0,1:T(8,128)(2,1)}, bf16[1,3,192,512]{3,2,0,1:T(8,128)(2,1)S(1)}, u32[]{:S(2)}, u32[]{:S(2)}) collective-permute-start(bf16[1,3,192,512]{3,2,0,1:T(8,128)(2,1)} %get-tuple-element.130), channel_id=1, source_target_pairs={{0,12},{4,8},{8,4},{12,0},{1,13},{5,9},{9,5},{13,1},{2,14},{6,10},... | collective-permute-start | bytes 1769480 | tf_op jit(solution)/shard_map/ppermute | solution.py:114
  1720.8 220.8 %all-gather.99.cloned.1.call-start = ((), (), s32[]{:S(2)}) async-start(), calls=%async_computation.77 | async-start | bytes 3538944 | tf_op jit(solution)/shard_map/all_gather | solution.py:141
  1725.3 216.3 %all-gather.97.cloned.1.call-start = ((), (), s32[]{:S(2)}) async-start(), calls=%async_computation.76 | async-start | bytes 3538944 | tf_op jit(solution)/shard_map/all_gather | solution.py:141
  (197 other events, 3933.8 us)
Sparse Core Ops, SparseCore 0:
  13.9 66.6 all-gather.40
  85.8 29.0 all-gather.42
  138.1 29.7 reduce-scatter.82
  170.8 66.3 all-gather.44
  240.5 53.2 all-gather.48
  295.4 10.9 all-gather.46
  309.0 45.1 all-gather.50
  356.1 43.9 all-gather.52
  418.1 30.3 reduce-scatter.42
  450.4 26.4 all-gather.54
  478.4 10.9 all-gather.84
  491.4 64.6 all-gather.56
  561.7 29.0 all-gather.58
  613.9 29.7 reduce-scatter.84
  646.9 65.5 all-gather.60
  714.7 29.4 all-gather.88
  746.6 43.0 all-gather.66
  791.3 10.9 all-gather.62
  804.9 45.1 all-gather.64
  851.7 10.9 all-gather.90
  864.5 45.1 all-gather.68
  935.3 30.3 reduce-scatter.52
  969.7 26.4 all-gather.72
  997.8 10.9 all-gather.92
  1024.4 30.3 reduce-scatter.54
  1074.0 11.0 reduce-scatter.46
  1088.0 29.7 reduce-scatter.86
  1119.9 29.1 reduce-scatter.48
  1151.9 29.1 all-gather.74
  1204.6 11.0 reduce-scatter.58
  1218.0 30.3 reduce-scatter.60
  1252.4 26.4 all-gather.78
  1280.3 10.9 all-gather.94
  1306.1 30.3 reduce-scatter.62
  1353.8 28.8 all-gather.70
  1385.6 43.9 reduce-scatter.78
  1433.1 43.9 reduce-scatter.76
  1479.9 43.9 reduce-scatter.80
  1526.7 43.9 reduce-scatter.70
  1573.5 43.9 reduce-scatter.72
  1620.3 43.9 reduce-scatter.74
  1667.1 28.5 reduce-scatter.88
  1697.5 27.7 all-gather.82
  1740.5 62.3 reduce-scatter.68
  1805.6 60.2 reduce-scatter.66
  1868.3 27.7 all-gather.80
  1897.7 10.9 all-gather.98
  1910.2 12.1 all-gather.96
  (8 shorter events, 75.6 us)

commit v3 on v2

--- a/solution.py
+++ b/solution.py
@@ -3,6 +3,8 @@
 import jax
 import jax.numpy as jnp
 from jax import lax
+from jax.experimental import pallas as pl
+from jax.experimental.pallas import tpu as pltpu
 from jax.sharding import PartitionSpec as P
 
 HD = 128
@@ -123,32 +125,352 @@
     return jnp.where(allowed[:, None], raw_scores, MASKED)
 
 
+MESH = pl.DeviceIdType.MESH
+CHUNK = 256
+
+
+def greet(axes):
+    barrier = pltpu.get_barrier_semaphore()
+    count = 0
+    for axis in axes:
+        size = lax.axis_size(axis)
+        me = lax.axis_index(axis)
+        for step in range(1, size):
+            pl.semaphore_signal(
+                barrier, inc=1, device_id={axis: lax.rem(me + step, size)}, device_id_type=MESH
+            )
+        count += size - 1
+    pl.semaphore_wait(barrier, count)
+
+
+def remote(src, dst, send_sem, recv_sem, device_id):
+    return pltpu.make_async_remote_copy(
+        src_ref=src, dst_ref=dst, send_sem=send_sem, recv_sem=recv_sem,
+        device_id=device_id, device_id_type=MESH,
+    )
+
+
+def kernel_call(kernel, out_shape, scratch, collective_id, cost_us, *args):
+    in_vmem = pl.BlockSpec(memory_space=pltpu.VMEM)
+    return pl.pallas_call(
+        kernel,
+        out_shape=out_shape,
+        in_specs=[in_vmem] * len(args),
+        out_specs=jax.tree.map(lambda _: in_vmem, out_shape),
+        scratch_shapes=scratch,
+        cost_estimate=pl.CostEstimate(flops=0, bytes_accessed=cost_us * 3_000_000, transcendentals=0),
+        compiler_params=pltpu.CompilerParams(
+            collective_id=collective_id, has_side_effects=True, vmem_limit_bytes=40 << 20
+        ),
+    )(*args)
+
+
+def hub(partial_sums, own_args, body, own_outs, scatter, gathers, collective_id, cost_us):
+    trees = 2
+    rows, depth = own_args[0].shape
+    half = depth // 2
+    scatter_size = lax.axis_size(scatter) if scatter else 1
+    sizes = [lax.axis_size(axis) for axis in gathers]
+    n_args = len(own_args) + (1 if scatter else 0)
+    n_outs = len(own_outs) + len(gathers)
+
+    def kernel(*refs):
+        args, outs, scratch = refs[:n_args], refs[n_args : n_args + n_outs], refs[n_args + n_outs :]
+        own_out_refs, gathered = outs[: len(own_outs)], outs[len(own_outs) :]
+        core = lax.axis_index("section")
+        sibling = 1 - core
+        axes = ["section"] + sorted(set(gathers) | ({scatter} if scatter else set()))
+
+        if scatter:
+            terms = args[0]
+            args = args[1:]
+            to_sib, from_sib, to_peer, from_peer, total_ref = scratch[:5]
+            sib_send, sib_recv, peer_send, peer_recv = scratch[5:9]
+            scratch = scratch[9:]
+            me = lax.axis_index(scatter)
+
+            def packed(tree, place, at):
+                low = rows * place // 16 * 16
+                high = -(-rows * (place + 1) // 16) * 16
+                skip = rows * place - low
+                parts = [
+                    terms[tree, low:high, pl.ds(side * half + at, CHUNK)].astype(F32)[
+                        skip : skip + rows
+                    ]
+                    for side in range(2)
+                ]
+                return jnp.concatenate(parts, axis=0)
+
+            def columns(step):
+                return pl.multiple_of(step * CHUNK, CHUNK)
+
+            for place in range(scatter_size):
+                @pl.loop(0, half // CHUNK)
+                def _(step):
+                    at = columns(step)
+                    to_sib[place, :, pl.ds(at, CHUNK)] = packed(sibling, place, at).astype(BF16)
+
+            greet(axes)
+            to_sibling = [
+                remote(
+                    to_sib.at[place], from_sib.at[place], sib_send.at[place], sib_recv.at[place],
+                    {"section": sibling},
+                )
+                for place in range(scatter_size)
+            ]
+            for copy in to_sibling:
+                copy.start()
+
+            def peer_copy(place, slot):
+                return remote(
+                    to_peer.at[place], from_peer.at[slot], peer_send.at[place],
+                    peer_recv.at[slot], {scatter: place},
+                )
+
+            for place in range(scatter_size):
+                to_sibling[place].wait_recv()
+
+                @pl.loop(0, half // CHUNK)
+                def _(step):
+                    at = columns(step)
+                    both = packed(core, place, at) + from_sib[place, :, pl.ds(at, CHUNK)].astype(F32)
+                    to_peer[place, :, pl.ds(at, CHUNK)] = both.astype(BF16)
+
+                    @pl.when(place == me)
+                    def _():
+                        total_ref[:, pl.ds(at, CHUNK)] = both
+
+                @pl.when(place != me)
+                def _():
+                    peer_copy(place, me).start()
+
+            for place in range(scatter_size):
+                @pl.when(place != me)
+                def _():
+                    peer_copy(place, place).wait_recv()
+                    total_ref[...] += from_peer[place].astype(F32)
+
+            total = total_ref[...]
+            total = jnp.concatenate([total[:rows], total[rows:]], axis=1)
+        else:
+            greet(axes)
+            total = None
+
+        result = body(total, args, own_out_refs)
+        piece = jnp.concatenate([result[:, :half], result[:, half:]], axis=0).astype(BF16)
+        gather_state = []
+        for index, axis in enumerate(gathers):
+            board, send, recv, relay_send, relay_recv = scratch[5 * index : 5 * index + 5]
+            me_there = lax.axis_index(axis)
+            board[core, me_there] = piece
+
+            def spread(place, slot, board=board, send=send, recv=recv, axis=axis):
+                return remote(
+                    board.at[core, slot], board.at[core, slot], send.at[place], recv.at[slot],
+                    {axis: place},
+                )
+
+            def relay(tree, slot, board=board, send=relay_send, recv=relay_recv):
+                return remote(
+                    board.at[tree, slot], board.at[tree, slot], send.at[slot], recv.at[slot],
+                    {"section": sibling},
+                )
+
+            for place in range(sizes[index]):
+                @pl.when(place != me_there)
+                def _():
+                    spread(place, me_there).start()
+
+            relay(core, me_there).start()
+            gather_state.append((board, me_there, spread, relay))
+
+        def unpack(out, board, tree, size):
+            @pl.loop(0, half // CHUNK)
+            def _(step):
+                at = pl.multiple_of(step * CHUNK, CHUNK)
+                blocks = [board[tree, place, :, pl.ds(at, CHUNK)].astype(F32) for place in range(size)]
+                for side in range(2):
+                    whole = jnp.concatenate(
+                        [block[side * rows : (side + 1) * rows] for block in blocks], axis=0
+                    )
+                    out[tree, :, pl.ds(side * half + at, CHUNK)] = whole.astype(BF16)
+
+        for (board, me_there, spread, relay), size in zip(gather_state, sizes):
+            for place in range(size):
+                @pl.when(place != me_there)
+                def _():
+                    spread(place, place).wait_recv()
+                    relay(core, place).start()
+
+        for (board, me_there, spread, relay), size, out in zip(gather_state, sizes, gathered):
+            unpack(out, board, core, size)
+
+        for (board, me_there, spread, relay), size, out in zip(gather_state, sizes, gathered):
+            for place in range(size):
+                relay(sibling, place).wait_recv()
+            unpack(out, board, sibling, size)
+
+        if scatter:
+            for place in range(scatter_size):
+                to_sibling[place].wait_send()
+
+                @pl.when(place != me)
+                def _():
+                    peer_copy(place, me).wait_send()
+
+        for (board, me_there, spread, relay), size in zip(gather_state, sizes):
+            for place in range(size):
+                relay(core, place).wait_send()
+
+                @pl.when(place != me_there)
+                def _():
+                    spread(place, me_there).wait_send()
+
+    sem = pltpu.SemaphoreType.DMA
+    scratch = []
+    if scatter:
+        boxes = pltpu.VMEM((scatter_size, 2 * rows, half), BF16)
+        scratch += [boxes] * 4 + [pltpu.VMEM((2 * rows, half), F32)] + [sem((scatter_size,))] * 4
+    for size in sizes:
+        scratch += [pltpu.VMEM((trees, size, 2 * rows, half), BF16)] + [sem((size,))] * 4
+    out_shape = [jax.ShapeDtypeStruct(shape, F32) for shape in own_outs] + [
+        jax.ShapeDtypeStruct((trees, size * rows, depth), BF16) for size in sizes
+    ]
+    ins = ([partial_sums] if scatter else []) + list(own_args)
+    return kernel_call(kernel, out_shape, scratch, collective_id, cost_us, *ins)
+
+
+def hub_plain(partial_sums, own_args, body, own_outs, scatter, gathers):
+    total = None
+    if scatter:
+        mine = lax.psum_scatter(partial_sums, "section", scatter_dimension=0, tiled=True)
+        mine = lax.psum_scatter(mine, scatter, scatter_dimension=1, tiled=True)[0]
+        total = mine.astype(F32)
+
+    class Cell:
+        def __setitem__(self, _, value):
+            self.value = value
+
+    cells = [Cell() for _ in own_outs]
+    result = body(total, own_args, cells).astype(BF16)
+    gathered = [
+        lax.all_gather(lax.all_gather(result, axis, axis=0, tiled=True), "section", axis=0)
+        for axis in gathers
+    ]
+    return [cell.value for cell in cells] + gathered
+
+
 def gather_kv(own):
-    return lax.all_gather(own, "dp", axis=1, tiled=True)
+    trees, rows, width = own.shape
+    if rows % 16:
+        return lax.all_gather(own, "dp", axis=1, tiled=True)
+    size = lax.axis_size("dp")
+
+    def kernel(own_ref, out_ref, send, recv):
+        me = lax.axis_index("dp")
+        greet(["dp"])
+
+        def spread(place, slot):
+            return remote(
+                own_ref, out_ref.at[:, slot], send.at[place], recv.at[slot], {"dp": place}
+            )
+
+        for place in range(size):
+            @pl.when(place != me)
+            def _():
+                spread(place, me).start()
+
+        out_ref[:, me] = own_ref[...]
+        for place in range(size):
+            @pl.when(place != me)
+            def _():
+                spread(place, place).wait_recv()
+                spread(place, me).wait_send()
+
+    shape = jax.ShapeDtypeStruct((trees, size, rows, width), BF16)
+    sem = pltpu.SemaphoreType.DMA
+    whole = kernel_call(kernel, shape, [sem((size,))] * 2, 1, 30, own)
+    return whole.reshape(trees, size * rows, width)
 
 
 def scatter_kv(whole):
-    return lax.psum_scatter(whole, "dp", scatter_dimension=1, tiled=True)
-
-
-def scatter_attn(whole):
-    mine = lax.psum_scatter(whole, "section", scatter_dimension=0, tiled=True)
-    return lax.psum_scatter(mine, "tensor", scatter_dimension=1, tiled=True)[0]
-
-
-def gather_rows(own):
-    mine = lax.all_gather(own, "tensor", axis=0, tiled=True)
-    return lax.all_gather(mine, "section", axis=0)
-
-
-def gather_mlp(own):
-    mine = lax.all_gather(own, "dp", axis=0, tiled=True)
-    return lax.all_gather(mine, "section", axis=0, tiled=True)
-
-
-def scatter_mlp(whole):
-    mine = lax.psum_scatter(whole, "section", scatter_dimension=0, tiled=True)
-    return lax.psum_scatter(mine, "dp", scatter_dimension=0, tiled=True)
+    trees, all_rows, width = whole.shape
+    size = lax.axis_size("dp")
+    rows = all_rows // size
+    if rows % 16:
+        return lax.psum_scatter(whole, "dp", scatter_dimension=1, tiled=True)
+
+    def kernel(in_ref, out_ref, boxes, send, recv):
+        me = lax.axis_index("dp")
+        greet(["dp"])
+
+        def spread(place, slot):
+            return remote(
+                in_ref.at[:, place], boxes.at[slot], send.at[place], recv.at[slot], {"dp": place}
+            )
+
+        for place in range(size):
+            @pl.when(place != me)
+            def _():
+                spread(place, me).start()
+
+        boxes[me] = in_ref[:, me]
+        for place in range(size):
+            @pl.when(place != me)
+            def _():
+                spread(place, place).wait_recv()
+
+        total = boxes[0].astype(F32)
+        for place in range(1, size):
+            total += boxes[place].astype(F32)
+        out_ref[...] = total.astype(BF16)
+        for place in range(size):
+            @pl.when(place != me)
+            def _():
+                spread(place, me).wait_send()
+
+    shape = jax.ShapeDtypeStruct((trees, rows, width), BF16)
+    sem = pltpu.SemaphoreType.DMA
+    scratch = [pltpu.VMEM((size, trees, rows, width), BF16), sem((size,)), sem((size,))]
+    return kernel_call(
+        kernel, shape, scratch, 2, 30, whole.reshape(trees, size, rows, width)
+    )
+
+
+def meet(partial_sums, own_args, body, own_outs, scatter, gathers, collective_id, cost_us):
+    rows, depth = own_args[0].shape
+    if rows % 8 or depth % (2 * CHUNK):
+        return hub_plain(partial_sums, own_args, body, own_outs, scatter, gathers)
+    return hub(partial_sums, own_args, body, own_outs, scatter, gathers, collective_id, cost_us)
+
+
+def norm_body(total, args, outs):
+    middle = args[0][...] + total
+    outs[0][...] = middle
+    mean_sq = jnp.mean(middle * middle, axis=1, keepdims=True)
+    return middle * lax.rsqrt(mean_sq + EPSILON) * args[1][...]
+
+
+def add_body(total, args, outs):
+    result = args[0][...] + total
+    outs[0][...] = result
+    return result
+
+
+def norm_back_body(total, args, outs):
+    values, gain = args[0][...], args[1][...]
+    scale = lax.rsqrt(jnp.mean(values * values, axis=1, keepdims=True) + EPSILON)
+    unit = values * scale
+    outs[1][...] = jnp.sum(total * unit, axis=0, keepdims=True)
+    scaled = total * gain
+    along = jnp.mean(scaled * unit, axis=1, keepdims=True)
+    result = (scaled - unit * along) * scale + args[2][...]
+    outs[0][...] = result
+    return result
+
+
+def pass_body(total, args, outs):
+    return args[0][...]
 
 
 def embed(q_pre, k_pre, q_scale, k_scale, cos_table, sine_table):
@@ -185,22 +507,26 @@
     attended = jnp.einsum("bgrt,btd->brgd", prob_bf, value_all, preferred_element_type=F32)
     attended_bf = attended.reshape(trees * row_count, -1).astype(BF16)
     attn_partial = dot_inner(attended_bf, w_outt).astype(BF16).reshape(trees, row_count, depth)
-    middle = own_in + scatter_attn(attn_partial).astype(F32)
-    mlp_in = gather_mlp(rms_scale(middle, mlp_scale).astype(BF16))
+    own_shape = own_in.shape
+    middle, mlp_in = meet(
+        attn_partial, [own_in, mlp_scale[None]], norm_body, [own_shape], "tensor", ["dp"], 3, 50
+    )
+    mlp_in = mlp_in.reshape(-1, depth)
     gate_pre = dot_inner(mlp_in, w_gate)
     upward = dot_inner(mlp_in, w_up)
     hidden_bf = swiglu(gate_pre, upward).astype(BF16)
-    mlp_rows = scatter_mlp(dot(hidden_bf, w_down).astype(BF16))
-    output_own = (middle + mlp_rows.astype(F32)).astype(BF16)
-    output_bf = gather_rows(output_own)
+    mlp_partial = dot(hidden_bf, w_down).astype(BF16).reshape(trees, -1, depth)
+    output_own, output_bf = meet(
+        mlp_partial, [middle], add_body, [own_shape], "dp", ["tensor"], 4, 50
+    )
     stored = (
         own_in, normed, q_pre, k_pre, query_bf, key_all, value_all, log_total, attended_bf,
         middle, mlp_in, gate_pre, upward, hidden_bf,
     )
-    return (output_bf, output_own.astype(F32), stored)
-
-
-def layer_backward(grad_own, stored, weights, gains, slot, shared_kv):
+    return (output_bf, output_own.astype(BF16).astype(F32), stored)
+
+
+def layer_backward(grad_own, grad_mlp, stored, weights, gains, slot, shared_kv, is_first):
     attn_scale, mlp_scale, q_scale, k_scale = gains
     w_qkv, w_outt, w_gate, w_up, w_down = weights
     allowed, cos_table, sine_table = slot
@@ -210,17 +536,19 @@
     ) = stored
     trees, row_count = query_bf.shape[:2]
     depth = normed.shape[1]
-    grad_mlp = gather_mlp(grad_own)
     grad_hidden = dot_inner(grad_mlp, w_down)
     _, swiglu_pull = jax.vjp(swiglu, gate_pre, upward)
     grad_gate, grad_upward = swiglu_pull(grad_hidden)
     gate_bf = grad_gate.astype(BF16)
     up_bf = grad_upward.astype(BF16)
-    mlp_rows = scatter_mlp((dot(gate_bf, w_gate) + dot(up_bf, w_up)).astype(BF16))
-    _, mlp_norm_pull = jax.vjp(rms_scale, middle, mlp_scale)
-    grad_middle, grad_mlp_scale = mlp_norm_pull(mlp_rows.astype(F32))
-    grad_middle = grad_middle + grad_own.astype(F32)
-    grad_attn = gather_rows(grad_middle.astype(BF16)).reshape(-1, depth)
+    mlp_partial = (dot(gate_bf, w_gate) + dot(up_bf, w_up)).astype(BF16)
+    own_outs = [own_in.shape, (1, depth)]
+    grad_middle, grad_mlp_scale, grad_attn = meet(
+        mlp_partial.reshape(trees, -1, depth),
+        [middle, mlp_scale[None], grad_own],
+        norm_back_body, own_outs, "dp", ["tensor"], 5, 50,
+    )
+    grad_attn = grad_attn.reshape(-1, depth)
     grad_heads = dot(grad_attn, w_outt).astype(BF16).reshape(query_bf.shape)
     scores = masked_scores(query_bf, key_all, allowed)
     prob_full = jnp.exp(scores - log_total)
@@ -258,11 +586,11 @@
         axis=2,
     ).reshape(trees * row_count, -1)
     attn_partial = dot_inner(qkv_grad, w_qkv).astype(BF16).reshape(trees, row_count, depth)
-    attn_rows = scatter_attn(attn_partial)
-    _, attn_norm_pull = jax.vjp(rms_scale, own_in, attn_scale)
-    grad_residual, grad_attn_scale = attn_norm_pull(attn_rows.astype(F32))
-    incoming_own = (grad_residual + grad_middle).astype(BF16)
-    incoming = gather_rows(incoming_own)
+    gathers = ["tensor"] if is_first else ["tensor", "dp"]
+    incoming_own, grad_attn_scale, *gathered = meet(
+        attn_partial, [own_in, attn_scale[None], grad_middle],
+        norm_back_body, own_outs, "tensor", gathers, 6 if is_first else 7, 40,
+    )
     products = (
         (normed, qkv_grad),
         (grad_attn, attended_bf),
@@ -270,8 +598,10 @@
         (up_bf, mlp_in),
         (hidden_bf, grad_mlp),
     )
-    gain_grads = jnp.concatenate([grad_attn_scale, grad_mlp_scale, grad_q_scale, grad_k_scale])
-    return (incoming, incoming_own, products, gain_grads)
+    gain_grads = jnp.concatenate(
+        [grad_attn_scale[0], grad_mlp_scale[0], grad_q_scale, grad_k_scale]
+    )
+    return (gathered, incoming_own.astype(BF16).astype(F32), products, gain_grads)
 
 
 def swap_cores(mine, other):
@@ -368,12 +698,15 @@
         outputs.append(hidden)
         kept.append(stored)
 
-    grad_own = own_part(cotangent)
+    grad_own = own_part(cotangent).astype(F32)
+    (grad_mlp,) = meet(None, [grad_own], pass_body, [], None, ["dp"], 8, 30)
     grads, weight_grads, gain_grads = [None, None], [None, None], [None, None]
     for layer in (1, 0):
-        grads[layer], grad_own, products, gain_grads[layer] = layer_backward(
-            grad_own, kept[layer], weights[layer], gains[layer], slot, shared_kv
+        gathered, grad_own, products, gain_grads[layer] = layer_backward(
+            grad_own, grad_mlp.reshape(-1, depth), kept[layer], weights[layer], gains[layer], slot,
+            shared_kv, layer == 0,
         )
+        grads[layer], grad_mlp = gathered[0], gathered[-1]
         whole = [dot_outer(left, right).astype(BF16) for left, right in products]
         attn_grad = lax.psum_scatter(
             jnp.concatenate(whole[:2], axis=1), "dp", scatter_dimension=0, tiled=True

time: 1960 us -> 1270 us (0.65)
  waiting for transfers between devices: 1480 us -> 190 us
  Pallas kernels: 0 us -> 586 us
  blocking collectives: 65.2 us -> 101 us
  other arithmetic: 97.8 us -> 65.1 us
  matrix products: 161 us -> 137 us
    pallas_call x0 -> x13, Pallas kernels: none -> 586 us  [kernel_call(): pl.pallas_call(kernel, out_shape=out_shape, in_specs=[in_vmem] * len(args...]
    all_gather x22 -> x0, waiting for transfers between devices: 283 us -> none  [the longest x6 96.6 us: gather_rows(): mine = lax.all_gather(own, 'tensor', axis=0, tiled=True)]
    all_gather x6, waiting for transfers between devices: 263 us -> 0.01 us  [on_device(): lax.all_gather(pieces[i], 'tensor', axis=0, tiled=True)]
    reduce_scatter x14 -> x0, waiting for transfers between devices: 243 us -> none  [the longest x4 127 us: scatter_mlp(): return lax.psum_scatter(mine, 'dp', scatter_dimension=0, tiled=True)]
    reduce_scatter x6, waiting for transfers between devices: 235 us -> 0.05 us  [on_device(): lax.psum_scatter(item, 'tensor', scatter_dimension=0, tiled=True)]
    reduce_scatter x2, waiting for transfers between devices: 120 us -> 0.01 us  [on_device(): lax.psum_scatter(jnp.concatenate(whole[:2], axis=1), 'dp', scatter_dimens...]
    all_gather x2, waiting for transfers between devices: 93.2 us -> 0.04 us  [on_device(): attn_all = lax.all_gather(attn_shards[layer], 'dp', axis=0, tiled=True)]
    unnamed x60 -> x16, waiting for transfers between devices: 91.9 us -> 0.78 us
  transfers between devices with their start and end apart: 72 -> 32, of which waited for: 56 -> 11; matrix products, arithmetic and copies ran while one was open for 11% -> 20% of each run, Pallas kernels for 0% -> 47%
where the time goes in v3:
time: 1270 us; the launch traced here: 1250 us
  Pallas kernels  586 us (46%)
  waiting for transfers between devices  190 us (15%)
  matrix products  137 us (11%)
  local copies, waits for them, and re-layouts  110 us (9%)
  blocking collectives  101 us (8%)
  other arithmetic  65.1 us (5%)
  starting transfers between devices  38.8 us (3%)
  between operations  21.4 us (2%)
    pallas_call x13, Pallas kernels, kernel_call(): pl.pallas_call(kernel, out_shape=out_shape, in_specs=[in_vmem] * len(args...  586 us
    ppermute x12, waiting for transfers between devices, exchange(): arrived = lax.ppermute(piece, axis, [(i, i ^ step) for i in range(size)])  183 us
    psum x1, blocking collectives, on_device(): gain_total = lax.psum(jnp.stack(gain_grads), ('section', 'dp', 'tensor'))  68.1 us
    unnamed x384, local copies, waits for them, and re-layouts  54.2 us
    dot_general x10, matrix products, dot_inner(): return lax.dot_general(left, right, INNER, preferred_element_type=F32)  42.1 us
    dot_general x10, matrix products, dot_outer(): return lax.dot_general(left, right, OUTER, preferred_element_type=F32)  38.2 us
    ppermute x12, starting transfers between devices, exchange(): arrived = lax.ppermute(piece, axis, [(i, i ^ step) for i in range(size)])  36.7 us
    dot_general x10, matrix products, dot(): return jnp.dot(left, right, preferred_element_type=F32)  33 us
  transfers between devices with their start and end apart: 32, of which 11 were waited for; matrix products, arithmetic and copies ran while one was open for 20% of the time, Pallas kernels for 47%

profile of v3, /device:TPU:0, one launch (start us, length us, event | category | flops | bytes accessed | tf_op | source)
XLA Modules:
  0.0 1249.3 jit_solution(17766343727762167326)
XLA Ops:
  24.6 4.3 collective-permute-done.1
  37.6 50.4 %collective-permute-done.2 = bf16[1,3,192,512]{3,2,0,1:T(8,128)(2,1)S(1)} collective-permute-done((bf16[1,3,192,512]{3,2,0,1:T(8,128)(2,1)S(1)}, bf16[1,3,192,512]{3,2,0,1:T(8,128)(2,1)S(1)}, u32[]{:S(2)}, u32[]{:S(2)}) %collective-permute-start.2) | collective-permute-done | bytes 589856 | tf_op jit(solution)/shard_map/ppermute | solution.py:116
  88.0 4.1 collective-permute-done.3
  92.2 22.4 %collective-permute-done.4 = bf16[1,3,192,512]{3,2,0,1:T(8,128)(2,1)S(1)} collective-permute-done((bf16[1,3,192,512]{3,2,0,1:T(8,128)(2,1)S(1)}, bf16[1,3,192,512]{3,2,0,1:T(8,128)(2,1)S(1)}, u32[]{:S(2)}, u32[]{:S(2)}) %collective-permute-start.4) | collective-permute-done | bytes 589856 | tf_op jit(solution)/shard_map/ppermute | solution.py:116
  123.2 19.9 %collective-permute-start.5 = (bf16[1,3,192,512]{3,2,0,1:T(8,128)(2,1)S(1)}, bf16[1,3,192,512]{3,2,0,1:T(8,128)(2,1)S(1)}, u32[]{:S(2)}, u32[]{:S(2)}) collective-permute-start(bf16[1,3,192,512]{3,2,0,1:T(8,128)(2,1)S(1)} %get-tuple-element.166), channel_id=1, source_target_pairs={{0,4},{4,0},{8,12},{12,8},{1,5},{5,1},{9,13},{13,9},{2,6},{6,2},{1... | collective-permute-start | bytes 1769480 | tf_op jit(solution)/shard_map/ppermute | solution.py:116
  145.6 21.6 %collective-permute-done.5 = bf16[1,3,192,512]{3,2,0,1:T(8,128)(2,1)S(1)} collective-permute-done((bf16[1,3,192,512]{3,2,0,1:T(8,128)(2,1)S(1)}, bf16[1,3,192,512]{3,2,0,1:T(8,128)(2,1)S(1)}, u32[]{:S(2)}, u32[]{:S(2)}) %collective-permute-start.5) | collective-permute-done | bytes 589856 | tf_op jit(solution)/shard_map/ppermute | solution.py:116
  167.2 18.4 %collective-permute-done.6 = bf16[1,3,192,512]{3,2,0,1:T(8,128)(2,1)S(1)} collective-permute-done((bf16[1,3,192,512]{3,2,0,1:T(8,128)(2,1)S(1)}, bf16[1,3,192,512]{3,2,0,1:T(8,128)(2,1)S(1)}, u32[]{:S(2)}, u32[]{:S(2)}) %collective-permute-start.6) | collective-permute-done | bytes 589856 | tf_op jit(solution)/shard_map/ppermute | solution.py:116
  193.6 32.8 %all-gather.1 = bf16[8,1,1280]{2,1,0:T(2,128)(2,1)S(1)} all-gather(bf16[1,1,1280]{2,1,0:T(2,128)(2,1)S(1)} %reshape.676), channel_id=2, replica_groups=mesh['section'=2,'dp'=4,'tensor'=4] {'section','dp'}, dimensions={0}, use_global_device_ids=true | all-gather | bytes 23040 | tf_op jit(solution)/shard_map/all_gather | solution.py:636
  230.1 25.6 %shard_map.261 = bf16[2,288,2048]{2,1,0:T(8,128)(2,1)S(1)} custom-call(f32[72,2048]{1,0:T(8,128)S(1)} %bitcast_convert_fusion.2.refs_0_.refs_3_), custom_call_target="tpu_custom_call" | custom-call | bytes 90000000 | tf_op jit(solution)/shard_map/pallas_call | solution.py:155
  269.3 3.4 fusion.38
  278.4 47.6 %shard_map.255 = bf16[2,4,288,256]{3,2,1,0:T(8,128)(2,1)S(1)} custom-call(bf16[2,288,256]{2,1,0:T(8,128)(2,1)S(1)} %pad_maximum_fusion.10.own_ref), custom_call_target="tpu_custom_call" | custom-call | bytes 90000000 | tf_op jit(solution)/shard_map/pallas_call | solution.py:155
  334.2 62.1 %shard_map.256 = (f32[72,2048]{1,0:T(8,128)S(1)}, bf16[2,288,2048]{2,1,0:T(8,128)(2,1)S(1)}) custom-call(bf16[2,288,2048]{2,1,0:T(8,128)(2,1)S(1)} %bitcast.405, f32[72,2048]{1,0:T(8,128)S(1)} %bitcast_convert_fusion.3.refs_1_, f32[1,2048]{1,0:T(1,128)S(1)} %bitcast.422), custom_call_target="tpu_custom_call" | custom-call | bytes 150000000 | tf_op jit(solution)/shard_map/pallas_call | solution.py:155
  397.7 6.1 fusion.180
  403.8 6.0 multiply_convert_fusion.3
  409.8 4.2 convolution_convert_fusion.10
  414.0 51.8 %shard_map.257 = (f32[72,2048]{1,0:T(8,128)S(1)}, bf16[2,288,2048]{2,1,0:T(8,128)(2,1)S(1)}) custom-call(bf16[2,288,2048]{2,1,0:T(8,128)(2,1)S(1)} %bitcast.421, f32[72,2048]{1,0:T(8,128)S(1)} %get-tuple-element.33.refs_1_), custom_call_target="tpu_custom_call" | custom-call | bytes 150000000 | tf_op jit(solution)/shard_map/pallas_call | solution.py:155
  485.4 27.7 %shard_map.258 = bf16[2,4,288,256]{3,2,1,0:T(8,128)(2,1)S(1)} custom-call(bf16[2,288,256]{2,1,0:T(8,128)(2,1)S(1)} %pad_maximum_fusion.12.own_ref), custom_call_target="tpu_custom_call" | custom-call | bytes 90000000 | tf_op jit(solution)/shard_map/pallas_call | solution.py:155
  522.1 47.9 %shard_map.259 = (f32[72,2048]{1,0:T(8,128)S(1)}, bf16[2,288,2048]{2,1,0:T(8,128)(2,1)S(1)}) custom-call(bf16[2,288,2048]{2,1,0:T(8,128)(2,1)S(1)} %bitcast.404, f32[72,2048]{1,0:T(8,128)S(1)} %convert_convert_fusion.1.refs_1_, f32[1,2048]{1,0:T(1,128)S(1)} %bitcast.424), custom_call_target="tpu_custom_call" | custom-call | bytes 150000000 | tf_op jit(solution)/shard_map/pallas_call | solution.py:155
  572.2 5.8 fusion.181
  578.1 5.9 fusion.182
  583.9 7.6 multiply_convert_fusion.1
  592.5 4.0 convolution_convert_fusion.2
  596.6 6.3 convolution_convert_fusion.1
  604.6 4.3 fusion.183
  611.0 49.1 %shard_map.262 = (f32[72,2048]{1,0:T(8,128)S(1)}, f32[1,2048]{1,0:T(1,128)S(1)}, bf16[2,288,2048]{2,1,0:T(8,128)(2,1)S(1)}) custom-call(bf16[2,288,2048]{2,1,0:T(8,128)(2,1)S(1)} %bitcast.417, f32[72,2048]{1,0:T(8,128)S(1)} %copy-done.13, f32[1,2048]{1,0:T(1,128)S(1)} %bitcast.425, f32[72,2048]{1,0:T(8,128)S(1)} %bitcast_convert_fusion.2.refs_0_.refs_3_), custom_call_target="tpu_custom_call" | custom-call | bytes 150000000 | tf_op jit(solution)/shard_map/pallas_call | solution.py:155
  665.8 6.3 convolution_convert_fusion
  672.3 4.3 fusion.3
  683.2 29.4 %shard_map.263 = bf16[2,288,256]{2,1,0:T(8,128)(2,1)S(1)} custom-call(bf16[2,4,288,256]{3,2,1,0:T(8,128)(2,1)S(1)} %pad_maximum_fusion.4.in_ref), custom_call_target="tpu_custom_call" | custom-call | bytes 90000000 | tf_op jit(solution)/shard_map/pallas_call | solution.py:155
  720.3 53.1 %shard_map.264 = (f32[72,2048]{1,0:T(8,128)S(1)}, f32[1,2048]{1,0:T(1,128)S(1)}, bf16[2,288,2048]{2,1,0:T(8,128)(2,1)S(1)}, bf16[2,288,2048]{2,1,0:T(8,128)(2,1)S(1)}) custom-call(bf16[2,288,2048]{2,1,0:T(8,128)(2,1)S(1)} %bitcast.418, f32[72,2048]{1,0:T(8,128)S(1)} %convert_convert_fusion.1.refs_1_, f32[1,2048]{1,0:T(1,128)S(1)} %bitcast.426, ...), custom_call_target="tpu_custom_call" | custom-call | bytes 120000000 | tf_op jit(solution)/shard_map/pallas_call | solution.py:155
  773.5 3.5 multiply_convert_fusion
  777.9 4.1 convolution_convert_fusion.5
  783.2 5.7 convolution_convert_fusion.4
  790.0 5.7 convolution_convert_fusion.3
  797.1 4.3 fusion.184
  803.5 52.3 %shard_map.265 = (f32[72,2048]{1,0:T(8,128)S(1)}, f32[1,2048]{1,0:T(1,128)S(1)}, bf16[2,288,2048]{2,1,0:T(8,128)(2,1)S(1)}) custom-call(bf16[2,288,2048]{2,1,0:T(8,128)(2,1)S(1)} %bitcast.419, f32[72,2048]{1,0:T(8,128)S(1)} %copy-done.16, f32[1,2048]{1,0:T(1,128)S(1)} %bitcast.423, f32[72,2048]{1,0:T(8,128)S(1)} %convert_convert_fusion.refs_3_), custom_call_target="tpu_custom_call" | custom-call | bytes 150000000 | tf_op jit(solution)/shard_map/pallas_call | solution.py:155
  861.4 3.5 convolution_convert_fusion.14
  866.7 4.0 fusion
  870.7 3.4 fusion.2
  877.4 34.4 %shard_map.266 = bf16[2,288,256]{2,1,0:T(8,128)(2,1)S(1)} custom-call(bf16[2,4,288,256]{3,2,1,0:T(8,128)(2,1)S(1)} %pad_maximum_fusion.5.in_ref), custom_call_target="tpu_custom_call" | custom-call | bytes 90000000 | tf_op jit(solution)/shard_map/pallas_call | solution.py:155
  923.1 4.2 convolution_convert_fusion.8
  927.3 68.9 %shard_map.260 = (f32[72,2048]{1,0:T(8,128)}, bf16[2,288,2048]{2,1,0:T(8,128)(2,1)S(1)}) custom-call(bf16[2,288,2048]{2,1,0:T(8,128)(2,1)S(1)} %bitcast.420, f32[72,2048]{1,0:T(8,128)S(1)} %copy-done.14), custom_call_target="tpu_custom_call" | custom-call | bytes 150000000 | tf_op jit(solution)/shard_map/pallas_call | solution.py:155
  998.3 36.3 %shard_map.267 = (f32[72,2048]{1,0:T(8,128)}, f32[1,2048]{1,0:T(1,128)S(1)}, bf16[2,288,2048]{2,1,0:T(8,128)(2,1)S(1)}) custom-call(bf16[2,288,2048]{2,1,0:T(8,128)(2,1)S(1)} %bitcast.416, f32[72,2048]{1,0:T(8,128)S(1)} %copy-done.1, f32[1,2048]{1,0:T(1,128)S(1)} %bitcast.427, f32[72,2048]{1,0:T(8,128)S(1)} %copy-done.18), custom_call_target="tpu_custom_call" | custom-call | bytes 120000000 | tf_op jit(solution)/shard_map/pallas_call | solution.py:155
  1036.1 68.1 %psum.7 = f32[2,4352]{1,0:T(2,128)S(1)} all-reduce(f32[2,4352]{1,0:T(2,128)S(1)} %pad_maximum_fusion.18), channel_id=1, replica_groups=mesh['section'=2,'dp'=4,'tensor'=4] {'section','dp','tensor'}, use_global_device_ids=true, to_apply=%region_26.27 | all-reduce | flops 8704 | bytes 69632 | tf_op jit(solution)/shard_map/psum | solution.py:735
  1141.4 5.8 collective-permute-done.12
  1150.0 12.3 collective-permute-done.13
  1164.6 7.9 collective-permute-done.9
  1172.6 40.2 %collective-permute-done.10 = bf16[1,3,192,512]{3,2,0,1:T(8,128)(2,1)S(1)} collective-permute-done((bf16[1,3,192,512]{3,2,0,1:T(8,128)(2,1)}, bf16[1,3,192,512]{3,2,0,1:T(8,128)(2,1)S(1)}, u32[]{:S(2)}, u32[]{:S(2)}) %collective-permute-start.10) | collective-permute-done | bytes 589856 | tf_op jit(solution)/shard_map/ppermute | solution.py:116
  1238.8 3.5 convert.76
  (647 shorter events, 227.5 us)
Async XLA Ops:
  7.2 262.1 %all-gather.11.cloned.1.call-start = ((), (), s32[]{:S(2)}) async-start(), calls=%async_computation.8 | async-start | bytes 3932160 | tf_op jit(solution)/shard_map/all_gather | solution.py:672
  12.7 2.7 collective-permute-start
  17.8 379.9 %all-gather.13.cloned.1.call-start = ((), (), s32[]{:S(2)}) async-start(), calls=%async_computation.9 | async-start | bytes 3932160 | tf_op jit(solution)/shard_map/all_gather | solution.py:675
  24.2 4.7 collective-permute-start.1
  32.3 55.7 %collective-permute-start.2 = (bf16[1,3,192,512]{3,2,0,1:T(8,128)(2,1)S(1)}, bf16[1,3,192,512]{3,2,0,1:T(8,128)(2,1)S(1)}, u32[]{:S(2)}, u32[]{:S(2)}) collective-permute-start(bf16[1,3,192,512]{3,2,0,1:T(8,128)(2,1)S(1)} %get-tuple-element.173), channel_id=1, source_target_pairs={{0,4},{4,0},{8,12},{12,8},{1,5},{5,1},{9,13},{13,9},{2,6},{6,2},{1... | collective-permute-start | bytes 1769480 | tf_op jit(solution)/shard_map/ppermute | solution.py:116
  35.0 57.1 %collective-permute-start.3 = (bf16[1,3,192,512]{3,2,0,1:T(8,128)(2,1)S(1)}, bf16[1,3,192,512]{3,2,0,1:T(8,128)(2,1)S(1)}, u32[]{:S(2)}, u32[]{:S(2)}) collective-permute-start(bf16[1,3,192,512]{3,2,0,1:T(8,128)(2,1)S(1)} %get-tuple-element.172), channel_id=1, source_target_pairs={{0,8},{4,12},{8,0},{12,4},{1,9},{5,13},{9,1},{13,5},{2,10},{6,14},... | collective-permute-start | bytes 1769480 | tf_op jit(solution)/shard_map/ppermute | solution.py:116
  37.6 76.9 %collective-permute-start.4 = (bf16[1,3,192,512]{3,2,0,1:T(8,128)(2,1)S(1)}, bf16[1,3,192,512]{3,2,0,1:T(8,128)(2,1)S(1)}, u32[]{:S(2)}, u32[]{:S(2)}) collective-permute-start(bf16[1,3,192,512]{3,2,0,1:T(8,128)(2,1)S(1)} %get-tuple-element.171), channel_id=1, source_target_pairs={{0,12},{4,8},{8,4},{12,0},{1,13},{5,9},{9,5},{13,1},{2,14},{6,10},... | collective-permute-start | bytes 1769480 | tf_op jit(solution)/shard_map/ppermute | solution.py:116
  117.4 286.4 %all-gather.15.cloned.1.call-start = ((), (), s32[]{:S(2)}) async-start(), calls=%async_computation.10 | async-start | bytes 3932160 | tf_op jit(solution)/shard_map/all_gather | solution.py:675
  120.3 289.5 %all-gather.17.cloned.1.call-start = ((), (), s32[]{:S(2)}) async-start(), calls=%async_computation.11 | async-start | bytes 3932160 | tf_op jit(solution)/shard_map/all_gather | solution.py:675
  122.1 345.1 %all-gather.19.cloned.1.call-start = ((), (), s32[]{:S(2)}) async-start(), calls=%async_computation.12 | async-start | bytes 3932160 | tf_op jit(solution)/shard_map/all_gather | solution.py:672
  122.7 449.5 %all-gather.21.cloned.1.call-start = ((), (), s32[]{:S(2)}) async-start(), calls=%async_computation.13 | async-start | bytes 3932160 | tf_op jit(solution)/shard_map/all_gather | solution.py:675
  123.2 43.9 %collective-permute-start.5 = (bf16[1,3,192,512]{3,2,0,1:T(8,128)(2,1)S(1)}, bf16[1,3,192,512]{3,2,0,1:T(8,128)(2,1)S(1)}, u32[]{:S(2)}, u32[]{:S(2)}) collective-permute-start(bf16[1,3,192,512]{3,2,0,1:T(8,128)(2,1)S(1)} %get-tuple-element.166), channel_id=1, source_target_pairs={{0,4},{4,0},{8,12},{12,8},{1,5},{5,1},{9,13},{13,9},{2,6},{6,2},{1... | collective-permute-start | bytes 1769480 | tf_op jit(solution)/shard_map/ppermute | solution.py:116
  143.1 42.4 %collective-permute-start.6 = (bf16[1,3,192,512]{3,2,0,1:T(8,128)(2,1)S(1)}, bf16[1,3,192,512]{3,2,0,1:T(8,128)(2,1)S(1)}, u32[]{:S(2)}, u32[]{:S(2)}) collective-permute-start(bf16[1,3,192,512]{3,2,0,1:T(8,128)(2,1)S(1)} %get-tuple-element.165), channel_id=1, source_target_pairs={{0,8},{4,12},{8,0},{12,4},{1,9},{5,13},{9,1},{13,5},{2,10},{6,14},... | collective-permute-start | bytes 1769480 | tf_op jit(solution)/shard_map/ppermute | solution.py:116
  143.1 42.5 %collective-permute-start.7 = (bf16[1,3,192,512]{3,2,0,1:T(8,128)(2,1)S(1)}, bf16[1,3,192,512]{3,2,0,1:T(8,128)(2,1)S(1)}, u32[]{:S(2)}, u32[]{:S(2)}) collective-permute-start(bf16[1,3,192,512]{3,2,0,1:T(8,128)(2,1)S(1)} %get-tuple-element.164), channel_id=1, source_target_pairs={{0,12},{4,8},{8,4},{12,0},{1,13},{5,9},{9,5},{13,1},{2,14},{6,10},... | collective-permute-start | bytes 1769480 | tf_op jit(solution)/shard_map/ppermute | solution.py:116
  188.5 389.5 %all-gather.23.cloned.1.call-start = ((), (), s32[]{:S(2)}) async-start(), calls=%async_computation.14 | async-start | bytes 3932160 | tf_op jit(solution)/shard_map/all_gather | solution.py:675
  190.2 66.9 %copy-start.138 = (s32[2,1152]{1,0:T(2,128)S(1)}, s32[2,1152]{1,0:T(2,128)}, u32[]{:S(2)}) copy-start(s32[2,1152]{1,0:T(2,128)} %param.18) | copy-start | bytes 27652
  190.2 67.1 %copy-start.160 = (s32[2,9]{1,0:T(2,128)S(1)}, s32[2,9]{1,0:T(2,128)}, u32[]{:S(2)}) copy-start(s32[2,9]{1,0:T(2,128)} %param.19) | copy-start | bytes 220
  190.3 393.7 %all-gather.25.cloned.1.call-start = ((), (), s32[]{:S(2)}) async-start(), calls=%async_computation.15 | async-start | bytes 3932160 | tf_op jit(solution)/shard_map/all_gather | solution.py:675
  264.8 69.3 %copy-start = (f32[72,2048]{1,0:T(8,128)}, f32[72,2048]{1,0:T(8,128)S(1)}, u32[]{:S(2)}) copy-start(f32[72,2048]{1,0:T(8,128)S(1)} %bitcast_convert_fusion.3.refs_1_) | copy-start | bytes 1769476
  269.2 838.0 %reduce-scatter.19.cloned.1.call-start = ((), (), s32[]{:S(2)}) async-start(), calls=%async_computation.21 | async-start | bytes 3932160 | tf_op jit(solution)/shard_map/reduce_scatter | solution.py:715
  272.8 53.2 %copy-start.49 = (f32[2,36,2,8,128]{4,3,2,1,0:T(8,128)}, f32[2,36,2,8,128]{4,3,2,1,0:T(8,128)S(1)}, u32[]{:S(2)}) copy-start(f32[2,36,2,8,128]{4,3,2,1,0:T(8,128)S(1)} %get-tuple-element.192) | copy-start | bytes 1769476
  332.0 64.3 %copy-start.89 = (bf16[2,288,2,128]{3,2,1,0:T(2,128)(2,1)}, bf16[2,288,2,128]{3,2,1,0:T(2,128)(2,1)S(1)}, u32[]{:S(2)}) copy-start(bf16[2,288,2,128]{3,2,1,0:T(2,128)(2,1)S(1)} %copy.279) | copy-start | bytes 884740
  596.5 513.0 %reduce-scatter.21.cloned.1.call-start = ((), (), s32[]{:S(2)}) async-start(), calls=%async_computation.22 | async-start | bytes 3932160 | tf_op jit(solution)/shard_map/reduce_scatter | solution.py:715
  602.9 509.6 %reduce-scatter.23.cloned.1.call-start = ((), (), s32[]{:S(2)}) async-start(), calls=%async_computation.23 | async-start | bytes 3932160 | tf_op jit(solution)/shard_map/reduce_scatter | solution.py:715
  672.1 450.7 %reduce-scatter.13.cloned.1.call-start = ((), (), s32[]{:S(2)}) async-start(), calls=%async_computation.18 | async-start | bytes 3932160 | tf_op jit(solution)/shard_map/reduce_scatter | solution.py:715
  718.8 54.7 %copy-start.172 = (f32[576,768]{1,0:T(8,128)S(1)}, f32[576,768]{1,0:T(8,128)}, u32[]{:S(2)}) copy-start(f32[576,768]{1,0:T(8,128)} %fusion.180) | copy-start | bytes 5308420
  718.8 54.7 %copy-start.173 = (f32[576,768]{1,0:T(8,128)S(1)}, f32[576,768]{1,0:T(8,128)}, u32[]{:S(2)}) copy-start(f32[576,768]{1,0:T(8,128)} %get-tuple-element.250) | copy-start | bytes 5308420
  720.3 53.2 %copy-start.164 = (bf16[768,2048]{1,0:T(8,128)(2,1)S(1)}, bf16[768,2048]{1,0:T(8,128)(2,1)}, u32[]{:S(2)}) copy-start(bf16[768,2048]{1,0:T(8,128)(2,1)} %all-gather.17.cloned.1.call-done) | copy-start | bytes 9437188
  782.0 343.1 %reduce-scatter.15.cloned.1.call-start = ((), (), s32[]{:S(2)}) async-start(), calls=%async_computation.19 | async-start | bytes 3932160 | tf_op jit(solution)/shard_map/reduce_scatter | solution.py:715
  788.9 339.3 %reduce-scatter.17.cloned.1.call-start = ((), (), s32[]{:S(2)}) async-start(), calls=%async_computation.20 | async-start | bytes 3932160 | tf_op jit(solution)/shard_map/reduce_scatter | solution.py:715
  795.7 342.9 %reduce-scatter.11.cloned.1.call-start = ((), (), s32[]{:S(2)}) async-start(), calls=%async_computation.17 | async-start | bytes 3932160 | tf_op jit(solution)/shard_map/reduce_scatter | solution.py:711
  803.4 52.3 %copy-start.87 = (bf16[2,288,2,128]{3,1,2,0:T(8,128)(2,1)S(1)}, bf16[2,288,2,128]{3,1,2,0:T(8,128)(2,1)}, u32[]{:S(2)}) copy-start(bf16[2,288,2,128]{3,1,2,0:T(8,128)(2,1)} %copy-done.86) | copy-start | bytes 884740
  803.4 52.4 %copy-start.34 = (bf16[2,288,2048]{2,1,0:T(8,128)(2,1)S(1)}, bf16[2,288,2048]{2,1,0:T(8,128)(2,1)}, u32[]{:S(2)}) copy-start(bf16[2,288,2048]{2,1,0:T(8,128)(2,1)} %copy-done.33) | copy-start | bytes 7077892
  803.5 52.4 %copy-start.92 = (bf16[2,288,2,128]{3,2,1,0:T(2,128)(2,1)S(1)}, bf16[2,288,2,128]{3,2,1,0:T(2,128)(2,1)}, u32[]{:S(2)}) copy-start(bf16[2,288,2,128]{3,2,1,0:T(2,128)(2,1)} %copy-done.91) | copy-start | bytes 884740
  861.3 277.3 %reduce-scatter.9.cloned.1.call-start = ((), (), s32[]{:S(2)}) async-start(), calls=%async_computation.16 | async-start | bytes 3932160 | tf_op jit(solution)/shard_map/reduce_scatter | solution.py:711
  927.3 69.0 %copy-start.27 = (f32[1,2048]{1,0:T(1,128)S(1)}, f32[1,2048]{1,0:T(1,128)}, u32[]{:S(2)}) copy-start(f32[1,2048]{1,0:T(1,128)} %copy-done.26) | copy-start | bytes 24580
  927.3 69.0 %copy-start.154 = (f32[128]{0:T(128)S(1)}, f32[128]{0:T(128)}, u32[]{:S(2)}) copy-start(f32[128]{0:T(128)} %get-tuple-element.133) | copy-start | bytes 1540
  927.3 69.0 %copy-start.155 = (f32[128]{0:T(128)S(1)}, f32[128]{0:T(128)}, u32[]{:S(2)}) copy-start(f32[128]{0:T(128)} %get-tuple-element.135) | copy-start | bytes 1540
  927.3 69.1 %copy-start.106 = (bf16[2048,768]{1,0:T(8,128)(2,1)S(1)}, bf16[2048,768]{1,0:T(8,128)(2,1)}, u32[]{:S(2)}) copy-start(bf16[2048,768]{1,0:T(8,128)(2,1)} %all-gather.11.cloned.1.call-done) | copy-start | bytes 9437188
  927.3 69.1 %copy-start.112 = (bf16[2,288,128]{2,1,0:T(8,128)(2,1)S(1)}, bf16[2,288,128]{2,1,0:T(8,128)(2,1)}, u32[]{:S(2)}) copy-start(bf16[2,288,128]{2,1,0:T(8,128)(2,1)} %copy-done.111) | copy-start | bytes 442372
  1118.5 28.7 %collective-permute-start.12 = (bf16[1,3,192,512]{3,2,0,1:T(8,128)(2,1)}, bf16[1,3,192,512]{3,2,0,1:T(8,128)(2,1)}, u32[]{:S(2)}, u32[]{:S(2)}) collective-permute-start(bf16[1,3,192,512]{3,2,0,1:T(8,128)(2,1)} %get-tuple-element.158), channel_id=1, source_target_pairs={{0,4},{4,0},{8,12},{12,8},{1,5},{5,1},{9,13},{13,9},{2,6},{6,2},{1... | collective-permute-start | bytes 1769480 | tf_op jit(solution)/shard_map/ppermute | solution.py:116
  1119.6 42.7 %collective-permute-start.13 = (bf16[1,3,192,512]{3,2,0,1:T(8,128)(2,1)}, bf16[1,3,192,512]{3,2,0,1:T(8,128)(2,1)}, u32[]{:S(2)}, u32[]{:S(2)}) collective-permute-start(bf16[1,3,192,512]{3,2,0,1:T(8,128)(2,1)} %get-tuple-element.157), channel_id=1, source_target_pairs={{0,8},{4,12},{8,0},{12,4},{1,9},{5,13},{9,1},{13,5},{2,10},{6,14},... | collective-permute-start | bytes 1769480 | tf_op jit(solution)/shard_map/ppermute | solution.py:116
  1121.3 42.1 %collective-permute-start.14 = (bf16[1,3,192,512]{3,2,0,1:T(8,128)(2,1)}, bf16[1,3,192,512]{3,2,0,1:T(8,128)(2,1)}, u32[]{:S(2)}, u32[]{:S(2)}) collective-permute-start(bf16[1,3,192,512]{3,2,0,1:T(8,128)(2,1)} %get-tuple-element.156), channel_id=1, source_target_pairs={{0,12},{4,8},{8,4},{12,0},{1,13},{5,9},{9,5},{13,1},{2,14},{6,10},... | collective-permute-start | bytes 1769480 | tf_op jit(solution)/shard_map/ppermute | solution.py:116
  1135.7 36.8 %collective-permute-start.9 = (bf16[1,3,192,512]{3,2,0,1:T(8,128)(2,1)}, bf16[1,3,192,512]{3,2,0,1:T(8,128)(2,1)S(1)}, u32[]{:S(2)}, u32[]{:S(2)}) collective-permute-start(bf16[1,3,192,512]{3,2,0,1:T(8,128)(2,1)} %get-tuple-element.155), channel_id=1, source_target_pairs={{0,4},{4,0},{8,12},{12,8},{1,5},{5,1},{9,13},{13,9},{2,6},{6,2},{1... | collective-permute-start | bytes 1769480 | tf_op jit(solution)/shard_map/ppermute | solution.py:116
  1136.0 76.8 %collective-permute-start.10 = (bf16[1,3,192,512]{3,2,0,1:T(8,128)(2,1)}, bf16[1,3,192,512]{3,2,0,1:T(8,128)(2,1)S(1)}, u32[]{:S(2)}, u32[]{:S(2)}) collective-permute-start(bf16[1,3,192,512]{3,2,0,1:T(8,128)(2,1)} %get-tuple-element.154), channel_id=1, source_target_pairs={{0,8},{4,12},{8,0},{12,4},{1,9},{5,13},{9,1},{13,5},{2,10},{6,14},... | collective-permute-start | bytes 1769480 | tf_op jit(solution)/shard_map/ppermute | solution.py:116
  1147.2 65.6 %collective-permute-start.11 = (bf16[1,3,192,512]{3,2,0,1:T(8,128)(2,1)S(1)}, bf16[1,3,192,512]{3,2,0,1:T(8,128)(2,1)S(1)}, u32[]{:S(2)}, u32[]{:S(2)}) collective-permute-start(bf16[1,3,192,512]{3,2,0,1:T(8,128)(2,1)S(1)} %copy-done.104), channel_id=1, source_target_pairs={{0,12},{4,8},{8,4},{12,0},{1,13},{5,9},{9,5},{13,1},{2,14},{6,10},... | collective-permute-start | bytes 1769480 | tf_op jit(solution)/shard_map/ppermute | solution.py:116
  1162.3 55.5 %collective-permute-start.8 = (bf16[512,768]{1,0:T(8,128)(2,1)S(1)}, bf16[512,768]{1,0:T(8,128)(2,1)S(1)}, u32[]{:S(2)}, u32[]{:S(2)}) collective-permute-start(bf16[512,768]{1,0:T(8,128)(2,1)S(1)} %broadcast_select_fusion.4), channel_id=1, source_target_pairs={{0,16},{16,0},{1,17},{17,1},{2,18},{18,2},{3,19},{19,3},{4,20},{20... | collective-permute-start | bytes 2359304 | tf_op jit(solution)/shard_map/ppermute | solution.py:722
  1214.6 12.5 collective-permute-start.15
  (162 other events, 1320.3 us)
Sparse Core Ops, SparseCore 0:
  18.0 113.6 all-gather.10
  134.0 44.8 all-gather.12
  181.4 43.9 all-gather.14
  227.1 43.9 all-gather.16
  273.1 88.3 all-gather.18
  363.2 42.4 all-gather.20
  407.6 52.7 all-gather.22
  462.2 44.8 all-gather.24
  596.7 51.2 reduce-scatter.18
  650.8 50.7 reduce-scatter.20
  704.6 50.3 reduce-scatter.22
  782.1 52.2 reduce-scatter.12
  837.5 56.0 reduce-scatter.14
  896.4 43.9 reduce-scatter.16
  943.1 76.5 reduce-scatter.10
  1022.4 62.9 reduce-scatter.8

commit v4 on v3

--- a/solution.py
+++ b/solution.py
@@ -116,6 +116,28 @@
         arrived = lax.ppermute(piece, axis, [(i, i ^ step) for i in range(size)])
         got = lax.dynamic_update_slice_in_dim(got, arrived, other, 0)
     return got
+
+
+def gather_by_permutes(own, axis):
+    size = lax.axis_size(axis)
+    me = lax.axis_index(axis)
+    got = lax.dynamic_update_slice_in_dim(
+        jnp.zeros((size,) + own.shape, own.dtype), own[None], me, 0
+    )
+    for step in range(1, size):
+        arrived = lax.ppermute(own, axis, [(i, i ^ step) for i in range(size)])
+        got = lax.dynamic_update_slice_in_dim(got, arrived[None], me ^ step, 0)
+    return got
+
+
+def scatter_by_permutes(pieces, axis):
+    size = lax.axis_size(axis)
+    me = lax.axis_index(axis)
+    total = lax.dynamic_index_in_dim(pieces, me, 0, keepdims=False).astype(F32)
+    for step in range(1, size):
+        piece = lax.dynamic_index_in_dim(pieces, me ^ step, 0, keepdims=False)
+        total += lax.ppermute(piece, axis, [(i, i ^ step) for i in range(size)]).astype(F32)
+    return total.astype(BF16)
 
 
 def masked_scores(query_bf, key_all, allowed):
@@ -360,6 +382,65 @@
     return [cell.value for cell in cells] + gathered
 
 
+class LineGather:
+    def __init__(self, own, block, send, recv, chunks):
+        self.own, self.block, self.send, self.recv, self.chunks = own, block, send, recv, chunks
+        self.me = lax.axis_index("dp")
+        self.size = lax.axis_size("dp")
+
+    def direct(self, place):
+        if self.size != 4:
+            return place != self.me
+        return (place != self.me) & (place + self.me != 3) | ((self.me == 3 - place) & (place % 3 != 0))
+
+    def copy(self, place, slot, chunk):
+        return remote(
+            self.own(chunk), self.block(slot, chunk),
+            self.send.at[place, chunk], self.recv.at[slot, chunk], {"dp": place},
+        )
+
+    def passed(self, place, slot, chunk):
+        return remote(
+            self.block(slot, chunk), self.block(slot, chunk),
+            self.send.at[self.me, chunk], self.recv.at[slot, chunk], {"dp": place},
+        )
+
+    def start(self, chunk):
+        for place in range(self.size):
+            @pl.when(self.direct(place))
+            def _():
+                self.copy(place, self.me, chunk).start()
+
+    def relays(self):
+        return [(2, 0, 3), (1, 3, 0)] if self.size == 4 else []
+
+    def arrive(self, place, chunk):
+        @pl.when(place != self.me)
+        def _():
+            self.copy(place, place, chunk).wait_recv()
+
+        for via, source, target in self.relays():
+            if source == place:
+                @pl.when(self.me == via)
+                def _():
+                    self.passed(target, source, chunk).start()
+
+    def finish(self):
+        for chunk in range(self.chunks):
+            for place in range(self.size):
+                @pl.when(self.direct(place))
+                def _():
+                    self.copy(place, self.me, chunk).wait_send()
+            for via, source, target in self.relays():
+                @pl.when(self.me == via)
+                def _():
+                    self.passed(target, source, chunk).wait_send()
+
+
+def line_order(size):
+    return [1, 2, 0, 3] if size == 4 else list(range(size))
+
+
 def gather_kv(own):
     trees, rows, width = own.shape
     if rows % 16:
@@ -367,12 +448,77 @@
     size = lax.axis_size("dp")
 
     def kernel(own_ref, out_ref, send, recv):
+        greet(["dp"])
+        line = LineGather(
+            lambda chunk: own_ref.at[chunk], lambda slot, chunk: out_ref.at[chunk, slot],
+            send, recv, trees,
+        )
+        for chunk in range(trees):
+            line.start(chunk)
+        out_ref[:, line.me] = own_ref[...]
+        for chunk in range(trees):
+            for place in line_order(size):
+                line.arrive(place, chunk)
+        line.finish()
+
+    shape = jax.ShapeDtypeStruct((trees, size, rows, width), BF16)
+    sem = pltpu.SemaphoreType.DMA
+    whole = kernel_call(kernel, shape, [sem((size, trees))] * 2, 1, 30, own)
+    return whole.reshape(trees, size * rows, width)
+
+
+def gather_shards(own):
+    rows, width = own.shape
+    chunks = 4
+    size = lax.axis_size("dp")
+    if rows % (16 * chunks):
+        return lax.all_gather(own, "dp", axis=0, tiled=True)
+
+    def kernel(own_ref, out_ref, keep, send, recv):
+        greet(["dp"])
+        line = LineGather(
+            lambda chunk: own_ref.at[chunk], lambda slot, chunk: out_ref.at[slot, chunk],
+            send, recv, chunks,
+        )
+        for chunk in range(chunks):
+            line.start(chunk)
+        local = pltpu.make_async_copy(own_ref, out_ref.at[line.me], keep)
+        local.start()
+        for chunk in range(chunks):
+            for place in line_order(size):
+                line.arrive(place, chunk)
+        local.wait()
+        line.finish()
+
+    sem = pltpu.SemaphoreType.DMA
+    hbm = pl.BlockSpec(memory_space=pl.ANY)
+    whole = pl.pallas_call(
+        kernel,
+        out_shape=jax.ShapeDtypeStruct((size, chunks, rows // chunks, width), BF16),
+        in_specs=[hbm],
+        out_specs=hbm,
+        scratch_shapes=[sem, sem((size, chunks)), sem((size, chunks))],
+        cost_estimate=pl.CostEstimate(flops=0, bytes_accessed=200_000_000, transcendentals=0),
+        compiler_params=pltpu.CompilerParams(collective_id=9, has_side_effects=True),
+    )(own.reshape(chunks, rows // chunks, width))
+    return whole.reshape(size * rows, width)
+
+
+def exchange_shards(pieces):
+    size, rows, width = pieces.shape
+    if rows % 16 or width % 128:
+        return exchange(pieces, "dp").transpose(1, 0, 2).reshape(rows, -1)
+
+    def kernel(in_ref, out_ref, keep, send, recv):
         me = lax.axis_index("dp")
         greet(["dp"])
 
+        def lands(slot):
+            return out_ref.at[:, pl.ds(pl.multiple_of(slot * width, width), width)]
+
         def spread(place, slot):
             return remote(
-                own_ref, out_ref.at[:, slot], send.at[place], recv.at[slot], {"dp": place}
+                in_ref.at[place], lands(slot), send.at[place], recv.at[slot], {"dp": place}
             )
 
         for place in range(size):
@@ -380,17 +526,27 @@
             def _():
                 spread(place, me).start()
 
-        out_ref[:, me] = own_ref[...]
+        local = pltpu.make_async_copy(in_ref.at[me], lands(me), keep)
+        local.start()
         for place in range(size):
             @pl.when(place != me)
             def _():
                 spread(place, place).wait_recv()
                 spread(place, me).wait_send()
 
-    shape = jax.ShapeDtypeStruct((trees, size, rows, width), BF16)
+        local.wait()
+
     sem = pltpu.SemaphoreType.DMA
-    whole = kernel_call(kernel, shape, [sem((size,))] * 2, 1, 30, own)
-    return whole.reshape(trees, size * rows, width)
+    hbm = pl.BlockSpec(memory_space=pl.ANY)
+    return pl.pallas_call(
+        kernel,
+        out_shape=jax.ShapeDtypeStruct((rows, size * width), BF16),
+        in_specs=[hbm],
+        out_specs=hbm,
+        scratch_shapes=[sem, sem((size,)), sem((size,))],
+        cost_estimate=pl.CostEstimate(flops=0, bytes_accessed=70_000_000, transcendentals=0),
+        compiler_params=pltpu.CompilerParams(collective_id=10, has_side_effects=True),
+    )(pieces)
 
 
 def scatter_kv(whole):
@@ -399,42 +555,132 @@
     rows = all_rows // size
     if rows % 16:
         return lax.psum_scatter(whole, "dp", scatter_dimension=1, tiled=True)
-
-    def kernel(in_ref, out_ref, boxes, send, recv):
+    relays = [(0, 1, 3), (3, 2, 0)] if size == 4 else []
+
+    def kernel(in_ref, out_ref, boxes, joint, send, recv, join_send, join_recv):
         me = lax.axis_index("dp")
         greet(["dp"])
 
-        def spread(place, slot):
+        def spread(place, slot, chunk):
             return remote(
-                in_ref.at[:, place], boxes.at[slot], send.at[place], recv.at[slot], {"dp": place}
+                in_ref.at[chunk, place], boxes.at[slot, chunk], send.at[place, chunk],
+                recv.at[slot, chunk], {"dp": place},
             )
 
-        for place in range(size):
-            @pl.when(place != me)
-            def _():
-                spread(place, me).start()
-
-        boxes[me] = in_ref[:, me]
-        for place in range(size):
-            @pl.when(place != me)
-            def _():
-                spread(place, place).wait_recv()
-
-        total = boxes[0].astype(F32)
-        for place in range(1, size):
-            total += boxes[place].astype(F32)
-        out_ref[...] = total.astype(BF16)
-        for place in range(size):
-            @pl.when(place != me)
-            def _():
-                spread(place, me).wait_send()
-
-    shape = jax.ShapeDtypeStruct((trees, rows, width), BF16)
+        def by_way(via, target, chunk):
+            return remote(
+                in_ref.at[chunk, target], joint.at[chunk], join_send.at[chunk],
+                join_recv.at[chunk], {"dp": via},
+            )
+
+        def joined(via, target, chunk):
+            return remote(
+                joint.at[chunk], boxes.at[via, chunk], send.at[target, chunk],
+                recv.at[via, chunk], {"dp": target},
+            )
+
+        def plain(place):
+            ok = place != me
+            for source, via, target in relays:
+                if place == target:
+                    ok = ok & (me != source) & (me != via)
+            return ok
+
+        def expected(place):
+            ok = place != me
+            for source, via, target in relays:
+                if place == source:
+                    ok = ok & (me != target)
+            return ok
+
+        for chunk in range(trees):
+            for source, via, target in relays:
+                @pl.when(me == source)
+                def _():
+                    by_way(via, target, chunk).start()
+
+            for place in range(size):
+                @pl.when(plain(place))
+                def _():
+                    spread(place, me, chunk).start()
+
+        for chunk in range(trees):
+            for source, via, target in relays:
+                @pl.when(me == via)
+                def _():
+                    by_way(via, target, chunk).wait_recv()
+                    both = joint[chunk].astype(F32) + in_ref[chunk, target].astype(F32)
+                    joint[chunk] = both.astype(BF16)
+                    joined(via, target, chunk).start()
+
+        for chunk in range(trees):
+            out_ref[chunk] = in_ref[chunk, me].astype(F32)
+            for place in range(size):
+                @pl.when(expected(place))
+                def _():
+                    spread(place, place, chunk).wait_recv()
+                    out_ref[chunk] += boxes[place, chunk].astype(F32)
+
+        for chunk in range(trees):
+            for place in range(size):
+                @pl.when(plain(place))
+                def _():
+                    spread(place, me, chunk).wait_send()
+
+            for source, via, target in relays:
+                @pl.when(me == source)
+                def _():
+                    by_way(via, target, chunk).wait_send()
+
+                @pl.when(me == via)
+                def _():
+                    joined(via, target, chunk).wait_send()
+
+    shape = jax.ShapeDtypeStruct((trees, rows, width), F32)
     sem = pltpu.SemaphoreType.DMA
-    scratch = [pltpu.VMEM((size, trees, rows, width), BF16), sem((size,)), sem((size,))]
+    box = pltpu.VMEM((size, trees, rows, width), BF16)
+    scratch = [box, pltpu.VMEM((trees, rows, width), BF16), sem((size, trees)), sem((size, trees))]
+    scratch += [sem((trees,)), sem((trees,))]
     return kernel_call(
         kernel, shape, scratch, 2, 30, whole.reshape(trees, size, rows, width)
     )
+
+
+def total_over_all(own):
+    axes = ["section", "tensor", "dp"]
+    sizes = [lax.axis_size(axis) for axis in axes]
+
+    def kernel(own_ref, out_ref, *scratch):
+        boxes, sends, recvs = scratch[:3], scratch[3:6], scratch[6:9]
+        greet(axes)
+        out_ref[...] = own_ref[...]
+        for axis, size, box, send, recv in zip(axes, sizes, boxes, sends, recvs):
+            me = lax.axis_index(axis)
+            box[me] = out_ref[...]
+
+            def spread(place, slot):
+                return remote(box.at[me], box.at[slot], send.at[place], recv.at[slot], {axis: place})
+
+            for place in range(size):
+                @pl.when(place != me)
+                def _():
+                    spread(place, me).start()
+
+            for place in range(size):
+                @pl.when(place != me)
+                def _():
+                    spread(place, place).wait_recv()
+                    spread(place, me).wait_send()
+
+            total = box[0]
+            for place in range(1, size):
+                total += box[place]
+            out_ref[...] = total
+
+    sem = pltpu.SemaphoreType.DMA
+    scratch = [pltpu.VMEM((size,) + own.shape, F32) for size in sizes]
+    scratch += [sem((size,)) for size in sizes] * 2
+    return kernel_call(kernel, jax.ShapeDtypeStruct(own.shape, F32), scratch, 11, 12, own)
 
 
 def meet(partial_sums, own_args, body, own_outs, scatter, gathers, collective_id, cost_us):
@@ -568,6 +814,7 @@
         "bgrt,brgd->btd", prob_full.astype(BF16), grad_heads, preferred_element_type=F32
     )
     grad_kv = scatter_kv(jnp.concatenate([grad_key_all, grad_value_all], axis=2).astype(BF16))
+    grad_kv = grad_kv.astype(BF16)
     if shared_kv:
         total = lax.psum(grad_kv, "section")
         grad_kv = jnp.where(lax.axis_index("section") == 0, total, jnp.zeros_like(total))
@@ -667,13 +914,32 @@
     unit_shards = swap_cores(pick(unit_blocks, core), pick(unit_blocks, 1 - core))
 
     qkv_width = q_width + 2 * k_width
-    weights = []
-    for layer in range(2):
-        attn_all = lax.all_gather(attn_shards[layer], "dp", axis=0, tiled=True)
-        pieces = exchange(unit_shards[layer], "dp")
-        pieces = pieces.transpose(1, 2, 0, 3).reshape(3, share, depth)
-        mats = [lax.all_gather(pieces[i], "tensor", axis=0, tiled=True) for i in range(3)]
-        weights.append((attn_all[:, :qkv_width], attn_all[:, qkv_width:], *mats))
+
+    def after(first, *then):
+        return lax.optimization_barrier((first, *then))[1:]
+
+    def spread_units(rows):
+        return gather_by_permutes(rows, "tensor").reshape(-1, depth)
+
+    def exchanged(pieces):
+        return exchange(pieces, "dp").transpose(1, 0, 2).reshape(share, depth)
+
+    gate_rows = exchange_shards(unit_shards[0][:, 0])
+    (attn_shard,) = after(gate_rows, attn_shards[0])
+    attn_all = gather_shards(attn_shard)
+    gate_all = spread_units(gate_rows)
+    units, attn_shard = after(attn_all, unit_shards[0], attn_shards[1])
+    up_all = spread_units(exchanged(units[:, 1]))
+    down_all = spread_units(exchanged(units[:, 2]))
+    weights = [(attn_all[:, :qkv_width], attn_all[:, qkv_width:], gate_all, up_all, down_all)]
+    attn_all = gather_by_permutes(attn_shard, "dp").reshape(depth, -1)
+    (units,) = after(attn_all, unit_shards[1])
+    weights.append(
+        (
+            attn_all[:, :qkv_width], attn_all[:, qkv_width:],
+            *(spread_units(exchanged(units[:, i])) for i in range(3)),
+        )
+    )
 
     def slot_setup(slot_index):
         tree_id = pick(order, slot_index)
@@ -699,7 +965,8 @@
         kept.append(stored)
 
     grad_own = own_part(cotangent).astype(F32)
-    (grad_mlp,) = meet(None, [grad_own], pass_body, [], None, ["dp"], 8, 30)
+    grad_mlp = gather_by_permutes(grad_own.astype(BF16), "dp").reshape(-1, depth)
+    grad_mlp = gather_by_permutes(grad_mlp, "section")
     grads, weight_grads, gain_grads = [None, None], [None, None], [None, None]
     for layer in (1, 0):
         gathered, grad_own, products, gain_grads[layer] = layer_backward(
@@ -708,11 +975,12 @@
         )
         grads[layer], grad_mlp = gathered[0], gathered[-1]
         whole = [dot_outer(left, right).astype(BF16) for left, right in products]
-        attn_grad = lax.psum_scatter(
-            jnp.concatenate(whole[:2], axis=1), "dp", scatter_dimension=0, tiled=True
+        attn_grad = scatter_by_permutes(
+            jnp.concatenate(whole[:2], axis=1).reshape(dp_size, own_depth, -1), "dp"
         )
         unit_grad = [
-            lax.psum_scatter(item, "tensor", scatter_dimension=0, tiled=True) for item in whole[2:]
+            scatter_by_permutes(item.reshape(tensor_size, share, depth), "tensor")
+            for item in whole[2:]
         ]
         pieces = jnp.stack(unit_grad).reshape(3, share, dp_size, own_depth).transpose(2, 0, 1, 3)
         weight_grads[layer] = (attn_grad, exchange(pieces, "dp"))
@@ -732,7 +1000,8 @@
             return parts[0].astype(F32)
         return jnp.concatenate(parts, axis=1).astype(F32)
 
-    gain_total = lax.psum(jnp.stack(gain_grads), ("section", "dp", "tensor"))
+    gain_total = jnp.stack(gain_grads)
+    gain_total = total_over_all(gain_total.reshape(-1, 128)).reshape(gain_total.shape)
     gain_own = pick(gain_total, core)
     share_width = attn_gain.shape[1]
     attn_gain_grad = lax.dynamic_slice_in_dim(gain_own, data_index * share_width, share_width, 0)

time: 1270 us -> 1540 us (1.21)
  starting transfers between devices: 38.8 us -> 181 us
  local copies, waits for them, and re-layouts: 110 us -> 212 us
  waiting for transfers between devices: 190 us -> 283 us
  blocking collectives: 101 us -> 29.5 us
  matrix products: 137 us -> 101 us
  Pallas kernels: 586 us -> 611 us
  other arithmetic: 65.1 us -> 89.9 us
    ppermute x0 -> x49, waiting for transfers between devices: none -> 210 us  [the longest x24 131 us: scatter_by_permutes(): lax.ppermute(piece, axis, [(i, i ^ step) for i in range(size)]).astype(F32)]
    ppermute x12 -> x21, waiting for transfers between devices: 183 us -> 72.7 us  [exchange(): arrived = lax.ppermute(piece, axis, [(i, i ^ step) for i in range(size)])]
    ppermute x0 -> x49, starting transfers between devices: none -> 82.4 us  [the longest x24 48.5 us: scatter_by_permutes(): lax.ppermute(piece, axis, [(i, i ^ step) for i in range(size)]).astype(F32)]
    pallas_call x0 -> x2, Pallas kernels: none -> 78.8 us  [the longest x1 61.3 us: gather_shards(): pl.pallas_call(kernel, out_shape=jax.ShapeDtypeStruct((size, chunks, rows...]
    psum x1 -> x0, blocking collectives: 68.1 us -> none  [on_device(): gain_total = lax.psum(jnp.stack(gain_grads), ('section', 'dp', 'tensor'))]
    ppermute x12 -> x21, starting transfers between devices: 36.7 us -> 97.9 us  [exchange(): arrived = lax.ppermute(piece, axis, [(i, i ^ step) for i in range(size)])]
    pallas_call x13, Pallas kernels: 586 us -> 532 us  [kernel_call(): pl.pallas_call(kernel, out_shape=out_shape, in_specs=[in_vmem] * len(args...]
    dynamic_update_slice x0 -> x33, local copies, waits for them, and re-layouts: none -> 27.4 us  [the longest x25 24.3 us: gather_by_permutes(): got = lax.dynamic_update_slice_in_dim(got, arrived[None], me ^ step, 0)]
  transfers between devices with their start and end apart: 32 -> 74, of which waited for: 11 -> 24; matrix products, arithmetic and copies ran while one was open for 20% -> 17% of each run, Pallas kernels for 47% -> 24%
where the time goes in v4:
time: 1540 us; the launch traced here: 1520 us
  Pallas kernels  611 us (40%)
  waiting for transfers between devices  283 us (18%)
  local copies, waits for them, and re-layouts  212 us (14%)
  starting transfers between devices  181 us (12%)
  matrix products  101 us (7%)
  other arithmetic  89.9 us (6%)
  blocking collectives  29.5 us (2%)
    pallas_call x13, Pallas kernels, kernel_call(): pl.pallas_call(kernel, out_shape=out_shape, in_specs=[in_vmem] * len(args...  532 us
    ppermute x24, waiting for transfers between devices, scatter_by_permutes(): lax.ppermute(piece, axis, [(i, i ^ step) for i in range(size)]).astype(F32)  131 us
    ppermute x21, starting transfers between devices, exchange(): arrived = lax.ppermute(piece, axis, [(i, i ^ step) for i in range(size)])  97.9 us
    ppermute x25, waiting for transfers between devices, gather_by_permutes(): arrived = lax.ppermute(own, axis, [(i, i ^ step) for i in range(size)])  79.4 us
    ppermute x21, waiting for transfers between devices, exchange(): arrived = lax.ppermute(piece, axis, [(i, i ^ step) for i in range(size)])  72.7 us
    pallas_call x1, Pallas kernels, gather_shards(): pl.pallas_call(kernel, out_shape=jax.ShapeDtypeStruct((size, chunks, rows...  61.3 us
    ppermute x24, starting transfers between devices, scatter_by_permutes(): lax.ppermute(piece, axis, [(i, i ^ step) for i in range(size)]).astype(F32)  48.5 us
    unnamed x477, local copies, waits for them, and re-layouts  48.4 us
  transfers between devices with their start and end apart: 74, of which 24 were waited for; matrix products, arithmetic and copies ran while one was open for 17% of the time, Pallas kernels for 24%

profile of v4, /device:TPU:0, one launch (start us, length us, event | category | flops | bytes accessed | tf_op | source)
XLA Modules:
  0.0 1515.8 jit_solution(4300271127016971146)
XLA Ops:
  23.8 29.5 %all-gather.1 = bf16[8,1,1280]{2,1,0:T(2,128)(2,1)S(1)} all-gather(bf16[1,1,1280]{2,1,0:T(2,128)(2,1)S(1)} %reshape.804), channel_id=2, replica_groups=mesh['section'=2,'dp'=4,'tensor'=4] {'section','dp'}, dimensions={0}, use_global_device_ids=true | all-gather | bytes 23040 | tf_op jit(solution)/shard_map/all_gather | solution.py:883
  91.6 17.5 %shard_map.255 = bf16[192,2048]{1,0:T(8,128)(2,1)} custom-call(bf16[4,192,512]{2,1,0:T(8,128)(2,1)} %slice_bitcast_fusion.in_ref), custom_call_target="tpu_custom_call" | custom-call | bytes 70000000 | tf_op jit(solution)/shard_map/pallas_call | solution.py:541
  109.1 61.3 %shard_map.256 = bf16[4,4,128,768]{3,2,1,0:T(8,128)(2,1)} custom-call(bf16[4,128,768]{2,1,0:T(8,128)(2,1)} %bitcast.687), custom_call_target="tpu_custom_call" | custom-call | bytes 200000000 | tf_op jit(solution)/shard_map/pallas_call | solution.py:495
  180.2 82.8 %shard_map.257 = bf16[2,4,288,256]{3,2,1,0:T(8,128)(2,1)S(1)} custom-call(bf16[2,288,256]{2,1,0:T(8,128)(2,1)S(1)} %pad_maximum_fusion.10.own_ref), custom_call_target="tpu_custom_call" | custom-call | bytes 90000000 | tf_op jit(solution)/shard_map/pallas_call | solution.py:177
  285.9 41.7 %shard_map.258 = (f32[72,2048]{1,0:T(8,128)S(1)}, bf16[2,288,2048]{2,1,0:T(8,128)(2,1)S(1)}) custom-call(bf16[2,288,2048]{2,1,0:T(8,128)(2,1)S(1)} %bitcast.590, f32[72,2048]{1,0:T(8,128)S(1)} %bitcast_convert_fusion.4.refs_1_, f32[1,2048]{1,0:T(1,128)S(1)} %bitcast.606), custom_call_target="tpu_custom_call" | custom-call | bytes 150000000 | tf_op jit(solution)/shard_map/pallas_call | solution.py:177
  327.8 8.7 collective-permute-start.13
  337.3 5.0 collective-permute-done.13
  354.6 5.7 collective-permute-done.6
  385.7 15.1 collective-permute-done.3
  412.6 5.1 collective-permute-done.21
  417.8 6.3 collective-permute-start.27
  437.1 4.3 collective-permute-start.33
  476.4 18.4 %collective-permute-done.9 = bf16[192,2048]{1,0:T(8,128)(2,1)} collective-permute-done((bf16[192,2048]{1,0:T(8,128)(2,1)}, bf16[192,2048]{1,0:T(8,128)(2,1)}, u32[]{:S(2)}, u32[]{:S(2)}) %collective-permute-start.9) | collective-permute-done | bytes 786464 | tf_op jit(solution)/shard_map/ppermute | solution.py:128
  506.3 49.2 %shard_map.259 = (f32[72,2048]{1,0:T(8,128)S(1)}, bf16[2,288,2048]{2,1,0:T(8,128)(2,1)S(1)}) custom-call(bf16[2,288,2048]{2,1,0:T(8,128)(2,1)S(1)} %bitcast.605, f32[72,2048]{1,0:T(8,128)S(1)} %get-tuple-element.39.refs_1_), custom_call_target="tpu_custom_call" | custom-call | bytes 150000000 | tf_op jit(solution)/shard_map/pallas_call | solution.py:177
  559.7 28.3 %shard_map.260 = bf16[2,4,288,256]{3,2,1,0:T(8,128)(2,1)S(1)} custom-call(bf16[2,288,256]{2,1,0:T(8,128)(2,1)S(1)} %pad_maximum_fusion.12.own_ref), custom_call_target="tpu_custom_call" | custom-call | bytes 90000000 | tf_op jit(solution)/shard_map/pallas_call | solution.py:177
  605.8 41.0 %shard_map.261 = (f32[72,2048]{1,0:T(8,128)S(1)}, bf16[2,288,2048]{2,1,0:T(8,128)(2,1)S(1)}) custom-call(bf16[2,288,2048]{2,1,0:T(8,128)(2,1)S(1)} %bitcast.591, f32[72,2048]{1,0:T(8,128)S(1)} %convert_convert_fusion.1.refs_1_, f32[1,2048]{1,0:T(1,128)S(1)} %bitcast.608), custom_call_target="tpu_custom_call" | custom-call | bytes 150000000 | tf_op jit(solution)/shard_map/pallas_call | solution.py:177
  658.2 10.8 collective-permute-done.31
  669.1 16.8 %collective-permute-done.35 = bf16[192,2048]{1,0:T(8,128)(2,1)S(1)} collective-permute-done((bf16[192,2048]{1,0:T(8,128)(2,1)S(1)}, bf16[192,2048]{1,0:T(8,128)(2,1)S(1)}, u32[]{:S(2)}, u32[]{:S(2)}) %collective-permute-start.35) | collective-permute-done | bytes 786464 | tf_op jit(solution)/shard_map/ppermute | solution.py:128
  688.1 14.3 collective-permute-done.37
  713.7 47.2 %shard_map.263 = (f32[72,2048]{1,0:T(8,128)S(1)}, f32[1,2048]{1,0:T(1,128)S(1)}, bf16[2,288,2048]{2,1,0:T(8,128)(2,1)S(1)}) custom-call(bf16[2,288,2048]{2,1,0:T(8,128)(2,1)S(1)} %bitcast.603, f32[72,2048]{1,0:T(8,128)S(1)} %get-tuple-element.45.refs_1_, f32[1,2048]{1,0:T(1,128)S(1)} %bitcast.609, f32[72,2048]{1,0:T(8,128)S(1)} %copy-done.10), custom_call_target="tpu_custom_call" | custom-call | bytes 150000000 | tf_op jit(solution)/shard_map/pallas_call | solution.py:177
  766.2 4.1 fusion.3
  787.9 31.1 %shard_map.264 = f32[2,288,256]{2,1,0:T(8,128)S(1)} custom-call(bf16[2,4,288,256]{3,2,1,0:T(8,128)(2,1)S(1)} %pad_maximum_fusion.4.in_ref), custom_call_target="tpu_custom_call" | custom-call | bytes 90000000 | tf_op jit(solution)/shard_map/pallas_call | solution.py:177
  822.5 43.6 %shard_map.265 = (f32[72,2048]{1,0:T(8,128)S(1)}, f32[1,2048]{1,0:T(1,128)S(1)}, bf16[2,288,2048]{2,1,0:T(8,128)(2,1)S(1)}, bf16[2,288,2048]{2,1,0:T(8,128)(2,1)S(1)}) custom-call(bf16[2,288,2048]{2,1,0:T(8,128)(2,1)S(1)} %bitcast.604, f32[72,2048]{1,0:T(8,128)S(1)} %convert_convert_fusion.1.refs_1_, f32[1,2048]{1,0:T(1,128)S(1)} %bitcast.611, ...), custom_call_target="tpu_custom_call" | custom-call | bytes 120000000 | tf_op jit(solution)/shard_map/pallas_call | solution.py:177
  873.8 4.1 convolution_convert_fusion.4
  886.2 47.8 %shard_map.266 = (f32[72,2048]{1,0:T(8,128)S(1)}, f32[1,2048]{1,0:T(1,128)S(1)}, bf16[2,288,2048]{2,1,0:T(8,128)(2,1)S(1)}) custom-call(bf16[2,288,2048]{2,1,0:T(8,128)(2,1)S(1)} %bitcast.601, f32[72,2048]{1,0:T(8,128)S(1)} %copy-done.13, f32[1,2048]{1,0:T(1,128)S(1)} %bitcast.607, f32[72,2048]{1,0:T(8,128)S(1)} %convert_convert_fusion.refs_3_), custom_call_target="tpu_custom_call" | custom-call | bytes 150000000 | tf_op jit(solution)/shard_map/pallas_call | solution.py:177
  984.0 4.6 copy.393
  991.8 29.0 %shard_map.267 = f32[2,288,256]{2,1,0:T(8,128)S(1)} custom-call(bf16[2,4,288,256]{3,2,1,0:T(8,128)(2,1)S(1)} %pad_maximum_fusion.5.in_ref), custom_call_target="tpu_custom_call" | custom-call | bytes 90000000 | tf_op jit(solution)/shard_map/pallas_call | solution.py:177
  1027.6 35.7 %shard_map.268 = (f32[72,2048]{1,0:T(8,128)}, f32[1,2048]{1,0:T(1,128)S(1)}, bf16[2,288,2048]{2,1,0:T(8,128)(2,1)S(1)}) custom-call(bf16[2,288,2048]{2,1,0:T(8,128)(2,1)S(1)} %bitcast.602, f32[72,2048]{1,0:T(8,128)S(1)} %copy-done.1, f32[1,2048]{1,0:T(1,128)S(1)} %bitcast.610, f32[72,2048]{1,0:T(8,128)S(1)} %copy-done.17), custom_call_target="tpu_custom_call" | custom-call | bytes 120000000 | tf_op jit(solution)/shard_map/pallas_call | solution.py:177
  1064.8 12.6 shard_map.269
  1079.2 42.1 %shard_map.262 = (f32[72,2048]{1,0:T(8,128)}, bf16[2,288,2048]{2,1,0:T(8,128)(2,1)S(1)}) custom-call(bf16[2,288,2048]{2,1,0:T(8,128)(2,1)S(1)} %bitcast.600, f32[72,2048]{1,0:T(8,128)S(1)} %copy-done.15), custom_call_target="tpu_custom_call" | custom-call | bytes 150000000 | tf_op jit(solution)/shard_map/pallas_call | solution.py:177
  1146.2 10.5 collective-permute-done.54
  1157.8 15.4 %collective-permute-done.49 = bf16[192,2048]{1,0:T(8,128)(2,1)S(1)} collective-permute-done((bf16[192,2048]{1,0:T(8,128)(2,1)S(1)}, bf16[192,2048]{1,0:T(8,128)(2,1)S(1)}, u32[]{:S(2)}, u32[]{:S(2)}) %collective-permute-start.49) | collective-permute-done | bytes 786464 | tf_op jit(solution)/shard_map/ppermute | solution.py:139
  1178.7 11.8 collective-permute-done.51
  1191.6 15.5 %collective-permute-done.67 = bf16[192,2048]{1,0:T(8,128)(2,1)} collective-permute-done((bf16[192,2048]{1,0:T(8,128)(2,1)S(1)}, bf16[192,2048]{1,0:T(8,128)(2,1)}, u32[]{:S(2)}, u32[]{:S(2)}) %collective-permute-start.67) | collective-permute-done | bytes 786464 | tf_op jit(solution)/shard_map/ppermute | solution.py:139
  1228.7 12.1 collective-permute-done.64
  1242.0 7.2 collective-permute-start.45
  1249.2 8.9 collective-permute-done.66
  1264.0 10.5 collective-permute-done.61
  1274.5 8.1 collective-permute-start.47
  1282.6 8.1 collective-permute-done.63
  1295.9 8.2 collective-permute-start.44
  1304.1 6.5 constant_dynamic-slice_fusion.4
  1325.7 5.6 constant_dynamic-slice_fusion
  1332.6 36.9 %collective-permute-start.59 = (bf16[1,3,192,512]{3,2,0,1:T(8,128)(2,1)S(1)}, bf16[1,3,192,512]{3,2,0,1:T(8,128)(2,1)S(1)}, u32[]{:S(2)}, u32[]{:S(2)}) collective-permute-start(bf16[1,3,192,512]{3,2,0,1:T(8,128)(2,1)S(1)} %bitcast.710), channel_id=1, source_target_pairs={{0,8},{4,12},{8,0},{12,4},{1,9},{5,13},{9,1},{13,5},{2,10},{6,14},... | collective-permute-start | bytes 1769480 | tf_op jit(solution)/shard_map/ppermute | solution.py:116
  1369.9 36.4 %collective-permute-done.43 = bf16[512,768]{1,0:T(8,128)(2,1)} collective-permute-done((bf16[512,768]{1,0:T(8,128)(2,1)}, bf16[512,768]{1,0:T(8,128)(2,1)}, u32[]{:S(2)}, u32[]{:S(2)}) %collective-permute-start.43) | collective-permute-done | bytes 786464 | tf_op jit(solution)/shard_map/ppermute | solution.py:139
  1409.7 18.8 %collective-permute-start.71 = (bf16[1,3,192,512]{3,2,0,1:T(8,128)(2,1)S(1)}, bf16[1,3,192,512]{3,2,0,1:T(8,128)(2,1)S(1)}, u32[]{:S(2)}, u32[]{:S(2)}) collective-permute-start(bf16[1,3,192,512]{3,2,0,1:T(8,128)(2,1)S(1)} %bitcast.711), channel_id=1, source_target_pairs={{0,8},{4,12},{8,0},{12,4},{1,9},{5,13},{9,1},{13,5},{2,10},{6,14},... | collective-permute-start | bytes 1769480 | tf_op jit(solution)/shard_map/ppermute | solution.py:116
  1434.1 26.9 %collective-permute-done.59 = bf16[1,3,192,512]{3,2,0,1:T(8,128)(2,1)S(1)} collective-permute-done((bf16[1,3,192,512]{3,2,0,1:T(8,128)(2,1)S(1)}, bf16[1,3,192,512]{3,2,0,1:T(8,128)(2,1)S(1)}, u32[]{:S(2)}, u32[]{:S(2)}) %collective-permute-start.59) | collective-permute-done | bytes 589856 | tf_op jit(solution)/shard_map/ppermute | solution.py:116
  1461.2 25.1 %collective-permute-done.71 = bf16[1,3,192,512]{3,2,0,1:T(8,128)(2,1)S(1)} collective-permute-done((bf16[1,3,192,512]{3,2,0,1:T(8,128)(2,1)S(1)}, bf16[1,3,192,512]{3,2,0,1:T(8,128)(2,1)S(1)}, u32[]{:S(2)}, u32[]{:S(2)}) %collective-permute-start.71) | collective-permute-done | bytes 589856 | tf_op jit(solution)/shard_map/ppermute | solution.py:116
  (906 shorter events, 470.6 us)
Async XLA Ops:
  3.9 59.7 %collective-permute-start.38 = (bf16[72,2048]{1,0:T(8,128)(2,1)}, bf16[72,2048]{1,0:T(8,128)(2,1)}, u32[]{:S(2)}, u32[]{:S(2)}) collective-permute-start(bf16[72,2048]{1,0:T(8,128)(2,1)} %get-tuple-element.166), channel_id=1, source_target_pairs={{0,4},{4,0},{8,12},{12,8},{1,5},{5,1},{9,13},{13,9},{2,6},{6,2},{1... | collective-permute-start | bytes 884744 | tf_op jit(solution)/shard_map/ppermute | solution.py:128
  7.0 58.6 %collective-permute-start.39 = (bf16[72,2048]{1,0:T(8,128)(2,1)}, bf16[72,2048]{1,0:T(8,128)(2,1)}, u32[]{:S(2)}, u32[]{:S(2)}) collective-permute-start(bf16[72,2048]{1,0:T(8,128)(2,1)} %get-tuple-element.166), channel_id=1, source_target_pairs={{0,8},{4,12},{8,0},{12,4},{1,9},{5,13},{9,1},{13,5},{2,10},{6,14},... | collective-permute-start | bytes 884744 | tf_op jit(solution)/shard_map/ppermute | solution.py:128
  9.6 57.7 %collective-permute-start.40 = (bf16[72,2048]{1,0:T(8,128)(2,1)}, bf16[72,2048]{1,0:T(8,128)(2,1)S(1)}, u32[]{:S(2)}, u32[]{:S(2)}) collective-permute-start(bf16[72,2048]{1,0:T(8,128)(2,1)} %get-tuple-element.166), channel_id=1, source_target_pairs={{0,12},{4,8},{8,4},{12,0},{1,13},{5,9},{9,5},{13,1},{2,14},{6,10},... | collective-permute-start | bytes 884744 | tf_op jit(solution)/shard_map/ppermute | solution.py:128
  13.0 67.5 %collective-permute-start.1 = (bf16[512,768]{1,0:T(8,128)(2,1)}, bf16[512,768]{1,0:T(8,128)(2,1)}, u32[]{:S(2)}, u32[]{:S(2)}) collective-permute-start(bf16[512,768]{1,0:T(8,128)(2,1)} %bitcast.25), channel_id=1, source_target_pairs={{0,16},{16,0},{1,17},{17,1},{2,18},{18,2},{3,19},{19,3},{4,20},{20... | collective-permute-start | bytes 2359304 | tf_op jit(solution)/shard_map/ppermute | solution.py:856
  20.0 65.9 %collective-permute-start = (bf16[4,3,192,512]{3,2,0,1:T(8,128)(2,1)}, bf16[4,3,192,512]{3,2,0,1:T(8,128)(2,1)}, u32[]{:S(2)}, u32[]{:S(2)}) collective-permute-start(bf16[4,3,192,512]{3,2,0,1:T(8,128)(2,1)} %dynamic-slice_bitcast_fusion), channel_id=1, source_target_pairs={{0,16},{16,0},{1,17},{17,1},{2,18},{18,2},{3,19},{19,3},{4,20},{20... | collective-permute-start | bytes 7077896 | tf_op jit(solution)/shard_map/ppermute | solution.py:856
  170.4 196.8 %collective-permute-start.17 = (bf16[512,768]{1,0:T(8,128)(2,1)}, bf16[512,768]{1,0:T(8,128)(2,1)}, u32[]{:S(2)}, u32[]{:S(2)}) collective-permute-start(bf16[512,768]{1,0:T(8,128)(2,1)} %get-tuple-element.41), channel_id=1, source_target_pairs={{0,4},{4,0},{8,12},{12,8},{1,5},{5,1},{9,13},{13,9},{2,6},{6,2},{1... | collective-permute-start | bytes 2359304 | tf_op jit(solution)/shard_map/ppermute | solution.py:128
  170.5 200.3 %collective-permute-start.18 = (bf16[512,768]{1,0:T(8,128)(2,1)}, bf16[512,768]{1,0:T(8,128)(2,1)}, u32[]{:S(2)}, u32[]{:S(2)}) collective-permute-start(bf16[512,768]{1,0:T(8,128)(2,1)} %get-tuple-element.41), channel_id=1, source_target_pairs={{0,8},{4,12},{8,0},{12,4},{1,9},{5,13},{9,1},{13,5},{2,10},{6,14},... | collective-permute-start | bytes 2359304 | tf_op jit(solution)/shard_map/ppermute | solution.py:128
  171.6 202.0 %collective-permute-start.19 = (bf16[512,768]{1,0:T(8,128)(2,1)}, bf16[512,768]{1,0:T(8,128)(2,1)}, u32[]{:S(2)}, u32[]{:S(2)}) collective-permute-start(bf16[512,768]{1,0:T(8,128)(2,1)} %get-tuple-element.41), channel_id=1, source_target_pairs={{0,12},{4,8},{8,4},{12,0},{1,13},{5,9},{9,5},{13,1},{2,14},{6,10},... | collective-permute-start | bytes 2359304 | tf_op jit(solution)/shard_map/ppermute | solution.py:128
  279.5 48.3 %collective-permute-start.11 = (bf16[1,192,512]{2,1,0:T(8,128)(2,1)S(1)}, bf16[1,192,512]{2,1,0:T(8,128)(2,1)S(1)}, u32[]{:S(2)}, u32[]{:S(2)}) collective-permute-start(bf16[1,192,512]{2,1,0:T(8,128)(2,1)S(1)} %get-tuple-element.264), channel_id=1, source_target_pairs={{0,4},{4,0},{8,12},{12,8},{1,5},{5,1},{9,13},{13,9},{2,6},{6,2},{1... | collective-permute-start | bytes 589832 | tf_op jit(solution)/shard_map/ppermute | solution.py:116
  279.6 57.0 %collective-permute-start.12 = (bf16[1,192,512]{2,1,0:T(8,128)(2,1)S(1)}, bf16[1,192,512]{2,1,0:T(8,128)(2,1)S(1)}, u32[]{:S(2)}, u32[]{:S(2)}) collective-permute-start(bf16[1,192,512]{2,1,0:T(8,128)(2,1)S(1)} %get-tuple-element.263), channel_id=1, source_target_pairs={{0,8},{4,12},{8,0},{12,4},{1,9},{5,13},{9,1},{13,5},{2,10},{6,14},... | collective-permute-start | bytes 589832 | tf_op jit(solution)/shard_map/ppermute | solution.py:116
  363.0 37.7 %collective-permute-start.3 = (bf16[192,2048]{1,0:T(8,128)(2,1)}, bf16[192,2048]{1,0:T(8,128)(2,1)}, u32[]{:S(2)}, u32[]{:S(2)}) collective-permute-start(bf16[192,2048]{1,0:T(8,128)(2,1)} %shard_map.255), channel_id=1, source_target_pairs={{0,2},{1,3},{2,0},{3,1},{4,6},{5,7},{6,4},{7,5},{8,10},{9,11},{10,... | collective-permute-start | bytes 2359304 | tf_op jit(solution)/shard_map/ppermute | solution.py:128
  370.9 95.7 %collective-permute-start.14 = (bf16[192,2048]{1,0:T(8,128)(2,1)}, bf16[192,2048]{1,0:T(8,128)(2,1)}, u32[]{:S(2)}, u32[]{:S(2)}) collective-permute-start(bf16[192,2048]{1,0:T(8,128)(2,1)} %bitcast.286), channel_id=1, source_target_pairs={{0,1},{1,0},{2,3},{3,2},{4,5},{5,4},{6,7},{7,6},{8,9},{9,8},{10,11... | collective-permute-start | bytes 2359304 | tf_op jit(solution)/shard_map/ppermute | solution.py:128
  373.6 97.3 %collective-permute-start.15 = (bf16[192,2048]{1,0:T(8,128)(2,1)}, bf16[192,2048]{1,0:T(8,128)(2,1)}, u32[]{:S(2)}, u32[]{:S(2)}) collective-permute-start(bf16[192,2048]{1,0:T(8,128)(2,1)} %bitcast.286), channel_id=1, source_target_pairs={{0,2},{1,3},{2,0},{3,1},{4,6},{5,7},{6,4},{7,5},{8,10},{9,11},{10,... | collective-permute-start | bytes 2359304 | tf_op jit(solution)/shard_map/ppermute | solution.py:128
  381.1 120.2 %collective-permute-start.16 = (bf16[192,2048]{1,0:T(8,128)(2,1)}, bf16[192,2048]{1,0:T(8,128)(2,1)}, u32[]{:S(2)}, u32[]{:S(2)}) collective-permute-start(bf16[192,2048]{1,0:T(8,128)(2,1)} %bitcast.286), channel_id=1, source_target_pairs={{0,3},{1,2},{2,1},{3,0},{4,7},{5,6},{6,5},{7,4},{8,11},{9,10},{10,... | collective-permute-start | bytes 2359304 | tf_op jit(solution)/shard_map/ppermute | solution.py:128
  470.9 176.6 %collective-permute-start.23 = (bf16[192,2048]{1,0:T(8,128)(2,1)}, bf16[192,2048]{1,0:T(8,128)(2,1)}, u32[]{:S(2)}, u32[]{:S(2)}) collective-permute-start(bf16[192,2048]{1,0:T(8,128)(2,1)} %bitcast.269), channel_id=1, source_target_pairs={{0,1},{1,0},{2,3},{3,2},{4,5},{5,4},{6,7},{7,6},{8,9},{9,8},{10,11... | collective-permute-start | bytes 2359304 | tf_op jit(solution)/shard_map/ppermute | solution.py:128
  473.1 177.5 %collective-permute-start.24 = (bf16[192,2048]{1,0:T(8,128)(2,1)}, bf16[192,2048]{1,0:T(8,128)(2,1)}, u32[]{:S(2)}, u32[]{:S(2)}) collective-permute-start(bf16[192,2048]{1,0:T(8,128)(2,1)} %bitcast.269), channel_id=1, source_target_pairs={{0,2},{1,3},{2,0},{3,1},{4,6},{5,7},{6,4},{7,5},{8,10},{9,11},{10,... | collective-permute-start | bytes 2359304 | tf_op jit(solution)/shard_map/ppermute | solution.py:128
  494.8 209.7 %collective-permute-start.25 = (bf16[192,2048]{1,0:T(8,128)(2,1)}, bf16[192,2048]{1,0:T(8,128)(2,1)}, u32[]{:S(2)}, u32[]{:S(2)}) collective-permute-start(bf16[192,2048]{1,0:T(8,128)(2,1)} %bitcast.269), channel_id=1, source_target_pairs={{0,3},{1,2},{2,1},{3,0},{4,7},{5,6},{6,5},{7,4},{8,11},{9,10},{10,... | collective-permute-start | bytes 2359304 | tf_op jit(solution)/shard_map/ppermute | solution.py:128
  497.3 155.7 %collective-permute-start.29 = (bf16[192,2048]{1,0:T(8,128)(2,1)}, bf16[192,2048]{1,0:T(8,128)(2,1)}, u32[]{:S(2)}, u32[]{:S(2)}) collective-permute-start(bf16[192,2048]{1,0:T(8,128)(2,1)} %bitcast.271), channel_id=1, source_target_pairs={{0,1},{1,0},{2,3},{3,2},{4,5},{5,4},{6,7},{7,6},{8,9},{9,8},{10,11... | collective-permute-start | bytes 2359304 | tf_op jit(solution)/shard_map/ppermute | solution.py:128
  501.3 153.9 %collective-permute-start.30 = (bf16[192,2048]{1,0:T(8,128)(2,1)}, bf16[192,2048]{1,0:T(8,128)(2,1)}, u32[]{:S(2)}, u32[]{:S(2)}) collective-permute-start(bf16[192,2048]{1,0:T(8,128)(2,1)} %bitcast.271), channel_id=1, source_target_pairs={{0,2},{1,3},{2,0},{3,1},{4,6},{5,7},{6,4},{7,5},{8,10},{9,11},{10,... | collective-permute-start | bytes 2359304 | tf_op jit(solution)/shard_map/ppermute | solution.py:128
  655.3 47.1 %collective-permute-start.37 = (bf16[192,2048]{1,0:T(8,128)(2,1)S(1)}, bf16[192,2048]{1,0:T(8,128)(2,1)S(1)}, u32[]{:S(2)}, u32[]{:S(2)}) collective-permute-start(bf16[192,2048]{1,0:T(8,128)(2,1)S(1)} %bitcast.708), channel_id=1, source_target_pairs={{0,3},{1,2},{2,1},{3,0},{4,7},{5,6},{6,5},{7,4},{8,11},{9,10},{10,... | collective-permute-start | bytes 2359304 | tf_op jit(solution)/shard_map/ppermute | solution.py:128
  966.8 168.5 %collective-permute-start.55 = (bf16[192,2048]{1,0:T(8,128)(2,1)}, bf16[192,2048]{1,0:T(8,128)(2,1)}, u32[]{:S(2)}, u32[]{:S(2)}) collective-permute-start(bf16[192,2048]{1,0:T(8,128)(2,1)} %get-tuple-element.179), channel_id=1, source_target_pairs={{0,1},{1,0},{2,3},{3,2},{4,5},{5,4},{6,7},{7,6},{8,9},{9,8},{10,11... | collective-permute-start | bytes 2359304 | tf_op jit(solution)/shard_map/ppermute | solution.py:139
  967.2 170.4 %collective-permute-start.56 = (bf16[192,2048]{1,0:T(8,128)(2,1)}, bf16[192,2048]{1,0:T(8,128)(2,1)}, u32[]{:S(2)}, u32[]{:S(2)}) collective-permute-start(bf16[192,2048]{1,0:T(8,128)(2,1)} %get-tuple-element.181), channel_id=1, source_target_pairs={{0,2},{1,3},{2,0},{3,1},{4,6},{5,7},{6,4},{7,5},{8,10},{9,11},{10,... | collective-permute-start | bytes 2359304 | tf_op jit(solution)/shard_map/ppermute | solution.py:139
  969.3 170.1 %collective-permute-start.57 = (bf16[192,2048]{1,0:T(8,128)(2,1)}, bf16[192,2048]{1,0:T(8,128)(2,1)}, u32[]{:S(2)}, u32[]{:S(2)}) collective-permute-start(bf16[192,2048]{1,0:T(8,128)(2,1)} %get-tuple-element.180), channel_id=1, source_target_pairs={{0,3},{1,2},{2,1},{3,0},{4,7},{5,6},{6,5},{7,4},{8,11},{9,10},{10,... | collective-permute-start | bytes 2359304 | tf_op jit(solution)/shard_map/ppermute | solution.py:139
  971.9 168.6 %collective-permute-start.52 = (bf16[192,2048]{1,0:T(8,128)(2,1)}, bf16[192,2048]{1,0:T(8,128)(2,1)}, u32[]{:S(2)}, u32[]{:S(2)}) collective-permute-start(bf16[192,2048]{1,0:T(8,128)(2,1)} %get-tuple-element.182), channel_id=1, source_target_pairs={{0,1},{1,0},{2,3},{3,2},{4,5},{5,4},{6,7},{7,6},{8,9},{9,8},{10,11... | collective-permute-start | bytes 2359304 | tf_op jit(solution)/shard_map/ppermute | solution.py:139
  972.3 170.3 %collective-permute-start.53 = (bf16[192,2048]{1,0:T(8,128)(2,1)}, bf16[192,2048]{1,0:T(8,128)(2,1)}, u32[]{:S(2)}, u32[]{:S(2)}) collective-permute-start(bf16[192,2048]{1,0:T(8,128)(2,1)} %get-tuple-element.184), channel_id=1, source_target_pairs={{0,2},{1,3},{2,0},{3,1},{4,6},{5,7},{6,4},{7,5},{8,10},{9,11},{10,... | collective-permute-start | bytes 2359304 | tf_op jit(solution)/shard_map/ppermute | solution.py:139
  1139.5 38.0 %collective-permute-start.50 = (bf16[192,2048]{1,0:T(8,128)(2,1)S(1)}, bf16[192,2048]{1,0:T(8,128)(2,1)S(1)}, u32[]{:S(2)}, u32[]{:S(2)}) collective-permute-start(bf16[192,2048]{1,0:T(8,128)(2,1)S(1)} %copy-done.153), channel_id=1, source_target_pairs={{0,2},{1,3},{2,0},{3,1},{4,6},{5,7},{6,4},{7,5},{8,10},{9,11},{10,... | collective-permute-start | bytes 2359304 | tf_op jit(solution)/shard_map/ppermute | solution.py:139
  1140.5 50.1 %collective-permute-start.51 = (bf16[192,2048]{1,0:T(8,128)(2,1)S(1)}, bf16[192,2048]{1,0:T(8,128)(2,1)S(1)}, u32[]{:S(2)}, u32[]{:S(2)}) collective-permute-start(bf16[192,2048]{1,0:T(8,128)(2,1)S(1)} %copy-done.152), channel_id=1, source_target_pairs={{0,3},{1,2},{2,1},{3,0},{4,7},{5,6},{6,5},{7,4},{8,11},{9,10},{10,... | collective-permute-start | bytes 2359304 | tf_op jit(solution)/shard_map/ppermute | solution.py:139
  1142.6 64.5 %collective-permute-start.67 = (bf16[192,2048]{1,0:T(8,128)(2,1)S(1)}, bf16[192,2048]{1,0:T(8,128)(2,1)}, u32[]{:S(2)}, u32[]{:S(2)}) collective-permute-start(bf16[192,2048]{1,0:T(8,128)(2,1)S(1)} %copy-done.151), channel_id=1, source_target_pairs={{0,1},{1,0},{2,3},{3,2},{4,5},{5,4},{6,7},{7,6},{8,9},{9,8},{10,11... | collective-permute-start | bytes 2359304 | tf_op jit(solution)/shard_map/ppermute | solution.py:139
  1156.8 64.8 %collective-permute-start.68 = (bf16[192,2048]{1,0:T(8,128)(2,1)}, bf16[192,2048]{1,0:T(8,128)(2,1)}, u32[]{:S(2)}, u32[]{:S(2)}) collective-permute-start(bf16[192,2048]{1,0:T(8,128)(2,1)} %get-tuple-element.190), channel_id=1, source_target_pairs={{0,2},{1,3},{2,0},{3,1},{4,6},{5,7},{6,4},{7,5},{8,10},{9,11},{10,... | collective-permute-start | bytes 2359304 | tf_op jit(solution)/shard_map/ppermute | solution.py:139
  1173.2 51.2 %collective-permute-start.69 = (bf16[192,2048]{1,0:T(8,128)(2,1)}, bf16[192,2048]{1,0:T(8,128)(2,1)}, u32[]{:S(2)}, u32[]{:S(2)}) collective-permute-start(bf16[192,2048]{1,0:T(8,128)(2,1)} %get-tuple-element.189), channel_id=1, source_target_pairs={{0,3},{1,2},{2,1},{3,0},{4,7},{5,6},{6,5},{7,4},{8,11},{9,10},{10,... | collective-permute-start | bytes 2359304 | tf_op jit(solution)/shard_map/ppermute | solution.py:139
  1177.5 63.4 %collective-permute-start.64 = (bf16[192,2048]{1,0:T(8,128)(2,1)}, bf16[192,2048]{1,0:T(8,128)(2,1)}, u32[]{:S(2)}, u32[]{:S(2)}) collective-permute-start(bf16[192,2048]{1,0:T(8,128)(2,1)} %get-tuple-element.191), channel_id=1, source_target_pairs={{0,1},{1,0},{2,3},{3,2},{4,5},{5,4},{6,7},{7,6},{8,9},{9,8},{10,11... | collective-permute-start | bytes 2359304 | tf_op jit(solution)/shard_map/ppermute | solution.py:139
  1190.5 51.5 %collective-permute-start.65 = (bf16[192,2048]{1,0:T(8,128)(2,1)}, bf16[192,2048]{1,0:T(8,128)(2,1)}, u32[]{:S(2)}, u32[]{:S(2)}) collective-permute-start(bf16[192,2048]{1,0:T(8,128)(2,1)} %get-tuple-element.193), channel_id=1, source_target_pairs={{0,2},{1,3},{2,0},{3,1},{4,6},{5,7},{6,4},{7,5},{8,10},{9,11},{10,... | collective-permute-start | bytes 2359304 | tf_op jit(solution)/shard_map/ppermute | solution.py:139
  1207.1 51.1 %collective-permute-start.66 = (bf16[192,2048]{1,0:T(8,128)(2,1)}, bf16[192,2048]{1,0:T(8,128)(2,1)}, u32[]{:S(2)}, u32[]{:S(2)}) collective-permute-start(bf16[192,2048]{1,0:T(8,128)(2,1)} %get-tuple-element.192), channel_id=1, source_target_pairs={{0,3},{1,2},{2,1},{3,0},{4,7},{5,6},{6,5},{7,4},{8,11},{9,10},{10,... | collective-permute-start | bytes 2359304 | tf_op jit(solution)/shard_map/ppermute | solution.py:139
  1221.6 52.8 %collective-permute-start.61 = (bf16[192,2048]{1,0:T(8,128)(2,1)}, bf16[192,2048]{1,0:T(8,128)(2,1)S(1)}, u32[]{:S(2)}, u32[]{:S(2)}) collective-permute-start(bf16[192,2048]{1,0:T(8,128)(2,1)} %get-tuple-element.194), channel_id=1, source_target_pairs={{0,1},{1,0},{2,3},{3,2},{4,5},{5,4},{6,7},{7,6},{8,9},{9,8},{10,11... | collective-permute-start | bytes 2359304 | tf_op jit(solution)/shard_map/ppermute | solution.py:139
  1224.4 58.2 %collective-permute-start.62 = (bf16[192,2048]{1,0:T(8,128)(2,1)}, bf16[192,2048]{1,0:T(8,128)(2,1)S(1)}, u32[]{:S(2)}, u32[]{:S(2)}) collective-permute-start(bf16[192,2048]{1,0:T(8,128)(2,1)} %get-tuple-element.196), channel_id=1, source_target_pairs={{0,2},{1,3},{2,0},{3,1},{4,6},{5,7},{6,4},{7,5},{8,10},{9,11},{10,... | collective-permute-start | bytes 2359304 | tf_op jit(solution)/shard_map/ppermute | solution.py:139
  1240.8 49.9 %collective-permute-start.63 = (bf16[192,2048]{1,0:T(8,128)(2,1)S(1)}, bf16[192,2048]{1,0:T(8,128)(2,1)S(1)}, u32[]{:S(2)}, u32[]{:S(2)}) collective-permute-start(bf16[192,2048]{1,0:T(8,128)(2,1)S(1)} %copy-done.156), channel_id=1, source_target_pairs={{0,3},{1,2},{2,1},{3,0},{4,7},{5,6},{6,5},{7,4},{8,11},{9,10},{10,... | collective-permute-start | bytes 2359304 | tf_op jit(solution)/shard_map/ppermute | solution.py:139
  1242.0 53.0 %collective-permute-start.45 = (bf16[512,768]{1,0:T(8,128)(2,1)S(1)}, bf16[512,768]{1,0:T(8,128)(2,1)S(1)}, u32[]{:S(2)}, u32[]{:S(2)}) collective-permute-start(bf16[512,768]{1,0:T(8,128)(2,1)S(1)} %copy-done.150), channel_id=1, source_target_pairs={{0,4},{4,0},{8,12},{12,8},{1,5},{5,1},{9,13},{13,9},{2,6},{6,2},{1... | collective-permute-start | bytes 2359304 | tf_op jit(solution)/shard_map/ppermute | solution.py:139
  1258.1 73.5 %collective-permute-start.46 = (bf16[512,768]{1,0:T(8,128)(2,1)}, bf16[512,768]{1,0:T(8,128)(2,1)}, u32[]{:S(2)}, u32[]{:S(2)}) collective-permute-start(bf16[512,768]{1,0:T(8,128)(2,1)} %get-tuple-element.199), channel_id=1, source_target_pairs={{0,8},{4,12},{8,0},{12,4},{1,9},{5,13},{9,1},{13,5},{2,10},{6,14},... | collective-permute-start | bytes 2359304 | tf_op jit(solution)/shard_map/ppermute | solution.py:139
  1274.5 57.9 %collective-permute-start.47 = (bf16[512,768]{1,0:T(8,128)(2,1)}, bf16[512,768]{1,0:T(8,128)(2,1)}, u32[]{:S(2)}, u32[]{:S(2)}) collective-permute-start(bf16[512,768]{1,0:T(8,128)(2,1)} %get-tuple-element.198), channel_id=1, source_target_pairs={{0,12},{4,8},{8,4},{12,0},{1,13},{5,9},{9,5},{13,1},{2,14},{6,10},... | collective-permute-start | bytes 2359304 | tf_op jit(solution)/shard_map/ppermute | solution.py:139
  1282.6 86.9 %collective-permute-start.42 = (bf16[512,768]{1,0:T(8,128)(2,1)}, bf16[512,768]{1,0:T(8,128)(2,1)}, u32[]{:S(2)}, u32[]{:S(2)}) collective-permute-start(bf16[512,768]{1,0:T(8,128)(2,1)} %get-tuple-element.200), channel_id=1, source_target_pairs={{0,4},{4,0},{8,12},{12,8},{1,5},{5,1},{9,13},{13,9},{2,6},{6,2},{1... | collective-permute-start | bytes 2359304 | tf_op jit(solution)/shard_map/ppermute | solution.py:139
  1290.7 115.6 %collective-permute-start.43 = (bf16[512,768]{1,0:T(8,128)(2,1)}, bf16[512,768]{1,0:T(8,128)(2,1)}, u32[]{:S(2)}, u32[]{:S(2)}) collective-permute-start(bf16[512,768]{1,0:T(8,128)(2,1)} %get-tuple-element.202), channel_id=1, source_target_pairs={{0,8},{4,12},{8,0},{12,4},{1,9},{5,13},{9,1},{13,5},{2,10},{6,14},... | collective-permute-start | bytes 2359304 | tf_op jit(solution)/shard_map/ppermute | solution.py:139
  1295.9 113.8 %collective-permute-start.44 = (bf16[512,768]{1,0:T(8,128)(2,1)}, bf16[512,768]{1,0:T(8,128)(2,1)}, u32[]{:S(2)}, u32[]{:S(2)}) collective-permute-start(bf16[512,768]{1,0:T(8,128)(2,1)} %get-tuple-element.201), channel_id=1, source_target_pairs={{0,12},{4,8},{8,4},{12,0},{1,13},{5,9},{9,5},{13,1},{2,14},{6,10},... | collective-permute-start | bytes 2359304 | tf_op jit(solution)/shard_map/ppermute | solution.py:139
  1332.4 101.2 %collective-permute-start.58 = (bf16[1,3,192,512]{3,2,0,1:T(8,128)(2,1)S(1)}, bf16[1,3,192,512]{3,2,0,1:T(8,128)(2,1)S(1)}, u32[]{:S(2)}, u32[]{:S(2)}) collective-permute-start(bf16[1,3,192,512]{3,2,0,1:T(8,128)(2,1)S(1)} %bitcast.713), channel_id=1, source_target_pairs={{0,4},{4,0},{8,12},{12,8},{1,5},{5,1},{9,13},{13,9},{2,6},{6,2},{1... | collective-permute-start | bytes 1769480 | tf_op jit(solution)/shard_map/ppermute | solution.py:116
  1332.6 128.5 %collective-permute-start.59 = (bf16[1,3,192,512]{3,2,0,1:T(8,128)(2,1)S(1)}, bf16[1,3,192,512]{3,2,0,1:T(8,128)(2,1)S(1)}, u32[]{:S(2)}, u32[]{:S(2)}) collective-permute-start(bf16[1,3,192,512]{3,2,0,1:T(8,128)(2,1)S(1)} %bitcast.710), channel_id=1, source_target_pairs={{0,8},{4,12},{8,0},{12,4},{1,9},{5,13},{9,1},{13,5},{2,10},{6,14},... | collective-permute-start | bytes 1769480 | tf_op jit(solution)/shard_map/ppermute | solution.py:116
  1369.5 91.6 %collective-permute-start.60 = (bf16[1,3,192,512]{3,2,0,1:T(8,128)(2,1)S(1)}, bf16[1,3,192,512]{3,2,0,1:T(8,128)(2,1)S(1)}, u32[]{:S(2)}, u32[]{:S(2)}) collective-permute-start(bf16[1,3,192,512]{3,2,0,1:T(8,128)(2,1)S(1)} %bitcast.709), channel_id=1, source_target_pairs={{0,12},{4,8},{8,4},{12,0},{1,13},{5,9},{9,5},{13,1},{2,14},{6,10},... | collective-permute-start | bytes 1769480 | tf_op jit(solution)/shard_map/ppermute | solution.py:116
  1406.3 54.9 %collective-permute-start.70 = (bf16[1,3,192,512]{3,2,0,1:T(8,128)(2,1)S(1)}, bf16[1,3,192,512]{3,2,0,1:T(8,128)(2,1)S(1)}, u32[]{:S(2)}, u32[]{:S(2)}) collective-permute-start(bf16[1,3,192,512]{3,2,0,1:T(8,128)(2,1)S(1)} %bitcast.712), channel_id=1, source_target_pairs={{0,4},{4,0},{8,12},{12,8},{1,5},{5,1},{9,13},{13,9},{2,6},{6,2},{1... | collective-permute-start | bytes 1769480 | tf_op jit(solution)/shard_map/ppermute | solution.py:116
  1409.7 76.6 %collective-permute-start.71 = (bf16[1,3,192,512]{3,2,0,1:T(8,128)(2,1)S(1)}, bf16[1,3,192,512]{3,2,0,1:T(8,128)(2,1)S(1)}, u32[]{:S(2)}, u32[]{:S(2)}) collective-permute-start(bf16[1,3,192,512]{3,2,0,1:T(8,128)(2,1)S(1)} %bitcast.711), channel_id=1, source_target_pairs={{0,8},{4,12},{8,0},{12,4},{1,9},{5,13},{9,1},{13,5},{2,10},{6,14},... | collective-permute-start | bytes 1769480 | tf_op jit(solution)/shard_map/ppermute | solution.py:116
  1433.6 52.8 %collective-permute-start.72 = (bf16[1,3,192,512]{3,2,0,1:T(8,128)(2,1)S(1)}, bf16[1,3,192,512]{3,2,0,1:T(8,128)(2,1)S(1)}, u32[]{:S(2)}, u32[]{:S(2)}) collective-permute-start(bf16[1,3,192,512]{3,2,0,1:T(8,128)(2,1)S(1)} %bitcast.714), channel_id=1, source_target_pairs={{0,12},{4,8},{8,4},{12,0},{1,13},{5,9},{9,5},{13,1},{2,14},{6,10},... | collective-permute-start | bytes 1769480 | tf_op jit(solution)/shard_map/ppermute | solution.py:116
  (252 other events, 5379.2 us)

commit v5 on v2

--- a/solution.py
+++ b/solution.py
@@ -3,6 +3,8 @@
 import jax
 import jax.numpy as jnp
 from jax import lax
+from jax.experimental import pallas as pl
+from jax.experimental.pallas import tpu as pltpu
 from jax.sharding import PartitionSpec as P
 
 HD = 128
@@ -123,32 +125,858 @@
     return jnp.where(allowed[:, None], raw_scores, MASKED)
 
 
-def gather_kv(own):
-    return lax.all_gather(own, "dp", axis=1, tiled=True)
-
-
-def scatter_kv(whole):
-    return lax.psum_scatter(whole, "dp", scatter_dimension=1, tiled=True)
-
-
-def scatter_attn(whole):
-    mine = lax.psum_scatter(whole, "section", scatter_dimension=0, tiled=True)
-    return lax.psum_scatter(mine, "tensor", scatter_dimension=1, tiled=True)[0]
-
-
-def gather_rows(own):
-    mine = lax.all_gather(own, "tensor", axis=0, tiled=True)
-    return lax.all_gather(mine, "section", axis=0)
-
-
-def gather_mlp(own):
-    mine = lax.all_gather(own, "dp", axis=0, tiled=True)
-    return lax.all_gather(mine, "section", axis=0, tiled=True)
-
-
-def scatter_mlp(whole):
-    mine = lax.psum_scatter(whole, "section", scatter_dimension=0, tiled=True)
-    return lax.psum_scatter(mine, "dp", scatter_dimension=0, tiled=True)
+MESH = pl.DeviceIdType.MESH
+CHUNK = 256
+SEM = pltpu.SemaphoreType.DMA
+VMEM = pl.BlockSpec(memory_space=pltpu.VMEM)
+HBM = pl.BlockSpec(memory_space=pl.ANY)
+
+
+def remote(src, dst, send_sem, recv_sem, device_id):
+    return pltpu.make_async_remote_copy(
+        src_ref=src, dst_ref=dst, send_sem=send_sem, recv_sem=recv_sem,
+        device_id=device_id, device_id_type=MESH,
+    )
+
+
+def greet(axes, across):
+    barrier = pltpu.get_barrier_semaphore()
+    count = 0
+    for axis in axes:
+        size = lax.axis_size(axis)
+        me = lax.axis_index(axis)
+        for step in range(1, size):
+            pl.semaphore_signal(
+                barrier, inc=1, device_id={axis: lax.rem(me + step, size)}, device_id_type=MESH
+            )
+        count += size - 1
+    if across:
+        size = lax.axis_size("dp")
+        me = lax.axis_index("dp")
+        sibling = 1 - lax.axis_index("section")
+        for step in range(1, size):
+            pl.semaphore_signal(
+                barrier, inc=1, device_id={"section": sibling, "dp": lax.rem(me + step, size)},
+                device_id_type=MESH,
+            )
+        count += size - 1
+    pl.semaphore_wait(barrier, count)
+
+
+class Part:
+    ins, outs, scratch = (), (), ()
+
+    def bind(self, ins, outs, scratch):
+        self.in_refs, self.out_refs, self.refs = ins, outs, scratch
+
+    def prepare(self):
+        pass
+
+    def start(self):
+        pass
+
+    def run(self):
+        pass
+
+    def finish(self):
+        pass
+
+
+def fused(parts, axes, across, collective_id, cost_us):
+    counts = [(len(part.ins), len(part.outs), len(part.scratch)) for part in parts]
+
+    def kernel(*refs):
+        refs = list(refs)
+        groups = []
+        for kind in range(3):
+            groups.append([])
+            for count in counts:
+                groups[kind].append(refs[: count[kind]])
+                del refs[: count[kind]]
+        for part, ins, outs, scratch in zip(parts, *groups):
+            part.bind(ins, outs, scratch)
+        for part in parts:
+            part.prepare()
+        greet(axes, across)
+        for part in parts:
+            part.start()
+        for part in parts:
+            part.run()
+        for part in parts:
+            part.finish()
+
+    ins = [item for part in parts for item in part.ins]
+    outs = [item for part in parts for item in part.outs]
+    results = pl.pallas_call(
+        kernel,
+        out_shape=[item[0] for item in outs],
+        in_specs=[item[1] for item in ins],
+        out_specs=[item[1] for item in outs],
+        scratch_shapes=[item for part in parts for item in part.scratch],
+        cost_estimate=pl.CostEstimate(
+            flops=0, bytes_accessed=cost_us * 3_000_000, transcendentals=0
+        ),
+        compiler_params=pltpu.CompilerParams(
+            collective_id=collective_id, has_side_effects=True, vmem_limit_bytes=40 << 20
+        ),
+    )(*[item[0] for item in ins])
+    results = list(results)
+    split = []
+    for count in counts:
+        split.append(results[: count[1]])
+        del results[: count[1]]
+    return split
+
+
+def columns_of(place, width):
+    return pl.ds(pl.multiple_of(place * width, width), width)
+
+
+class UnitsOut(Part):
+    def __init__(self, pieces, layer):
+        self.layer = layer
+        cores, self.size, mats, share, self.width = pieces.shape
+        self.ins = [(pieces, HBM)]
+        shape = jax.ShapeDtypeStruct((mats, share, self.size * self.width), BF16)
+        self.outs = [(shape, HBM)]
+        self.scratch = [SEM, SEM((cores, self.size)), SEM((self.size,))]
+
+    def bind(self, ins, outs, scratch):
+        (self.src,), (self.dst,), (self.keep, self.send, self.recv) = ins, outs, scratch
+        self.core, self.me = lax.axis_index("section"), lax.axis_index("dp")
+
+    def lands(self, slot):
+        return self.dst.at[:, :, columns_of(slot, self.width)]
+
+    def copy(self, core, place, slot):
+        return remote(
+            self.src.at[core, place], self.lands(slot), self.send.at[core, place],
+            self.recv.at[slot], {"section": core, "dp": place},
+        )
+
+    def local(self):
+        return pltpu.make_async_copy(self.src.at[self.layer, self.me], self.lands(self.me), self.keep)
+
+    def targets(self):
+        for core in range(2):
+            for place in range(self.size):
+                yield core, place, (place != self.me) | (core != self.layer)
+
+    def start(self):
+        @pl.when(self.core == self.layer)
+        def _():
+            for core, place, is_other in self.targets():
+                @pl.when(is_other)
+                def _():
+                    self.copy(core, place, self.me).start()
+
+            self.local().start()
+
+    def finish(self):
+        for place in range(self.size):
+            @pl.when((self.core != self.layer) | (place != self.me))
+            def _():
+                self.copy(0, 0, place).wait_recv()
+
+        @pl.when(self.core == self.layer)
+        def _():
+            for core, place, is_other in self.targets():
+                @pl.when(is_other)
+                def _():
+                    self.copy(core, place, self.me).wait_send()
+
+            self.local().wait()
+
+
+class UnitsHome(Part):
+    def __init__(self, rows, layer):
+        self.layer = layer
+        self.size = lax.axis_size("dp")
+        mats, share, depth = rows.shape
+        self.width = depth // self.size
+        self.ins = [(rows, HBM)]
+        shape = jax.ShapeDtypeStruct((mats, 2, self.size, share, self.width), BF16)
+        self.outs = [(shape, HBM)]
+        self.scratch = [SEM, SEM((self.size,)), SEM((2, self.size))]
+
+    def bind(self, ins, outs, scratch):
+        (self.src,), (self.dst,), (self.keep, self.send, self.recv) = ins, outs, scratch
+        self.core, self.me = lax.axis_index("section"), lax.axis_index("dp")
+
+    def copy(self, place, core, slot):
+        return remote(
+            self.src.at[:, :, columns_of(place, self.width)], self.dst.at[:, core, slot],
+            self.send.at[place], self.recv.at[core, slot], {"section": self.layer, "dp": place},
+        )
+
+    def local(self):
+        return pltpu.make_async_copy(
+            self.src.at[:, :, columns_of(self.me, self.width)],
+            self.dst.at[:, self.layer, self.me], self.keep,
+        )
+
+    def start(self):
+        for place in range(self.size):
+            @pl.when((self.core != self.layer) | (place != self.me))
+            def _():
+                self.copy(place, self.core, self.me).start()
+
+        @pl.when(self.core == self.layer)
+        def _():
+            self.local().start()
+
+    def finish(self):
+        @pl.when(self.core == self.layer)
+        def _():
+            for core in range(2):
+                for place in range(self.size):
+                    @pl.when((core != self.layer) | (place != self.me))
+                    def _():
+                        self.copy(0, core, place).wait_recv()
+
+            self.local().wait()
+
+        for place in range(self.size):
+            @pl.when((self.core != self.layer) | (place != self.me))
+            def _():
+                self.copy(place, self.core, self.me).wait_send()
+
+
+class SharedRows(Part):
+    def __init__(self, own):
+        self.size = lax.axis_size("dp")
+        self.ins = [(own, VMEM)]
+        self.outs = [(jax.ShapeDtypeStruct((2, self.size) + own.shape, F32), VMEM)]
+        self.scratch = [SEM((2, self.size)), SEM((2, self.size))]
+
+    def copy(self, core, place, from_core, from_place):
+        return remote(
+            self.in_refs[0], self.out_refs[0].at[from_core, from_place],
+            self.refs[0].at[core, place], self.refs[1].at[from_core, from_place],
+            {"section": core, "dp": place},
+        )
+
+    def others(self):
+        core, me = lax.axis_index("section"), lax.axis_index("dp")
+        for other in range(2):
+            for place in range(self.size):
+                yield other, place, (other != core) | (place != me)
+
+    def start(self):
+        core, me = lax.axis_index("section"), lax.axis_index("dp")
+        for other, place, is_other in self.others():
+            @pl.when(is_other)
+            def _():
+                self.copy(other, place, core, me).start()
+
+        self.out_refs[0][core, me] = self.in_refs[0][...]
+
+    def finish(self):
+        core, me = lax.axis_index("section"), lax.axis_index("dp")
+        for other, place, is_other in self.others():
+            @pl.when(is_other)
+            def _():
+                self.copy(other, place, other, place).wait_recv()
+                self.copy(other, place, core, me).wait_send()
+
+
+def far_pair(place, me):
+    return (place + me == 3) & ((place == 0) | (place == 3))
+
+
+def line_relays(size):
+    return [(2, 0, 3), (1, 3, 0)] if size == 4 else []
+
+
+def line_order(size):
+    return [1, 2, 0, 3] if size == 4 else list(range(size))
+
+
+class AttnOut(Part):
+    def __init__(self, halves, layer):
+        self.layer = layer
+        self.size = lax.axis_size("dp")
+        self.chunks = halves.shape[1]
+        self.ins = [(halves, HBM)]
+        self.outs = [(jax.ShapeDtypeStruct((self.size,) + halves.shape[1:], BF16), HBM)]
+        self.scratch = [
+            SEM, SEM((2, self.size, self.chunks)), SEM((self.size, self.chunks)), SEM((self.chunks,)),
+        ]
+
+    def bind(self, ins, outs, scratch):
+        (self.src,), (self.dst,) = ins, outs
+        self.keep, self.send, self.recv, self.relay_send = scratch
+        self.core, self.me = lax.axis_index("section"), lax.axis_index("dp")
+
+    def copy(self, core, place, slot, chunk):
+        return remote(
+            self.src.at[core, chunk], self.dst.at[slot, chunk], self.send.at[core, place, chunk],
+            self.recv.at[slot, chunk], {"section": core, "dp": place},
+        )
+
+    def relay(self, source, target, chunk):
+        return remote(
+            self.dst.at[source, chunk], self.dst.at[source, chunk], self.relay_send.at[chunk],
+            self.recv.at[source, chunk], {"dp": target},
+        )
+
+    def local(self):
+        return pltpu.make_async_copy(self.src.at[self.layer], self.dst.at[self.me], self.keep)
+
+    def targets(self):
+        for chunk in range(self.chunks):
+            for core in range(2):
+                for place in range(self.size):
+                    sent = (place != self.me) | (core != self.layer)
+                    if self.size == 4:
+                        sent = sent & jnp.logical_not(far_pair(place, self.me))
+                    yield core, place, chunk, sent
+
+    def start(self):
+        @pl.when(self.core == self.layer)
+        def _():
+            for core, place, chunk, sent in self.targets():
+                @pl.when(sent)
+                def _():
+                    self.copy(core, place, self.me, chunk).start()
+
+            self.local().start()
+
+    def run(self):
+        for chunk in range(self.chunks):
+            for place in line_order(self.size):
+                @pl.when((self.core != self.layer) | (place != self.me))
+                def _():
+                    self.copy(0, 0, place, chunk).wait_recv()
+
+                for via, source, target in line_relays(self.size):
+                    if source == place:
+                        @pl.when(self.me == via)
+                        def _():
+                            self.relay(source, target, chunk).start()
+
+    def finish(self):
+        @pl.when(self.core == self.layer)
+        def _():
+            for core, place, chunk, sent in self.targets():
+                @pl.when(sent)
+                def _():
+                    self.copy(core, place, self.me, chunk).wait_send()
+
+            self.local().wait()
+
+        for via, source, target in line_relays(self.size):
+            @pl.when(self.me == via)
+            def _():
+                for chunk in range(self.chunks):
+                    self.relay(source, target, chunk).wait_send()
+
+
+class HalfOver(Part):
+    def __init__(self, halves):
+        self.ins = [(halves, HBM)]
+        self.outs = [(jax.ShapeDtypeStruct(halves.shape[1:], BF16), HBM)]
+        self.scratch = [SEM, SEM, SEM]
+
+    def start(self):
+        self.over = remote(
+            self.in_refs[0].at[0], self.out_refs[0], self.refs[0], self.refs[1], {"section": 0}
+        )
+        self.keep = pltpu.make_async_copy(self.in_refs[0].at[1], self.out_refs[0], self.refs[2])
+
+        @pl.when(lax.axis_index("section") == 1)
+        def _():
+            self.over.start()
+            self.keep.start()
+
+    def finish(self):
+        @pl.when(lax.axis_index("section") == 1)
+        def _():
+            self.over.wait_send()
+            self.keep.wait()
+
+        @pl.when(lax.axis_index("section") == 0)
+        def _():
+            self.over.wait_recv()
+
+
+class Swap(Part):
+    def __init__(self, own):
+        self.ins = [(own, HBM)]
+        self.outs = [(jax.ShapeDtypeStruct(own.shape, own.dtype), HBM)]
+        self.scratch = [SEM, SEM]
+
+    def start(self):
+        sibling = 1 - lax.axis_index("section")
+        self.copy = remote(
+            self.in_refs[0], self.out_refs[0], self.refs[0], self.refs[1], {"section": sibling}
+        )
+        self.copy.start()
+
+    def finish(self):
+        self.copy.wait()
+
+
+class GatherKV(Part):
+    def __init__(self, own):
+        trees, rows, width = own.shape
+        self.trees, self.size = trees, lax.axis_size("dp")
+        self.ins = [(own, VMEM)]
+        self.outs = [(jax.ShapeDtypeStruct((trees, self.size, rows, width), BF16), VMEM)]
+        self.scratch = [SEM((self.size, trees)), SEM((self.size, trees)), SEM((trees,))]
+
+    def bind(self, ins, outs, scratch):
+        (self.own,), (self.out,) = ins, outs
+        self.send, self.recv, self.relay_send = scratch
+        self.me = lax.axis_index("dp")
+
+    def copy(self, place, slot, tree):
+        return remote(
+            self.own.at[tree], self.out.at[tree, slot], self.send.at[place, tree],
+            self.recv.at[slot, tree], {"dp": place},
+        )
+
+    def relay(self, source, target, tree):
+        return remote(
+            self.out.at[tree, source], self.out.at[tree, source], self.relay_send.at[tree],
+            self.recv.at[source, tree], {"dp": target},
+        )
+
+    def targets(self):
+        for tree in range(self.trees):
+            for place in range(self.size):
+                sent = place != self.me
+                if self.size == 4:
+                    sent = sent & jnp.logical_not(far_pair(place, self.me))
+                yield place, tree, sent
+
+    def start(self):
+        for place, tree, sent in self.targets():
+            @pl.when(sent)
+            def _():
+                self.copy(place, self.me, tree).start()
+
+        self.out[:, self.me] = self.own[...]
+
+    def run(self):
+        for tree in range(self.trees):
+            for place in line_order(self.size):
+                @pl.when(place != self.me)
+                def _():
+                    self.copy(place, place, tree).wait_recv()
+
+                for via, source, target in line_relays(self.size):
+                    if source == place:
+                        @pl.when(self.me == via)
+                        def _():
+                            self.relay(source, target, tree).start()
+
+    def finish(self):
+        for place, tree, sent in self.targets():
+            @pl.when(sent)
+            def _():
+                self.copy(place, self.me, tree).wait_send()
+
+        for via, source, target in line_relays(self.size):
+            @pl.when(self.me == via)
+            def _():
+                for tree in range(self.trees):
+                    self.relay(source, target, tree).wait_send()
+
+
+class ScatterKV(Part):
+    def __init__(self, whole):
+        trees, size, rows, width = whole.shape
+        self.trees, self.size = trees, size
+        self.sides = [(0, 1, 3), (3, 2, 0)] if size == 4 else []
+        self.ins = [(whole, VMEM)]
+        self.outs = [(jax.ShapeDtypeStruct((trees, rows, width), F32), VMEM)]
+        self.scratch = [
+            pltpu.VMEM((size, trees, rows, width), BF16), pltpu.VMEM((trees, rows, width), BF16),
+            SEM((size, trees)), SEM((size, trees)), SEM((trees,)), SEM((trees,)),
+        ]
+
+    def bind(self, ins, outs, scratch):
+        (self.terms,), (self.out,) = ins, outs
+        self.boxes, self.joint, self.send, self.recv, self.join_send, self.join_recv = scratch
+        self.me = lax.axis_index("dp")
+
+    def copy(self, place, slot, tree):
+        return remote(
+            self.terms.at[tree, place], self.boxes.at[slot, tree], self.send.at[place, tree],
+            self.recv.at[slot, tree], {"dp": place},
+        )
+
+    def by_way(self, via, target, tree):
+        return remote(
+            self.terms.at[tree, target], self.joint.at[tree], self.join_send.at[tree],
+            self.join_recv.at[tree], {"dp": via},
+        )
+
+    def joined(self, via, target, tree):
+        return remote(
+            self.joint.at[tree], self.boxes.at[via, tree], self.send.at[target, tree],
+            self.recv.at[via, tree], {"dp": target},
+        )
+
+    def plain(self, place):
+        ok = place != self.me
+        for source, via, target in self.sides:
+            if place == target:
+                ok = ok & (self.me != source) & (self.me != via)
+        return ok
+
+    def expected(self, place):
+        ok = place != self.me
+        for source, via, target in self.sides:
+            if place == source:
+                ok = ok & (self.me != target)
+        return ok
+
+    def start(self):
+        for tree in range(self.trees):
+            for source, via, target in self.sides:
+                @pl.when(self.me == source)
+                def _():
+                    self.by_way(via, target, tree).start()
+
+            for place in range(self.size):
+                @pl.when(self.plain(place))
+                def _():
+                    self.copy(place, self.me, tree).start()
+
+    def run(self):
+        for tree in range(self.trees):
+            for source, via, target in self.sides:
+                @pl.when(self.me == via)
+                def _():
+                    self.by_way(via, target, tree).wait_recv()
+                    both = self.joint[tree].astype(F32) + self.terms[tree, target].astype(F32)
+                    self.joint[tree] = both.astype(BF16)
+                    self.joined(via, target, tree).start()
+
+        for tree in range(self.trees):
+            self.out[tree] = self.terms[tree, self.me].astype(F32)
+            for place in line_order(self.size):
+                @pl.when(self.expected(place))
+                def _():
+                    self.copy(place, place, tree).wait_recv()
+                    self.out[tree] += self.boxes[place, tree].astype(F32)
+
+    def finish(self):
+        for tree in range(self.trees):
+            for place in range(self.size):
+                @pl.when(self.plain(place))
+                def _():
+                    self.copy(place, self.me, tree).wait_send()
+
+            for source, via, target in self.sides:
+                @pl.when(self.me == source)
+                def _():
+                    self.by_way(via, target, tree).wait_send()
+
+                @pl.when(self.me == via)
+                def _():
+                    self.joined(via, target, tree).wait_send()
+
+
+class TotalOverAll(Part):
+    axes = ("section", "tensor", "dp")
+
+    def __init__(self, own):
+        sizes = [lax.axis_size(axis) for axis in self.axes]
+        self.ins = [(own, VMEM)]
+        self.outs = [(jax.ShapeDtypeStruct(own.shape, F32), VMEM)]
+        self.scratch = [pltpu.VMEM((size,) + own.shape, F32) for size in sizes]
+        self.scratch += [SEM((size,)) for size in sizes] * 2
+
+    def run(self):
+        out = self.out_refs[0]
+        out[...] = self.in_refs[0][...]
+        for axis, box, send, recv in zip(self.axes, self.refs[:3], self.refs[3:6], self.refs[6:9]):
+            size, me = lax.axis_size(axis), lax.axis_index(axis)
+            box[me] = out[...]
+
+            def spread(place, slot):
+                return remote(box.at[me], box.at[slot], send.at[place], recv.at[slot], {axis: place})
+
+            for place in range(size):
+                @pl.when(place != me)
+                def _():
+                    spread(place, me).start()
+
+            for place in range(size):
+                @pl.when(place != me)
+                def _():
+                    spread(place, place).wait_recv()
+                    spread(place, me).wait_send()
+
+            total = box[0]
+            for place in range(1, size):
+                total += box[place]
+            out[...] = total
+
+
+class Hub(Part):
+    def __init__(self, terms, own_args, body, own_outs, scatter, gathers):
+        self.body, self.scatter, self.gathers = body, scatter, gathers
+        self.n_own = len(own_outs)
+        self.rows, depth = own_args[0].shape
+        rows, half = self.rows, depth // 2
+        self.half = half
+        self.sizes = [lax.axis_size(axis) for axis in gathers]
+        self.ins = [(arg, VMEM) for arg in own_args]
+        self.outs = [(jax.ShapeDtypeStruct(shape, F32), VMEM) for shape in own_outs]
+        self.outs += [
+            (jax.ShapeDtypeStruct((2, size * rows, depth), BF16), VMEM) for size in self.sizes
+        ]
+        self.scratch = []
+        if scatter:
+            self.ins = [(terms, VMEM)] + self.ins
+            size = self.size = lax.axis_size(scatter)
+            boxes = pltpu.VMEM((size, 2 * rows, half), BF16)
+            self.scratch += [boxes] * 4 + [pltpu.VMEM((2 * rows, half), F32)] + [SEM((size,))] * 4
+        for size in self.sizes:
+            self.scratch += [pltpu.VMEM((2, size, 2 * rows, half), BF16)] + [SEM((size,))] * 4
+
+    def bind(self, ins, outs, scratch):
+        self.own_outs, self.gathered = outs[: self.n_own], outs[self.n_own :]
+        self.core = lax.axis_index("section")
+        self.sibling = 1 - self.core
+        if self.scatter:
+            self.terms, *self.args = ins
+            self.to_sib, self.from_sib, self.to_peer, self.from_peer, self.total = scratch[:5]
+            self.sib_send, self.sib_recv, self.peer_send, self.peer_recv = scratch[5:9]
+            scratch = scratch[9:]
+            self.me = lax.axis_index(self.scatter)
+        else:
+            self.args = ins
+        self.boards = [scratch[5 * i : 5 * i + 5] for i in range(len(self.gathers))]
+
+    def packed(self, tree, place, at):
+        rows = self.rows
+        low = rows * place // 16 * 16
+        high = -(-rows * (place + 1) // 16) * 16
+        skip = rows * place - low
+        parts = [
+            self.terms[tree, low:high, pl.ds(side * self.half + at, CHUNK)].astype(F32)[
+                skip : skip + rows
+            ]
+            for side in range(2)
+        ]
+        return jnp.concatenate(parts, axis=0)
+
+    def over_columns(self, step_body):
+        @pl.loop(0, self.half // CHUNK)
+        def _(step):
+            step_body(pl.multiple_of(step * CHUNK, CHUNK))
+
+    def prepare(self):
+        if not self.scatter:
+            return
+        for place in range(self.size):
+            def pack(at):
+                self.to_sib[place, :, pl.ds(at, CHUNK)] = self.packed(
+                    self.sibling, place, at
+                ).astype(BF16)
+
+            self.over_columns(pack)
+
+    def sib_copy(self, place):
+        return remote(
+            self.to_sib.at[place], self.from_sib.at[place], self.sib_send.at[place],
+            self.sib_recv.at[place], {"section": self.sibling},
+        )
+
+    def peer_copy(self, place, slot):
+        return remote(
+            self.to_peer.at[place], self.from_peer.at[slot], self.peer_send.at[place],
+            self.peer_recv.at[slot], {self.scatter: place},
+        )
+
+    def spread(self, index, place, slot):
+        board, send, recv, _, _ = self.boards[index]
+        return remote(
+            board.at[self.core, slot], board.at[self.core, slot], send.at[place], recv.at[slot],
+            {self.gathers[index]: place},
+        )
+
+    def relay(self, index, tree, slot):
+        board, _, _, send, recv = self.boards[index]
+        return remote(
+            board.at[tree, slot], board.at[tree, slot], send.at[slot], recv.at[slot],
+            {"section": self.sibling},
+        )
+
+    def start(self):
+        if self.scatter:
+            for place in range(self.size):
+                self.sib_copy(place).start()
+
+    def summed(self):
+        for place in range(self.size):
+            self.sib_copy(place).wait_recv()
+
+            def add(at):
+                both = self.packed(self.core, place, at)
+                both += self.from_sib[place, :, pl.ds(at, CHUNK)].astype(F32)
+                self.to_peer[place, :, pl.ds(at, CHUNK)] = both.astype(BF16)
+
+                @pl.when(place == self.me)
+                def _():
+                    self.total[:, pl.ds(at, CHUNK)] = both
+
+            self.over_columns(add)
+
+            @pl.when(place != self.me)
+            def _():
+                self.peer_copy(place, self.me).start()
+
+        for place in range(self.size):
+            @pl.when(place != self.me)
+            def _():
+                self.peer_copy(place, place).wait_recv()
+                self.total[...] += self.from_peer[place].astype(F32)
+
+        total = self.total[...]
+        return jnp.concatenate([total[: self.rows], total[self.rows :]], axis=1)
+
+    def unpack(self, index, tree):
+        board, out, rows = self.boards[index][0], self.gathered[index], self.rows
+
+        def step_body(at):
+            blocks = [
+                board[tree, place, :, pl.ds(at, CHUNK)].astype(F32)
+                for place in range(self.sizes[index])
+            ]
+            for side in range(2):
+                whole = [block[side * rows : (side + 1) * rows] for block in blocks]
+                out[tree, :, pl.ds(side * self.half + at, CHUNK)] = jnp.concatenate(
+                    whole, axis=0
+                ).astype(BF16)
+
+        self.over_columns(step_body)
+
+    def run(self):
+        total = self.summed() if self.scatter else None
+        result = self.body(total, self.args, self.own_outs)
+        half = self.half
+        piece = jnp.concatenate([result[:, :half], result[:, half:]], axis=0).astype(BF16)
+        places = [lax.axis_index(axis) for axis in self.gathers]
+        for index, size in enumerate(self.sizes):
+            self.boards[index][0][self.core, places[index]] = piece
+            for place in range(size):
+                @pl.when(place != places[index])
+                def _():
+                    self.spread(index, place, places[index]).start()
+
+            self.relay(index, self.core, places[index]).start()
+
+        for index, size in enumerate(self.sizes):
+            for place in range(size):
+                @pl.when(place != places[index])
+                def _():
+                    self.spread(index, place, place).wait_recv()
+                    self.relay(index, self.core, place).start()
+
+        for index in range(len(self.sizes)):
+            self.unpack(index, self.core)
+        for index, size in enumerate(self.sizes):
+            for place in range(size):
+                self.relay(index, self.sibling, place).wait_recv()
+            self.unpack(index, self.sibling)
+
+    def finish(self):
+        if self.scatter:
+            for place in range(self.size):
+                self.sib_copy(place).wait_send()
+
+                @pl.when(place != self.me)
+                def _():
+                    self.peer_copy(place, self.me).wait_send()
+
+        for index, size in enumerate(self.sizes):
+            me = lax.axis_index(self.gathers[index])
+            for place in range(size):
+                self.relay(index, self.core, place).wait_send()
+
+                @pl.when(place != me)
+                def _():
+                    self.spread(index, place, me).wait_send()
+
+
+def hub_plain(terms, own_args, body, own_outs, scatter, gathers):
+    total = None
+    if scatter:
+        mine = lax.psum_scatter(terms, "section", scatter_dimension=0, tiled=True)
+        mine = lax.psum_scatter(mine, scatter, scatter_dimension=1, tiled=True)[0]
+        total = mine.astype(F32)
+
+    class Cell:
+        def __setitem__(self, _, value):
+            self.value = value
+
+    cells = [Cell() for _ in own_outs]
+    result = body(total, own_args, cells).astype(BF16)
+    gathered = [
+        lax.all_gather(lax.all_gather(result, axis, axis=0, tiled=True), "section", axis=0)
+        for axis in gathers
+    ]
+    return [cell.value for cell in cells] + gathered
+
+
+def gather_kv(own, cargo, fast, collective_id):
+    trees, rows, width = own.shape
+    if not fast:
+        return lax.all_gather(own, "dp", axis=1, tiled=True), []
+    whole, *outs = fused(
+        cargo + [GatherKV(own)], ["section", "dp"], bool(cargo), collective_id, 30
+    )[::-1]
+    return whole[0].reshape(trees, -1, width), outs[::-1]
+
+
+def scatter_kv(whole, cargo, fast, collective_id):
+    trees, all_rows, width = whole.shape
+    size = lax.axis_size("dp")
+    if not fast:
+        return lax.psum_scatter(whole, "dp", scatter_dimension=1, tiled=True).astype(F32), []
+    part = ScatterKV(whole.reshape(trees, size, all_rows // size, width))
+    total, *outs = fused(cargo + [part], ["section", "dp"], bool(cargo), collective_id, 30)[::-1]
+    return total[0], outs[::-1]
+
+
+def meet(terms, own_args, body, own_outs, scatter, gathers, cargo, fast, collective_id):
+    if not fast:
+        return hub_plain(terms, own_args, body, own_outs, scatter, gathers), []
+    axes = ["section"] + sorted(set(gathers) | {scatter} | ({"dp"} if cargo else set()))
+    part = Hub(terms, own_args, body, own_outs, scatter, gathers)
+    outs, *others = fused(cargo + [part], axes, bool(cargo), collective_id, 50)[::-1]
+    return outs, others[::-1]
+
+
+def norm_body(total, args, outs):
+    middle = args[0][...] + total
+    outs[0][...] = middle
+    mean_sq = jnp.mean(middle * middle, axis=1, keepdims=True)
+    return middle * lax.rsqrt(mean_sq + EPSILON) * args[1][...]
+
+
+def add_body(total, args, outs):
+    result = args[0][...] + total
+    outs[0][...] = result
+    return result
+
+
+def norm_back_body(total, args, outs):
+    values, gain = args[0][...], args[1][...]
+    scale = lax.rsqrt(jnp.mean(values * values, axis=1, keepdims=True) + EPSILON)
+    unit = values * scale
+    outs[1][...] = jnp.sum(total * unit, axis=0, keepdims=True)
+    scaled = total * gain
+    along = jnp.mean(scaled * unit, axis=1, keepdims=True)
+    result = (scaled - unit * along) * scale + args[2][...]
+    outs[0][...] = result
+    return result
 
 
 def embed(q_pre, k_pre, q_scale, k_scale, cos_table, sine_table):
@@ -160,9 +988,10 @@
     )
 
 
-def layer_forward(hidden_in, own_in, weights, gains, slot):
+def layer_forward(hidden_in, own_in, weights, gains, slot, cargo, fast, ids):
     attn_scale, mlp_scale, q_scale, k_scale = gains
     w_qkv, w_outt, w_gate, w_up, w_down = weights
+    carried = []
     allowed, cos_table, sine_table = slot
     trees, row_count, depth = hidden_in.shape
     q_width = w_outt.shape[1]
@@ -173,7 +1002,10 @@
     value_bf = qkv[:, :, q_width + HD :].astype(BF16)
     queries, keys_rot = embed(q_pre, k_pre, q_scale, k_scale, cos_table, sine_table)
     query_bf = queries.astype(BF16)
-    kv_all = gather_kv(jnp.concatenate([keys_rot.astype(BF16), value_bf], axis=2))
+    kv_all, outs = gather_kv(
+        jnp.concatenate([keys_rot.astype(BF16), value_bf], axis=2), cargo(0), fast, ids[0]
+    )
+    carried += outs
     key_all = kv_all[:, :, :HD]
     value_all = kv_all[:, :, HD:]
     scores = masked_scores(query_bf, key_all, allowed)
@@ -185,22 +1017,29 @@
     attended = jnp.einsum("bgrt,btd->brgd", prob_bf, value_all, preferred_element_type=F32)
     attended_bf = attended.reshape(trees * row_count, -1).astype(BF16)
     attn_partial = dot_inner(attended_bf, w_outt).astype(BF16).reshape(trees, row_count, depth)
-    middle = own_in + scatter_attn(attn_partial).astype(F32)
-    mlp_in = gather_mlp(rms_scale(middle, mlp_scale).astype(BF16))
+    own_shape = own_in.shape
+    (middle, mlp_in), outs = meet(
+        attn_partial, [own_in, mlp_scale[None]], norm_body, [own_shape], "tensor", ["dp"],
+        cargo(1), fast, ids[1],
+    )
+    carried += outs
+    mlp_in = mlp_in.reshape(-1, depth)
     gate_pre = dot_inner(mlp_in, w_gate)
     upward = dot_inner(mlp_in, w_up)
     hidden_bf = swiglu(gate_pre, upward).astype(BF16)
-    mlp_rows = scatter_mlp(dot(hidden_bf, w_down).astype(BF16))
-    output_own = (middle + mlp_rows.astype(F32)).astype(BF16)
-    output_bf = gather_rows(output_own)
+    mlp_partial = dot(hidden_bf, w_down).astype(BF16).reshape(trees, -1, depth)
+    (output_own, output_bf), outs = meet(
+        mlp_partial, [middle], add_body, [own_shape], "dp", ["tensor"], cargo(2), fast, ids[2]
+    )
+    carried += outs
     stored = (
         own_in, normed, q_pre, k_pre, query_bf, key_all, value_all, log_total, attended_bf,
         middle, mlp_in, gate_pre, upward, hidden_bf,
     )
-    return (output_bf, output_own.astype(F32), stored)
-
-
-def layer_backward(grad_own, stored, weights, gains, slot, shared_kv):
+    return (output_bf, output_own.astype(BF16).astype(F32), stored, carried)
+
+
+def layer_backward(grad_own, grad_mlp, stored, weights, gains, slot, shared_kv, is_first, cargo, fast, ids):
     attn_scale, mlp_scale, q_scale, k_scale = gains
     w_qkv, w_outt, w_gate, w_up, w_down = weights
     allowed, cos_table, sine_table = slot
@@ -210,17 +1049,19 @@
     ) = stored
     trees, row_count = query_bf.shape[:2]
     depth = normed.shape[1]
-    grad_mlp = gather_mlp(grad_own)
     grad_hidden = dot_inner(grad_mlp, w_down)
     _, swiglu_pull = jax.vjp(swiglu, gate_pre, upward)
     grad_gate, grad_upward = swiglu_pull(grad_hidden)
     gate_bf = grad_gate.astype(BF16)
     up_bf = grad_upward.astype(BF16)
-    mlp_rows = scatter_mlp((dot(gate_bf, w_gate) + dot(up_bf, w_up)).astype(BF16))
-    _, mlp_norm_pull = jax.vjp(rms_scale, middle, mlp_scale)
-    grad_middle, grad_mlp_scale = mlp_norm_pull(mlp_rows.astype(F32))
-    grad_middle = grad_middle + grad_own.astype(F32)
-    grad_attn = gather_rows(grad_middle.astype(BF16)).reshape(-1, depth)
+    mlp_partial = (dot(gate_bf, w_gate) + dot(up_bf, w_up)).astype(BF16)
+    own_outs = [own_in.shape, (1, depth)]
+    (grad_middle, grad_mlp_scale, grad_attn), carried = meet(
+        mlp_partial.reshape(trees, -1, depth),
+        [middle, mlp_scale[None], grad_own],
+        norm_back_body, own_outs, "dp", ["tensor"], cargo(0), fast, ids[0],
+    )
+    grad_attn = grad_attn.reshape(-1, depth)
     grad_heads = dot(grad_attn, w_outt).astype(BF16).reshape(query_bf.shape)
     scores = masked_scores(query_bf, key_all, allowed)
     prob_full = jnp.exp(scores - log_total)
@@ -239,7 +1080,12 @@
     grad_value_all = jnp.einsum(
         "bgrt,brgd->btd", prob_full.astype(BF16), grad_heads, preferred_element_type=F32
     )
-    grad_kv = scatter_kv(jnp.concatenate([grad_key_all, grad_value_all], axis=2).astype(BF16))
+    grad_kv, outs = scatter_kv(
+        jnp.concatenate([grad_key_all, grad_value_all], axis=2).astype(BF16),
+        cargo(1), fast, ids[1],
+    )
+    carried += outs
+    grad_kv = grad_kv.astype(BF16)
     if shared_kv:
         total = lax.psum(grad_kv, "section")
         grad_kv = jnp.where(lax.axis_index("section") == 0, total, jnp.zeros_like(total))
@@ -258,11 +1104,12 @@
         axis=2,
     ).reshape(trees * row_count, -1)
     attn_partial = dot_inner(qkv_grad, w_qkv).astype(BF16).reshape(trees, row_count, depth)
-    attn_rows = scatter_attn(attn_partial)
-    _, attn_norm_pull = jax.vjp(rms_scale, own_in, attn_scale)
-    grad_residual, grad_attn_scale = attn_norm_pull(attn_rows.astype(F32))
-    incoming_own = (grad_residual + grad_middle).astype(BF16)
-    incoming = gather_rows(incoming_own)
+    gathers = ["tensor"] if is_first else ["tensor", "dp"]
+    (incoming_own, grad_attn_scale, *gathered), outs = meet(
+        attn_partial, [own_in, attn_scale[None], grad_middle],
+        norm_back_body, own_outs, "tensor", gathers, cargo(2), fast, ids[2],
+    )
+    carried += outs
     products = (
         (normed, qkv_grad),
         (grad_attn, attended_bf),
@@ -270,8 +1117,10 @@
         (up_bf, mlp_in),
         (hidden_bf, grad_mlp),
     )
-    gain_grads = jnp.concatenate([grad_attn_scale, grad_mlp_scale, grad_q_scale, grad_k_scale])
-    return (incoming, incoming_own, products, gain_grads)
+    gain_grads = jnp.concatenate(
+        [grad_attn_scale[0], grad_mlp_scale[0], grad_q_scale, grad_k_scale]
+    )
+    return (gathered, incoming_own.astype(BF16).astype(F32), products, gain_grads, carried)
 
 
 def swap_cores(mine, other):
@@ -302,18 +1151,14 @@
     def pick(stacked, index):
         return lax.dynamic_index_in_dim(stacked, index, 0, keepdims=False)
 
-    gains_own = jnp.concatenate([attn_gain[0], mlp_gain[0], q_gain[0], k_gain[0]])
-    gains_all = lax.all_gather(gains_own, ("section", "dp")).astype(F32)
-    gains_all = gains_all.reshape(2, dp_size, -1)
-    gains = [
-        (
-            gains_all[layer, :, :own_depth].reshape(depth),
-            gains_all[layer, :, own_depth : 2 * own_depth].reshape(depth),
-            gains_all[layer, 0, 2 * own_depth : 2 * own_depth + HD],
-            gains_all[layer, 0, 2 * own_depth + HD :],
-        )
-        for layer in range(2)
-    ]
+    fast = (
+        own_rows % 8 == 0
+        and depth % (2 * CHUNK) == 0
+        and row_count % 16 == 0
+        and share % 16 == 0
+        and own_depth % 128 == 0
+        and not shared_kv
+    )
 
     def halves(width, array):
         return [array[:, :width], array[:, array.shape[1] - width :]]
@@ -329,21 +1174,64 @@
             )
         ]
     )
-    attn_shards = swap_cores(pick(attn_halves, core), pick(attn_halves, 1 - core))
     unit_blocks = jnp.stack([w_gate[0].T, w_up[0].T, w_down[0]]).reshape(
         3, 2, dp_size, share, own_depth
     )
     unit_blocks = unit_blocks.transpose(1, 2, 0, 3, 4)
-    unit_shards = swap_cores(pick(unit_blocks, core), pick(unit_blocks, 1 - core))
-
     qkv_width = q_width + 2 * k_width
-    weights = []
-    for layer in range(2):
-        attn_all = lax.all_gather(attn_shards[layer], "dp", axis=0, tiled=True)
-        pieces = exchange(unit_shards[layer], "dp")
-        pieces = pieces.transpose(1, 2, 0, 3).reshape(3, share, depth)
-        mats = [lax.all_gather(pieces[i], "tensor", axis=0, tiled=True) for i in range(3)]
-        weights.append((attn_all[:, :qkv_width], attn_all[:, qkv_width:], *mats))
+    gains_own = jnp.concatenate([attn_gain[0], mlp_gain[0], q_gain[0], k_gain[0]]).astype(F32)
+
+    def spread_units(rows):
+        return lax.all_gather(rows, "tensor", axis=0, tiled=True)
+
+    def attn_of(whole):
+        whole = whole.reshape(depth, -1)
+        return (whole[:, :qkv_width], whole[:, qkv_width:])
+
+    def joint(gate_up, down):
+        return (spread_units(gate_up[0]), spread_units(gate_up[1]), spread_units(down[0]))
+
+    if fast:
+        group = ["section", "dp"]
+        (gate_up,), (gains_all,) = fused(
+            [
+                UnitsOut(unit_blocks[:, :, :2], 0),
+                SharedRows(gains_own.reshape(-1, 128)),
+            ],
+            group, True, 1, 45,
+        )
+        attn_chunks = attn_halves.reshape(2, 4, own_depth // 4, -1)
+        attn_chunks, gate_up = lax.optimization_barrier((attn_chunks, gate_up))
+        (attn_all,), (down,), (attn_shard,) = fused(
+            [
+                AttnOut(attn_chunks, 0), UnitsOut(unit_blocks[:, :, 2:], 0), HalfOver(attn_chunks),
+            ],
+            group, True, 2, 80,
+        )
+        attn_next = lax.all_gather(attn_shard.reshape(own_depth, -1), "dp", axis=0, tiled=True)
+        first_weights = attn_of(attn_all) + joint(gate_up, down)
+    else:
+        gains_all = lax.all_gather(gains_own, ("section", "dp"))
+        attn_shards = swap_cores(pick(attn_halves, core), pick(attn_halves, 1 - core))
+        unit_shards = swap_cores(pick(unit_blocks, core), pick(unit_blocks, 1 - core))
+        both_weights = []
+        for layer in range(2):
+            attn_all = lax.all_gather(attn_shards[layer], "dp", axis=0, tiled=True)
+            pieces = exchange(unit_shards[layer], "dp")
+            pieces = pieces.transpose(1, 2, 0, 3).reshape(3, share, depth)
+            both_weights.append(attn_of(attn_all) + joint(pieces[:2], pieces[2:]))
+        first_weights = both_weights[0]
+
+    gains_all = gains_all.reshape(2, dp_size, -1)
+    gains = [
+        (
+            gains_all[layer, :, :own_depth].reshape(depth),
+            gains_all[layer, :, own_depth : 2 * own_depth].reshape(depth),
+            gains_all[layer, 0, 2 * own_depth : 2 * own_depth + HD],
+            gains_all[layer, 0, 2 * own_depth + HD :],
+        )
+        for layer in range(2)
+    ]
 
     def slot_setup(slot_index):
         tree_id = pick(order, slot_index)
@@ -362,36 +1250,83 @@
         )
 
     own_in = own_part(hidden).astype(F32)
-    outputs, kept = [], []
-    for layer in range(2):
-        hidden, own_in, stored = layer_forward(hidden, own_in, weights[layer], gains[layer], slot)
-        outputs.append(hidden)
-        kept.append(stored)
-
-    grad_own = own_part(cotangent)
+    def no_cargo(_):
+        return []
+
+    def next_units(index):
+        return [UnitsOut(unit_blocks[:, :, index : index + 1], 1)] if fast else []
+
+    output, own_in, kept_first, carried = layer_forward(
+        hidden, own_in, first_weights, gains[0], slot, next_units, fast, (3, 4, 5)
+    )
+    outputs, kept = [output], [kept_first]
+    if fast:
+        rows = [out[0][0] for out in carried]
+        second_weights = attn_of(attn_next) + tuple(spread_units(item) for item in rows)
+    else:
+        second_weights = both_weights[1]
+    output, _, kept_second, _ = layer_forward(
+        output, own_in, second_weights, gains[1], slot, no_cargo, fast, (6, 7, 8)
+    )
+    outputs.append(output)
+    kept.append(kept_second)
+    weights = [first_weights, second_weights]
+
+    grad_own = own_part(cotangent).astype(F32)
+    grad_mlp = lax.all_gather(grad_own.astype(BF16), "dp", axis=0, tiled=True)
+    grad_mlp = lax.all_gather(grad_mlp, "section", axis=0)
     grads, weight_grads, gain_grads = [None, None], [None, None], [None, None]
+    unit_grad = None
     for layer in (1, 0):
-        grads[layer], grad_own, products, gain_grads[layer] = layer_backward(
-            grad_own, kept[layer], weights[layer], gains[layer], slot, shared_kv
-        )
+        def home_units(index):
+            if not fast or layer == 1 or index == 0:
+                return []
+            return [UnitsHome(unit_grad[:1] if index == 1 else unit_grad[1:], 1)]
+
+        gathered, grad_own, products, gain_grads[layer], carried = layer_backward(
+            grad_own, grad_mlp.reshape(-1, depth), kept[layer], weights[layer], gains[layer], slot,
+            shared_kv, layer == 0, home_units, fast, (9, 10, 11) if layer else (12, 13, 14),
+        )
+        grads[layer], grad_mlp = gathered[0], gathered[-1]
         whole = [dot_outer(left, right).astype(BF16) for left, right in products]
+        unit_grad = jnp.stack(
+            [
+                lax.psum_scatter(item, "tensor", scatter_dimension=0, tiled=True)
+                for item in whole[2:]
+            ]
+        )
         attn_grad = lax.psum_scatter(
             jnp.concatenate(whole[:2], axis=1), "dp", scatter_dimension=0, tiled=True
         )
-        unit_grad = [
-            lax.psum_scatter(item, "tensor", scatter_dimension=0, tiled=True) for item in whole[2:]
-        ]
-        pieces = jnp.stack(unit_grad).reshape(3, share, dp_size, own_depth).transpose(2, 0, 1, 3)
-        weight_grads[layer] = (attn_grad, exchange(pieces, "dp"))
-
-    def bring_home(first, second):
-        mine, other = jnp.where(core == 0, first, second), jnp.where(core == 0, second, first)
-        arrived = lax.ppermute(other, "section", [(0, 1), (1, 0)])
-        return (jnp.where(core == 0, mine, arrived), jnp.where(core == 0, arrived, mine))
-
-    attn_home = bring_home(weight_grads[0][0], weight_grads[1][0])
-    unit_home = jnp.stack(bring_home(weight_grads[0][1], weight_grads[1][1]))
-    unit_home = unit_home.transpose(2, 0, 1, 3, 4).reshape(3, own_units, own_depth)
+        weight_grads[layer] = (attn_grad, unit_grad)
+
+    gain_total = jnp.stack(gain_grads)
+    if fast:
+        mine = jnp.where(core == 0, weight_grads[0][0], weight_grads[1][0])
+        other = jnp.where(core == 0, weight_grads[1][0], weight_grads[0][0])
+        (gain_total,), (arrived,), (first_home,) = fused(
+            [TotalOverAll(gain_total.reshape(-1, 128)), Swap(other), UnitsHome(unit_grad, 0)],
+            ["section", "dp", "tensor"], True, 15, 60,
+        )
+        attn_home = (jnp.where(core == 0, mine, arrived), jnp.where(core == 0, arrived, mine))
+        second_home = jnp.concatenate([out[0] for out in carried], axis=0)
+        unit_home = jnp.where(core == 0, first_home, second_home).reshape(3, own_units, own_depth)
+        gain_total = gain_total.reshape(2, -1)
+    else:
+        def bring_home(first, second):
+            mine, other = jnp.where(core == 0, first, second), jnp.where(core == 0, second, first)
+            arrived = lax.ppermute(other, "section", [(0, 1), (1, 0)])
+            return (jnp.where(core == 0, mine, arrived), jnp.where(core == 0, arrived, mine))
+
+        def pieces_of(grad):
+            return exchange(
+                grad.reshape(3, share, dp_size, own_depth).transpose(2, 0, 1, 3), "dp"
+            )
+
+        attn_home = bring_home(weight_grads[0][0], weight_grads[1][0])
+        unit_home = jnp.stack(bring_home(pieces_of(weight_grads[0][1]), pieces_of(weight_grads[1][1])))
+        unit_home = unit_home.transpose(2, 0, 1, 3, 4).reshape(3, own_units, own_depth)
+        gain_total = lax.psum(gain_total, ("section", "dp", "tensor"))
 
     def joined(start, width):
         parts = [half[:, start : start + width] for half in attn_home]
@@ -399,7 +1334,6 @@
             return parts[0].astype(F32)
         return jnp.concatenate(parts, axis=1).astype(F32)
 
-    gain_total = lax.psum(jnp.stack(gain_grads), ("section", "dp", "tensor"))
     gain_own = pick(gain_total, core)
     share_width = attn_gain.shape[1]
     attn_gain_grad = lax.dynamic_slice_in_dim(gain_own, data_index * share_width, share_width, 0)

time: 1960 us -> 1170 us (0.60)
  waiting for transfers between devices: 1480 us -> 6.88 us
  Pallas kernels: 0 us -> 839 us
  blocking collectives: 65.2 us -> 0 us
  other arithmetic: 97.8 us -> 67.9 us
  starting transfers between devices: 23.4 us -> 1.79 us
    pallas_call x0 -> x15, Pallas kernels: none -> 839 us  [fused(): pl.pallas_call(kernel, out_shape=[item[0] for item in outs], in_specs=[it...]
    all_gather x30 -> x9, waiting for transfers between devices: 639 us -> 0.07 us  [the longest x6 0.03 us: spread_units(): return lax.all_gather(rows, 'tensor', axis=0, tiled=True)]
    reduce_scatter x14 -> x0, waiting for transfers between devices: 243 us -> none  [the longest x4 127 us: scatter_mlp(): return lax.psum_scatter(mine, 'dp', scatter_dimension=0, tiled=True)]
    reduce_scatter x6, waiting for transfers between devices: 235 us -> 0.06 us  [on_device(): lax.psum_scatter(item, 'tensor', scatter_dimension=0, tiled=True)]
    ppermute x16 -> x0, waiting for transfers between devices: 154 us -> none  [the longest x12 152 us: exchange(): arrived = lax.ppermute(piece, axis, [(i, i ^ step) for i in range(size)])]
    reduce_scatter x2, waiting for transfers between devices: 120 us -> 3.97 us  [on_device(): lax.psum_scatter(jnp.concatenate(whole[:2], axis=1), 'dp', scatter_dimens...]
    unnamed x60 -> x17, waiting for transfers between devices: 91.9 us -> 2.78 us
    psum x1 -> x0, blocking collectives: 39.7 us -> none  [on_device(): gain_total = lax.psum(jnp.stack(gain_grads), ('section', 'dp', 'tensor'))]
  transfers between devices with their start and end apart: 72 -> 17, of which waited for: 56 -> 1; matrix products, arithmetic and copies ran while one was open for 11% -> 18% of each run, Pallas kernels for 0% -> 66%
where the time goes in v5:
time: 1170 us; the launch traced here: 1160 us
  Pallas kernels  839 us (72%)
  matrix products  144 us (12%)
  local copies, waits for them, and re-layouts  82.7 us (7%)
  other arithmetic  67.9 us (6%)
  between operations  21.1 us (2%)
    pallas_call x15, Pallas kernels, fused(): pl.pallas_call(kernel, out_shape=[item[0] for item in outs], in_specs=[it...  839 us
    dot_general x10, matrix products, dot_inner(): return lax.dot_general(left, right, INNER, preferred_element_type=F32)  48.2 us
    unnamed x377, local copies, waits for them, and re-layouts  46 us
    dot_general x10, matrix products, dot_outer(): return lax.dot_general(left, right, OUTER, preferred_element_type=F32)  40.5 us
    dot_general x10, matrix products, dot(): return jnp.dot(left, right, preferred_element_type=F32)  30.7 us
  transfers between devices with their start and end apart: 17, of which 1 were waited for; matrix products, arithmetic and copies ran while one was open for 18% of the time, Pallas kernels for 66%

profile of v5, /device:TPU:0, one launch (start us, length us, event | category | flops | bytes accessed | tf_op | source)
XLA Modules:
  0.0 1163.2 jit_solution(9165024731074220781)
XLA Ops:
  20.0 57.3 %shard_map.255 = (bf16[2,192,2048]{2,1,0:T(8,128)(2,1)S(1)}, f32[2,4,10,128]{3,2,1,0:T(8,128)S(1)}) custom-call(bf16[2,4,2,192,512]{4,3,2,1,0:T(8,128)(2,1)S(1)} %slice.257.refs_0_, f32[10,128]{1,0:T(8,128)S(1)} %fusion.163.refs_1_), custom_call_target="tpu_custom_call" | custom-call | bytes 135000000 | tf_op jit(solution)/shard_map/pallas_call | solution.py:210
  79.6 4.5 fusion.196
  84.1 66.6 %shard_map.256 = (bf16[4,4,128,768]{3,2,1,0:T(8,128)(2,1)S(1)}, bf16[1,192,2048]{2,1,0:T(8,128)(2,1)S(1)}, bf16[4,128,768]{2,1,0:T(8,128)(2,1)S(1)}) custom-call(bf16[2,4,128,768]{3,2,1,0:T(8,128)(2,1)S(1)} %pad_maximum_fusion.4.refs_0_.refs_2_, bf16[2,4,1,192,512]{4,3,2,1,0:T(8,128)(2,1)S(1)} %get-tuple-element.182.refs_1_.refs_0_, ...), custom_call_target="tpu_custom_call" | custom-call | bytes 240000000 | tf_op jit(solution)/shard_map/pallas_call | solution.py:210
  177.0 42.4 %shard_map.257 = (bf16[1,192,2048]{2,1,0:T(8,128)(2,1)}, bf16[2,4,288,256]{3,2,1,0:T(8,128)(2,1)S(1)}) custom-call(bf16[2,4,1,192,512]{4,3,2,1,0:T(8,128)(2,1)S(1)} %copy-done.3, bf16[2,288,256]{2,1,0:T(8,128)(2,1)S(1)} %pad_maximum_fusion.14.refs_1_), custom_call_target="tpu_custom_call" | custom-call | bytes 90000000 | tf_op jit(solution)/shard_map/pallas_call | solution.py:210
  231.8 2.3 convolution_convert_fusion.9
  234.1 86.3 %shard_map.258 = (bf16[1,192,2048]{2,1,0:T(8,128)(2,1)}, f32[72,2048]{1,0:T(8,128)S(1)}, bf16[2,288,2048]{2,1,0:T(8,128)(2,1)S(1)}) custom-call(bf16[2,4,1,192,512]{4,3,2,1,0:T(8,128)(2,1)S(1)} %copy-done.2, bf16[2,288,2048]{2,1,0:T(8,128)(2,1)S(1)} %bitcast.373, f32[72,2048]{1,0:T(8,128)S(1)} %bitcast_convert_fusion.6.refs_2_, f32[1,2048]{1,0:T(1,128)S(1)} %bitcast.395), custom_call_target="tpu_custom_call" | custom-call | bytes 150000000 | tf_op jit(solution)/shard_map/pallas_call | solution.py:210
  322.9 5.9 fusion.38
  328.9 7.0 multiply_convert_fusion.3
  335.9 4.3 fusion.40
  340.2 55.9 %shard_map.259 = (bf16[1,192,2048]{2,1,0:T(8,128)(2,1)}, f32[72,2048]{1,0:T(8,128)S(1)}, bf16[2,288,2048]{2,1,0:T(8,128)(2,1)S(1)}) custom-call(bf16[2,4,1,192,512]{4,3,2,1,0:T(8,128)(2,1)S(1)} %get-tuple-element.182.refs_1_.refs_0_, bf16[2,288,2048]{2,1,0:T(8,128)(2,1)S(1)} %bitcast.383, f32[72,2048]{1,0:T(8,128)S(1)} %get-tuple-element.57.refs_2_.refs_1_), custom_call_target="tpu_custom_call" | custom-call | bytes 150000000 | tf_op jit(solution)/shard_map/pallas_call | solution.py:210
  401.9 3.1 fusion.70
  406.6 31.6 %shard_map.260 = bf16[2,4,288,256]{3,2,1,0:T(8,128)(2,1)S(1)} custom-call(bf16[2,288,256]{2,1,0:T(8,128)(2,1)S(1)} %pad_maximum_fusion.16.refs_0_), custom_call_target="tpu_custom_call" | custom-call | bytes 90000000 | tf_op jit(solution)/shard_map/pallas_call | solution.py:210
  441.7 2.5 multiply_reduce_fusion.2
  455.3 2.3 convolution_convert_fusion.8
  457.6 47.6 %shard_map.261 = (f32[72,2048]{1,0:T(8,128)S(1)}, bf16[2,288,2048]{2,1,0:T(8,128)(2,1)S(1)}) custom-call(bf16[2,288,2048]{2,1,0:T(8,128)(2,1)S(1)} %bitcast.374, f32[72,2048]{1,0:T(8,128)S(1)} %convert_convert_fusion.1.refs_1_, f32[1,2048]{1,0:T(1,128)S(1)} %bitcast.397), custom_call_target="tpu_custom_call" | custom-call | bytes 150000000 | tf_op jit(solution)/shard_map/pallas_call | solution.py:210
  506.6 6.0 fusion.22
  512.7 5.8 fusion.16
  518.5 7.7 fusion.84
  527.2 4.0 convolution_convert_fusion.3
  531.3 6.3 convolution_convert_fusion.4
  540.2 6.3 convolution_convert_fusion.5
  546.8 4.5 fusion.20
  553.4 52.0 %shard_map.263 = (f32[72,2048]{1,0:T(8,128)S(1)}, f32[1,2048]{1,0:T(1,128)S(1)}, bf16[2,288,2048]{2,1,0:T(8,128)(2,1)S(1)}) custom-call(bf16[2,288,2048]{2,1,0:T(8,128)(2,1)S(1)} %bitcast.380, f32[72,2048]{1,0:T(8,128)S(1)} %get-tuple-element.65.refs_1_, f32[1,2048]{1,0:T(1,128)S(1)} %bitcast.398, f32[72,2048]{1,0:T(8,128)S(1)} %copy-done.17), custom_call_target="tpu_custom_call" | custom-call | bytes 150000000 | tf_op jit(solution)/shard_map/pallas_call | solution.py:210
  610.3 4.1 fusion.3
  614.5 3.3 fusion.5
  620.9 34.4 %shard_map.264 = f32[2,288,256]{2,1,0:T(8,128)S(1)} custom-call(bf16[2,4,288,256]{3,2,1,0:T(8,128)(2,1)S(1)} %pad_maximum_fusion.6.refs_0_), custom_call_target="tpu_custom_call" | custom-call | bytes 90000000 | tf_op jit(solution)/shard_map/pallas_call | solution.py:210
  663.2 54.4 %shard_map.265 = (f32[72,2048]{1,0:T(8,128)S(1)}, f32[1,2048]{1,0:T(1,128)S(1)}, bf16[2,288,2048]{2,1,0:T(8,128)(2,1)S(1)}, bf16[2,288,2048]{2,1,0:T(8,128)(2,1)S(1)}) custom-call(bf16[2,288,2048]{2,1,0:T(8,128)(2,1)S(1)} %bitcast.381, f32[72,2048]{1,0:T(8,128)S(1)} %convert_convert_fusion.1.refs_1_, f32[1,2048]{1,0:T(1,128)S(1)} %bitcast.399, ...), custom_call_target="tpu_custom_call" | custom-call | bytes 150000000 | tf_op jit(solution)/shard_map/pallas_call | solution.py:210
  720.5 4.0 convolution_convert_fusion
  724.6 7.2 fusion.87
  732.7 4.1 convolution_convert_fusion.1
  737.0 6.7 convolution_convert_fusion.2
  745.3 3.0 convolution_convert_fusion.11
  752.4 4.3 fusion.32
  758.7 55.9 %shard_map.266 = (f32[72,2048]{1,0:T(8,128)S(1)}, f32[1,2048]{1,0:T(1,128)S(1)}, bf16[2,288,2048]{2,1,0:T(8,128)(2,1)S(1)}) custom-call(bf16[2,288,2048]{2,1,0:T(8,128)(2,1)S(1)} %bitcast.382, f32[72,2048]{1,0:T(8,128)S(1)} %copy-done.12, f32[1,2048]{1,0:T(1,128)S(1)} %bitcast.396, f32[72,2048]{1,0:T(8,128)S(1)} %convert_convert_fusion.refs_3_), custom_call_target="tpu_custom_call" | custom-call | bytes 150000000 | tf_op jit(solution)/shard_map/pallas_call | solution.py:210
  817.4 2.8 convolution_convert_fusion.12
  822.0 4.0 fusion
  826.0 3.3 fusion.2
  841.9 45.7 %shard_map.267 = (bf16[1,2,4,192,512]{4,3,2,1,0:T(8,128)(2,1)S(1)}, f32[2,288,256]{2,1,0:T(8,128)S(1)}) custom-call(bf16[1,192,2048]{2,1,0:T(8,128)(2,1)S(1)} %bitcast.390, bf16[2,4,288,256]{3,2,1,0:T(8,128)(2,1)S(1)} %pad_maximum_fusion.7.refs_1_), custom_call_target="tpu_custom_call" | custom-call | bytes 90000000 | tf_op jit(solution)/shard_map/pallas_call | solution.py:210
  895.5 4.3 fusion.43
  899.8 57.4 %shard_map.262 = (f32[72,2048]{1,0:T(8,128)}, bf16[2,288,2048]{2,1,0:T(8,128)(2,1)S(1)}) custom-call(bf16[2,288,2048]{2,1,0:T(8,128)(2,1)S(1)} %bitcast.384, f32[72,2048]{1,0:T(8,128)S(1)} %copy-done.19), custom_call_target="tpu_custom_call" | custom-call | bytes 150000000 | tf_op jit(solution)/shard_map/pallas_call | solution.py:210
  961.4 2.5 convolution_convert_fusion.6
  964.0 78.6 %shard_map.268 = (bf16[2,2,4,192,512]{4,3,2,1,0:T(8,128)(2,1)S(1)}, f32[72,2048]{1,0:T(8,128)}, f32[1,2048]{1,0:T(1,128)S(1)}, bf16[2,288,2048]{2,1,0:T(8,128)(2,1)S(1)}) custom-call(bf16[2,192,2048]{2,1,0:T(8,128)(2,1)S(1)} %pad_maximum_fusion.5.refs_0_, bf16[2,288,2048]{2,1,0:T(8,128)(2,1)S(1)} %bitcast.379, f32[72,2048]{1,0:T(8,128)S(1)} %copy-done.5, ...), custom_call_target="tpu_custom_call" | custom-call | bytes 150000000 | tf_op jit(solution)/shard_map/pallas_call | solution.py:210
  1050.6 4.0 reduce-scatter.17.cloned.1.call-done
  1055.9 73.0 %shard_map.269 = (f32[68,128]{1,0:T(8,128)S(1)}, bf16[512,768]{1,0:T(8,128)(2,1)S(1)}, bf16[3,2,4,192,512]{4,3,2,1,0:T(8,128)(2,1)S(1)}) custom-call(f32[68,128]{1,0:T(8,128)S(1)} %reshape.641.refs_0_, bf16[512,768]{1,0:T(8,128)(2,1)S(1)} %broadcast_select_fusion.3.refs_1_, bf16[3,192,2048]{2,1,0:T(8,128)(2,1)S(1)} %pad_maximum_fusion.3.refs_2_), custom_call_target="tpu_custom_call" | custom-call | bytes 180000000 | tf_op jit(solution)/shard_map/pallas_call | solution.py:210
  1133.0 3.5 maximum_select_fusion
  1139.9 2.2 bitcast_convert_fusion.2
  1142.7 2.4 copy.216
  1146.9 2.4 copy.215
  (580 shorter events, 162.5 us)
Async XLA Ops:
  7.2 314.7 %all-gather.32.cloned.1.call-start = ((), (), s32[]{:S(2)}) async-start(), calls=%async_computation.23 | async-start | bytes 1474560 | tf_op jit(solution)/shard_map/all_gather | solution.py:1276
  9.4 313.5 %all-gather.20.cloned.1.call-start = ((), (), s32[]{:S(2)}) async-start(), calls=%async_computation.17 | async-start | bytes 3932160 | tf_op jit(solution)/shard_map/all_gather | solution.py:1185
  19.9 57.4 %copy-start.83 = (bf16[512,768]{1,0:T(8,128)(2,1)S(1)}, bf16[512,768]{1,0:T(8,128)(2,1)}, u32[]{:S(2)}) copy-start(bf16[512,768]{1,0:T(8,128)(2,1)} %copy.191) | copy-start | bytes 2359300
  19.9 57.4 %copy-start.84 = (bf16[512,768]{1,0:T(8,128)(2,1)S(1)}, bf16[512,768]{1,0:T(8,128)(2,1)}, u32[]{:S(2)}) copy-start(bf16[512,768]{1,0:T(8,128)(2,1)} %copy.192) | copy-start | bytes 2359300
  78.8 250.0 %all-gather.22.cloned.1.call-start = ((), (), s32[]{:S(2)}) async-start(), calls=%async_computation.18 | async-start | bytes 3932160 | tf_op jit(solution)/shard_map/all_gather | solution.py:1185
  79.6 256.3 %all-gather.24.cloned.1.call-start = ((), (), s32[]{:S(2)}) async-start(), calls=%async_computation.19 | async-start | bytes 3932160 | tf_op jit(solution)/shard_map/all_gather | solution.py:1185
  84.1 70.7 %copy-start.166 = (s32[2]{0:T(128)S(1)}, s32[2]{0:T(128)}, u32[]{:S(2)}) copy-start(s32[2]{0:T(128)} %param.20) | copy-start | bytes 28
  154.2 247.7 %all-gather.18.cloned.1.call-start = ((), (), s32[]{:S(2)}) async-start(), calls=%async_computation.8 | async-start | bytes 3932160 | tf_op jit(solution)/shard_map/all_gather | solution.py:1211
  154.8 351.9 %all-gather.28.cloned.1.call-start = ((), (), s32[]{:S(2)}) async-start(), calls=%async_computation.21 | async-start | bytes 3932160 | tf_op jit(solution)/shard_map/all_gather | solution.py:1185
  158.6 10.5 copy-start.146
  158.6 65.5 %copy-start.150 = (f32[128]{0:T(128)}, f32[128]{0:T(128)S(1)}, u32[]{:S(2)}) copy-start(f32[128]{0:T(128)S(1)} %get-tuple-element.244) | copy-start | bytes 1540
  158.6 246.7 %copy-start.148 = (f32[128]{0:T(128)}, f32[128]{0:T(128)S(1)}, u32[]{:S(2)}) copy-start(f32[128]{0:T(128)S(1)} %get-tuple-element.243) | copy-start | bytes 1540
  173.8 50.3 %copy-start.129 = (f32[2,288,2]{1,2,0:T(2,128)}, f32[2,288,2]{1,2,0:T(2,128)S(1)}, u32[]{:S(2)}) copy-start(f32[2,288,2]{1,2,0:T(2,128)S(1)} %copy.193) | copy-start | bytes 13828
  173.8 46.8 %copy-start.167 = (s32[2,9]{1,0:T(2,128)S(1)}, s32[2,9]{1,0:T(2,128)}, u32[]{:S(2)}) copy-start(s32[2,9]{1,0:T(2,128)} %param.19) | copy-start | bytes 220
  175.8 49.9 %copy-start.62 = (f32[2,288,64]{2,1,0:T(8,128)}, f32[2,288,64]{2,1,0:T(8,128)S(1)}, u32[]{:S(2)}) copy-start(f32[2,288,64]{2,1,0:T(8,128)S(1)} %get-tuple-element.230) | copy-start | bytes 442372
  231.8 88.6 %copy-start.4 = (f32[72,2048]{1,0:T(8,128)}, f32[72,2048]{1,0:T(8,128)S(1)}, u32[]{:S(2)}) copy-start(f32[72,2048]{1,0:T(8,128)S(1)} %bitcast_convert_fusion.6.refs_2_) | copy-start | bytes 1769476
  321.8 18.3 %copy-start.11 = (f32[72,2048]{1,0:T(8,128)}, f32[72,2048]{1,0:T(8,128)S(1)}, u32[]{:S(2)}) copy-start(f32[72,2048]{1,0:T(8,128)S(1)} %get-tuple-element.57.refs_2_.refs_1_) | copy-start | bytes 1769476
  321.9 190.8 %all-gather.34.cloned.1.call-start = ((), (), s32[]{:S(2)}) async-start(), calls=%async_computation.24 | async-start | bytes 3538944 | tf_op jit(solution)/shard_map/all_gather | solution.py:1277
  322.6 190.1 %all-gather.30.cloned.1.call-start = ((), (), s32[]{:S(2)}) async-start(), calls=%async_computation.22 | async-start | bytes 3932160 | tf_op jit(solution)/shard_map/all_gather | solution.py:1185
  398.3 120.2 %all-gather.26.cloned.1.call-start = ((), (), s32[]{:S(2)}) async-start(), calls=%async_computation.20 | async-start | bytes 3932160 | tf_op jit(solution)/shard_map/all_gather | solution.py:1185
  399.1 441.7 %reduce-scatter.13.cloned.1.call-start = ((), (), s32[]{:S(2)}) async-start(), calls=%async_computation.11 | async-start | bytes 3932160 | tf_op jit(solution)/shard_map/reduce_scatter | solution.py:1294
  405.0 33.2 %copy-start.87 = (f32[2,288,512]{2,1,0:T(8,128)}, f32[2,288,512]{2,1,0:T(8,128)S(1)}, u32[]{:S(2)}) copy-start(f32[2,288,512]{2,1,0:T(8,128)S(1)} %fusion.70) | copy-start | bytes 3538948
  438.3 14.2 %copy-start.6 = (bf16[2,4,288,256]{3,2,1,0:T(8,128)(2,1)}, bf16[2,4,288,256]{3,2,1,0:T(8,128)(2,1)S(1)}, u32[]{:S(2)}) copy-start(bf16[2,4,288,256]{3,2,1,0:T(8,128)(2,1)S(1)} %shard_map.260) | copy-start | bytes 3538948
  506.6 46.7 %copy-start.18 = (f32[72,2048]{1,0:T(8,128)}, f32[72,2048]{1,0:T(8,128)S(1)}, u32[]{:S(2)}) copy-start(f32[72,2048]{1,0:T(8,128)S(1)} %get-tuple-element.65.refs_1_) | copy-start | bytes 1769476
  531.2 427.8 %reduce-scatter.11.cloned.1.call-start = ((), (), s32[]{:S(2)}) async-start(), calls=%async_computation.10 | async-start | bytes 3932160 | tf_op jit(solution)/shard_map/reduce_scatter | solution.py:1294
  537.6 421.5 %reduce-scatter.9.cloned.1.call-start = ((), (), s32[]{:S(2)}) async-start(), calls=%async_computation.9 | async-start | bytes 3932160 | tf_op jit(solution)/shard_map/reduce_scatter | solution.py:1294
  546.6 499.2 %reduce-scatter.23.cloned.1.call-start = ((), (), s32[]{:S(2)}) async-start(), calls=%async_computation.16 | async-start | bytes 3932160 | tf_op jit(solution)/shard_map/reduce_scatter | solution.py:1294
  610.3 9.0 slice-start.2
  620.8 34.6 %copy-start.7 = (bf16[2,4,288,256]{3,2,1,0:T(8,128)(2,1)S(1)}, bf16[2,4,288,256]{3,2,1,0:T(8,128)(2,1)}, u32[]{:S(2)}) copy-start(bf16[2,4,288,256]{3,2,1,0:T(8,128)(2,1)} %copy-done.6) | copy-start | bytes 3538948
  663.1 57.3 %copy-start.177 = (bf16[576,768]{1,0:T(8,128)(2,1)S(1)}, bf16[576,768]{1,0:T(8,128)(2,1)}, u32[]{:S(2)}) copy-start(bf16[576,768]{1,0:T(8,128)(2,1)} %copy-done.176) | copy-start | bytes 2654212
  724.5 321.3 %reduce-scatter.21.cloned.1.call-start = ((), (), s32[]{:S(2)}) async-start(), calls=%async_computation.15 | async-start | bytes 3932160 | tf_op jit(solution)/shard_map/reduce_scatter | solution.py:1294
  736.8 309.0 %reduce-scatter.19.cloned.1.call-start = ((), (), s32[]{:S(2)}) async-start(), calls=%async_computation.14 | async-start | bytes 3932160 | tf_op jit(solution)/shard_map/reduce_scatter | solution.py:1294
  743.8 306.8 %reduce-scatter.15.cloned.1.call-start = ((), (), s32[]{:S(2)}) async-start(), calls=%async_computation.12 | async-start | bytes 3932160 | tf_op jit(solution)/shard_map/reduce_scatter | solution.py:1298
  752.3 302.3 %reduce-scatter.17.cloned.1.call-start = ((), (), s32[]{:S(2)}) async-start(), calls=%async_computation.13 | async-start | bytes 3932160 | tf_op jit(solution)/shard_map/reduce_scatter | solution.py:1298
  841.9 45.9 %copy-start.71 = (f32[1,288,64]{2,1,0:T(8,128)S(1)}, f32[1,288,64]{2,1,0:T(8,128)}, u32[]{:S(2)}) copy-start(f32[1,288,64]{2,1,0:T(8,128)} %get-tuple-element.250) | copy-start | bytes 221188
  841.9 45.9 %copy-start.74 = (f32[1,288,64]{2,1,0:T(8,128)S(1)}, f32[1,288,64]{2,1,0:T(8,128)}, u32[]{:S(2)}) copy-start(f32[1,288,64]{2,1,0:T(8,128)} %get-tuple-element.251) | copy-start | bytes 221188
  841.9 45.9 %copy-start.77 = (f32[1,288,64]{2,1,0:T(8,128)S(1)}, f32[1,288,64]{2,1,0:T(8,128)}, u32[]{:S(2)}) copy-start(f32[1,288,64]{2,1,0:T(8,128)} %get-tuple-element.256) | copy-start | bytes 221188
  841.9 46.0 %copy-start.80 = (f32[1,288,64]{2,1,0:T(8,128)S(1)}, f32[1,288,64]{2,1,0:T(8,128)}, u32[]{:S(2)}) copy-start(f32[1,288,64]{2,1,0:T(8,128)} %get-tuple-element.257) | copy-start | bytes 221188
  841.9 46.1 %copy-start.86 = (f32[2,288,512]{2,1,0:T(8,128)S(1)}, f32[2,288,512]{2,1,0:T(8,128)}, u32[]{:S(2)}) copy-start(f32[2,288,512]{2,1,0:T(8,128)} %copy-done.85) | copy-start | bytes 3538948
  841.9 46.1 %copy-start.133 = (f32[2,288]{1,0:T(2,128)S(1)}, f32[2,288]{1,0:T(2,128)}, u32[]{:S(2)}) copy-start(f32[2,288]{1,0:T(2,128)} %copy-done.132) | copy-start | bytes 6916
  841.9 46.1 %copy-start.147 = (f32[128]{0:T(128)S(1)}, f32[128]{0:T(128)}, u32[]{:S(2)}) copy-start(f32[128]{0:T(128)} %copy-done.146) | copy-start | bytes 1540
  899.8 57.5 %copy-start.39 = (f32[1,2048]{1,0:T(1,128)S(1)}, f32[1,2048]{1,0:T(1,128)}, u32[]{:S(2)}) copy-start(f32[1,2048]{1,0:T(1,128)} %copy-done.38) | copy-start | bytes 24580
  899.8 57.5 %copy-start.161 = (f32[128]{0:T(128)S(1)}, f32[128]{0:T(128)}, u32[]{:S(2)}) copy-start(f32[128]{0:T(128)} %get-tuple-element.167) | copy-start | bytes 1540
  899.8 57.5 %copy-start.162 = (f32[128]{0:T(128)S(1)}, f32[128]{0:T(128)}, u32[]{:S(2)}) copy-start(f32[128]{0:T(128)} %get-tuple-element.169) | copy-start | bytes 1540
  964.0 81.7 %copy-start.41 = (f32[1,2048]{1,0:T(1,128)S(1)}, f32[1,2048]{1,0:T(1,128)}, u32[]{:S(2)}) copy-start(f32[1,2048]{1,0:T(1,128)} %copy-done.40) | copy-start | bytes 24580
  964.0 81.7 %copy-start.163 = (f32[128]{0:T(128)S(1)}, f32[128]{0:T(128)}, u32[]{:S(2)}) copy-start(f32[128]{0:T(128)} %get-tuple-element.163) | copy-start | bytes 1540
  1054.6 74.3 %copy-start.81 = (bf16[512,768]{1,0:T(8,128)(2,1)S(1)}, bf16[512,768]{1,0:T(8,128)(2,1)}, u32[]{:S(2)}) copy-start(bf16[512,768]{1,0:T(8,128)(2,1)} %reduce-scatter.15.cloned.1.call-done) | copy-start | bytes 2359300
  1054.6 74.3 %copy-start.82 = (bf16[512,768]{1,0:T(8,128)(2,1)S(1)}, bf16[512,768]{1,0:T(8,128)(2,1)}, u32[]{:S(2)}) copy-start(bf16[512,768]{1,0:T(8,128)(2,1)} %reduce-scatter.17.cloned.1.call-done) | copy-start | bytes 2359300
  (151 other events, 364.9 us)
Sparse Core Ops, SparseCore 0:
  9.6 46.2 all-gather.31
  79.0 42.8 all-gather.19
  124.3 43.9 all-gather.21
  170.6 43.9 all-gather.23
  216.6 99.9 all-gather.17
  322.0 45.6 all-gather.27
  369.2 11.6 all-gather.33
  398.5 48.0 all-gather.29
  448.4 56.2 all-gather.25
  531.3 48.0 reduce-scatter.12
  583.0 56.4 reduce-scatter.10
  643.0 54.5 reduce-scatter.8
  724.7 50.8 reduce-scatter.22
  778.4 55.5 reduce-scatter.20
  836.9 43.9 reduce-scatter.18
  883.0 79.0 reduce-scatter.14
  964.2 90.3 reduce-scatter.16

commit v6 on v5

--- a/solution.py
+++ b/solution.py
@@ -182,7 +182,7 @@
         pass
 
 
-def fused(parts, axes, across, collective_id, cost_us):
+def fused(parts, axes, across, collective_id, cost_us, vmem=40):
     counts = [(len(part.ins), len(part.outs), len(part.scratch)) for part in parts]
 
     def kernel(*refs):
@@ -217,7 +217,7 @@
             flops=0, bytes_accessed=cost_us * 3_000_000, transcendentals=0
         ),
         compiler_params=pltpu.CompilerParams(
-            collective_id=collective_id, has_side_effects=True, vmem_limit_bytes=40 << 20
+            collective_id=collective_id, has_side_effects=True, vmem_limit_bytes=vmem << 20
         ),
     )(*[item[0] for item in ins])
     results = list(results)
@@ -717,42 +717,191 @@
             out[...] = total
 
 
-class Hub(Part):
-    def __init__(self, terms, own_args, body, own_outs, scatter, gathers):
-        self.body, self.scatter, self.gathers = body, scatter, gathers
-        self.n_own = len(own_outs)
-        self.rows, depth = own_args[0].shape
-        rows, half = self.rows, depth // 2
-        self.half = half
-        self.sizes = [lax.axis_size(axis) for axis in gathers]
-        self.ins = [(arg, VMEM) for arg in own_args]
-        self.outs = [(jax.ShapeDtypeStruct(shape, F32), VMEM) for shape in own_outs]
-        self.outs += [
-            (jax.ShapeDtypeStruct((2, size * rows, depth), BF16), VMEM) for size in self.sizes
-        ]
-        self.scratch = []
-        if scatter:
-            self.ins = [(terms, VMEM)] + self.ins
-            size = self.size = lax.axis_size(scatter)
-            boxes = pltpu.VMEM((size, 2 * rows, half), BF16)
-            self.scratch += [boxes] * 4 + [pltpu.VMEM((2 * rows, half), F32)] + [SEM((size,))] * 4
-        for size in self.sizes:
-            self.scratch += [pltpu.VMEM((2, size, 2 * rows, half), BF16)] + [SEM((size,))] * 4
-
-    def bind(self, ins, outs, scratch):
-        self.own_outs, self.gathered = outs[: self.n_own], outs[self.n_own :]
+class Gatherer:
+    def __init__(self, axis, rows, half):
+        self.axis, self.rows, self.half = axis, rows, half
+        self.size = size = lax.axis_size(axis)
+        self.scratch = [pltpu.VMEM((2, size, 2 * rows, half), BF16)]
+        self.scratch += [SEM((size,))] * 4 + [SEM]
+
+    def bind(self, refs):
+        self.board, self.send, self.recv, self.sib_send, self.sib_recv, self.relay_send = refs
         self.core = lax.axis_index("section")
         self.sibling = 1 - self.core
-        if self.scatter:
-            self.terms, *self.args = ins
-            self.to_sib, self.from_sib, self.to_peer, self.from_peer, self.total = scratch[:5]
-            self.sib_send, self.sib_recv, self.peer_send, self.peer_recv = scratch[5:9]
-            scratch = scratch[9:]
-            self.me = lax.axis_index(self.scatter)
-        else:
-            self.args = ins
-        self.boards = [scratch[5 * i : 5 * i + 5] for i in range(len(self.gathers))]
-
+        self.me = lax.axis_index(self.axis)
+        self.relays = line_relays(self.size) if self.axis == "dp" else []
+
+    def direct(self, place):
+        sent = place != self.me
+        if self.relays:
+            sent = sent & jnp.logical_not(far_pair(place, self.me))
+        return sent
+
+    def spread(self, place, slot):
+        return remote(
+            self.board.at[self.core, slot], self.board.at[self.core, slot], self.send.at[place],
+            self.recv.at[slot], {self.axis: place},
+        )
+
+    def passed(self, source, target):
+        return remote(
+            self.board.at[self.core, source], self.board.at[self.core, source], self.relay_send,
+            self.recv.at[source], {self.axis: target},
+        )
+
+    def over(self, tree, slot):
+        return remote(
+            self.board.at[tree, slot], self.board.at[tree, slot], self.sib_send.at[slot],
+            self.sib_recv.at[slot], {"section": self.sibling},
+        )
+
+    def begin(self, result):
+        half = self.half
+        piece = jnp.concatenate([result[:, :half], result[:, half:]], axis=0)
+        self.board[self.core, self.me] = piece.astype(BF16)
+        for place in range(self.size):
+            @pl.when(self.direct(place))
+            def _():
+                self.spread(place, self.me).start()
+
+        self.over(self.core, self.me).start()
+
+    def arrive(self, place):
+        @pl.when(place != self.me)
+        def _():
+            self.spread(place, place).wait_recv()
+
+        for via, source, target in self.relays:
+            @pl.when((self.me == via) & (place == source))
+            def _():
+                self.passed(source, target).start()
+
+        @pl.when(place != self.me)
+        def _():
+            self.over(self.core, place).start()
+
+    def arrive_over(self, place):
+        self.over(self.sibling, place).wait_recv()
+
+    def unpack(self, out, tree):
+        rows = self.rows
+
+        @pl.loop(0, self.half // CHUNK)
+        def _(step):
+            at = pl.multiple_of(step * CHUNK, CHUNK)
+            blocks = [
+                self.board[tree, place, :, pl.ds(at, CHUNK)].astype(F32)
+                for place in range(self.size)
+            ]
+            for side in range(2):
+                whole = [block[side * rows : (side + 1) * rows] for block in blocks]
+                out[tree, :, pl.ds(side * self.half + at, CHUNK)] = jnp.concatenate(
+                    whole, axis=0
+                ).astype(BF16)
+
+    def unpack_place(self, out, place):
+        rows = self.rows
+
+        @pl.loop(0, self.half // CHUNK)
+        def _(step):
+            at = pl.multiple_of(step * CHUNK, CHUNK)
+            blocks = [self.board[tree, place, :, pl.ds(at, CHUNK)].astype(F32) for tree in range(2)]
+            for side in range(2):
+                whole = [block[side * rows : (side + 1) * rows] for block in blocks]
+                out[place, :, pl.ds(side * self.half + at, CHUNK)] = jnp.concatenate(
+                    whole, axis=0
+                ).astype(BF16)
+
+    def complete(self, out):
+        for place in range(self.size):
+            self.arrive(place)
+        self.unpack(out, self.core)
+        for place in range(self.size):
+            self.arrive_over(place)
+        self.unpack(out, self.sibling)
+
+    def finish(self):
+        for place in range(self.size):
+            @pl.when(self.direct(place))
+            def _():
+                self.spread(place, self.me).wait_send()
+
+            self.over(self.core, place).wait_send()
+
+        for via, source, target in self.relays:
+            @pl.when(self.me == via)
+            def _():
+                self.passed(source, target).wait_send()
+
+
+class Scatterer:
+    def __init__(self, axis, rows, half):
+        self.axis, self.rows, self.half = axis, rows, half
+        self.size = size = lax.axis_size(axis)
+        self.scratch = [pltpu.VMEM((size, 2 * rows, half), BF16)] * 4
+        self.scratch += [pltpu.VMEM((2 * rows, half), F32)] + [SEM((size,))] * 4
+
+    def bind(self, refs):
+        self.to_sib, self.from_sib, self.to_peer, self.from_peer, self.total = refs[:5]
+        self.sib_send, self.sib_recv, self.peer_send, self.peer_recv = refs[5:]
+        self.core = lax.axis_index("section")
+        self.sibling = 1 - self.core
+        self.me = lax.axis_index(self.axis)
+
+    def over(self, place):
+        return remote(
+            self.to_sib.at[place], self.from_sib.at[place], self.sib_send.at[place],
+            self.sib_recv.at[place], {"section": self.sibling},
+        )
+
+    def spread(self, place, slot):
+        return remote(
+            self.to_peer.at[place], self.from_peer.at[slot], self.peer_send.at[place],
+            self.peer_recv.at[slot], {self.axis: place},
+        )
+
+    def over_columns(self, body):
+        @pl.loop(0, self.half // CHUNK)
+        def _(step):
+            body(pl.multiple_of(step * CHUNK, CHUNK))
+
+    def absorb(self, place, mine):
+        self.over(place).wait_recv()
+
+        def add(at):
+            both = mine(at) + self.from_sib[place, :, pl.ds(at, CHUNK)].astype(F32)
+            self.to_peer[place, :, pl.ds(at, CHUNK)] = both.astype(BF16)
+
+            @pl.when(place == self.me)
+            def _():
+                self.total[:, pl.ds(at, CHUNK)] = both
+
+        self.over_columns(add)
+
+        @pl.when(place != self.me)
+        def _():
+            self.spread(place, self.me).start()
+
+    def collect(self):
+        for place in range(self.size):
+            @pl.when(place != self.me)
+            def _():
+                self.spread(place, place).wait_recv()
+                self.total[...] += self.from_peer[place].astype(F32)
+
+        total = self.total[...]
+        return jnp.concatenate([total[: self.rows], total[self.rows :]], axis=1)
+
+    def finish(self):
+        for place in range(self.size):
+            self.over(place).wait_send()
+
+            @pl.when(place != self.me)
+            def _():
+                self.spread(place, self.me).wait_send()
+
+
+class RowScatterer(Scatterer):
     def packed(self, tree, place, at):
         rows = self.rows
         low = rows * place // 16 * 16
@@ -766,14 +915,8 @@
         ]
         return jnp.concatenate(parts, axis=0)
 
-    def over_columns(self, step_body):
-        @pl.loop(0, self.half // CHUNK)
-        def _(step):
-            step_body(pl.multiple_of(step * CHUNK, CHUNK))
-
-    def prepare(self):
-        if not self.scatter:
-            return
+    def prepare(self, terms):
+        self.terms = terms
         for place in range(self.size):
             def pack(at):
                 self.to_sib[place, :, pl.ds(at, CHUNK)] = self.packed(
@@ -782,127 +925,268 @@
 
             self.over_columns(pack)
 
-    def sib_copy(self, place):
-        return remote(
-            self.to_sib.at[place], self.from_sib.at[place], self.sib_send.at[place],
-            self.sib_recv.at[place], {"section": self.sibling},
-        )
-
-    def peer_copy(self, place, slot):
-        return remote(
-            self.to_peer.at[place], self.from_peer.at[slot], self.peer_send.at[place],
-            self.peer_recv.at[slot], {self.scatter: place},
-        )
-
-    def spread(self, index, place, slot):
-        board, send, recv, _, _ = self.boards[index]
-        return remote(
-            board.at[self.core, slot], board.at[self.core, slot], send.at[place], recv.at[slot],
-            {self.gathers[index]: place},
-        )
-
-    def relay(self, index, tree, slot):
-        board, _, _, send, recv = self.boards[index]
-        return remote(
-            board.at[tree, slot], board.at[tree, slot], send.at[slot], recv.at[slot],
-            {"section": self.sibling},
-        )
-
     def start(self):
-        if self.scatter:
-            for place in range(self.size):
-                self.sib_copy(place).start()
+        for place in range(self.size):
+            self.over(place).start()
 
     def summed(self):
         for place in range(self.size):
-            self.sib_copy(place).wait_recv()
-
-            def add(at):
-                both = self.packed(self.core, place, at)
-                both += self.from_sib[place, :, pl.ds(at, CHUNK)].astype(F32)
-                self.to_peer[place, :, pl.ds(at, CHUNK)] = both.astype(BF16)
-
-                @pl.when(place == self.me)
-                def _():
-                    self.total[:, pl.ds(at, CHUNK)] = both
-
-            self.over_columns(add)
-
-            @pl.when(place != self.me)
-            def _():
-                self.peer_copy(place, self.me).start()
-
-        for place in range(self.size):
-            @pl.when(place != self.me)
-            def _():
-                self.peer_copy(place, place).wait_recv()
-                self.total[...] += self.from_peer[place].astype(F32)
-
-        total = self.total[...]
-        return jnp.concatenate([total[: self.rows], total[self.rows :]], axis=1)
-
-    def unpack(self, index, tree):
-        board, out, rows = self.boards[index][0], self.gathered[index], self.rows
-
-        def step_body(at):
-            blocks = [
-                board[tree, place, :, pl.ds(at, CHUNK)].astype(F32)
-                for place in range(self.sizes[index])
+            self.absorb(place, lambda at: self.packed(self.core, place, at))
+        return self.collect()
+
+
+class Staged(Part):
+    def __init__(self, ins, outs, scratch, helpers):
+        self.in_names, self.out_names, self.scratch_names = list(ins), list(outs), list(scratch)
+        self.ins, self.outs = list(ins.values()), list(outs.values())
+        self.helpers = helpers
+        self.scratch = list(scratch.values())
+        for helper in helpers:
+            self.scratch += helper.scratch
+
+    def bind(self, ins, outs, scratch):
+        scratch = list(scratch)
+        names = self.in_names + self.out_names + self.scratch_names
+        count = len(self.scratch_names)
+        for name, ref in zip(names, list(ins) + list(outs) + scratch[:count]):
+            setattr(self, name, ref)
+        del scratch[:count]
+        for helper in self.helpers:
+            helper.bind(scratch[: len(helper.scratch)])
+            del scratch[: len(helper.scratch)]
+
+    def finish(self):
+        for helper in self.helpers:
+            helper.finish()
+
+
+def vmem_f32(*shape):
+    return (jax.ShapeDtypeStruct(shape, F32), VMEM)
+
+
+def vmem_bf16(*shape):
+    return (jax.ShapeDtypeStruct(shape, BF16), VMEM)
+
+
+class LastHub(Staged):
+    def __init__(self, terms, values, gain, add):
+        rows, depth = values.shape
+        half = depth // 2
+        self.rows_in = RowScatterer("tensor", rows, half)
+        self.rows_out = Gatherer("tensor", rows, half)
+        super().__init__(
+            {"terms": (terms, VMEM), "values": (values, VMEM), "gain": (gain, VMEM), "add": (add, VMEM)},
+            {
+                "gain_grad": vmem_f32(1, depth),
+                "gathered": vmem_bf16(2, self.rows_out.size * rows, depth),
+            },
+            {},
+            [self.rows_in, self.rows_out],
+        )
+
+    def prepare(self):
+        self.rows_in.prepare(self.terms)
+
+    def start(self):
+        self.rows_in.start()
+
+    def run(self):
+        total = self.rows_in.summed()
+        result, self.gain_grad[...] = norm_back(total, self.values[...], self.gain[...])
+        self.rows_out.begin(result + self.add[...])
+        self.rows_out.complete(self.gathered)
+
+
+class FeedForward(Staged):
+    def __init__(self, terms, own, gain, weights, forward, backward, extra):
+        rows, depth = own.shape
+        half = depth // 2
+        units = weights[0].shape[0]
+        self.has_forward, self.has_backward, self.units = forward, backward, units
+        self.depth = depth
+        self.block = 2 * rows
+        self.size = size = lax.axis_size("dp")
+        self.rows_in = RowScatterer("tensor", rows, half)
+        self.spread_in = Gatherer("dp", rows, half)
+        helpers = [self.rows_in, self.spread_in]
+        group_rows = 2 * rows
+        tensor_rows = lax.axis_size("tensor") * rows
+        matrix = pltpu.VMEM((units, depth), BF16)
+        ins = {"terms": (terms, VMEM), "own": (own, VMEM), "gain": (gain, VMEM)}
+        ins |= {name: (w, HBM) for name, w in zip(("gate_hbm", "up_hbm", "down_hbm"), weights)}
+        ins |= {name: (value, VMEM) for name, value in extra.items()}
+        outs = {}
+        scratch = {"w_gate": matrix, "w_up": matrix, "w_down": matrix, "load": SEM((3,))}
+        if forward:
+            outs |= {
+                "middle": vmem_f32(rows, depth),
+                "mlp_in": vmem_bf16(size, group_rows, depth),
+                "hidden": vmem_bf16(size, group_rows, units),
+                "own_out": vmem_f32(rows, depth),
+                "out": vmem_bf16(2, tensor_rows, depth),
+            }
+            self.back = Scatterer("dp", rows, half)
+            self.out_rows = Gatherer("tensor", rows, half)
+            helpers += [self.back, self.out_rows]
+            scratch["kept"] = pltpu.VMEM((group_rows, half), F32)
+        if forward and not backward:
+            outs |= {"gate": vmem_f32(size, group_rows, units), "up": vmem_f32(size, group_rows, units)}
+        if forward and backward:
+            scratch |= {
+                "gate": pltpu.VMEM((size, group_rows, units), F32),
+                "up": pltpu.VMEM((size, group_rows, units), F32),
+            }
+        if backward:
+            outs |= {
+                "grad_gate": vmem_bf16(size, group_rows, units),
+                "grad_up": vmem_bf16(size, group_rows, units),
+                "grad_middle": vmem_f32(rows, depth),
+                "mlp_gain_grad": vmem_f32(1, depth),
+                "grad_attn": vmem_bf16(2, tensor_rows, depth),
+            }
+            self.grad_back = Scatterer("dp", rows, half)
+            self.grad_rows = Gatherer("tensor", rows, half)
+            helpers += [self.grad_back, self.grad_rows]
+            scratch["grad_kept"] = pltpu.VMEM((group_rows, half), F32)
+        if backward and not forward:
+            outs |= {
+                "gain_grad": vmem_f32(1, depth),
+                "incoming": vmem_bf16(2, tensor_rows, depth),
+                "grad_mlp": vmem_bf16(size, group_rows, depth),
+            }
+            scratch["grad_own"] = pltpu.VMEM((rows, depth), F32)
+            self.incoming_rows = Gatherer("tensor", rows, half)
+            helpers += [self.incoming_rows]
+        super().__init__(ins, outs, scratch, helpers)
+
+    def loads(self):
+        pairs = [(self.gate_hbm, self.w_gate), (self.up_hbm, self.w_up), (self.down_hbm, self.w_down)]
+        return [
+            pltpu.make_async_copy(src, dst, self.load.at[i]) for i, (src, dst) in enumerate(pairs)
+        ]
+
+    def prepare(self):
+        for copy in self.loads():
+            copy.start()
+        self.rows_in.prepare(self.terms)
+
+    def start(self):
+        self.rows_in.start()
+
+    def run(self):
+        total = self.rows_in.summed()
+        if self.has_forward:
+            middle = self.own[...] + total
+            self.middle[...] = middle
+            mean_sq = jnp.mean(middle * middle, axis=1, keepdims=True)
+            self.spread_in.begin(middle * lax.rsqrt(mean_sq + EPSILON) * self.gain[...])
+        else:
+            result, self.gain_grad[...] = norm_back(total, self.own[...], self.gain[...])
+            result = (result + self.add[...]).astype(BF16).astype(F32)
+            self.grad_own[...] = result
+            self.spread_in.begin(result)
+            self.incoming_rows.begin(result)
+        for copy in self.loads():
+            copy.wait()
+
+        me = lax.axis_index("dp")
+        turn = 1 - 2 * (me // (self.size // 2))
+
+        @pl.loop(0, self.size)
+        def _(step):
+            place = lax.rem(me + turn * step + self.size, self.size)
+            self.spread_in.arrive(place)
+            self.spread_in.arrive_over(place)
+            if self.has_forward:
+                self.spread_in.unpack_place(self.mlp_in, place)
+                self.forward_place(place)
+            else:
+                self.spread_in.unpack_place(self.grad_mlp, place)
+            if self.has_backward:
+                self.backward_place(place)
+            if self.has_forward:
+                self.back.absorb(place, lambda at: self.kept[:, pl.ds(at, CHUNK)])
+            if self.has_backward:
+                self.grad_back.absorb(place, lambda at: self.grad_kept[:, pl.ds(at, CHUNK)])
+
+        if self.has_forward:
+            output = (self.middle[...] + self.back.collect()).astype(BF16).astype(F32)
+            self.own_out[...] = output
+            if not self.has_backward:
+                self.out_rows.begin(output)
+        if self.has_backward:
+            values = self.middle if self.has_forward else self.middle_in
+            gain = self.gain if self.has_forward else self.mlp_gain
+            result, self.mlp_gain_grad[...] = norm_back(
+                self.grad_back.collect(), values[...], gain[...]
+            )
+            result += self.grad_own[...]
+            self.grad_middle[...] = result
+            self.grad_rows.begin(result)
+            if self.has_forward:
+                self.out_rows.begin(self.own_out[...])
+            self.grad_rows.complete(self.grad_attn)
+        if self.has_forward:
+            self.out_rows.complete(self.out)
+        else:
+            self.incoming_rows.complete(self.incoming)
+
+    def unit_tiles(self, body):
+        tile = 256
+
+        @pl.loop(0, self.units // tile)
+        def _(step):
+            body(pl.ds(pl.multiple_of(step * tile, tile), tile))
+
+    def forward_place(self, place):
+        def tile(at):
+            rows = self.mlp_in[place]
+            gate = dot_inner(rows, self.w_gate[at, :])
+            up = dot_inner(rows, self.w_up[at, :])
+            self.gate[place, :, at] = gate
+            self.up[place, :, at] = up
+            self.hidden[place, :, at] = (gate * jax.nn.sigmoid(gate) * up).astype(BF16)
+
+        self.unit_tiles(tile)
+        self.terms_out(
+            place, self.back, self.kept, lambda at: dot(self.hidden[place], self.w_down[:, at])
+        )
+
+    def backward_place(self, place):
+        def tile(at):
+            grad_hidden = dot_inner(self.grad_mlp[place], self.w_down[at, :])
+            gate, up = self.gate[place, :, at], self.up[place, :, at]
+            share = jax.nn.sigmoid(gate)
+            act = gate * share
+            self.grad_up[place, :, at] = (grad_hidden * act).astype(BF16)
+            self.grad_gate[place, :, at] = (
+                grad_hidden * up * (share + act * (1.0 - share))
+            ).astype(BF16)
+
+        self.unit_tiles(tile)
+        self.terms_out(
+            place, self.grad_back, self.grad_kept,
+            lambda at: dot(self.grad_gate[place], self.w_gate[:, at])
+            + dot(self.grad_up[place], self.w_up[:, at]),
+        )
+
+    def terms_out(self, place, scatterer, kept, product):
+        rows, half = self.block // 2, self.depth // 2
+        first = lax.axis_index("section") == 0
+
+        @pl.loop(0, half // CHUNK)
+        def _(step):
+            low = pl.multiple_of(step * CHUNK, CHUNK)
+            sides = [product(pl.ds(side * half + low, CHUNK)) for side in range(2)]
+            trees = [
+                jnp.concatenate([side[tree * rows : (tree + 1) * rows] for side in sides], axis=0)
+                for tree in range(2)
             ]
-            for side in range(2):
-                whole = [block[side * rows : (side + 1) * rows] for block in blocks]
-                out[tree, :, pl.ds(side * self.half + at, CHUNK)] = jnp.concatenate(
-                    whole, axis=0
-                ).astype(BF16)
-
-        self.over_columns(step_body)
-
-    def run(self):
-        total = self.summed() if self.scatter else None
-        result = self.body(total, self.args, self.own_outs)
-        half = self.half
-        piece = jnp.concatenate([result[:, :half], result[:, half:]], axis=0).astype(BF16)
-        places = [lax.axis_index(axis) for axis in self.gathers]
-        for index, size in enumerate(self.sizes):
-            self.boards[index][0][self.core, places[index]] = piece
-            for place in range(size):
-                @pl.when(place != places[index])
-                def _():
-                    self.spread(index, place, places[index]).start()
-
-            self.relay(index, self.core, places[index]).start()
-
-        for index, size in enumerate(self.sizes):
-            for place in range(size):
-                @pl.when(place != places[index])
-                def _():
-                    self.spread(index, place, place).wait_recv()
-                    self.relay(index, self.core, place).start()
-
-        for index in range(len(self.sizes)):
-            self.unpack(index, self.core)
-        for index, size in enumerate(self.sizes):
-            for place in range(size):
-                self.relay(index, self.sibling, place).wait_recv()
-            self.unpack(index, self.sibling)
-
-    def finish(self):
-        if self.scatter:
-            for place in range(self.size):
-                self.sib_copy(place).wait_send()
-
-                @pl.when(place != self.me)
-                def _():
-                    self.peer_copy(place, self.me).wait_send()
-
-        for index, size in enumerate(self.sizes):
-            me = lax.axis_index(self.gathers[index])
-            for place in range(size):
-                self.relay(index, self.core, place).wait_send()
-
-                @pl.when(place != me)
-                def _():
-                    self.spread(index, place, me).wait_send()
+            at = pl.ds(low, CHUNK)
+            kept[:, at] = jnp.where(first, trees[0], trees[1])
+            scatterer.to_sib[place, :, at] = jnp.where(first, trees[1], trees[0]).astype(BF16)
+
+        scatterer.over(place).start()
 
 
 def hub_plain(terms, own_args, body, own_outs, scatter, gathers):
@@ -925,56 +1209,35 @@
     return [cell.value for cell in cells] + gathered
 
 
-def gather_kv(own, cargo, fast, collective_id):
-    trees, rows, width = own.shape
-    if not fast:
-        return lax.all_gather(own, "dp", axis=1, tiled=True), []
-    whole, *outs = fused(
-        cargo + [GatherKV(own)], ["section", "dp"], bool(cargo), collective_id, 30
-    )[::-1]
-    return whole[0].reshape(trees, -1, width), outs[::-1]
-
-
-def scatter_kv(whole, cargo, fast, collective_id):
-    trees, all_rows, width = whole.shape
-    size = lax.axis_size("dp")
-    if not fast:
-        return lax.psum_scatter(whole, "dp", scatter_dimension=1, tiled=True).astype(F32), []
-    part = ScatterKV(whole.reshape(trees, size, all_rows // size, width))
-    total, *outs = fused(cargo + [part], ["section", "dp"], bool(cargo), collective_id, 30)[::-1]
-    return total[0], outs[::-1]
-
-
-def meet(terms, own_args, body, own_outs, scatter, gathers, cargo, fast, collective_id):
-    if not fast:
-        return hub_plain(terms, own_args, body, own_outs, scatter, gathers), []
-    axes = ["section"] + sorted(set(gathers) | {scatter} | ({"dp"} if cargo else set()))
-    part = Hub(terms, own_args, body, own_outs, scatter, gathers)
-    outs, *others = fused(cargo + [part], axes, bool(cargo), collective_id, 50)[::-1]
-    return outs, others[::-1]
+def with_cargo(part, cargo, axes, collective_id, cost_us, vmem=40):
+    outs = fused(cargo + [part], axes, bool(cargo), collective_id, cost_us, vmem)
+    return outs[-1], outs[:-1]
+
+
+def norm_back(total, values, gain):
+    scale = lax.rsqrt(jnp.mean(values * values, axis=1, keepdims=True) + EPSILON)
+    unit = values * scale
+    gain_grad = jnp.sum(total * unit, axis=0, keepdims=True)
+    scaled = total * gain
+    along = jnp.mean(scaled * unit, axis=1, keepdims=True)
+    return ((scaled - unit * along) * scale, gain_grad)
 
 
 def norm_body(total, args, outs):
-    middle = args[0][...] + total
+    middle = args[0] + total
     outs[0][...] = middle
-    mean_sq = jnp.mean(middle * middle, axis=1, keepdims=True)
-    return middle * lax.rsqrt(mean_sq + EPSILON) * args[1][...]
+    return rms_scale(middle, args[1])
 
 
 def add_body(total, args, outs):
-    result = args[0][...] + total
+    result = args[0] + total
     outs[0][...] = result
     return result
 
 
 def norm_back_body(total, args, outs):
-    values, gain = args[0][...], args[1][...]
-    scale = lax.rsqrt(jnp.mean(values * values, axis=1, keepdims=True) + EPSILON)
-    unit = values * scale
-    outs[1][...] = jnp.sum(total * unit, axis=0, keepdims=True)
-    scaled = total * gain
-    along = jnp.mean(scaled * unit, axis=1, keepdims=True)
-    result = (scaled - unit * along) * scale + args[2][...]
+    result, outs[1][...] = norm_back(total, args[0], args[1])
+    result += args[2]
     outs[0][...] = result
     return result
 
@@ -988,10 +1251,9 @@
     )
 
 
-def layer_forward(hidden_in, own_in, weights, gains, slot, cargo, fast, ids):
-    attn_scale, mlp_scale, q_scale, k_scale = gains
-    w_qkv, w_outt, w_gate, w_up, w_down = weights
-    carried = []
+def attn_forward(hidden_in, weights, gains, slot, gather):
+    attn_scale, _, q_scale, k_scale = gains
+    w_qkv, w_outt = weights[:2]
     allowed, cos_table, sine_table = slot
     trees, row_count, depth = hidden_in.shape
     q_width = w_outt.shape[1]
@@ -1002,10 +1264,7 @@
     value_bf = qkv[:, :, q_width + HD :].astype(BF16)
     queries, keys_rot = embed(q_pre, k_pre, q_scale, k_scale, cos_table, sine_table)
     query_bf = queries.astype(BF16)
-    kv_all, outs = gather_kv(
-        jnp.concatenate([keys_rot.astype(BF16), value_bf], axis=2), cargo(0), fast, ids[0]
-    )
-    carried += outs
+    kv_all = gather(jnp.concatenate([keys_rot.astype(BF16), value_bf], axis=2))
     key_all = kv_all[:, :, :HD]
     value_all = kv_all[:, :, HD:]
     scores = masked_scores(query_bf, key_all, allowed)
@@ -1016,51 +1275,18 @@
     log_total = row_max + jnp.log(row_total)
     attended = jnp.einsum("bgrt,btd->brgd", prob_bf, value_all, preferred_element_type=F32)
     attended_bf = attended.reshape(trees * row_count, -1).astype(BF16)
-    attn_partial = dot_inner(attended_bf, w_outt).astype(BF16).reshape(trees, row_count, depth)
-    own_shape = own_in.shape
-    (middle, mlp_in), outs = meet(
-        attn_partial, [own_in, mlp_scale[None]], norm_body, [own_shape], "tensor", ["dp"],
-        cargo(1), fast, ids[1],
-    )
-    carried += outs
-    mlp_in = mlp_in.reshape(-1, depth)
-    gate_pre = dot_inner(mlp_in, w_gate)
-    upward = dot_inner(mlp_in, w_up)
-    hidden_bf = swiglu(gate_pre, upward).astype(BF16)
-    mlp_partial = dot(hidden_bf, w_down).astype(BF16).reshape(trees, -1, depth)
-    (output_own, output_bf), outs = meet(
-        mlp_partial, [middle], add_body, [own_shape], "dp", ["tensor"], cargo(2), fast, ids[2]
-    )
-    carried += outs
-    stored = (
-        own_in, normed, q_pre, k_pre, query_bf, key_all, value_all, log_total, attended_bf,
-        middle, mlp_in, gate_pre, upward, hidden_bf,
-    )
-    return (output_bf, output_own.astype(BF16).astype(F32), stored, carried)
-
-
-def layer_backward(grad_own, grad_mlp, stored, weights, gains, slot, shared_kv, is_first, cargo, fast, ids):
-    attn_scale, mlp_scale, q_scale, k_scale = gains
-    w_qkv, w_outt, w_gate, w_up, w_down = weights
+    terms = dot_inner(attended_bf, w_outt).astype(BF16).reshape(trees, row_count, depth)
+    saved = (normed, q_pre, k_pre, query_bf, key_all, value_all, log_total, attended_bf)
+    return (terms, saved)
+
+
+def attn_backward(grad_attn, saved, weights, gains, slot, scatter):
+    _, _, q_scale, k_scale = gains
+    w_qkv, w_outt = weights[:2]
     allowed, cos_table, sine_table = slot
-    (
-        own_in, normed, q_pre, k_pre, query_bf, key_all, value_all, log_total, attended_bf,
-        middle, mlp_in, gate_pre, upward, hidden_bf,
-    ) = stored
+    normed, q_pre, k_pre, query_bf, key_all, value_all, log_total, attended_bf = saved
     trees, row_count = query_bf.shape[:2]
     depth = normed.shape[1]
-    grad_hidden = dot_inner(grad_mlp, w_down)
-    _, swiglu_pull = jax.vjp(swiglu, gate_pre, upward)
-    grad_gate, grad_upward = swiglu_pull(grad_hidden)
-    gate_bf = grad_gate.astype(BF16)
-    up_bf = grad_upward.astype(BF16)
-    mlp_partial = (dot(gate_bf, w_gate) + dot(up_bf, w_up)).astype(BF16)
-    own_outs = [own_in.shape, (1, depth)]
-    (grad_middle, grad_mlp_scale, grad_attn), carried = meet(
-        mlp_partial.reshape(trees, -1, depth),
-        [middle, mlp_scale[None], grad_own],
-        norm_back_body, own_outs, "dp", ["tensor"], cargo(0), fast, ids[0],
-    )
     grad_attn = grad_attn.reshape(-1, depth)
     grad_heads = dot(grad_attn, w_outt).astype(BF16).reshape(query_bf.shape)
     scores = masked_scores(query_bf, key_all, allowed)
@@ -1080,15 +1306,7 @@
     grad_value_all = jnp.einsum(
         "bgrt,brgd->btd", prob_full.astype(BF16), grad_heads, preferred_element_type=F32
     )
-    grad_kv, outs = scatter_kv(
-        jnp.concatenate([grad_key_all, grad_value_all], axis=2).astype(BF16),
-        cargo(1), fast, ids[1],
-    )
-    carried += outs
-    grad_kv = grad_kv.astype(BF16)
-    if shared_kv:
-        total = lax.psum(grad_kv, "section")
-        grad_kv = jnp.where(lax.axis_index("section") == 0, total, jnp.zeros_like(total))
+    grad_kv = scatter(jnp.concatenate([grad_key_all, grad_value_all], axis=2).astype(BF16))
     _, embedding_pull = jax.vjp(
         partial(embed, cos_table=cos_table, sine_table=sine_table), q_pre, k_pre, q_scale, k_scale
     )
@@ -1099,28 +1317,72 @@
         [
             grad_q_pre.astype(BF16).reshape(trees, row_count, -1),
             grad_k_pre.astype(BF16),
-            grad_kv[:, :, HD:],
+            grad_kv[:, :, HD:].astype(BF16),
         ],
         axis=2,
     ).reshape(trees * row_count, -1)
-    attn_partial = dot_inner(qkv_grad, w_qkv).astype(BF16).reshape(trees, row_count, depth)
-    gathers = ["tensor"] if is_first else ["tensor", "dp"]
-    (incoming_own, grad_attn_scale, *gathered), outs = meet(
-        attn_partial, [own_in, attn_scale[None], grad_middle],
-        norm_back_body, own_outs, "tensor", gathers, cargo(2), fast, ids[2],
-    )
-    carried += outs
-    products = (
-        (normed, qkv_grad),
-        (grad_attn, attended_bf),
-        (gate_bf, mlp_in),
-        (up_bf, mlp_in),
-        (hidden_bf, grad_mlp),
-    )
-    gain_grads = jnp.concatenate(
-        [grad_attn_scale[0], grad_mlp_scale[0], grad_q_scale, grad_k_scale]
-    )
-    return (gathered, incoming_own.astype(BF16).astype(F32), products, gain_grads, carried)
+    terms = dot_inner(qkv_grad, w_qkv).astype(BF16).reshape(trees, row_count, depth)
+    return (terms, [(normed, qkv_grad), (grad_attn, attended_bf)], [grad_q_scale, grad_k_scale])
+
+
+def plain_layers(hidden, own_in, grad_own, weights, gains, slot, shared_kv):
+    depth = own_in.shape[1]
+    own_shape = own_in.shape
+
+    def gather(own):
+        return lax.all_gather(own, "dp", axis=1, tiled=True)
+
+    def scatter(whole):
+        total = lax.psum_scatter(whole, "dp", scatter_dimension=1, tiled=True)
+        if shared_kv:
+            total = lax.psum(total, "section")
+            total = jnp.where(lax.axis_index("section") == 0, total, jnp.zeros_like(total))
+        return total
+
+    outputs, kept = [], []
+    for layer in range(2):
+        _, _, w_gate, w_up, w_down = weights[layer]
+        terms, saved = attn_forward(hidden, weights[layer], gains[layer], slot, gather)
+        mlp_scale = gains[layer][1][None]
+        middle, mlp_in = hub_plain(
+            terms, [own_in, mlp_scale], norm_body, [own_shape], "tensor", ["dp"]
+        )
+        mlp_in = mlp_in.reshape(-1, depth)
+        gate, up = dot_inner(mlp_in, w_gate), dot_inner(mlp_in, w_up)
+        hidden_bf = swiglu(gate, up).astype(BF16)
+        terms = dot(hidden_bf, w_down).astype(BF16).reshape(2, -1, depth)
+        kept.append((own_in, saved, middle, mlp_in, gate, up, hidden_bf))
+        own_in, hidden = hub_plain(terms, [middle], add_body, [own_shape], "dp", ["tensor"])
+        own_in = own_in.astype(BF16).astype(F32)
+        outputs.append(hidden)
+
+    own_outs = [own_shape, (1, depth)]
+    grads, products, gain_grads = [None, None], [None, None], [None, None]
+    (grad_mlp,) = hub_plain(None, [grad_own], lambda total, args, outs: args[0], [], None, ["dp"])
+    for layer in (1, 0):
+        _, _, w_gate, w_up, w_down = weights[layer]
+        own_in, saved, middle, mlp_in, gate, up, hidden_bf = kept[layer]
+        grad_mlp = grad_mlp.reshape(-1, depth)
+        _, pull = jax.vjp(swiglu, gate, up)
+        grad_gate, grad_up = (item.astype(BF16) for item in pull(dot_inner(grad_mlp, w_down)))
+        terms = (dot(grad_gate, w_gate) + dot(grad_up, w_up)).astype(BF16).reshape(2, -1, depth)
+        grad_middle, mlp_gain_grad, grad_attn = hub_plain(
+            terms, [middle, gains[layer][1][None], grad_own], norm_back_body, own_outs, "dp",
+            ["tensor"],
+        )
+        terms, pairs, head_grads = attn_backward(
+            grad_attn, saved, weights[layer], gains[layer], slot, scatter
+        )
+        grad_own, gain_grad, grads[layer], grad_next = hub_plain(
+            terms, [own_in, gains[layer][0][None], grad_middle], norm_back_body, own_outs, "tensor",
+            ["tensor", "dp"],
+        )
+        grad_own = grad_own.astype(BF16).astype(F32)
+        pairs += [(grad_gate, mlp_in), (grad_up, mlp_in), (hidden_bf, grad_mlp)]
+        products[layer] = pairs
+        gain_grads[layer] = jnp.concatenate([gain_grad[0], mlp_gain_grad[0], *head_grads])
+        grad_mlp = grad_next
+    return (outputs, grads, products, gain_grads)
 
 
 def swap_cores(mine, other):
@@ -1220,7 +1482,6 @@
             pieces = exchange(unit_shards[layer], "dp")
             pieces = pieces.transpose(1, 2, 0, 3).reshape(3, share, depth)
             both_weights.append(attn_of(attn_all) + joint(pieces[:2], pieces[2:]))
-        first_weights = both_weights[0]
 
     gains_all = gains_all.reshape(2, dp_size, -1)
     gains = [
@@ -1250,55 +1511,132 @@
         )
 
     own_in = own_part(hidden).astype(F32)
-    def no_cargo(_):
-        return []
-
-    def next_units(index):
-        return [UnitsOut(unit_blocks[:, :, index : index + 1], 1)] if fast else []
-
-    output, own_in, kept_first, carried = layer_forward(
-        hidden, own_in, first_weights, gains[0], slot, next_units, fast, (3, 4, 5)
-    )
-    outputs, kept = [output], [kept_first]
+    grad_own = own_part(cotangent).astype(F32)
+
+    def weight_products(pairs):
+        return [dot_outer(left, right).astype(BF16) for left, right in pairs]
+
+    def scatter_units(products):
+        return jnp.stack(
+            [lax.psum_scatter(item, "tensor", scatter_dimension=0, tiled=True) for item in products]
+        )
+
+    def scatter_shards(products):
+        return lax.psum_scatter(
+            jnp.concatenate(products, axis=1), "dp", scatter_dimension=0, tiled=True
+        )
+
     if fast:
-        rows = [out[0][0] for out in carried]
-        second_weights = attn_of(attn_next) + tuple(spread_units(item) for item in rows)
+        line = ["section", "dp"]
+        everyone = ["section", "dp", "tensor"]
+
+        def units_on(index):
+            return [UnitsOut(unit_blocks[:, :, index : index + 1], 1)]
+
+        def kv_gather(own, cargo, collective_id, carried):
+            (whole,), outs = with_cargo(GatherKV(own), cargo, line, collective_id, 30)
+            carried += outs
+            return whole.reshape(trees, -1, 2 * HD)
+
+        def kv_scatter(whole, cargo, collective_id, carried):
+            part = ScatterKV(whole.reshape(trees, dp_size, row_count, 2 * HD))
+            (total,), outs = with_cargo(part, cargo, line, collective_id, 30)
+            carried += outs
+            return total
+
+        def flat(array):
+            return array.reshape(-1, array.shape[-1])
+
+        carried = []
+        terms, saved_first = attn_forward(
+            hidden, first_weights, gains[0], slot,
+            lambda own: kv_gather(own, units_on(0), 3, carried),
+        )
+        part = FeedForward(
+            terms, own_in, gains[0][1][None], first_weights[2:], True, False, {}
+        )
+        outs, others = with_cargo(part, units_on(1) + units_on(2), everyone, 4, 90, 56)
+        carried += others
+        middle_first, mlp_in_first, hidden_first, own_next, output_first, gate_first, up_first = outs
+        terms, grad_late = lax.optimization_barrier((terms, grad_own.astype(BF16)))
+        grad_mlp = lax.all_gather(grad_late, "dp", axis=0)
+        grad_mlp = lax.all_gather(grad_mlp, "section", axis=0).transpose(1, 0, 2, 3)
+        grad_mlp = grad_mlp.reshape(dp_size, -1, depth)
+        second_weights = attn_of(attn_next) + tuple(spread_units(out[0][0]) for out in carried)
+        terms, saved_second = attn_forward(
+            output_first, second_weights, gains[1], slot, lambda own: kv_gather(own, [], 5, [])
+        )
+        part = FeedForward(
+            terms, own_next, gains[1][1][None], second_weights[2:], True, True,
+            {"grad_mlp": grad_mlp, "grad_own": grad_own},
+        )
+        outs, _ = with_cargo(part, [], everyone, 6, 100, 60)
+        (
+            middle, mlp_in, hidden_bf, _, output_second,
+            grad_gate, grad_up, grad_middle, mlp_gain_second, grad_attn,
+        ) = outs
+        unit_grad = scatter_units(
+            weight_products(
+                [
+                    (flat(grad_gate), flat(mlp_in)),
+                    (flat(grad_up), flat(mlp_in)),
+                    (flat(hidden_bf), flat(grad_mlp)),
+                ]
+            )
+        )
+        terms, pairs, head_second = attn_backward(
+            grad_attn, saved_second, second_weights, gains[1], slot,
+            lambda whole: kv_scatter(whole, [], 7, []),
+        )
+        attn_second = scatter_shards(weight_products(pairs))
+        part = FeedForward(
+            terms, own_next, gains[1][0][None], first_weights[2:], False, True,
+            {
+                "add": grad_middle, "gate": gate_first, "up": up_first,
+                "middle_in": middle_first, "mlp_gain": gains[0][1][None],
+            },
+        )
+        outs, _ = with_cargo(part, [], everyone, 8, 90, 60)
+        (
+            grad_gate, grad_up, grad_middle, mlp_gain_first, grad_attn,
+            attn_gain_second, incoming_second, grad_mlp,
+        ) = outs
+        unit_home_second = unit_grad
+        unit_grad = scatter_units(
+            weight_products(
+                [
+                    (flat(grad_gate), flat(mlp_in_first)),
+                    (flat(grad_up), flat(mlp_in_first)),
+                    (flat(hidden_first), flat(grad_mlp)),
+                ]
+            )
+        )
+        carried = []
+        terms, pairs, head_first = attn_backward(
+            grad_attn, saved_first, first_weights, gains[0], slot,
+            lambda whole: kv_scatter(whole, [UnitsHome(unit_home_second[:1], 1)], 9, carried),
+        )
+        attn_first = scatter_shards(weight_products(pairs))
+        part = LastHub(terms, own_in, gains[0][0][None], grad_middle)
+        (attn_gain_first, incoming_first), others = with_cargo(
+            part, [UnitsHome(unit_home_second[1:], 1)], everyone, 10, 50
+        )
+        carried += others
+        outputs = [output_first, output_second]
+        grads = [incoming_first, incoming_second]
+        weight_grads = [(attn_first, unit_grad), (attn_second, None)]
+        gain_grads = [
+            jnp.concatenate([attn_gain_first[0], mlp_gain_first[0], *head_first]),
+            jnp.concatenate([attn_gain_second[0], mlp_gain_second[0], *head_second]),
+        ]
     else:
-        second_weights = both_weights[1]
-    output, _, kept_second, _ = layer_forward(
-        output, own_in, second_weights, gains[1], slot, no_cargo, fast, (6, 7, 8)
-    )
-    outputs.append(output)
-    kept.append(kept_second)
-    weights = [first_weights, second_weights]
-
-    grad_own = own_part(cotangent).astype(F32)
-    grad_mlp = lax.all_gather(grad_own.astype(BF16), "dp", axis=0, tiled=True)
-    grad_mlp = lax.all_gather(grad_mlp, "section", axis=0)
-    grads, weight_grads, gain_grads = [None, None], [None, None], [None, None]
-    unit_grad = None
-    for layer in (1, 0):
-        def home_units(index):
-            if not fast or layer == 1 or index == 0:
-                return []
-            return [UnitsHome(unit_grad[:1] if index == 1 else unit_grad[1:], 1)]
-
-        gathered, grad_own, products, gain_grads[layer], carried = layer_backward(
-            grad_own, grad_mlp.reshape(-1, depth), kept[layer], weights[layer], gains[layer], slot,
-            shared_kv, layer == 0, home_units, fast, (9, 10, 11) if layer else (12, 13, 14),
-        )
-        grads[layer], grad_mlp = gathered[0], gathered[-1]
-        whole = [dot_outer(left, right).astype(BF16) for left, right in products]
-        unit_grad = jnp.stack(
-            [
-                lax.psum_scatter(item, "tensor", scatter_dimension=0, tiled=True)
-                for item in whole[2:]
-            ]
-        )
-        attn_grad = lax.psum_scatter(
-            jnp.concatenate(whole[:2], axis=1), "dp", scatter_dimension=0, tiled=True
-        )
-        weight_grads[layer] = (attn_grad, unit_grad)
+        outputs, grads, products, gain_grads = plain_layers(
+            hidden, own_in, grad_own, both_weights, gains, slot, shared_kv
+        )
+        weight_grads = []
+        for pairs in products:
+            whole = weight_products(pairs)
+            weight_grads.append((scatter_shards(whole[:2]), scatter_units(whole[2:])))
 
     gain_total = jnp.stack(gain_grads)
     if fast:
@@ -1306,7 +1644,7 @@
         other = jnp.where(core == 0, weight_grads[1][0], weight_grads[0][0])
         (gain_total,), (arrived,), (first_home,) = fused(
             [TotalOverAll(gain_total.reshape(-1, 128)), Swap(other), UnitsHome(unit_grad, 0)],
-            ["section", "dp", "tensor"], True, 15, 60,
+            everyone, True, 11, 60,
         )
         attn_home = (jnp.where(core == 0, mine, arrived), jnp.where(core == 0, arrived, mine))
         second_home = jnp.concatenate([out[0] for out in carried], axis=0)

time: 1170 us -> 1370 us (1.17)
  waiting for transfers between devices: 6.88 us -> 334 us
  Pallas kernels: 839 us -> 767 us
  matrix products: 144 us -> 98.2 us
    all_gather x6, waiting for transfers between devices: 0.03 us -> 167 us  [spread_units(): return lax.all_gather(rows, 'tensor', axis=0, tiled=True)]
    reduce_scatter x8, waiting for transfers between devices: 4.03 us -> 132 us  [the longest x2 120 us: scatter_shards(): lax.psum_scatter(jnp.concatenate(products, axis=1), 'dp', scatter_dimensi...]
    pallas_call x15 -> x11, Pallas kernels: 839 us -> 767 us  [fused(): pl.pallas_call(kernel, out_shape=[item[0] for item in outs], in_specs=[it...]
    dot_general x10 -> x4, matrix products: 48.2 us -> 12.5 us  [dot_inner(): return lax.dot_general(left, right, INNER, preferred_element_type=F32)]
    all_gather x2, waiting for transfers between devices: 0.02 us -> 32.2 us  [the longest x1 32.2 us: on_device(): grad_mlp = lax.all_gather(grad_late, 'dp', axis=0)]
    dot_general x10 -> x4, matrix products: 30.7 us -> 12.8 us  [dot(): return jnp.dot(left, right, preferred_element_type=F32)]
    unnamed x377 -> x239, local copies, waits for them, and re-layouts: 46 us -> 29.2 us
  transfers between devices with their start and end apart: 17 -> 17, of which waited for: 1 -> 8; matrix products, arithmetic and copies ran while one was open for 18% -> 9% of each run, Pallas kernels for 66% -> 31%
where the time goes in v6:
time: 1370 us; the launch traced here: 1360 us
  Pallas kernels  767 us (56%)
  waiting for transfers between devices  334 us (24%)
  matrix products  98.2 us (7%)
  local copies, waits for them, and re-layouts  79.9 us (6%)
  other arithmetic  62.6 us (5%)
  between operations  20.2 us (1%)
    pallas_call x11, Pallas kernels, fused(): pl.pallas_call(kernel, out_shape=[item[0] for item in outs], in_specs=[it...  767 us
    all_gather x6, waiting for transfers between devices, spread_units(): return lax.all_gather(rows, 'tensor', axis=0, tiled=True)  167 us
    reduce_scatter x2, waiting for transfers between devices, scatter_shards(): lax.psum_scatter(jnp.concatenate(products, axis=1), 'dp', scatter_dimensi...  120 us
    dot_general x10, matrix products, dot_outer(): return lax.dot_general(left, right, OUTER, preferred_element_type=F32)  47.1 us
    all_gather x1, waiting for transfers between devices, on_device(): grad_mlp = lax.all_gather(grad_late, 'dp', axis=0)  32.2 us
    unnamed x239, local copies, waits for them, and re-layouts  29.2 us
  transfers between devices with their start and end apart: 17, of which 8 were waited for; matrix products, arithmetic and copies ran while one was open for 9% of the time, Pallas kernels for 31%

profile of v6, /device:TPU:0, one launch (start us, length us, event | category | flops | bytes accessed | tf_op | source)
XLA Modules:
  0.0 1363.7 jit_solution(582980352670144409)
XLA Ops:
  24.9 2.4 copy-done.1
  27.3 41.3 %shard_map.255 = (bf16[2,192,2048]{2,1,0:T(8,128)(2,1)S(1)}, f32[2,4,10,128]{3,2,1,0:T(8,128)S(1)}) custom-call(bf16[2,4,2,192,512]{4,3,2,1,0:T(8,128)(2,1)S(1)} %copy-done.1, f32[10,128]{1,0:T(8,128)S(1)} %fusion.121.refs_1_), custom_call_target="tpu_custom_call" | custom-call | bytes 135000000 | tf_op jit(solution)/shard_map/pallas_call | solution.py:210
  81.1 2.3 copy.196
  83.3 2.3 copy.197
  90.0 67.1 %shard_map.256 = (bf16[4,4,128,768]{3,2,1,0:T(8,128)(2,1)S(1)}, bf16[1,192,2048]{2,1,0:T(8,128)(2,1)}, bf16[4,128,768]{2,1,0:T(8,128)(2,1)}) custom-call(bf16[2,4,128,768]{3,2,1,0:T(8,128)(2,1)S(1)} %pad_maximum_fusion.4.refs_0_.refs_2_, bf16[2,4,1,192,512]{4,3,2,1,0:T(8,128)(2,1)S(1)} %get-tuple-element.195.refs_1_, ...), custom_call_target="tpu_custom_call" | custom-call | bytes 240000000 | tf_op jit(solution)/shard_map/pallas_call | solution.py:210
  163.3 2.5 multiply_reduce_fusion.3
  167.9 2.3 fusion.34
  170.3 2.3 fusion.35
  175.8 42.5 %shard_map.257 = (bf16[1,192,2048]{2,1,0:T(8,128)(2,1)}, bf16[2,4,288,256]{3,2,1,0:T(8,128)(2,1)S(1)}) custom-call(bf16[2,4,1,192,512]{4,3,2,1,0:T(8,128)(2,1)S(1)} %get-tuple-element.194.refs_0_, bf16[2,288,256]{2,1,0:T(8,128)(2,1)S(1)} %pad_maximum_fusion.14.refs_1_), custom_call_target="tpu_custom_call" | custom-call | bytes 90000000 | tf_op jit(solution)/shard_map/pallas_call | solution.py:210
  223.8 3.6 convolution_convert_fusion.4
  232.0 32.2 %all-gather.32.cloned.1.call-done = bf16[288,2048]{1,0:T(8,128)(2,1)} async-done(((bf16[72,2048]{1,0:T(8,128)(2,1)}), bf16[288,2048]{1,0:T(8,128)(2,1)}) %all-gather.32.cloned.1.call-update) | async-done | bytes 1179664 | tf_op jit(solution)/shard_map/all_gather | solution.py:1562
  267.3 42.5 %all-gather.22.cloned.1.call-done = bf16[1,768,2048]{2,1,0:T(8,128)(2,1)} async-done(((bf16[1,192,2048]{2,1,0:T(8,128)(2,1)}), bf16[1,768,2048]{2,1,0:T(8,128)(2,1)}) %all-gather.22.cloned.1.call-update) | async-done | bytes 3145744 | tf_op jit(solution)/shard_map/all_gather | solution.py:1447
  309.8 46.4 %all-gather.20.cloned.1.call-done = bf16[1,768,2048]{2,1,0:T(8,128)(2,1)} async-done(((bf16[1,192,2048]{2,1,0:T(8,128)(2,1)}), bf16[1,768,2048]{2,1,0:T(8,128)(2,1)}) %all-gather.20.cloned.1.call-update) | async-done | bytes 3145744 | tf_op jit(solution)/shard_map/all_gather | solution.py:1447
  356.2 45.7 %all-gather.24.cloned.1.call-done = bf16[1,768,2048]{2,1,0:T(8,128)(2,1)} async-done(((bf16[1,192,2048]{2,1,0:T(8,128)(2,1)}), bf16[1,768,2048]{2,1,0:T(8,128)(2,1)}) %all-gather.24.cloned.1.call-update) | async-done | bytes 3145744 | tf_op jit(solution)/shard_map/all_gather | solution.py:1447
  401.9 171.7 %shard_map.258 = (bf16[1,192,2048]{2,1,0:T(8,128)(2,1)}, bf16[1,192,2048]{2,1,0:T(8,128)(2,1)}, f32[72,2048]{1,0:T(8,128)}, bf16[4,144,2048]{2,1,0:T(8,128)(2,1)...) custom-call(bf16[2,4,1,192,512]{4,3,2,1,0:T(8,128)(2,1)} %get-tuple-, ...), custom_call_target="tpu_custom_call" | custom-call | bytes 270000000 | tf_op jit(solution)/shard_map/pallas_call | solution.py:210
  574.3 3.4 copy.204
  580.2 4.2 fusion.36
  585.3 28.9 %shard_map.259 = bf16[2,4,288,256]{3,2,1,0:T(8,128)(2,1)S(1)} custom-call(bf16[2,288,256]{2,1,0:T(8,128)(2,1)S(1)} %pad_maximum_fusion.16.refs_0_), custom_call_target="tpu_custom_call" | custom-call | bytes 90000000 | tf_op jit(solution)/shard_map/pallas_call | solution.py:210
  617.4 2.5 multiply_reduce_fusion.2
  628.6 3.6 convolution_convert_fusion.3
  632.2 32.0 %all-gather.30.cloned.1.call-done = bf16[1,768,2048]{2,1,0:T(8,128)(2,1)} async-done(((bf16[1,192,2048]{2,1,0:T(8,128)(2,1)}), bf16[1,768,2048]{2,1,0:T(8,128)(2,1)}) %all-gather.30.cloned.1.call-update) | async-done | bytes 3145744 | tf_op jit(solution)/shard_map/all_gather | solution.py:1447
  664.2 141.7 %shard_map.260 = (f32[72,2048]{1,0:T(8,128)}, bf16[4,144,2048]{2,1,0:T(8,128)(2,1)}, bf16[4,144,768]{2,1,0:T(8,128)(2,1)}, f32[72,2048]{1,0:T(8,128)}, bf16[2,28...) custom-call(bf16[2,288,2048]{2,1,0:T(8,128)(2,1)} %bitcast.362, ...), custom_call_target="tpu_custom_call" | custom-call | bytes 300000000 | tf_op jit(solution)/shard_map/pallas_call | solution.py:210
  805.9 6.3 bitcast_convert_fusion.3
  812.3 6.3 convolution_convert_fusion
  818.7 6.3 bitcast_convert_fusion.4
  826.2 3.6 convolution_convert_fusion.8
  831.6 4.0 fusion.3
  835.7 3.3 fusion.5
  842.1 24.1 %shard_map.261 = f32[2,288,256]{2,1,0:T(8,128)S(1)} custom-call(bf16[2,4,288,256]{3,2,1,0:T(8,128)(2,1)S(1)} %pad_maximum_fusion.6.refs_0_), custom_call_target="tpu_custom_call" | custom-call | bytes 90000000 | tf_op jit(solution)/shard_map/pallas_call | solution.py:210
  871.7 2.8 convolution_convert_fusion.2
  874.5 100.6 %shard_map.262 = (bf16[4,144,768]{2,1,0:T(8,128)(2,1)}, bf16[4,144,768]{2,1,0:T(8,128)(2,1)}, f32[72,2048]{1,0:T(8,128)}, f32[1,2048]{1,0:T(1,128)}, bf16[2,288,...) custom-call(bf16[2,288,2048]{2,1,0:T(8,128)(2,1)} %bitcast.372, ...), custom_call_target="tpu_custom_call" | custom-call | bytes 270000000 | tf_op jit(solution)/shard_map/pallas_call | solution.py:210
  975.1 6.3 bitcast_convert_fusion
  981.5 6.3 bitcast_convert_fusion.1
  987.9 6.6 bitcast_convert_fusion.2
  995.5 2.9 convolution_convert_fusion.6
  1002.7 3.5 convolution_convert_fusion.7
  1008.0 4.0 fusion
  1023.6 40.4 %shard_map.263 = (bf16[1,2,4,192,512]{4,3,2,1,0:T(8,128)(2,1)S(1)}, f32[2,288,256]{2,1,0:T(8,128)S(1)}) custom-call(bf16[1,192,2048]{2,1,0:T(8,128)(2,1)S(1)} %bitcast.342, bf16[2,4,288,256]{3,2,1,0:T(8,128)(2,1)S(1)} %pad_maximum_fusion.7.refs_1_), custom_call_target="tpu_custom_call" | custom-call | bytes 90000000 | tf_op jit(solution)/shard_map/pallas_call | solution.py:210
  1076.1 2.5 convolution_convert_fusion.1
  1078.6 50.6 %shard_map.264 = (bf16[2,2,4,192,512]{4,3,2,1,0:T(8,128)(2,1)S(1)}, f32[1,2048]{1,0:T(1,128)S(1)}, bf16[2,288,2048]{2,1,0:T(8,128)(2,1)S(1)}) custom-call(bf16[2,192,2048]{2,1,0:T(8,128)(2,1)S(1)} %pad_maximum_fusion.5.refs_0_, bf16[2,288,2048]{2,1,0:T(8,128)(2,1)S(1)} %bitcast.337, f32[72,2048]{1,0:T(8,128)S(1)} %copy-done.2, f32[1,2048]{1,0:T(1,128)S(1)} %bitcast.347, ...), custom_call_target="tpu_custom_call" | custom-call | bytes 150000000 | tf_op jit(solution)/shard_map/pallas_call | solution.py:210
  1132.5 12.3 reduce-scatter.19.cloned.1.call-done
  1149.5 57.7 %reduce-scatter.15.cloned.1.call-done = bf16[512,768]{1,0:T(8,128)(2,1)} async-done(((bf16[2048,768]{1,0:T(8,128)(2,1)}), bf16[512,768]{1,0:T(8,128)(2,1)}) %reduce-scatter.15.cloned.1.call-update) | async-done | bytes 786448 | tf_op jit(solution)/shard_map/reduce_scatter | solution.py:1525
  1207.2 62.4 %reduce-scatter.17.cloned.1.call-done = bf16[512,768]{1,0:T(8,128)(2,1)} async-done(((bf16[2048,768]{1,0:T(8,128)(2,1)}), bf16[512,768]{1,0:T(8,128)(2,1)}) %reduce-scatter.17.cloned.1.call-update) | async-done | bytes 786448 | tf_op jit(solution)/shard_map/reduce_scatter | solution.py:1525
  1271.0 58.5 %shard_map.265 = (f32[68,128]{1,0:T(8,128)S(1)}, bf16[512,768]{1,0:T(8,128)(2,1)S(1)}, bf16[3,2,4,192,512]{4,3,2,1,0:T(8,128)(2,1)S(1)}) custom-call(f32[68,128]{1,0:T(8,128)S(1)} %reshape.627.refs_0_, bf16[512,768]{1,0:T(8,128)(2,1)S(1)} %broadcast_select_fusion.3.refs_1_, bf16[3,192,2048]{2,1,0:T(8,128)(2,1)S(1)} %pad_maximum_fusion.3.refs_2_), custom_call_target="tpu_custom_call" | custom-call | bytes 180000000 | tf_op jit(solution)/shard_map/pallas_call | solution.py:210
  1333.6 3.5 maximum_select_fusion
  1340.5 2.2 bitcast_convert_fusion.7
  1343.3 2.4 copy.222
  1347.5 2.4 copy.221
  (423 shorter events, 138.3 us)
Async XLA Ops:
  7.2 257.1 %all-gather.32.cloned.1.call-start = ((), (), s32[]{:S(2)}) async-start(), calls=%async_computation.23 | async-start | bytes 1474560 | tf_op jit(solution)/shard_map/all_gather | solution.py:1562
  24.8 65.1 %copy-start = (bf16[2,4,1,192,512]{4,3,2,1,0:T(8,128)(2,1)}, bf16[2,4,1,192,512]{4,3,2,1,0:T(8,128)(2,1)S(1)}, u32[]{:S(2)}) copy-start(bf16[2,4,1,192,512]{4,3,2,1,0:T(8,128)(2,1)S(1)} %get-tuple-element.195.refs_1_) | copy-start | bytes 4718596
  87.5 69.5 %copy-start.17 = (bf16[1,288,2048]{2,1,0:T(8,128)(2,1)}, bf16[1,288,2048]{2,1,0:T(8,128)(2,1)S(1)}, u32[]{:S(2)}) copy-start(bf16[1,288,2048]{2,1,0:T(8,128)(2,1)S(1)} %get-tuple-element.199) | copy-start | bytes 3538948
  87.6 69.5 %copy-start.20 = (bf16[1,288,2048]{2,1,0:T(8,128)(2,1)}, bf16[1,288,2048]{2,1,0:T(8,128)(2,1)S(1)}, u32[]{:S(2)}) copy-start(bf16[1,288,2048]{2,1,0:T(8,128)(2,1)S(1)} %get-tuple-element.200) | copy-start | bytes 3538948
  88.2 68.9 %copy-start.97 = (f32[2,288]{1,0:T(2,128)}, f32[2,288]{1,0:T(2,128)S(1)}, u32[]{:S(2)}) copy-start(f32[2,288]{1,0:T(2,128)S(1)} %add_rsqrt_fusion.1) | copy-start | bytes 6916
  90.0 67.1 %copy-start.95 = (f32[1,4,4,128]{3,1,2,0:T(4,128)}, f32[1,4,4,128]{3,1,2,0:T(4,128)S(1)}, u32[]{:S(2)}) copy-start(f32[1,4,4,128]{3,1,2,0:T(4,128)S(1)} %copy.242) | copy-start | bytes 24580
  158.7 15.1 %copy-start.47 = (f32[2,288,512]{2,1,0:T(8,128)}, f32[2,288,512]{2,1,0:T(8,128)S(1)}, u32[]{:S(2)}) copy-start(f32[2,288,512]{2,1,0:T(8,128)S(1)} %fusion.38) | copy-start | bytes 3538948
  158.7 9.2 copy-start.101
  167.9 5.9 copy-start.88
  173.8 45.1 %copy-start.71 = (pred[2,288,1152]{2,1,0:T(8,128)(4,1)}, pred[2,288,1152]{2,1,0:T(8,128)(4,1)S(1)}, u32[]{:S(2)}) copy-start(pred[2,288,1152]{2,1,0:T(8,128)(4,1)S(1)} %pad_add_fusion) | copy-start | bytes 1990660
  175.1 43.2 %copy-start.90 = (f32[128]{0:T(128)S(1)}, f32[128]{0:T(128)}, u32[]{:S(2)}) copy-start(f32[128]{0:T(128)} %get-tuple-element.249) | copy-start | bytes 1540
  175.3 43.5 %copy-start.25 = (f32[2,288,64]{2,1,0:T(8,128)}, f32[2,288,64]{2,1,0:T(8,128)S(1)}, u32[]{:S(2)}) copy-start(f32[2,288,64]{2,1,0:T(8,128)S(1)} %get-tuple-element.235) | copy-start | bytes 442372
  175.3 43.5 %copy-start.27 = (f32[2,288,64]{2,1,0:T(8,128)}, f32[2,288,64]{2,1,0:T(8,128)S(1)}, u32[]{:S(2)}) copy-start(f32[2,288,64]{2,1,0:T(8,128)S(1)} %get-tuple-element.236) | copy-start | bytes 442372
  223.8 5.6 copy-start.9
  229.3 80.5 %all-gather.22.cloned.1.call-start = ((), (), s32[]{:S(2)}) async-start(), calls=%async_computation.18 | async-start | bytes 3932160 | tf_op jit(solution)/shard_map/all_gather | solution.py:1447
  230.7 35.0 %copy-start.86 = (f32[1,1,4,512]{3,2,1,0:T(4,128)S(1)}, f32[1,1,4,512]{3,2,1,0:T(4,128)}, u32[]{:S(2)}) copy-start(f32[1,1,4,512]{3,2,1,0:T(4,128)} %get-tuple-element.245) | copy-start | bytes 24580
  230.7 35.6 %copy-start.18 = (bf16[1,288,2048]{2,1,0:T(8,128)(2,1)S(1)}, bf16[1,288,2048]{2,1,0:T(8,128)(2,1)}, u32[]{:S(2)}) copy-start(bf16[1,288,2048]{2,1,0:T(8,128)(2,1)} %copy-done.17) | copy-start | bytes 3538948
  230.7 125.6 %all-gather.20.cloned.1.call-start = ((), (), s32[]{:S(2)}) async-start(), calls=%async_computation.17 | async-start | bytes 3932160 | tf_op jit(solution)/shard_map/all_gather | solution.py:1447
  231.4 170.5 %all-gather.24.cloned.1.call-start = ((), (), s32[]{:S(2)}) async-start(), calls=%async_computation.19 | async-start | bytes 3932160 | tf_op jit(solution)/shard_map/all_gather | solution.py:1447
  232.0 342.3 %all-gather.34.cloned.1.call-start = ((), (), s32[]{:S(2)}) async-start(), calls=%async_computation.24 | async-start | bytes 3538944 | tf_op jit(solution)/shard_map/all_gather | solution.py:1563
  264.3 315.9 %all-gather.18.cloned.1.call-start = ((), (), s32[]{:S(2)}) async-start(), calls=%async_computation.8 | async-start | bytes 3932160 | tf_op jit(solution)/shard_map/all_gather | solution.py:1473
  264.9 367.3 %all-gather.26.cloned.1.call-start = ((), (), s32[]{:S(2)}) async-start(), calls=%async_computation.20 | async-start | bytes 3932160 | tf_op jit(solution)/shard_map/all_gather | solution.py:1447
  265.6 366.6 %all-gather.28.cloned.1.call-start = ((), (), s32[]{:S(2)}) async-start(), calls=%async_computation.21 | async-start | bytes 3932160 | tf_op jit(solution)/shard_map/all_gather | solution.py:1447
  401.9 171.8 %copy-start.85 = (f32[1,1,4,512]{3,2,1,0:T(4,128)S(1)}, f32[1,1,4,512]{3,2,1,0:T(4,128)}, u32[]{:S(2)}) copy-start(f32[1,1,4,512]{3,2,1,0:T(4,128)} %get-tuple-element.243) | copy-start | bytes 24580
  401.9 172.4 %copy-start.84 = (f32[1,4,4,128]{3,2,1,0:T(4,128)S(1)}, f32[1,4,4,128]{3,2,1,0:T(4,128)}, u32[]{:S(2)}) copy-start(f32[1,4,4,128]{3,2,1,0:T(4,128)} %get-tuple-element.244) | copy-start | bytes 24580
  573.7 90.6 %all-gather.30.cloned.1.call-start = ((), (), s32[]{:S(2)}) async-start(), calls=%async_computation.22 | async-start | bytes 3932160 | tf_op jit(solution)/shard_map/all_gather | solution.py:1447
  577.7 444.7 %reduce-scatter.13.cloned.1.call-start = ((), (), s32[]{:S(2)}) async-start(), calls=%async_computation.11 | async-start | bytes 3932160 | tf_op jit(solution)/shard_map/reduce_scatter | solution.py:1521
  584.5 29.7 %copy-start.49 = (f32[2,288,512]{2,1,0:T(8,128)}, f32[2,288,512]{2,1,0:T(8,128)S(1)}, u32[]{:S(2)}) copy-start(f32[2,288,512]{2,1,0:T(8,128)S(1)} %fusion.36) | copy-start | bytes 3538948
  614.1 6.9 copy-start.91
  614.1 8.3 copy-start.26
  812.3 261.4 %reduce-scatter.11.cloned.1.call-start = ((), (), s32[]{:S(2)}) async-start(), calls=%async_computation.10 | async-start | bytes 3932160 | tf_op jit(solution)/shard_map/reduce_scatter | solution.py:1521
  818.6 255.1 %reduce-scatter.9.cloned.1.call-start = ((), (), s32[]{:S(2)}) async-start(), calls=%async_computation.9 | async-start | bytes 3932160 | tf_op jit(solution)/shard_map/reduce_scatter | solution.py:1521
  824.9 307.5 %reduce-scatter.23.cloned.1.call-start = ((), (), s32[]{:S(2)}) async-start(), calls=%async_computation.16 | async-start | bytes 3932160 | tf_op jit(solution)/shard_map/reduce_scatter | solution.py:1521
  831.6 8.9 slice-start.2
  835.7 4.8 slice-start.3
  866.3 4.7 copy-start.79
  981.5 151.0 %reduce-scatter.21.cloned.1.call-start = ((), (), s32[]{:S(2)}) async-start(), calls=%async_computation.15 | async-start | bytes 3932160 | tf_op jit(solution)/shard_map/reduce_scatter | solution.py:1521
  987.9 156.9 %reduce-scatter.19.cloned.1.call-start = ((), (), s32[]{:S(2)}) async-start(), calls=%async_computation.14 | async-start | bytes 3932160 | tf_op jit(solution)/shard_map/reduce_scatter | solution.py:1521
  994.6 212.6 %reduce-scatter.15.cloned.1.call-start = ((), (), s32[]{:S(2)}) async-start(), calls=%async_computation.12 | async-start | bytes 3932160 | tf_op jit(solution)/shard_map/reduce_scatter | solution.py:1525
  1002.4 267.2 %reduce-scatter.17.cloned.1.call-start = ((), (), s32[]{:S(2)}) async-start(), calls=%async_computation.13 | async-start | bytes 3932160 | tf_op jit(solution)/shard_map/reduce_scatter | solution.py:1525
  1006.2 5.9 slice-start
  1020.3 43.8 %copy-start.34 = (f32[1,288,64]{2,1,0:T(8,128)S(1)}, f32[1,288,64]{2,1,0:T(8,128)}, u32[]{:S(2)}) copy-start(f32[1,288,64]{2,1,0:T(8,128)} %copy-done.31) | copy-start | bytes 221188
  1020.3 43.8 %copy-start.38 = (f32[1,288,64]{2,1,0:T(8,128)S(1)}, f32[1,288,64]{2,1,0:T(8,128)}, u32[]{:S(2)}) copy-start(f32[1,288,64]{2,1,0:T(8,128)} %copy-done.35) | copy-start | bytes 221188
  1020.3 43.8 %copy-start.42 = (f32[1,288,64]{2,1,0:T(8,128)S(1)}, f32[1,288,64]{2,1,0:T(8,128)}, u32[]{:S(2)}) copy-start(f32[1,288,64]{2,1,0:T(8,128)} %copy-done.39) | copy-start | bytes 221188
  1020.4 44.0 %copy-start.48 = (f32[2,288,512]{2,1,0:T(8,128)S(1)}, f32[2,288,512]{2,1,0:T(8,128)}, u32[]{:S(2)}) copy-start(f32[2,288,512]{2,1,0:T(8,128)} %copy-done.47) | copy-start | bytes 3538948
  1078.6 53.7 %copy-start.93 = (f32[1,2048]{1,0:T(1,128)S(1)}, f32[1,2048]{1,0:T(1,128)}, u32[]{:S(2)}) copy-start(f32[1,2048]{1,0:T(1,128)} %get-tuple-element.86) | copy-start | bytes 24580
  1269.6 59.9 %copy-start.43 = (bf16[512,768]{1,0:T(8,128)(2,1)S(1)}, bf16[512,768]{1,0:T(8,128)(2,1)}, u32[]{:S(2)}) copy-start(bf16[512,768]{1,0:T(8,128)(2,1)} %reduce-scatter.15.cloned.1.call-done) | copy-start | bytes 2359300
  1269.6 59.9 %copy-start.44 = (bf16[512,768]{1,0:T(8,128)(2,1)S(1)}, bf16[512,768]{1,0:T(8,128)(2,1)}, u32[]{:S(2)}) copy-start(bf16[512,768]{1,0:T(8,128)(2,1)} %reduce-scatter.17.cloned.1.call-done) | copy-start | bytes 2359300
  (82 other events, 174.0 us)
Sparse Core Ops, SparseCore 0:
  229.4 34.7 all-gather.31
  266.7 43.0 all-gather.21
  312.2 43.9 all-gather.19
  357.9 43.9 all-gather.23
  403.3 10.9 all-gather.33
  415.7 92.1 all-gather.17
  509.8 54.9 all-gather.25
  573.8 44.5 all-gather.27
  620.2 43.9 all-gather.29
  812.4 42.0 reduce-scatter.12
  858.1 63.7 reduce-scatter.10
  925.3 54.5 reduce-scatter.8
  982.9 43.9 reduce-scatter.22
  1029.7 43.9 reduce-scatter.20
  1076.5 68.2 reduce-scatter.18
  1146.9 60.2 reduce-scatter.14
  1209.3 60.2 reduce-scatter.16

commit v7 on v6

--- a/solution.py
+++ b/solution.py
@@ -233,113 +233,173 @@
 
 
 class UnitsOut(Part):
-    def __init__(self, pieces, layer):
-        self.layer = layer
-        cores, self.size, mats, share, self.width = pieces.shape
-        self.ins = [(pieces, HBM)]
-        shape = jax.ShapeDtypeStruct((mats, share, self.size * self.width), BF16)
-        self.outs = [(shape, HBM)]
-        self.scratch = [SEM, SEM((cores, self.size)), SEM((self.size,))]
+    def __init__(self, mats, layer):
+        self.layer, self.count = layer, len(mats)
+        self.size = lax.axis_size("dp")
+        rows, self.width = mats[0].shape
+        self.share = rows // (2 * self.size)
+        self.ins = [(mat, HBM) for mat in mats]
+        shape = jax.ShapeDtypeStruct((self.share, self.size * self.width), BF16)
+        self.outs = [(shape, HBM)] * self.count
+        self.scratch = [SEM((self.count,)), SEM((self.count, 2, self.size)), SEM((self.count, self.size))]
 
     def bind(self, ins, outs, scratch):
-        (self.src,), (self.dst,), (self.keep, self.send, self.recv) = ins, outs, scratch
+        self.src, self.dst = ins, outs
+        self.keep, self.send, self.recv = scratch
         self.core, self.me = lax.axis_index("section"), lax.axis_index("dp")
 
-    def lands(self, slot):
-        return self.dst.at[:, :, columns_of(slot, self.width)]
-
-    def copy(self, core, place, slot):
+    def piece(self, index, core, place):
+        start = pl.multiple_of((core * self.size + place) * self.share, self.share)
+        return self.src[index].at[pl.ds(start, self.share)]
+
+    def lands(self, index, slot):
+        return self.dst[index].at[:, columns_of(slot, self.width)]
+
+    def copy(self, index, core, place, slot):
         return remote(
-            self.src.at[core, place], self.lands(slot), self.send.at[core, place],
-            self.recv.at[slot], {"section": core, "dp": place},
-        )
-
-    def local(self):
-        return pltpu.make_async_copy(self.src.at[self.layer, self.me], self.lands(self.me), self.keep)
+            self.piece(index, core, place), self.lands(index, slot),
+            self.send.at[index, core, place], self.recv.at[index, slot],
+            {"section": core, "dp": place},
+        )
+
+    def local(self, index):
+        return pltpu.make_async_copy(
+            self.piece(index, self.layer, self.me), self.lands(index, self.me), self.keep.at[index]
+        )
 
     def targets(self):
-        for core in range(2):
-            for place in range(self.size):
-                yield core, place, (place != self.me) | (core != self.layer)
+        for index in range(self.count):
+            for core in range(2):
+                for place in range(self.size):
+                    yield index, core, place, (place != self.me) | (core != self.layer)
 
     def start(self):
         @pl.when(self.core == self.layer)
         def _():
-            for core, place, is_other in self.targets():
+            for index, core, place, is_other in self.targets():
                 @pl.when(is_other)
                 def _():
-                    self.copy(core, place, self.me).start()
-
-            self.local().start()
+                    self.copy(index, core, place, self.me).start()
+
+            for index in range(self.count):
+                self.local(index).start()
+
+    def finish(self):
+        for index in range(self.count):
+            for place in range(self.size):
+                @pl.when((self.core != self.layer) | (place != self.me))
+                def _():
+                    self.copy(index, 0, 0, place).wait_recv()
+
+        @pl.when(self.core == self.layer)
+        def _():
+            for index, core, place, is_other in self.targets():
+                @pl.when(is_other)
+                def _():
+                    self.copy(index, core, place, self.me).wait_send()
+
+            for index in range(self.count):
+                self.local(index).wait()
+
+
+class UnitsHome(Part):
+    def __init__(self, mats, layer):
+        self.layer, self.count = layer, len(mats)
+        self.size = lax.axis_size("dp")
+        self.share, depth = mats[0].shape
+        self.width = depth // self.size
+        self.ins = [(mat, HBM) for mat in mats]
+        shape = jax.ShapeDtypeStruct((2 * self.size * self.share, self.width), BF16)
+        self.outs = [(shape, HBM)] * self.count
+        self.scratch = [SEM((self.count,)), SEM((self.count, self.size)), SEM((self.count, 2, self.size))]
+
+    def bind(self, ins, outs, scratch):
+        self.src, self.dst = ins, outs
+        self.keep, self.send, self.recv = scratch
+        self.core, self.me = lax.axis_index("section"), lax.axis_index("dp")
+
+    def lands(self, index, core, slot):
+        start = pl.multiple_of((core * self.size + slot) * self.share, self.share)
+        return self.dst[index].at[pl.ds(start, self.share)]
+
+    def copy(self, index, place, core, slot):
+        return remote(
+            self.src[index].at[:, columns_of(place, self.width)], self.lands(index, core, slot),
+            self.send.at[index, place], self.recv.at[index, core, slot],
+            {"section": self.layer, "dp": place},
+        )
+
+    def local(self, index):
+        return pltpu.make_async_copy(
+            self.src[index].at[:, columns_of(self.me, self.width)],
+            self.lands(index, self.layer, self.me), self.keep.at[index],
+        )
+
+    def start(self):
+        for index in range(self.count):
+            for place in range(self.size):
+                @pl.when((self.core != self.layer) | (place != self.me))
+                def _():
+                    self.copy(index, place, self.core, self.me).start()
+
+            @pl.when(self.core == self.layer)
+            def _():
+                self.local(index).start()
+
+    def finish(self):
+        for index in range(self.count):
+            @pl.when(self.core == self.layer)
+            def _():
+                for core in range(2):
+                    for place in range(self.size):
+                        @pl.when((core != self.layer) | (place != self.me))
+                        def _():
+                            self.copy(index, 0, core, place).wait_recv()
+
+                self.local(index).wait()
+
+            for place in range(self.size):
+                @pl.when((self.core != self.layer) | (place != self.me))
+                def _():
+                    self.copy(index, place, self.core, self.me).wait_send()
+
+
+class UnitsSpread(Part):
+    def __init__(self, rows):
+        self.size = lax.axis_size("tensor")
+        self.share, depth = rows.shape
+        self.ins = [(rows, HBM)]
+        self.outs = [(jax.ShapeDtypeStruct((self.size * self.share, depth), BF16), HBM)]
+        self.scratch = [SEM, SEM((self.size,)), SEM((self.size,))]
+
+    def bind(self, ins, outs, scratch):
+        (self.src,), (self.dst,), (self.keep, self.send, self.recv) = ins, outs, scratch
+        self.me = lax.axis_index("tensor")
+
+    def lands(self, slot):
+        return self.dst.at[pl.ds(pl.multiple_of(slot * self.share, self.share), self.share)]
+
+    def copy(self, place, slot):
+        return remote(
+            self.src, self.lands(slot), self.send.at[place], self.recv.at[slot], {"tensor": place}
+        )
+
+    def start(self):
+        for place in range(self.size):
+            @pl.when(place != self.me)
+            def _():
+                self.copy(place, self.me).start()
+
+        pltpu.make_async_copy(self.src, self.lands(self.me), self.keep).start()
 
     def finish(self):
         for place in range(self.size):
-            @pl.when((self.core != self.layer) | (place != self.me))
+            @pl.when(place != self.me)
             def _():
-                self.copy(0, 0, place).wait_recv()
-
-        @pl.when(self.core == self.layer)
-        def _():
-            for core, place, is_other in self.targets():
-                @pl.when(is_other)
-                def _():
-                    self.copy(core, place, self.me).wait_send()
-
-            self.local().wait()
-
-
-class UnitsHome(Part):
-    def __init__(self, rows, layer):
-        self.layer = layer
-        self.size = lax.axis_size("dp")
-        mats, share, depth = rows.shape
-        self.width = depth // self.size
-        self.ins = [(rows, HBM)]
-        shape = jax.ShapeDtypeStruct((mats, 2, self.size, share, self.width), BF16)
-        self.outs = [(shape, HBM)]
-        self.scratch = [SEM, SEM((self.size,)), SEM((2, self.size))]
-
-    def bind(self, ins, outs, scratch):
-        (self.src,), (self.dst,), (self.keep, self.send, self.recv) = ins, outs, scratch
-        self.core, self.me = lax.axis_index("section"), lax.axis_index("dp")
-
-    def copy(self, place, core, slot):
-        return remote(
-            self.src.at[:, :, columns_of(place, self.width)], self.dst.at[:, core, slot],
-            self.send.at[place], self.recv.at[core, slot], {"section": self.layer, "dp": place},
-        )
-
-    def local(self):
-        return pltpu.make_async_copy(
-            self.src.at[:, :, columns_of(self.me, self.width)],
-            self.dst.at[:, self.layer, self.me], self.keep,
-        )
-
-    def start(self):
-        for place in range(self.size):
-            @pl.when((self.core != self.layer) | (place != self.me))
-            def _():
-                self.copy(place, self.core, self.me).start()
-
-        @pl.when(self.core == self.layer)
-        def _():
-            self.local().start()
-
-    def finish(self):
-        @pl.when(self.core == self.layer)
-        def _():
-            for core in range(2):
-                for place in range(self.size):
-                    @pl.when((core != self.layer) | (place != self.me))
-                    def _():
-                        self.copy(0, core, place).wait_recv()
-
-            self.local().wait()
-
-        for place in range(self.size):
-            @pl.when((self.core != self.layer) | (place != self.me))
-            def _():
-                self.copy(place, self.core, self.me).wait_send()
+                self.copy(place, place).wait_recv()
+                self.copy(place, self.me).wait_send()
+
+        pltpu.make_async_copy(self.src, self.lands(self.me), self.keep).wait()
 
 
 class SharedRows(Part):
@@ -392,112 +452,182 @@
     return [1, 2, 0, 3] if size == 4 else list(range(size))
 
 
+class AttnShards:
+    def __init__(self, w_query, w_key, w_value, w_out):
+        self.arrays = [w_query, w_key, w_value, w_out]
+        self.depth = w_query.shape[0]
+        self.q_width, self.k_width = w_query.shape[1] // 2, w_key.shape[1] // 2
+        self.width = self.q_width + 2 * self.k_width
+        half = self.depth // 2
+        parts = self.q_width // 2
+        self.items = [
+            (0, lambda ref, core: ref.at[pl.ds(0, half), columns_of(core, self.q_width)]),
+            (0, lambda ref, core: ref.at[pl.ds(half, half), columns_of(core, self.q_width)]),
+            (1, lambda ref, core: ref.at[:, columns_of(core, self.k_width)]),
+            (2, lambda ref, core: ref.at[:, columns_of(core, self.k_width)]),
+            (3, lambda ref, core: ref.at[pl.ds(core * self.q_width, parts)]),
+            (3, lambda ref, core: ref.at[pl.ds(core * self.q_width + parts, parts)]),
+        ]
+        q_width, k_width, depth = self.q_width, self.k_width, self.depth
+        self.qkv_rows = [(0, half), (half, half), (0, depth), (0, depth)]
+        self.qkv_columns = [
+            (0, q_width), (0, q_width), (q_width, k_width), (q_width + k_width, k_width)
+        ]
+        self.out_rows = [(0, parts), (parts, parts)]
+
+    def source(self, refs, index, core):
+        array, cut = self.items[index]
+        return cut(refs[array], core)
+
+    def lands(self, qkv, out, index, slot):
+        if index < 4:
+            (start, rows), (left, columns) = self.qkv_rows[index], self.qkv_columns[index]
+            at = pl.multiple_of(slot * self.depth + start, rows)
+            return qkv.at[pl.ds(at, rows), pl.ds(left, columns)]
+        start, rows = self.out_rows[index - 4]
+        return out.at[pl.ds(start, rows), columns_of(slot, self.depth)]
+
+
 class AttnOut(Part):
-    def __init__(self, halves, layer):
-        self.layer = layer
+    def __init__(self, shards, layer):
+        self.layer, self.shards = layer, shards
         self.size = lax.axis_size("dp")
-        self.chunks = halves.shape[1]
-        self.ins = [(halves, HBM)]
-        self.outs = [(jax.ShapeDtypeStruct((self.size,) + halves.shape[1:], BF16), HBM)]
+        self.count = len(shards.items)
+        depth = self.size * shards.depth
+        self.ins = [(array, HBM) for array in shards.arrays]
+        self.outs = [
+            (jax.ShapeDtypeStruct((depth, shards.width), BF16), HBM),
+            (jax.ShapeDtypeStruct((shards.q_width, depth), BF16), HBM),
+        ]
         self.scratch = [
-            SEM, SEM((2, self.size, self.chunks)), SEM((self.size, self.chunks)), SEM((self.chunks,)),
+            SEM((self.count,)), SEM((2, self.size, self.count)), SEM((self.size, self.count)),
+            SEM((self.count,)),
         ]
 
     def bind(self, ins, outs, scratch):
-        (self.src,), (self.dst,) = ins, outs
+        self.src = ins
+        self.qkv, self.out = outs
         self.keep, self.send, self.recv, self.relay_send = scratch
         self.core, self.me = lax.axis_index("section"), lax.axis_index("dp")
 
-    def copy(self, core, place, slot, chunk):
+    def lands(self, index, slot):
+        return self.shards.lands(self.qkv, self.out, index, slot)
+
+    def copy(self, core, place, slot, index):
         return remote(
-            self.src.at[core, chunk], self.dst.at[slot, chunk], self.send.at[core, place, chunk],
-            self.recv.at[slot, chunk], {"section": core, "dp": place},
-        )
-
-    def relay(self, source, target, chunk):
+            self.shards.source(self.src, index, core), self.lands(index, slot),
+            self.send.at[core, place, index], self.recv.at[slot, index],
+            {"section": core, "dp": place},
+        )
+
+    def relay(self, source, target, index):
+        block = self.lands(index, source)
         return remote(
-            self.dst.at[source, chunk], self.dst.at[source, chunk], self.relay_send.at[chunk],
-            self.recv.at[source, chunk], {"dp": target},
-        )
-
-    def local(self):
-        return pltpu.make_async_copy(self.src.at[self.layer], self.dst.at[self.me], self.keep)
+            block, block, self.relay_send.at[index], self.recv.at[source, index], {"dp": target}
+        )
+
+    def local(self, index):
+        return pltpu.make_async_copy(
+            self.shards.source(self.src, index, self.layer), self.lands(index, self.me),
+            self.keep.at[index],
+        )
 
     def targets(self):
-        for chunk in range(self.chunks):
+        for index in range(self.count):
             for core in range(2):
                 for place in range(self.size):
                     sent = (place != self.me) | (core != self.layer)
                     if self.size == 4:
                         sent = sent & jnp.logical_not(far_pair(place, self.me))
-                    yield core, place, chunk, sent
+                    yield core, place, index, sent
 
     def start(self):
         @pl.when(self.core == self.layer)
         def _():
-            for core, place, chunk, sent in self.targets():
+            for core, place, index, sent in self.targets():
                 @pl.when(sent)
                 def _():
-                    self.copy(core, place, self.me, chunk).start()
-
-            self.local().start()
+                    self.copy(core, place, self.me, index).start()
+
+            for index in range(self.count):
+                self.local(index).start()
 
     def run(self):
-        for chunk in range(self.chunks):
+        for index in range(self.count):
             for place in line_order(self.size):
                 @pl.when((self.core != self.layer) | (place != self.me))
                 def _():
-                    self.copy(0, 0, place, chunk).wait_recv()
+                    self.copy(0, 0, place, index).wait_recv()
 
                 for via, source, target in line_relays(self.size):
                     if source == place:
                         @pl.when(self.me == via)
                         def _():
-                            self.relay(source, target, chunk).start()
+                            self.relay(source, target, index).start()
 
     def finish(self):
         @pl.when(self.core == self.layer)
         def _():
-            for core, place, chunk, sent in self.targets():
+            for core, place, index, sent in self.targets():
                 @pl.when(sent)
                 def _():
-                    self.copy(core, place, self.me, chunk).wait_send()
-
-            self.local().wait()
+                    self.copy(core, place, self.me, index).wait_send()
+
+            for index in range(self.count):
+                self.local(index).wait()
 
         for via, source, target in line_relays(self.size):
             @pl.when(self.me == via)
             def _():
-                for chunk in range(self.chunks):
-                    self.relay(source, target, chunk).wait_send()
+                for index in range(self.count):
+                    self.relay(source, target, index).wait_send()
 
 
 class HalfOver(Part):
-    def __init__(self, halves):
-        self.ins = [(halves, HBM)]
-        self.outs = [(jax.ShapeDtypeStruct(halves.shape[1:], BF16), HBM)]
-        self.scratch = [SEM, SEM, SEM]
+    def __init__(self, shards):
+        self.shards = shards
+        self.count = len(shards.items)
+        rows = shards.depth + shards.q_width
+        self.ins = [(array, HBM) for array in shards.arrays]
+        self.outs = [(jax.ShapeDtypeStruct((rows, shards.depth), BF16), HBM)]
+        self.scratch = [SEM((self.count,)), SEM((self.count,)), SEM((self.count,))]
+
+    def lands(self, index):
+        depth, q_width = self.shards.depth, self.shards.q_width
+        packed = self.out_refs[0]
+        return self.shards.lands(
+            packed.at[pl.ds(0, depth)], packed.at[pl.ds(depth, q_width)], index, 0
+        )
+
+    def over(self, index):
+        return remote(
+            self.shards.source(self.in_refs, index, 0), self.lands(index), self.refs[0].at[index],
+            self.refs[1].at[index], {"section": 0},
+        )
+
+    def keep(self, index):
+        return pltpu.make_async_copy(
+            self.shards.source(self.in_refs, index, 1), self.lands(index), self.refs[2].at[index]
+        )
 
     def start(self):
-        self.over = remote(
-            self.in_refs[0].at[0], self.out_refs[0], self.refs[0], self.refs[1], {"section": 0}
-        )
-        self.keep = pltpu.make_async_copy(self.in_refs[0].at[1], self.out_refs[0], self.refs[2])
-
         @pl.when(lax.axis_index("section") == 1)
         def _():
-            self.over.start()
-            self.keep.start()
+            for index in range(self.count):
+                self.over(index).start()
+                self.keep(index).start()
 
     def finish(self):
         @pl.when(lax.axis_index("section") == 1)
         def _():
-            self.over.wait_send()
-            self.keep.wait()
+            for index in range(self.count):
+                self.over(index).wait_send()
+                self.keep(index).wait()
 
         @pl.when(lax.axis_index("section") == 0)
         def _():
-            self.over.wait_recv()
+            for index in range(self.count):
+                self.over(index).wait_recv()
 
 
 class Swap(Part):
@@ -1032,6 +1162,9 @@
         if forward and not backward:
             outs |= {"gate": vmem_f32(size, group_rows, units), "up": vmem_f32(size, group_rows, units)}
         if forward and backward:
+            outs["grad_mlp"] = vmem_bf16(size, group_rows, depth)
+            self.grad_in = Gatherer("dp", rows, half)
+            helpers += [self.grad_in]
             scratch |= {
                 "gate": pltpu.VMEM((size, group_rows, units), F32),
                 "up": pltpu.VMEM((size, group_rows, units), F32),
@@ -1072,6 +1205,8 @@
 
     def start(self):
         self.rows_in.start()
+        if self.has_forward and self.has_backward:
+            self.grad_in.begin(self.grad_own[...])
 
     def run(self):
         total = self.rows_in.summed()
@@ -1092,11 +1227,21 @@
         me = lax.axis_index("dp")
         turn = 1 - 2 * (me // (self.size // 2))
 
+        def turned(step):
+            return lax.rem(me + turn * step + self.size, self.size)
+
+        if self.has_forward and self.has_backward:
+            for place in line_order(self.size):
+                self.grad_in.arrive(place)
+        self.spread_in.arrive(me)
+
         @pl.loop(0, self.size)
         def _(step):
-            place = lax.rem(me + turn * step + self.size, self.size)
-            self.spread_in.arrive(place)
+            place = turned(step)
             self.spread_in.arrive_over(place)
+            if self.has_forward and self.has_backward:
+                self.grad_in.arrive_over(place)
+                self.grad_in.unpack_place(self.grad_mlp, place)
             if self.has_forward:
                 self.spread_in.unpack_place(self.mlp_in, place)
                 self.forward_place(place)
@@ -1104,6 +1249,11 @@
                 self.spread_in.unpack_place(self.grad_mlp, place)
             if self.has_backward:
                 self.backward_place(place)
+
+            @pl.when(step + 1 < self.size)
+            def _():
+                self.spread_in.arrive(turned(step + 1))
+
             if self.has_forward:
                 self.back.absorb(place, lambda at: self.kept[:, pl.ds(at, CHUNK)])
             if self.has_backward:
@@ -1253,10 +1403,10 @@
 
 def attn_forward(hidden_in, weights, gains, slot, gather):
     attn_scale, _, q_scale, k_scale = gains
-    w_qkv, w_outt = weights[:2]
+    w_qkv, w_out = weights[:2]
     allowed, cos_table, sine_table = slot
     trees, row_count, depth = hidden_in.shape
-    q_width = w_outt.shape[1]
+    q_width = w_out.shape[0]
     normed = rms_scale(hidden_in.astype(F32), attn_scale).astype(BF16).reshape(-1, depth)
     qkv = dot(normed, w_qkv).reshape(trees, row_count, -1)
     q_pre = qkv[:, :, :q_width].reshape(trees, row_count, -1, HD)
@@ -1275,20 +1425,20 @@
     log_total = row_max + jnp.log(row_total)
     attended = jnp.einsum("bgrt,btd->brgd", prob_bf, value_all, preferred_element_type=F32)
     attended_bf = attended.reshape(trees * row_count, -1).astype(BF16)
-    terms = dot_inner(attended_bf, w_outt).astype(BF16).reshape(trees, row_count, depth)
+    terms = dot(attended_bf, w_out).astype(BF16).reshape(trees, row_count, depth)
     saved = (normed, q_pre, k_pre, query_bf, key_all, value_all, log_total, attended_bf)
     return (terms, saved)
 
 
 def attn_backward(grad_attn, saved, weights, gains, slot, scatter):
     _, _, q_scale, k_scale = gains
-    w_qkv, w_outt = weights[:2]
+    w_qkv, w_out = weights[:2]
     allowed, cos_table, sine_table = slot
     normed, q_pre, k_pre, query_bf, key_all, value_all, log_total, attended_bf = saved
     trees, row_count = query_bf.shape[:2]
     depth = normed.shape[1]
     grad_attn = grad_attn.reshape(-1, depth)
-    grad_heads = dot(grad_attn, w_outt).astype(BF16).reshape(query_bf.shape)
+    grad_heads = dot_inner(grad_attn, w_out).astype(BF16).reshape(query_bf.shape)
     scores = masked_scores(query_bf, key_all, allowed)
     prob_full = jnp.exp(scores - log_total)
     grad_prob = jnp.einsum("brgd,btd->bgrt", grad_heads, value_all, preferred_element_type=F32)
@@ -1425,63 +1575,57 @@
     def halves(width, array):
         return [array[:, :width], array[:, array.shape[1] - width :]]
 
-    attn_halves = jnp.stack(
-        [
-            jnp.concatenate(parts, axis=1)
-            for parts in zip(
-                halves(q_width, w_query[0]),
-                halves(k_width, w_key[0]),
-                halves(k_width, w_value[0]),
-                halves(q_width, w_out[0].T),
-            )
-        ]
-    )
-    unit_blocks = jnp.stack([w_gate[0].T, w_up[0].T, w_down[0]]).reshape(
-        3, 2, dp_size, share, own_depth
-    )
-    unit_blocks = unit_blocks.transpose(1, 2, 0, 3, 4)
+    unit_mats = [w_gate[0].T, w_up[0].T, w_down[0]]
     qkv_width = q_width + 2 * k_width
     gains_own = jnp.concatenate([attn_gain[0], mlp_gain[0], q_gain[0], k_gain[0]]).astype(F32)
 
     def spread_units(rows):
         return lax.all_gather(rows, "tensor", axis=0, tiled=True)
 
-    def attn_of(whole):
-        whole = whole.reshape(depth, -1)
-        return (whole[:, :qkv_width], whole[:, qkv_width:])
-
-    def joint(gate_up, down):
-        return (spread_units(gate_up[0]), spread_units(gate_up[1]), spread_units(down[0]))
+    def tied(value, *before):
+        return lax.optimization_barrier((value, *before))[0]
 
     if fast:
-        group = ["section", "dp"]
-        (gate_up,), (gains_all,) = fused(
-            [
-                UnitsOut(unit_blocks[:, :, :2], 0),
-                SharedRows(gains_own.reshape(-1, 128)),
-            ],
-            group, True, 1, 45,
-        )
-        attn_chunks = attn_halves.reshape(2, 4, own_depth // 4, -1)
-        attn_chunks, gate_up = lax.optimization_barrier((attn_chunks, gate_up))
-        (attn_all,), (down,), (attn_shard,) = fused(
-            [
-                AttnOut(attn_chunks, 0), UnitsOut(unit_blocks[:, :, 2:], 0), HalfOver(attn_chunks),
-            ],
-            group, True, 2, 80,
-        )
-        attn_next = lax.all_gather(attn_shard.reshape(own_depth, -1), "dp", axis=0, tiled=True)
-        first_weights = attn_of(attn_all) + joint(gate_up, down)
+        line = ["section", "dp"]
+        everyone = ["section", "dp", "tensor"]
+        (gate_rows, up_rows), (gains_all,) = fused(
+            [UnitsOut(unit_mats[:2], 0), SharedRows(gains_own.reshape(-1, 128))], line, True, 1, 45
+        )
+        shards = AttnShards(w_query[0], w_key[0], w_value[0], w_out[0])
+        shards.arrays[0] = tied(shards.arrays[0], gate_rows)
+        (w_qkv, w_heads), (down_rows,), (attn_shard,) = fused(
+            [AttnOut(shards, 0), UnitsOut(unit_mats[2:], 0), HalfOver(shards)], line, True, 2, 80
+        )
+        first_weights = [w_qkv, w_heads, spread_units(gate_rows), spread_units(up_rows)]
+        attn_next = lax.all_gather(attn_shard, "dp", axis=0)
     else:
         gains_all = lax.all_gather(gains_own, ("section", "dp"))
+        attn_halves = jnp.stack(
+            [
+                jnp.concatenate(parts, axis=1)
+                for parts in zip(
+                    halves(q_width, w_query[0]),
+                    halves(k_width, w_key[0]),
+                    halves(k_width, w_value[0]),
+                    halves(q_width, w_out[0].T),
+                )
+            ]
+        )
         attn_shards = swap_cores(pick(attn_halves, core), pick(attn_halves, 1 - core))
+        unit_blocks = jnp.stack(unit_mats).reshape(3, 2, dp_size, share, own_depth)
+        unit_blocks = unit_blocks.transpose(1, 2, 0, 3, 4)
         unit_shards = swap_cores(pick(unit_blocks, core), pick(unit_blocks, 1 - core))
         both_weights = []
         for layer in range(2):
             attn_all = lax.all_gather(attn_shards[layer], "dp", axis=0, tiled=True)
             pieces = exchange(unit_shards[layer], "dp")
             pieces = pieces.transpose(1, 2, 0, 3).reshape(3, share, depth)
-            both_weights.append(attn_of(attn_all) + joint(pieces[:2], pieces[2:]))
+            both_weights.append(
+                (
+                    attn_all[:, :qkv_width], attn_all[:, qkv_width:].T,
+                    *(spread_units(pieces[i]) for i in range(3)),
+                )
+            )
 
     gains_all = gains_all.reshape(2, dp_size, -1)
     gains = [
@@ -1517,9 +1661,9 @@
         return [dot_outer(left, right).astype(BF16) for left, right in pairs]
 
     def scatter_units(products):
-        return jnp.stack(
-            [lax.psum_scatter(item, "tensor", scatter_dimension=0, tiled=True) for item in products]
-        )
+        return [
+            lax.psum_scatter(item, "tensor", scatter_dimension=0, tiled=True) for item in products
+        ]
 
     def scatter_shards(products):
         return lax.psum_scatter(
@@ -1527,14 +1671,11 @@
         )
 
     if fast:
-        line = ["section", "dp"]
-        everyone = ["section", "dp", "tensor"]
-
-        def units_on(index):
-            return [UnitsOut(unit_blocks[:, :, index : index + 1], 1)]
+        def units_on(*which):
+            return [UnitsOut([unit_mats[i] for i in which], 1)]
 
         def kv_gather(own, cargo, collective_id, carried):
-            (whole,), outs = with_cargo(GatherKV(own), cargo, line, collective_id, 30)
+            (whole,), outs = with_cargo(GatherKV(own), cargo, everyone, collective_id, 40)
             carried += outs
             return whole.reshape(trees, -1, 2 * HD)
 
@@ -1550,32 +1691,41 @@
         carried = []
         terms, saved_first = attn_forward(
             hidden, first_weights, gains[0], slot,
-            lambda own: kv_gather(own, units_on(0), 3, carried),
-        )
+            lambda own: kv_gather(
+                tied(own, *first_weights[2:]), [UnitsSpread(down_rows)] + units_on(0), 3, carried
+            ),
+        )
+        (down_all,), (gate_rows,) = carried
+        first_weights.append(down_all)
         part = FeedForward(
             terms, own_in, gains[0][1][None], first_weights[2:], True, False, {}
         )
-        outs, others = with_cargo(part, units_on(1) + units_on(2), everyone, 4, 90, 56)
-        carried += others
+        outs, ((up_rows, down_rows),) = with_cargo(part, units_on(1, 2), everyone, 4, 90, 56)
         middle_first, mlp_in_first, hidden_first, own_next, output_first, gate_first, up_first = outs
-        terms, grad_late = lax.optimization_barrier((terms, grad_own.astype(BF16)))
-        grad_mlp = lax.all_gather(grad_late, "dp", axis=0)
-        grad_mlp = lax.all_gather(grad_mlp, "section", axis=0).transpose(1, 0, 2, 3)
-        grad_mlp = grad_mlp.reshape(dp_size, -1, depth)
-        second_weights = attn_of(attn_next) + tuple(spread_units(out[0][0]) for out in carried)
+        second_weights = [
+            attn_next[:, :own_depth].reshape(depth, -1),
+            attn_next[:, own_depth:].transpose(1, 0, 2).reshape(q_width, depth),
+            spread_units(gate_rows), spread_units(up_rows),
+        ]
+        carried = []
         terms, saved_second = attn_forward(
-            output_first, second_weights, gains[1], slot, lambda own: kv_gather(own, [], 5, [])
-        )
+            output_first, second_weights, gains[1], slot,
+            lambda own: kv_gather(
+                tied(own, second_weights[2]), [UnitsSpread(down_rows)], 5, carried
+            ),
+        )
+        ((down_all,),) = carried
+        second_weights.append(down_all)
         part = FeedForward(
             terms, own_next, gains[1][1][None], second_weights[2:], True, True,
-            {"grad_mlp": grad_mlp, "grad_own": grad_own},
+            {"grad_own": grad_own},
         )
         outs, _ = with_cargo(part, [], everyone, 6, 100, 60)
         (
-            middle, mlp_in, hidden_bf, _, output_second,
+            middle, mlp_in, hidden_bf, _, output_second, grad_mlp,
             grad_gate, grad_up, grad_middle, mlp_gain_second, grad_attn,
         ) = outs
-        unit_grad = scatter_units(
+        unit_second = scatter_units(
             weight_products(
                 [
                     (flat(grad_gate), flat(mlp_in)),
@@ -1601,8 +1751,7 @@
             grad_gate, grad_up, grad_middle, mlp_gain_first, grad_attn,
             attn_gain_second, incoming_second, grad_mlp,
         ) = outs
-        unit_home_second = unit_grad
-        unit_grad = scatter_units(
+        unit_first = scatter_units(
             weight_products(
                 [
                     (flat(grad_gate), flat(mlp_in_first)),
@@ -1614,17 +1763,18 @@
         carried = []
         terms, pairs, head_first = attn_backward(
             grad_attn, saved_first, first_weights, gains[0], slot,
-            lambda whole: kv_scatter(whole, [UnitsHome(unit_home_second[:1], 1)], 9, carried),
-        )
-        attn_first = scatter_shards(weight_products(pairs))
+            lambda whole: kv_scatter(whole, [UnitsHome(unit_second, 1)], 9, carried),
+        )
+        (home_second,) = carried
+        whole = jnp.concatenate(weight_products(pairs), axis=1).reshape(dp_size, 4, -1, q_width + qkv_width)
         part = LastHub(terms, own_in, gains[0][0][None], grad_middle)
-        (attn_gain_first, incoming_first), others = with_cargo(
-            part, [UnitsHome(unit_home_second[1:], 1)], everyone, 10, 50
-        )
-        carried += others
+        (attn_gain_first, incoming_first), ((attn_first,),) = with_cargo(
+            part, [ScatterKV(whole.transpose(1, 0, 2, 3))], everyone, 10, 60, 56
+        )
+        attn_first = attn_first.reshape(own_depth, -1).astype(BF16)
         outputs = [output_first, output_second]
         grads = [incoming_first, incoming_second]
-        weight_grads = [(attn_first, unit_grad), (attn_second, None)]
+        weight_grads = [(attn_first, None), (attn_second, None)]
         gain_grads = [
             jnp.concatenate([attn_gain_first[0], mlp_gain_first[0], *head_first]),
             jnp.concatenate([attn_gain_second[0], mlp_gain_second[0], *head_second]),
@@ -1642,13 +1792,14 @@
     if fast:
         mine = jnp.where(core == 0, weight_grads[0][0], weight_grads[1][0])
         other = jnp.where(core == 0, weight_grads[1][0], weight_grads[0][0])
-        (gain_total,), (arrived,), (first_home,) = fused(
-            [TotalOverAll(gain_total.reshape(-1, 128)), Swap(other), UnitsHome(unit_grad, 0)],
+        (gain_total,), (arrived,), home_first = fused(
+            [TotalOverAll(gain_total.reshape(-1, 128)), Swap(other), UnitsHome(unit_first, 0)],
             everyone, True, 11, 60,
         )
         attn_home = (jnp.where(core == 0, mine, arrived), jnp.where(core == 0, arrived, mine))
-        second_home = jnp.concatenate([out[0] for out in carried], axis=0)
-        unit_home = jnp.where(core == 0, first_home, second_home).reshape(3, own_units, own_depth)
+        unit_home = [
+            jnp.where(core == 0, first, second) for first, second in zip(home_first, home_second)
+        ]
         gain_total = gain_total.reshape(2, -1)
     else:
         def bring_home(first, second):
@@ -1658,7 +1809,7 @@
 
         def pieces_of(grad):
             return exchange(
-                grad.reshape(3, share, dp_size, own_depth).transpose(2, 0, 1, 3), "dp"
+                jnp.stack(grad).reshape(3, share, dp_size, own_depth).transpose(2, 0, 1, 3), "dp"
             )
 
         attn_home = bring_home(weight_grads[0][0], weight_grads[1][0])

time: 1370 us -> 1140 us (0.83)
  waiting for transfers between devices: 334 us -> 1.02 us
  Pallas kernels: 767 us -> 874 us
    all_gather x6 -> x4, waiting for transfers between devices: 167 us -> 0.04 us  [spread_units(): return lax.all_gather(rows, 'tensor', axis=0, tiled=True)]
    reduce_scatter x2 -> x1, waiting for transfers between devices: 120 us -> 0.02 us  [scatter_shards(): lax.psum_scatter(jnp.concatenate(products, axis=1), 'dp', scatter_dimensi...]
    pallas_call x11, Pallas kernels: 767 us -> 874 us  [fused(): pl.pallas_call(kernel, out_shape=[item[0] for item in outs], in_specs=[it...]
    all_gather x3 -> x1, waiting for transfers between devices: 32.3 us -> 0.01 us  [on_device(): attn_next = lax.all_gather(attn_shard, 'dp', axis=0)]
    unnamed x239 -> x267, local copies, waits for them, and re-layouts: 29.2 us -> 53.6 us
  transfers between devices with their start and end apart: 17 -> 12, of which waited for: 8 -> 0; matrix products, arithmetic and copies ran while one was open for 9% -> 14% of each run, Pallas kernels for 31% -> 56%
where the time goes in v7:
time: 1140 us; the launch traced here: 1130 us
  Pallas kernels  874 us (77%)
  matrix products  92.2 us (8%)
  local copies, waits for them, and re-layouts  85.5 us (8%)
  other arithmetic  56.4 us (5%)
  between operations  20.2 us (2%)
    pallas_call x11, Pallas kernels, fused(): pl.pallas_call(kernel, out_shape=[item[0] for item in outs], in_specs=[it...  874 us
    unnamed x267, local copies, waits for them, and re-layouts  53.6 us
    dot_general x10, matrix products, dot_outer(): return lax.dot_general(left, right, OUTER, preferred_element_type=F32)  43.6 us
  transfers between devices with their start and end apart: 12, of which 0 were waited for; matrix products, arithmetic and copies ran while one was open for 14% of the time, Pallas kernels for 56%

profile of v7, /device:TPU:0, one launch (start us, length us, event | category | flops | bytes accessed | tf_op | source)
XLA Modules:
  0.0 1130.1 jit_solution(12540050161127550351)
XLA Ops:
  12.2 41.5 %shard_map.255 = (bf16[192,2048]{1,0:T(8,128)(2,1)S(1)}, bf16[192,2048]{1,0:T(8,128)(2,1)S(1)}, f32[2,4,10,128]{3,2,1,0:T(8,128)S(1)}) custom-call(bf16[1536,512]{1,0:T(8,128)(2,1)S(1)} %bitcast.325, bf16[1536,512]{1,0:T(8,128)(2,1)S(1)} %bitcast.323, f32[10,128]{1,0:T(8,128)S(1)} %fusion.112.refs_2_), custom_call_target="tpu_custom_call" | custom-call | bytes 135000000 | tf_op jit(solution)/shard_map/pallas_call | solution.py:210
  60.8 68.4 %shard_map.256 = (bf16[2048,512]{1,0:T(8,128)(2,1)S(1)}, bf16[256,2048]{1,0:T(8,128)(2,1)S(1)}, bf16[192,2048]{1,0:T(8,128)(2,1)S(1)}, bf16[768,512]{1,0:T(8,128)(2,1)}) custom-call(bf16[512,512]{1,0:T(8,128)(2,1)S(1)} %bitcast.329, bf16[512,256]{1,0:T(8,128)(2,1)S(1)} %bitcast.341, bf16[512,256]{1,0:T(8,128)(2,1)S(1)} %bitcast.343, ...), custom_call_target="tpu_custom_call" | custom-call | bytes 240000000 | tf_op jit(solution)/shard_map/pallas_call | solution.py:210
  149.1 74.8 %shard_map.257 = (bf16[768,2048]{1,0:T(8,128)(2,1)S(1)}, bf16[192,2048]{1,0:T(8,128)(2,1)S(1)}, bf16[2,4,288,256]{3,2,1,0:T(8,128)(2,1)S(1)}) custom-call(bf16[192,2048]{1,0:T(8,128)(2,1)S(1)} %copy-done.30, bf16[1536,512]{1,0:T(8,128)(2,1)S(1)} %bitcast.326, bf16[2,288,256]{2,1,0:T(8,128)(2,1)S(1)} %pad_maximum_fusion.9.refs_2_), custom_call_target="tpu_custom_call" | custom-call | bytes 120000000 | tf_op jit(solution)/shard_map/pallas_call | solution.py:210
  234.7 1.9 bitcast_convert_fusion.9.refs_6_
  242.7 2.2 convolution_convert_fusion.3
  244.9 139.7 %shard_map.258 = (bf16[192,2048]{1,0:T(8,128)(2,1)}, bf16[192,2048]{1,0:T(8,128)(2,1)}, f32[72,2048]{1,0:T(8,128)}, bf16[4,144,2048]{2,1,0:T(8,128)(2,1)}, bf16[...) custom-call(bf16[1536,512]{1,0:T(8,128)(2,1)} %bitcast.324, ...), custom_call_target="tpu_custom_call" | custom-call | bytes 270000000 | tf_op jit(solution)/shard_map/pallas_call | solution.py:210
  384.8 2.2 fusion.9
  387.1 2.3 slice.200
  389.3 3.2 slice.188
  392.6 2.3 copy.202
  394.9 3.7 fusion.39
  400.6 2.4 reshape.585
  410.0 50.9 %shard_map.259 = (bf16[768,2048]{1,0:T(8,128)(2,1)S(1)}, bf16[2,4,288,256]{3,2,1,0:T(8,128)(2,1)S(1)}) custom-call(bf16[192,2048]{1,0:T(8,128)(2,1)S(1)} %copy-done.25, bf16[2,288,256]{2,1,0:T(8,128)(2,1)S(1)} %pad_maximum_fusion.11.refs_1_), custom_call_target="tpu_custom_call" | custom-call | bytes 120000000 | tf_op jit(solution)/shard_map/pallas_call | solution.py:210
  460.9 3.7 fusion.152
  468.5 2.2 convolution_convert_fusion.2
  470.7 135.2 %shard_map.260 = (f32[72,2048]{1,0:T(8,128)}, bf16[4,144,2048]{2,1,0:T(8,128)(2,1)}, bf16[4,144,768]{2,1,0:T(8,128)(2,1)}, f32[72,2048]{1,0:T(8,128)}, bf16[2,28...) custom-call(bf16[2,288,2048]{2,1,0:T(8,128)(2,1)} %bitcast.352, ...), custom_call_target="tpu_custom_call" | custom-call | bytes 300000000 | tf_op jit(solution)/shard_map/pallas_call | solution.py:210
  605.9 6.3 bitcast_convert_fusion.4
  612.3 6.3 bitcast_convert_fusion.5
  618.6 6.2 bitcast_convert_fusion.3
  624.9 2.7 convolution_convert_fusion.7
  627.7 4.0 fusion.3
  636.3 30.1 %shard_map.261 = f32[2,288,256]{2,1,0:T(8,128)S(1)} custom-call(bf16[2,4,288,256]{3,2,1,0:T(8,128)(2,1)S(1)} %pad_maximum_fusion.3.refs_0_), custom_call_target="tpu_custom_call" | custom-call | bytes 90000000 | tf_op jit(solution)/shard_map/pallas_call | solution.py:210
  673.0 2.0 bitcast_convert_fusion.6
  675.0 1.9 pad_maximum_fusion.1
  678.6 4.5 convolution_convert_fusion.1
  683.1 107.0 %shard_map.262 = (bf16[4,144,768]{2,1,0:T(8,128)(2,1)}, bf16[4,144,768]{2,1,0:T(8,128)(2,1)}, f32[72,2048]{1,0:T(8,128)}, f32[1,2048]{1,0:T(1,128)}, bf16[2,288,...) custom-call(bf16[2,288,2048]{2,1,0:T(8,128)(2,1)} %bitcast.357, ...), custom_call_target="tpu_custom_call" | custom-call | bytes 270000000 | tf_op jit(solution)/shard_map/pallas_call | solution.py:210
  790.1 5.8 bitcast_convert_fusion
  797.1 5.7 bitcast_convert_fusion.1
  804.1 3.3 convolution_convert_fusion.6
  809.1 6.2 bitcast_convert_fusion.2
  815.4 4.0 fusion
  830.3 2.0 convolution_convert_fusion.5
  838.1 75.1 %shard_map.263 = (bf16[1536,512]{1,0:T(8,128)(2,1)S(1)}, bf16[1536,512]{1,0:T(8,128)(2,1)S(1)}, bf16[1536,512]{1,0:T(8,128)(2,1)S(1)}, f32[2,288,256]{2,1,0:T(8,128)S(1)}) custom-call(bf16[192,2048]{1,0:T(8,128)(2,1)S(1)} %copy-done.20, bf16[192,2048]{1,0:T(8,128)(2,1)S(1)} %copy-done.19, bf16[192,2048]{1,0:T(8,128)(2,1)S(1)} %copy-done.21, ...), custom_call_target="tpu_custom_call" | custom-call | bytes 90000000 | tf_op jit(solution)/shard_map/pallas_call | solution.py:210
  913.5 2.6 multiply_reduce_fusion.5
  917.5 2.0 bitcast_convert_fusion.7
  919.5 1.9 pad_maximum_fusion
  921.4 4.9 copy.182
  926.3 4.0 copy.258
  930.3 2.8 convolution_convert_fusion
  933.1 92.4 %shard_map.264 = (f32[4,128,768]{2,1,0:T(8,128)}, f32[1,2048]{1,0:T(1,128)}, bf16[2,288,2048]{2,1,0:T(8,128)(2,1)}) custom-call(bf16[4,4,128,768]{3,2,1,0:T(8,128)(2,1)} %bitcast.350, bf16[2,288,2048]{2,1,0:T(8,128)(2,1)} %bitcast.360, f32[72,2048]{1,0:T(8,128)} %bitcast_convert_fusion.10.refs_3_.refs_2_, f32[1,2048]{1,0:T(1,128)} %bitcast.380, ...), custom_call_target="tpu_custom_call" | custom-call | bytes 180000000 | tf_op jit(solution)/shard_map/pallas_call | solution.py:210
  1031.6 58.4 %shard_map.265 = (f32[68,128]{1,0:T(8,128)S(1)}, bf16[512,768]{1,0:T(8,128)(2,1)S(1)}, bf16[1536,512]{1,0:T(8,128)(2,1)S(1)}, bf16[1536,512]{1,0:T(8,128)(2,1)S(1)}, bf16[1536,512]{1,0:T(8,128)(2,1)S(1)}) custom-call(f32[68,128]{1,0:T(8,128)S(1)} %reshape.596.refs_0_, bf16[512,768]{1,0:T(8,128)(2,1)S(1)} %bitcast_select_fusion.3.refs_1_, ...), custom_call_target="tpu_custom_call" | custom-call | bytes 180000000 | tf_op jit(solution)/shard_map/pallas_call | solution.py:210
  1095.2 2.1 convert_bitcast_fusion.2
  1097.4 2.5 copy.188
  1099.9 3.3 convert_bitcast_fusion.1
  1103.2 3.7 copy.189
  1106.8 3.3 convert_bitcast_fusion
  1110.1 3.5 copy.190
  1113.7 3.4 select_bitcast_fusion
  (419 shorter events, 109.2 us)
Async XLA Ops:
  7.2 140.8 %all-gather.9.cloned.1.call-start = ((), (), s32[]{:S(2)}) async-start(), calls=%async_computation.8 | async-start | bytes 3932160 | tf_op jit(solution)/shard_map/all_gather | solution.py:1583
  12.1 44.2 %copy-start = (bf16[1,512,1536]{1,2,0:T(8,128)(2,1)}, bf16[1,512,1536]{1,2,0:T(8,128)(2,1)S(1)}, u32[]{:S(2)}) copy-start(bf16[1,512,1536]{1,2,0:T(8,128)(2,1)S(1)} %copy.163) | copy-start | bytes 4718596
  12.2 44.2 %copy-start.14 = (bf16[1,512,256]{2,1,0:T(8,128)(2,1)S(1)}, bf16[1,512,256]{2,1,0:T(8,128)(2,1)}, u32[]{:S(2)}) copy-start(bf16[1,512,256]{2,1,0:T(8,128)(2,1)} %param.23) | copy-start | bytes 786436
  55.5 92.5 %all-gather.7.cloned.1.call-start = ((), (), s32[]{:S(2)}) async-start(), calls=%async_computation.7 | async-start | bytes 3932160 | tf_op jit(solution)/shard_map/all_gather | solution.py:1583
  56.3 330.8 %all-gather.15.cloned.1.call-start = ((), (), s32[]{:S(2)}) async-start(), calls=%async_computation.18 | async-start | bytes 3932160 | tf_op jit(solution)/shard_map/all_gather | solution.py:1600
  60.8 71.6 %copy-start.114 = (s32[2]{0:T(128)S(1)}, s32[2]{0:T(128)}, u32[]{:S(2)}) copy-start(s32[2]{0:T(128)} %param.20) | copy-start | bytes 28
  132.3 277.7 %all-gather.11.cloned.1.call-start = ((), (), s32[]{:S(2)}) async-start(), calls=%async_computation.9 | async-start | bytes 3932160 | tf_op jit(solution)/shard_map/all_gather | solution.py:1583
  146.8 260.4 %copy-start.53 = (f32[1,288,64]{2,1,0:T(8,128)}, f32[1,288,64]{2,1,0:T(8,128)S(1)}, u32[]{:S(2)}) copy-start(f32[1,288,64]{2,1,0:T(8,128)S(1)} %get-tuple-element.257) | copy-start | bytes 221188
  226.5 4.3 copy-start.115
  226.6 244.2 %all-gather.13.cloned.1.call-start = ((), (), s32[]{:S(2)}) async-start(), calls=%async_computation.10 | async-start | bytes 3932160 | tf_op jit(solution)/shard_map/all_gather | solution.py:1583
  228.2 8.4 copy-start.43
  384.6 450.1 %reduce-scatter.10.cloned.1.call-start = ((), (), s32[]{:S(2)}) async-start(), calls=%async_computation.12 | async-start | bytes 3932160 | tf_op jit(solution)/shard_map/reduce_scatter | solution.py:1665
  398.6 7.5 copy-start.102
  399.7 7.5 copy-start.56
  399.7 7.5 copy-start.59
  399.7 7.5 copy-start.62
  400.6 8.1 copy-start.45
  403.0 5.7 copy-start.105
  468.5 137.4 %copy-start.72 = (bf16[2,288,2,128]{3,2,1,0:T(2,128)(2,1)}, bf16[2,288,2,128]{3,2,1,0:T(2,128)(2,1)S(1)}, u32[]{:S(2)}) copy-start(bf16[2,288,2,128]{3,2,1,0:T(2,128)(2,1)S(1)} %copy.170) | copy-start | bytes 884740
  612.2 222.5 %reduce-scatter.8.cloned.1.call-start = ((), (), s32[]{:S(2)}) async-start(), calls=%async_computation.11 | async-start | bytes 3932160 | tf_op jit(solution)/shard_map/reduce_scatter | solution.py:1665
  618.5 216.2 %reduce-scatter.12.cloned.1.call-start = ((), (), s32[]{:S(2)}) async-start(), calls=%async_computation.13 | async-start | bytes 3932160 | tf_op jit(solution)/shard_map/reduce_scatter | solution.py:1665
  624.9 401.5 %reduce-scatter.14.cloned.1.call-start = ((), (), s32[]{:S(2)}) async-start(), calls=%async_computation.14 | async-start | bytes 3932160 | tf_op jit(solution)/shard_map/reduce_scatter | solution.py:1669
  627.7 4.3 slice-start.3
  636.1 30.4 %copy-start.54 = (f32[1,288,64]{2,1,0:T(8,128)S(1)}, f32[1,288,64]{2,1,0:T(8,128)}, u32[]{:S(2)}) copy-start(f32[1,288,64]{2,1,0:T(8,128)} %copy-done.53) | copy-start | bytes 221188
  636.1 30.4 %copy-start.57 = (f32[1,288,64]{2,1,0:T(8,128)S(1)}, f32[1,288,64]{2,1,0:T(8,128)}, u32[]{:S(2)}) copy-start(f32[1,288,64]{2,1,0:T(8,128)} %copy-done.55) | copy-start | bytes 221188
  636.1 30.4 %copy-start.60 = (f32[1,288,64]{2,1,0:T(8,128)S(1)}, f32[1,288,64]{2,1,0:T(8,128)}, u32[]{:S(2)}) copy-start(f32[1,288,64]{2,1,0:T(8,128)} %copy-done.58) | copy-start | bytes 221188
  636.1 30.4 %copy-start.63 = (f32[1,288,64]{2,1,0:T(8,128)S(1)}, f32[1,288,64]{2,1,0:T(8,128)}, u32[]{:S(2)}) copy-start(f32[1,288,64]{2,1,0:T(8,128)} %copy-done.61) | copy-start | bytes 221188
  636.3 30.4 %copy-start.67 = (f32[2,288,512]{2,1,0:T(8,128)S(1)}, f32[2,288,512]{2,1,0:T(8,128)}, u32[]{:S(2)}) copy-start(f32[2,288,512]{2,1,0:T(8,128)} %copy-done.66) | copy-start | bytes 3538948
  666.5 5.4 copy-start.91
  677.0 351.2 %reduce-scatter.20.cloned.1.call-start = ((), (), s32[]{:S(2)}) async-start(), calls=%async_computation.17 | async-start | bytes 3932160 | tf_op jit(solution)/shard_map/reduce_scatter | solution.py:1665
  683.1 107.0 %copy-start.120 = (bf16[4,144,768]{2,1,0:T(8,128)(2,1)S(1)}, bf16[4,144,768]{2,1,0:T(8,128)(2,1)}, u32[]{:S(2)}) copy-start(bf16[4,144,768]{2,1,0:T(8,128)(2,1)} %get-tuple-element.109) | copy-start | bytes 2654212
  796.0 232.2 %reduce-scatter.18.cloned.1.call-start = ((), (), s32[]{:S(2)}) async-start(), calls=%async_computation.16 | async-start | bytes 3932160 | tf_op jit(solution)/shard_map/reduce_scatter | solution.py:1665
  802.8 225.4 %reduce-scatter.16.cloned.1.call-start = ((), (), s32[]{:S(2)}) async-start(), calls=%async_computation.15 | async-start | bytes 3932160 | tf_op jit(solution)/shard_map/reduce_scatter | solution.py:1665
  815.4 4.2 slice-start.1
  833.0 80.3 %copy-start.64 = (f32[1,288,64]{2,1,0:T(8,128)S(1)}, f32[1,288,64]{2,1,0:T(8,128)}, u32[]{:S(2)}) copy-start(f32[1,288,64]{2,1,0:T(8,128)} %copy-done.61) | copy-start | bytes 221188
  833.0 80.5 %copy-start.94 = (f32[2,288]{1,0:T(2,128)S(1)}, f32[2,288]{1,0:T(2,128)}, u32[]{:S(2)}) copy-start(f32[2,288]{1,0:T(2,128)} %copy-done.93) | copy-start | bytes 6916
  833.0 80.5 %copy-start.101 = (f32[128]{0:T(128)S(1)}, f32[128]{0:T(128)}, u32[]{:S(2)}) copy-start(f32[128]{0:T(128)} %copy-done.100) | copy-start | bytes 1540
  913.2 6.3 copy-start.6
  913.2 6.3 copy-start.8
  933.1 92.4 %copy-start.107 = (f32[1,2048]{1,0:T(1,128)S(1)}, f32[1,2048]{1,0:T(1,128)}, u32[]{:S(2)}) copy-start(f32[1,2048]{1,0:T(1,128)} %get-tuple-element.102) | copy-start | bytes 24580
  933.1 92.4 %copy-start.113 = (f32[128]{0:T(128)S(1)}, f32[128]{0:T(128)}, u32[]{:S(2)}) copy-start(f32[128]{0:T(128)} %get-tuple-element.197) | copy-start | bytes 1540
  1031.6 58.5 %copy-start.51 = (f32[4,128,768]{2,1,0:T(8,128)S(1)}, f32[4,128,768]{2,1,0:T(8,128)}, u32[]{:S(2)}) copy-start(f32[4,128,768]{2,1,0:T(8,128)} %get-tuple-element.105) | copy-start | bytes 4718596
  1094.4 5.5 copy-start.9
  1113.7 4.7 copy-start.85
  1113.7 4.7 copy-start.87
  1113.7 5.5 copy-start.84
  1113.7 5.5 copy-start.86
  1113.7 6.3 copy-start.81
  (90 other events, 183.1 us)
Sparse Core Ops, SparseCore 0:
  55.6 44.3 all-gather.8
  102.4 43.9 all-gather.6
  148.0 95.2 all-gather.14
  245.5 59.5 all-gather.10
  384.7 72.1 all-gather.12
  612.3 49.3 reduce-scatter.9
  665.3 51.2 reduce-scatter.7
  719.6 45.2 reduce-scatter.11
  767.2 69.9 reduce-scatter.13
  840.0 43.9 reduce-scatter.19
  887.0 43.9 reduce-scatter.17
  933.9 43.9 reduce-scatter.15

commit v8 on v7

--- a/solution.py
+++ b/solution.py
@@ -200,7 +200,7 @@
         greet(axes, across)
         for part in parts:
             part.start()
-        for part in parts:
+        for part in reversed(parts):
             part.run()
         for part in parts:
             part.finish()
@@ -847,12 +847,18 @@
             out[...] = total
 
 
+def chunk_count(rows):
+    return 3 if rows % 24 == 0 else 1
+
+
 class Gatherer:
     def __init__(self, axis, rows, half):
-        self.axis, self.rows, self.half = axis, rows, half
+        self.axis, self.half = axis, half
         self.size = size = lax.axis_size(axis)
-        self.scratch = [pltpu.VMEM((2, size, 2 * rows, half), BF16)]
-        self.scratch += [SEM((size,))] * 4 + [SEM]
+        self.chunks = chunks = chunk_count(rows)
+        self.rows = rows // chunks
+        self.scratch = [pltpu.VMEM((2, chunks, size, 2 * self.rows, half), BF16)]
+        self.scratch += [SEM((chunks, size))] * 4 + [SEM((chunks,))]
 
     def bind(self, refs):
         self.board, self.send, self.recv, self.sib_send, self.sib_recv, self.relay_send = refs
@@ -860,6 +866,7 @@
         self.sibling = 1 - self.core
         self.me = lax.axis_index(self.axis)
         self.relays = line_relays(self.size) if self.axis == "dp" else []
+        self.order = line_order(self.size) if self.axis == "dp" else range(self.size)
 
     def direct(self, place):
         sent = place != self.me
@@ -867,179 +874,249 @@
             sent = sent & jnp.logical_not(far_pair(place, self.me))
         return sent
 
-    def spread(self, place, slot):
+    def spread(self, chunk, place, slot):
+        block = self.board.at[self.core, chunk, slot]
         return remote(
-            self.board.at[self.core, slot], self.board.at[self.core, slot], self.send.at[place],
-            self.recv.at[slot], {self.axis: place},
-        )
-
-    def passed(self, source, target):
+            block, block, self.send.at[chunk, place], self.recv.at[chunk, slot], {self.axis: place}
+        )
+
+    def passed(self, chunk, source, target):
+        block = self.board.at[self.core, chunk, source]
         return remote(
-            self.board.at[self.core, source], self.board.at[self.core, source], self.relay_send,
-            self.recv.at[source], {self.axis: target},
-        )
-
-    def over(self, tree, slot):
+            block, block, self.relay_send.at[chunk], self.recv.at[chunk, source],
+            {self.axis: target},
+        )
+
+    def over(self, tree, chunk, slot):
+        block = self.board.at[tree, chunk, slot]
         return remote(
-            self.board.at[tree, slot], self.board.at[tree, slot], self.sib_send.at[slot],
-            self.sib_recv.at[slot], {"section": self.sibling},
-        )
-
-    def begin(self, result):
+            block, block, self.sib_send.at[chunk, slot], self.sib_recv.at[chunk, slot],
+            {"section": self.sibling},
+        )
+
+    def begin(self, chunk, result):
         half = self.half
         piece = jnp.concatenate([result[:, :half], result[:, half:]], axis=0)
-        self.board[self.core, self.me] = piece.astype(BF16)
+        self.board[self.core, chunk, self.me] = piece.astype(BF16)
         for place in range(self.size):
             @pl.when(self.direct(place))
             def _():
-                self.spread(place, self.me).start()
-
-        self.over(self.core, self.me).start()
-
-    def arrive(self, place):
-        @pl.when(place != self.me)
-        def _():
-            self.spread(place, place).wait_recv()
-
-        for via, source, target in self.relays:
-            @pl.when((self.me == via) & (place == source))
+                self.spread(chunk, place, self.me).start()
+
+        self.over(self.core, chunk, self.me).start()
+
+    def arrive(self, chunk):
+        for place in self.order:
+            @pl.when(place != self.me)
             def _():
-                self.passed(source, target).start()
-
-        @pl.when(place != self.me)
-        def _():
-            self.over(self.core, place).start()
-
-    def arrive_over(self, place):
-        self.over(self.sibling, place).wait_recv()
+                self.spread(chunk, place, place).wait_recv()
+
+            for via, source, target in self.relays:
+                if source == place:
+                    @pl.when(self.me == via)
+                    def _():
+                        self.passed(chunk, source, target).start()
+
+            @pl.when(place != self.me)
+            def _():
+                self.over(self.core, chunk, place).start()
+
+    def arrive_over(self, chunk):
+        for place in range(self.size):
+            self.over(self.sibling, chunk, place).wait_recv()
+
+    def side_rows(self, block, side):
+        return block[side * self.rows : (side + 1) * self.rows]
 
     def unpack(self, out, tree):
-        rows = self.rows
-
         @pl.loop(0, self.half // CHUNK)
         def _(step):
             at = pl.multiple_of(step * CHUNK, CHUNK)
             blocks = [
-                self.board[tree, place, :, pl.ds(at, CHUNK)].astype(F32)
+                self.board[tree, chunk, place, :, pl.ds(at, CHUNK)].astype(F32)
                 for place in range(self.size)
+                for chunk in range(self.chunks)
             ]
             for side in range(2):
-                whole = [block[side * rows : (side + 1) * rows] for block in blocks]
+                whole = [self.side_rows(block, side) for block in blocks]
                 out[tree, :, pl.ds(side * self.half + at, CHUNK)] = jnp.concatenate(
                     whole, axis=0
                 ).astype(BF16)
 
-    def unpack_place(self, out, place):
-        rows = self.rows
-
+    def unpack_chunk(self, out, chunk):
         @pl.loop(0, self.half // CHUNK)
         def _(step):
             at = pl.multiple_of(step * CHUNK, CHUNK)
-            blocks = [self.board[tree, place, :, pl.ds(at, CHUNK)].astype(F32) for tree in range(2)]
+            blocks = [
+                self.board[tree, chunk, place, :, pl.ds(at, CHUNK)].astype(F32)
+                for place in range(self.size)
+                for tree in range(2)
+            ]
             for side in range(2):
-                whole = [block[side * rows : (side + 1) * rows] for block in blocks]
-                out[place, :, pl.ds(side * self.half + at, CHUNK)] = jnp.concatenate(
+                whole = [self.side_rows(block, side) for block in blocks]
+                out[chunk, :, pl.ds(side * self.half + at, CHUNK)] = jnp.concatenate(
                     whole, axis=0
                 ).astype(BF16)
 
     def complete(self, out):
-        for place in range(self.size):
-            self.arrive(place)
+        for chunk in range(self.chunks):
+            self.arrive(chunk)
         self.unpack(out, self.core)
-        for place in range(self.size):
-            self.arrive_over(place)
+        for chunk in range(self.chunks):
+            self.arrive_over(chunk)
         self.unpack(out, self.sibling)
 
     def finish(self):
-        for place in range(self.size):
-            @pl.when(self.direct(place))
-            def _():
-                self.spread(place, self.me).wait_send()
-
-            self.over(self.core, place).wait_send()
-
-        for via, source, target in self.relays:
-            @pl.when(self.me == via)
-            def _():
-                self.passed(source, target).wait_send()
+        for chunk in range(self.chunks):
+            for place in range(self.size):
+                @pl.when(self.direct(place))
+                def _():
+                    self.spread(chunk, place, self.me).wait_send()
+
+                self.over(self.core, chunk, place).wait_send()
+
+            for via, source, target in self.relays:
+                @pl.when(self.me == via)
+                def _():
+                    self.passed(chunk, source, target).wait_send()
 
 
 class Scatterer:
     def __init__(self, axis, rows, half):
-        self.axis, self.rows, self.half = axis, rows, half
+        self.axis, self.half = axis, half
         self.size = size = lax.axis_size(axis)
-        self.scratch = [pltpu.VMEM((size, 2 * rows, half), BF16)] * 4
-        self.scratch += [pltpu.VMEM((2 * rows, half), F32)] + [SEM((size,))] * 4
+        self.chunks = chunks = chunk_count(rows)
+        self.rows = rows // chunks
+        block = (2 * self.rows, half)
+        self.scratch = [pltpu.VMEM((chunks, size) + block, BF16)] * 4
+        self.scratch += [pltpu.VMEM((chunks,) + block, F32), pltpu.VMEM((chunks,) + block, BF16)]
+        self.scratch += [SEM((chunks, size))] * 4 + [SEM((chunks,))] * 2
 
     def bind(self, refs):
-        self.to_sib, self.from_sib, self.to_peer, self.from_peer, self.total = refs[:5]
-        self.sib_send, self.sib_recv, self.peer_send, self.peer_recv = refs[5:]
+        self.to_sib, self.from_sib, self.to_peer, self.from_peer, self.total, self.joint = refs[:6]
+        self.sib_send, self.sib_recv, self.peer_send, self.peer_recv = refs[6:10]
+        self.join_send, self.join_recv = refs[10:]
         self.core = lax.axis_index("section")
         self.sibling = 1 - self.core
         self.me = lax.axis_index(self.axis)
-
-    def over(self, place):
+        self.sides = [(0, 1, 3), (3, 2, 0)] if self.axis == "dp" and self.size == 4 else []
+        self.order = [0, 3, 1, 2] if self.sides else range(self.size)
+
+    def over(self, chunk, place):
         return remote(
-            self.to_sib.at[place], self.from_sib.at[place], self.sib_send.at[place],
-            self.sib_recv.at[place], {"section": self.sibling},
-        )
-
-    def spread(self, place, slot):
+            self.to_sib.at[chunk, place], self.from_sib.at[chunk, place],
+            self.sib_send.at[chunk, place], self.sib_recv.at[chunk, place],
+            {"section": self.sibling},
+        )
+
+    def spread(self, chunk, place, slot):
         return remote(
-            self.to_peer.at[place], self.from_peer.at[slot], self.peer_send.at[place],
-            self.peer_recv.at[slot], {self.axis: place},
-        )
+            self.to_peer.at[chunk, place], self.from_peer.at[chunk, slot],
+            self.peer_send.at[chunk, place], self.peer_recv.at[chunk, slot], {self.axis: place},
+        )
+
+    def by_way(self, chunk, via, target):
+        return remote(
+            self.to_peer.at[chunk, target], self.joint.at[chunk], self.join_send.at[chunk],
+            self.join_recv.at[chunk], {self.axis: via},
+        )
+
+    def plain(self, place):
+        ok = place != self.me
+        for source, via, target in self.sides:
+            if place == target:
+                ok = ok & (self.me != source) & (self.me != via)
+        return ok
+
+    def expected(self, place):
+        ok = place != self.me
+        for source, via, target in self.sides:
+            if place == source:
+                ok = ok & (self.me != target)
+        return ok
 
     def over_columns(self, body):
         @pl.loop(0, self.half // CHUNK)
         def _(step):
             body(pl.multiple_of(step * CHUNK, CHUNK))
 
-    def absorb(self, place, mine):
-        self.over(place).wait_recv()
-
-        def add(at):
-            both = mine(at) + self.from_sib[place, :, pl.ds(at, CHUNK)].astype(F32)
-            self.to_peer[place, :, pl.ds(at, CHUNK)] = both.astype(BF16)
-
-            @pl.when(place == self.me)
+    def absorb(self, chunk, mine):
+        for place in self.order:
+            self.over(chunk, place).wait_recv()
+
+            def add(at):
+                both = mine(place, at)
+                both += self.from_sib[chunk, place, :, pl.ds(at, CHUNK)].astype(F32)
+                self.to_peer[chunk, place, :, pl.ds(at, CHUNK)] = both.astype(BF16)
+
+                @pl.when(place == self.me)
+                def _():
+                    self.total[chunk, :, pl.ds(at, CHUNK)] = both
+
+            self.over_columns(add)
+
+            for source, via, target in self.sides:
+                if place == target:
+                    @pl.when(self.me == source)
+                    def _():
+                        self.by_way(chunk, via, target).start()
+
+            @pl.when(self.plain(place))
             def _():
-                self.total[:, pl.ds(at, CHUNK)] = both
-
-        self.over_columns(add)
-
-        @pl.when(place != self.me)
-        def _():
-            self.spread(place, self.me).start()
-
-    def collect(self):
-        for place in range(self.size):
-            @pl.when(place != self.me)
+                self.spread(chunk, place, self.me).start()
+
+        for source, via, target in self.sides:
+            @pl.when(self.me == via)
             def _():
-                self.spread(place, place).wait_recv()
-                self.total[...] += self.from_peer[place].astype(F32)
-
-        total = self.total[...]
+                self.by_way(chunk, via, target).wait_recv()
+
+                def add(at):
+                    at = pl.ds(at, CHUNK)
+                    both = self.to_peer[chunk, target, :, at].astype(F32)
+                    both += self.joint[chunk, :, at].astype(F32)
+                    self.to_peer[chunk, target, :, at] = both.astype(BF16)
+
+                self.over_columns(add)
+                self.spread(chunk, target, self.me).start()
+
+    def collect(self, chunk):
+        for place in self.order:
+            @pl.when(self.expected(place))
+            def _():
+                self.spread(chunk, place, place).wait_recv()
+                self.total[chunk] += self.from_peer[chunk, place].astype(F32)
+
+        total = self.total[chunk]
         return jnp.concatenate([total[: self.rows], total[self.rows :]], axis=1)
 
     def finish(self):
-        for place in range(self.size):
-            self.over(place).wait_send()
-
-            @pl.when(place != self.me)
-            def _():
-                self.spread(place, self.me).wait_send()
+        for chunk in range(self.chunks):
+            for place in range(self.size):
+                self.over(chunk, place).wait_send()
+
+                @pl.when(self.plain(place))
+                def _():
+                    self.spread(chunk, place, self.me).wait_send()
+
+            for source, via, target in self.sides:
+                @pl.when(self.me == source)
+                def _():
+                    self.by_way(chunk, via, target).wait_send()
+
+                @pl.when(self.me == via)
+                def _():
+                    self.spread(chunk, target, self.me).wait_send()
 
 
 class RowScatterer(Scatterer):
-    def packed(self, tree, place, at):
+    def packed(self, tree, chunk, place, at):
         rows = self.rows
-        low = rows * place // 16 * 16
-        high = -(-rows * (place + 1) // 16) * 16
-        skip = rows * place - low
+        first = rows * (place * self.chunks + chunk)
+        low = first // 16 * 16
+        high = -(-(first + rows) // 16) * 16
         parts = [
             self.terms[tree, low:high, pl.ds(side * self.half + at, CHUNK)].astype(F32)[
-                skip : skip + rows
+                first - low : first - low + rows
             ]
             for side in range(2)
         ]
@@ -1047,22 +1124,23 @@
 
     def prepare(self, terms):
         self.terms = terms
-        for place in range(self.size):
-            def pack(at):
-                self.to_sib[place, :, pl.ds(at, CHUNK)] = self.packed(
-                    self.sibling, place, at
-                ).astype(BF16)
-
-            self.over_columns(pack)
+        for chunk in range(self.chunks):
+            for place in range(self.size):
+                def pack(at):
+                    self.to_sib[chunk, place, :, pl.ds(at, CHUNK)] = self.packed(
+                        self.sibling, chunk, place, at
+                    ).astype(BF16)
+
+                self.over_columns(pack)
 
     def start(self):
-        for place in range(self.size):
-            self.over(place).start()
-
-    def summed(self):
-        for place in range(self.size):
-            self.absorb(place, lambda at: self.packed(self.core, place, at))
-        return self.collect()
+        for chunk in range(self.chunks):
+            for place in range(self.size):
+                self.over(chunk, place).start()
+
+    def send_on(self):
+        for chunk in range(self.chunks):
+            self.absorb(chunk, lambda place, at: self.packed(self.core, chunk, place, at))
 
 
 class Staged(Part):
@@ -1096,6 +1174,10 @@
 
 def vmem_bf16(*shape):
     return (jax.ShapeDtypeStruct(shape, BF16), VMEM)
+
+
+def rows_at(chunk, rows):
+    return pl.ds(pl.multiple_of(chunk * rows, 8), rows)
 
 
 class LastHub(Staged):
@@ -1121,9 +1203,15 @@
         self.rows_in.start()
 
     def run(self):
-        total = self.rows_in.summed()
-        result, self.gain_grad[...] = norm_back(total, self.values[...], self.gain[...])
-        self.rows_out.begin(result + self.add[...])
+        self.rows_in.send_on()
+        self.gain_grad[...] = jnp.zeros_like(self.gain_grad)
+        for chunk in range(self.rows_in.chunks):
+            at = rows_at(chunk, self.rows_in.rows)
+            result, gain_grad = norm_back(
+                self.rows_in.collect(chunk), self.values[at], self.gain[...]
+            )
+            self.gain_grad[...] += gain_grad
+            self.rows_out.begin(chunk, result + self.add[at])
         self.rows_out.complete(self.gathered)
 
 
@@ -1134,12 +1222,12 @@
         units = weights[0].shape[0]
         self.has_forward, self.has_backward, self.units = forward, backward, units
         self.depth = depth
-        self.block = 2 * rows
         self.size = size = lax.axis_size("dp")
         self.rows_in = RowScatterer("tensor", rows, half)
         self.spread_in = Gatherer("dp", rows, half)
+        self.chunks, self.rows = self.rows_in.chunks, self.rows_in.rows
+        chunks, chunk_rows = self.chunks, 2 * size * self.rows
         helpers = [self.rows_in, self.spread_in]
-        group_rows = 2 * rows
         tensor_rows = lax.axis_size("tensor") * rows
         matrix = pltpu.VMEM((units, depth), BF16)
         ins = {"terms": (terms, VMEM), "own": (own, VMEM), "gain": (gain, VMEM)}
@@ -1147,32 +1235,33 @@
         ins |= {name: (value, VMEM) for name, value in extra.items()}
         outs = {}
         scratch = {"w_gate": matrix, "w_up": matrix, "w_down": matrix, "load": SEM((3,))}
+        kept = pltpu.VMEM((size, 2 * self.rows, half), F32)
         if forward:
             outs |= {
                 "middle": vmem_f32(rows, depth),
-                "mlp_in": vmem_bf16(size, group_rows, depth),
-                "hidden": vmem_bf16(size, group_rows, units),
+                "mlp_in": vmem_bf16(chunks, chunk_rows, depth),
+                "hidden": vmem_bf16(chunks, chunk_rows, units),
                 "own_out": vmem_f32(rows, depth),
                 "out": vmem_bf16(2, tensor_rows, depth),
             }
             self.back = Scatterer("dp", rows, half)
             self.out_rows = Gatherer("tensor", rows, half)
             helpers += [self.back, self.out_rows]
-            scratch["kept"] = pltpu.VMEM((group_rows, half), F32)
+            scratch["kept"] = kept
         if forward and not backward:
-            outs |= {"gate": vmem_f32(size, group_rows, units), "up": vmem_f32(size, group_rows, units)}
+            outs |= {"gate": vmem_f32(chunks, chunk_rows, units), "up": vmem_f32(chunks, chunk_rows, units)}
         if forward and backward:
-            outs["grad_mlp"] = vmem_bf16(size, group_rows, depth)
+            outs["grad_mlp"] = vmem_bf16(chunks, chunk_rows, depth)
             self.grad_in = Gatherer("dp", rows, half)
             helpers += [self.grad_in]
             scratch |= {
-                "gate": pltpu.VMEM((size, group_rows, units), F32),
-                "up": pltpu.VMEM((size, group_rows, units), F32),
+                "gate": pltpu.VMEM((chunks, chunk_rows, units), F32),
+                "up": pltpu.VMEM((chunks, chunk_rows, units), F32),
             }
         if backward:
             outs |= {
-                "grad_gate": vmem_bf16(size, group_rows, units),
-                "grad_up": vmem_bf16(size, group_rows, units),
+                "grad_gate": vmem_bf16(chunks, chunk_rows, units),
+                "grad_up": vmem_bf16(chunks, chunk_rows, units),
                 "grad_middle": vmem_f32(rows, depth),
                 "mlp_gain_grad": vmem_f32(1, depth),
                 "grad_attn": vmem_bf16(2, tensor_rows, depth),
@@ -1180,12 +1269,12 @@
             self.grad_back = Scatterer("dp", rows, half)
             self.grad_rows = Gatherer("tensor", rows, half)
             helpers += [self.grad_back, self.grad_rows]
-            scratch["grad_kept"] = pltpu.VMEM((group_rows, half), F32)
+            scratch["grad_kept"] = kept
         if backward and not forward:
             outs |= {
                 "gain_grad": vmem_f32(1, depth),
                 "incoming": vmem_bf16(2, tensor_rows, depth),
-                "grad_mlp": vmem_bf16(size, group_rows, depth),
+                "grad_mlp": vmem_bf16(chunks, chunk_rows, depth),
             }
             scratch["grad_own"] = pltpu.VMEM((rows, depth), F32)
             self.incoming_rows = Gatherer("tensor", rows, half)
@@ -1206,81 +1295,92 @@
     def start(self):
         self.rows_in.start()
         if self.has_forward and self.has_backward:
-            self.grad_in.begin(self.grad_own[...])
+            for chunk in range(self.chunks):
+                self.grad_in.begin(chunk, self.grad_own[rows_at(chunk, self.rows)])
 
     def run(self):
-        total = self.rows_in.summed()
-        if self.has_forward:
-            middle = self.own[...] + total
-            self.middle[...] = middle
-            mean_sq = jnp.mean(middle * middle, axis=1, keepdims=True)
-            self.spread_in.begin(middle * lax.rsqrt(mean_sq + EPSILON) * self.gain[...])
-        else:
-            result, self.gain_grad[...] = norm_back(total, self.own[...], self.gain[...])
-            result = (result + self.add[...]).astype(BF16).astype(F32)
-            self.grad_own[...] = result
-            self.spread_in.begin(result)
-            self.incoming_rows.begin(result)
+        self.rows_in.send_on()
+        if self.has_backward:
+            self.mlp_gain_grad[...] = jnp.zeros_like(self.mlp_gain_grad)
+        if not self.has_forward:
+            self.gain_grad[...] = jnp.zeros_like(self.gain_grad)
+        for chunk in range(self.chunks):
+            at = rows_at(chunk, self.rows)
+            total = self.rows_in.collect(chunk)
+            if self.has_forward:
+                middle = self.own[at] + total
+                self.middle[at] = middle
+                mean_sq = jnp.mean(middle * middle, axis=1, keepdims=True)
+                normed = middle * lax.rsqrt(mean_sq + EPSILON) * self.gain[...]
+                self.spread_in.begin(chunk, normed)
+            else:
+                result, gain_grad = norm_back(total, self.own[at], self.gain[...])
+                self.gain_grad[...] += gain_grad
+                result = (result + self.add[at]).astype(BF16).astype(F32)
+                self.grad_own[at] = result
+                self.spread_in.begin(chunk, result)
+                self.incoming_rows.begin(chunk, result)
         for copy in self.loads():
             copy.wait()
 
-        me = lax.axis_index("dp")
-        turn = 1 - 2 * (me // (self.size // 2))
-
-        def turned(step):
-            return lax.rem(me + turn * step + self.size, self.size)
-
+        self.spread_in.arrive(0)
         if self.has_forward and self.has_backward:
-            for place in line_order(self.size):
-                self.grad_in.arrive(place)
-        self.spread_in.arrive(me)
-
-        @pl.loop(0, self.size)
-        def _(step):
-            place = turned(step)
-            self.spread_in.arrive_over(place)
+            self.grad_in.arrive(0)
+
+        @pl.loop(0, self.chunks)
+        def _(chunk):
+            self.spread_in.arrive_over(chunk)
+            if self.has_forward:
+                self.spread_in.unpack_chunk(self.mlp_in, chunk)
+                self.forward_chunk(chunk)
+            else:
+                self.spread_in.unpack_chunk(self.grad_mlp, chunk)
             if self.has_forward and self.has_backward:
-                self.grad_in.arrive_over(place)
-                self.grad_in.unpack_place(self.grad_mlp, place)
+                self.grad_in.arrive_over(chunk)
+                self.grad_in.unpack_chunk(self.grad_mlp, chunk)
+            if self.has_backward:
+                self.backward_chunk(chunk)
+
+            @pl.when(chunk + 1 < self.chunks)
+            def _():
+                self.spread_in.arrive(chunk + 1)
+                if self.has_forward and self.has_backward:
+                    self.grad_in.arrive(chunk + 1)
+
             if self.has_forward:
-                self.spread_in.unpack_place(self.mlp_in, place)
-                self.forward_place(place)
-            else:
-                self.spread_in.unpack_place(self.grad_mlp, place)
+                self.back.absorb(chunk, lambda place, at: self.kept[place, :, pl.ds(at, CHUNK)])
             if self.has_backward:
-                self.backward_place(place)
-
-            @pl.when(step + 1 < self.size)
+                self.grad_back.absorb(
+                    chunk, lambda place, at: self.grad_kept[place, :, pl.ds(at, CHUNK)]
+                )
+
+            @pl.when(chunk > 0)
             def _():
-                self.spread_in.arrive(turned(step + 1))
-
-            if self.has_forward:
-                self.back.absorb(place, lambda at: self.kept[:, pl.ds(at, CHUNK)])
-            if self.has_backward:
-                self.grad_back.absorb(place, lambda at: self.grad_kept[:, pl.ds(at, CHUNK)])
-
-        if self.has_forward:
-            output = (self.middle[...] + self.back.collect()).astype(BF16).astype(F32)
-            self.own_out[...] = output
-            if not self.has_backward:
-                self.out_rows.begin(output)
+                self.hand_back(chunk - 1)
+
+        self.hand_back(self.chunks - 1)
         if self.has_backward:
-            values = self.middle if self.has_forward else self.middle_in
-            gain = self.gain if self.has_forward else self.mlp_gain
-            result, self.mlp_gain_grad[...] = norm_back(
-                self.grad_back.collect(), values[...], gain[...]
-            )
-            result += self.grad_own[...]
-            self.grad_middle[...] = result
-            self.grad_rows.begin(result)
-            if self.has_forward:
-                self.out_rows.begin(self.own_out[...])
             self.grad_rows.complete(self.grad_attn)
         if self.has_forward:
             self.out_rows.complete(self.out)
         else:
             self.incoming_rows.complete(self.incoming)
 
+    def hand_back(self, chunk):
+        at = rows_at(chunk, self.rows)
+        if self.has_backward:
+            values = self.middle if self.has_forward else self.middle_in
+            gain = self.gain if self.has_forward else self.mlp_gain
+            result, gain_grad = norm_back(self.grad_back.collect(chunk), values[at], gain[...])
+            self.mlp_gain_grad[...] += gain_grad
+            result += self.grad_own[at]
+            self.grad_middle[at] = result
+            self.grad_rows.begin(chunk, result)
+        if self.has_forward:
+            output = (self.middle[at] + self.back.collect(chunk)).astype(BF16).astype(F32)
+            self.own_out[at] = output
+            self.out_rows.begin(chunk, output)
+
     def unit_tiles(self, body):
         tile = 256
 
@@ -1288,55 +1388,61 @@
         def _(step):
             body(pl.ds(pl.multiple_of(step * tile, tile), tile))
 
-    def forward_place(self, place):
+    def forward_chunk(self, chunk):
         def tile(at):
-            rows = self.mlp_in[place]
+            rows = self.mlp_in[chunk]
             gate = dot_inner(rows, self.w_gate[at, :])
             up = dot_inner(rows, self.w_up[at, :])
-            self.gate[place, :, at] = gate
-            self.up[place, :, at] = up
-            self.hidden[place, :, at] = (gate * jax.nn.sigmoid(gate) * up).astype(BF16)
+            self.gate[chunk, :, at] = gate
+            self.up[chunk, :, at] = up
+            self.hidden[chunk, :, at] = (gate * jax.nn.sigmoid(gate) * up).astype(BF16)
 
         self.unit_tiles(tile)
         self.terms_out(
-            place, self.back, self.kept, lambda at: dot(self.hidden[place], self.w_down[:, at])
-        )
-
-    def backward_place(self, place):
+            chunk, self.back, self.kept, lambda at: dot(self.hidden[chunk], self.w_down[:, at])
+        )
+
+    def backward_chunk(self, chunk):
         def tile(at):
-            grad_hidden = dot_inner(self.grad_mlp[place], self.w_down[at, :])
-            gate, up = self.gate[place, :, at], self.up[place, :, at]
+            grad_hidden = dot_inner(self.grad_mlp[chunk], self.w_down[at, :])
+            gate, up = self.gate[chunk, :, at], self.up[chunk, :, at]
             share = jax.nn.sigmoid(gate)
             act = gate * share
-            self.grad_up[place, :, at] = (grad_hidden * act).astype(BF16)
-            self.grad_gate[place, :, at] = (
+            self.grad_up[chunk, :, at] = (grad_hidden * act).astype(BF16)
+            self.grad_gate[chunk, :, at] = (
                 grad_hidden * up * (share + act * (1.0 - share))
             ).astype(BF16)
 
         self.unit_tiles(tile)
         self.terms_out(
-            place, self.grad_back, self.grad_kept,
-            lambda at: dot(self.grad_gate[place], self.w_gate[:, at])
-            + dot(self.grad_up[place], self.w_up[:, at]),
-        )
-
-    def terms_out(self, place, scatterer, kept, product):
-        rows, half = self.block // 2, self.depth // 2
+            chunk, self.grad_back, self.grad_kept,
+            lambda at: dot(self.grad_gate[chunk], self.w_gate[:, at])
+            + dot(self.grad_up[chunk], self.w_up[:, at]),
+        )
+
+    def terms_out(self, chunk, scatterer, kept, product):
+        rows, half = self.rows, self.depth // 2
         first = lax.axis_index("section") == 0
 
         @pl.loop(0, half // CHUNK)
         def _(step):
             low = pl.multiple_of(step * CHUNK, CHUNK)
+            at = pl.ds(low, CHUNK)
             sides = [product(pl.ds(side * half + low, CHUNK)) for side in range(2)]
-            trees = [
-                jnp.concatenate([side[tree * rows : (tree + 1) * rows] for side in sides], axis=0)
-                for tree in range(2)
-            ]
-            at = pl.ds(low, CHUNK)
-            kept[:, at] = jnp.where(first, trees[0], trees[1])
-            scatterer.to_sib[place, :, at] = jnp.where(first, trees[1], trees[0]).astype(BF16)
-
-        scatterer.over(place).start()
+            for place in range(self.size):
+                trees = []
+                for tree in range(2):
+                    start = (2 * place + tree) * rows
+                    trees.append(
+                        jnp.concatenate([side[start : start + rows] for side in sides], axis=0)
+                    )
+                kept[place, :, at] = jnp.where(first, trees[0], trees[1])
+                scatterer.to_sib[chunk, place, :, at] = jnp.where(
+                    first, trees[1], trees[0]
+                ).astype(BF16)
+
+        for place in range(self.size):
+            scatterer.over(chunk, place).start()
 
 
 def hub_plain(terms, own_args, body, own_outs, scatter, gathers):
@@ -1751,15 +1857,15 @@
             grad_gate, grad_up, grad_middle, mlp_gain_first, grad_attn,
             attn_gain_second, incoming_second, grad_mlp,
         ) = outs
-        unit_first = scatter_units(
-            weight_products(
-                [
-                    (flat(grad_gate), flat(mlp_in_first)),
-                    (flat(grad_up), flat(mlp_in_first)),
-                    (flat(hidden_first), flat(grad_mlp)),
-                ]
-            )
-        )
+        products = weight_products(
+            [
+                (flat(grad_gate), flat(mlp_in_first)),
+                (flat(grad_up), flat(mlp_in_first)),
+                (flat(hidden_first), flat(grad_mlp)),
+            ]
+        )
+        unit_first = scatter_units(products[:2])
+        unit_first += scatter_units([tied(products[2], *unit_first)])
         carried = []
         terms, pairs, head_first = attn_backward(
             grad_attn, saved_first, first_weights, gains[0], slot,
@@ -1768,8 +1874,9 @@
         (home_second,) = carried
         whole = jnp.concatenate(weight_products(pairs), axis=1).reshape(dp_size, 4, -1, q_width + qkv_width)
         part = LastHub(terms, own_in, gains[0][0][None], grad_middle)
-        (attn_gain_first, incoming_first), ((attn_first,),) = with_cargo(
-            part, [ScatterKV(whole.transpose(1, 0, 2, 3))], everyone, 10, 60, 56
+        (attn_gain_first, incoming_first), ((attn_first,), home_first) = with_cargo(
+            part, [ScatterKV(whole.transpose(1, 0, 2, 3)), UnitsHome(unit_first[:2], 0)], everyone,
+            10, 60, 56,
         )
         attn_first = attn_first.reshape(own_depth, -1).astype(BF16)
         outputs = [output_first, output_second]
@@ -1792,13 +1899,13 @@
     if fast:
         mine = jnp.where(core == 0, weight_grads[0][0], weight_grads[1][0])
         other = jnp.where(core == 0, weight_grads[1][0], weight_grads[0][0])
-        (gain_total,), (arrived,), home_first = fused(
-            [TotalOverAll(gain_total.reshape(-1, 128)), Swap(other), UnitsHome(unit_first, 0)],
+        (gain_total,), (arrived,), down_home = fused(
+            [TotalOverAll(gain_total.reshape(-1, 128)), Swap(other), UnitsHome(unit_first[2:], 0)],
             everyone, True, 11, 60,
         )
         attn_home = (jnp.where(core == 0, mine, arrived), jnp.where(core == 0, arrived, mine))
         unit_home = [
-            jnp.where(core == 0, first, second) for first, second in zip(home_first, home_second)
+            jnp.where(core == 0, first, second) for first, second in zip(home_first + down_home, home_second)
         ]
         gain_total = gain_total.reshape(2, -1)
     else:

time: 1140 us -> 1280 us (1.12)
  waiting for transfers between devices: 1.02 us -> 172 us
  Pallas kernels: 874 us -> 847 us
    reduce_scatter x6, waiting for transfers between devices: 0.06 us -> 171 us  [scatter_units(): lax.psum_scatter(item, 'tensor', scatter_dimension=0, tiled=True)]
    pallas_call x11, Pallas kernels: 874 us -> 847 us  [fused(): pl.pallas_call(kernel, out_shape=[item[0] for item in outs], in_specs=[it...]
    unnamed x267 -> x255, local copies, waits for them, and re-layouts: 53.6 us -> 46.7 us
  transfers between devices with their start and end apart: 12 -> 12, of which waited for: 0 -> 4; matrix products, arithmetic and copies ran while one was open for 14% -> 13% of each run, Pallas kernels for 56% -> 43%
where the time goes in v8:
time: 1280 us
  Pallas kernels  847 us (66%)
  waiting for transfers between devices  172 us (13%)
  matrix products  96.7 us (8%)
  local copies, waits for them, and re-layouts  79.8 us (6%)
  other arithmetic  60 us (5%)
  between operations  20.4 us (2%)
    pallas_call x11, Pallas kernels, fused(): pl.pallas_call(kernel, out_shape=[item[0] for item in outs], in_specs=[it...  847 us
    reduce_scatter x6, waiting for transfers between devices, scatter_units(): lax.psum_scatter(item, 'tensor', scatter_dimension=0, tiled=True)  171 us
    unnamed x255, local copies, waits for them, and re-layouts  46.7 us
    dot_general x10, matrix products, dot_outer(): return lax.dot_general(left, right, OUTER, preferred_element_type=F32)  44.6 us
  transfers between devices with their start and end apart: 12, of which 4 were waited for; matrix products, arithmetic and copies ran while one was open for 13% of the time, Pallas kernels for 43%

profile of v8, /device:TPU:0, one launch (start us, length us, event | category | flops | bytes accessed | tf_op | source)
XLA Modules:
  0.0 1277.4 jit_solution(7952933461032319450)
XLA Ops:
  12.2 41.5 %shard_map.255 = (bf16[192,2048]{1,0:T(8,128)(2,1)S(1)}, bf16[192,2048]{1,0:T(8,128)(2,1)S(1)}, f32[2,4,10,128]{3,2,1,0:T(8,128)S(1)}) custom-call(bf16[1536,512]{1,0:T(8,128)(2,1)S(1)} %bitcast.325, bf16[1536,512]{1,0:T(8,128)(2,1)S(1)} %bitcast.323, f32[10,128]{1,0:T(8,128)S(1)} %fusion.112.refs_2_), custom_call_target="tpu_custom_call" | custom-call | bytes 135000000 | tf_op jit(solution)/shard_map/pallas_call | solution.py:210
  60.8 68.4 %shard_map.256 = (bf16[2048,512]{1,0:T(8,128)(2,1)S(1)}, bf16[256,2048]{1,0:T(8,128)(2,1)S(1)}, bf16[192,2048]{1,0:T(8,128)(2,1)S(1)}, bf16[768,512]{1,0:T(8,128)(2,1)}) custom-call(bf16[512,512]{1,0:T(8,128)(2,1)S(1)} %bitcast.329, bf16[512,256]{1,0:T(8,128)(2,1)S(1)} %bitcast.341, bf16[512,256]{1,0:T(8,128)(2,1)S(1)} %bitcast.343, ...), custom_call_target="tpu_custom_call" | custom-call | bytes 240000000 | tf_op jit(solution)/shard_map/pallas_call | solution.py:210
  157.2 69.0 %shard_map.257 = (bf16[768,2048]{1,0:T(8,128)(2,1)S(1)}, bf16[192,2048]{1,0:T(8,128)(2,1)S(1)}, bf16[2,4,288,256]{3,2,1,0:T(8,128)(2,1)S(1)}) custom-call(bf16[192,2048]{1,0:T(8,128)(2,1)S(1)} %copy-done.26, bf16[1536,512]{1,0:T(8,128)(2,1)S(1)} %bitcast.326, bf16[2,288,256]{2,1,0:T(8,128)(2,1)S(1)} %pad_maximum_fusion.9.refs_2_), custom_call_target="tpu_custom_call" | custom-call | bytes 120000000 | tf_op jit(solution)/shard_map/pallas_call | solution.py:210
  243.3 131.6 %shard_map.258 = (bf16[192,2048]{1,0:T(8,128)(2,1)}, bf16[192,2048]{1,0:T(8,128)(2,1)}, f32[72,2048]{1,0:T(8,128)}, bf16[3,192,2048]{2,1,0:T(8,128)(2,1)}, bf16[...) custom-call(bf16[1536,512]{1,0:T(8,128)(2,1)} %bitcast.324, ...), custom_call_target="tpu_custom_call" | custom-call | bytes 270000000 | tf_op jit(solution)/shard_map/pallas_call | solution.py:210
  374.9 2.2 fusion.9
  377.4 2.3 slice.200
  379.7 3.1 slice.188
  382.7 2.3 copy.202
  385.0 4.1 fusion.39
  391.1 2.4 reshape.585
  400.4 55.3 %shard_map.259 = (bf16[768,2048]{1,0:T(8,128)(2,1)S(1)}, bf16[2,4,288,256]{3,2,1,0:T(8,128)(2,1)S(1)}) custom-call(bf16[192,2048]{1,0:T(8,128)(2,1)S(1)} %copy-done.24, bf16[2,288,256]{2,1,0:T(8,128)(2,1)S(1)} %pad_maximum_fusion.11.refs_1_), custom_call_target="tpu_custom_call" | custom-call | bytes 120000000 | tf_op jit(solution)/shard_map/pallas_call | solution.py:210
  455.8 3.7 fusion.152
  463.4 2.2 convolution_convert_fusion.2
  465.6 124.2 %shard_map.260 = (f32[72,2048]{1,0:T(8,128)}, bf16[3,192,2048]{2,1,0:T(8,128)(2,1)}, bf16[3,192,768]{2,1,0:T(8,128)(2,1)}, f32[72,2048]{1,0:T(8,128)}, bf16[2,28...) custom-call(bf16[2,288,2048]{2,1,0:T(8,128)(2,1)} %bitcast.352, ...), custom_call_target="tpu_custom_call" | custom-call | bytes 300000000 | tf_op jit(solution)/shard_map/pallas_call | solution.py:210
  589.8 2.7 convolution_convert_fusion.7
  592.6 4.1 fusion.24
  596.7 3.9 fusion.3
  604.5 26.6 %shard_map.261 = f32[2,288,256]{2,1,0:T(8,128)S(1)} custom-call(bf16[2,4,288,256]{3,2,1,0:T(8,128)(2,1)S(1)} %pad_maximum_fusion.3.refs_0_), custom_call_target="tpu_custom_call" | custom-call | bytes 90000000 | tf_op jit(solution)/shard_map/pallas_call | solution.py:210
  634.1 2.8 convolution_convert_fusion.1
  637.0 85.5 %shard_map.262 = (bf16[3,192,768]{2,1,0:T(8,128)(2,1)}, bf16[3,192,768]{2,1,0:T(8,128)(2,1)}, f32[72,2048]{1,0:T(8,128)}, f32[1,2048]{1,0:T(1,128)}, bf16[2,288,...) custom-call(bf16[2,288,2048]{2,1,0:T(8,128)(2,1)} %bitcast.357, ...), custom_call_target="tpu_custom_call" | custom-call | bytes 270000000 | tf_op jit(solution)/shard_map/pallas_call | solution.py:210
  722.5 6.3 bitcast_convert_fusion.1
  729.0 6.2 bitcast_convert_fusion.2
  735.3 6.6 bitcast_convert_fusion.4
  741.9 6.3 bitcast_convert_fusion.5
  748.3 6.3 bitcast_convert_fusion.3
  755.5 2.9 convolution_convert_fusion.4
  763.8 3.2 convolution_convert_fusion.6
  768.1 4.0 fusion
  776.3 2.3 fusion.31
  778.5 2.3 fusion.27
  780.8 4.1 bitcast_convert_fusion
  784.9 35.4 %reduce-scatter.14.cloned.1.call-done.refs_1_ = bf16[192,2048]{1,0:T(8,128)(2,1)} async-done(((bf16[768,2048]{1,0:T(8,128)(2,1)}), bf16[192,2048]{1,0:T(8,128)(2,1)}) %reduce-scatter.14.cloned.1.call-update) | async-done | bytes 786448 | tf_op jit(solution)/shard_map/reduce_scatter | solution.py:1771
  827.2 40.6 %reduce-scatter.10.cloned.1.call-done.refs_1_ = bf16[192,2048]{1,0:T(8,128)(2,1)} async-done(((bf16[768,2048]{1,0:T(8,128)(2,1)}), bf16[192,2048]{1,0:T(8,128)(2,1)}) %reduce-scatter.10.cloned.1.call-update) | async-done | bytes 786448 | tf_op jit(solution)/shard_map/reduce_scatter | solution.py:1771
  867.8 47.5 %reduce-scatter.8.cloned.1.call-done.refs_0_ = bf16[192,2048]{1,0:T(8,128)(2,1)} async-done(((bf16[768,2048]{1,0:T(8,128)(2,1)}), bf16[192,2048]{1,0:T(8,128)(2,1)}) %reduce-scatter.8.cloned.1.call-update) | async-done | bytes 786448 | tf_op jit(solution)/shard_map/reduce_scatter | solution.py:1771
  915.3 47.4 %reduce-scatter.12.cloned.1.call-done.refs_2_ = bf16[192,2048]{1,0:T(8,128)(2,1)} async-done(((bf16[768,2048]{1,0:T(8,128)(2,1)}), bf16[192,2048]{1,0:T(8,128)(2,1)}) %reduce-scatter.12.cloned.1.call-update) | async-done | bytes 786448 | tf_op jit(solution)/shard_map/reduce_scatter | solution.py:1771
  966.1 125.8 %shard_map.263 = (bf16[1536,512]{1,0:T(8,128)(2,1)S(1)}, bf16[1536,512]{1,0:T(8,128)(2,1)S(1)}, bf16[1536,512]{1,0:T(8,128)(2,1)S(1)}, f32[2,288,256]{2,1,0:T(8,128)S(1)}) custom-call(bf16[192,2048]{1,0:T(8,128)(2,1)S(1)} %copy-done.18, bf16[192,2048]{1,0:T(8,128)(2,1)S(1)} %copy-done.17, bf16[192,2048]{1,0:T(8,128)(2,1)S(1)} %copy-done.19, ...), custom_call_target="tpu_custom_call" | custom-call | bytes 90000000 | tf_op jit(solution)/shard_map/pallas_call | solution.py:210
  1092.3 2.6 multiply_reduce_fusion.5
  1100.1 4.6 copy.182
  1104.8 4.0 copy.258
  1108.8 2.8 convolution_convert_fusion
  1111.6 95.4 %shard_map.264 = (f32[4,128,768]{2,1,0:T(8,128)}, bf16[1536,512]{1,0:T(8,128)(2,1)}, bf16[1536,512]{1,0:T(8,128)(2,1)}, f32[1,2048]{1,0:T(1,128)}, bf16[2,288,2048]{2,1,0:T(8,128)(2,1)}) custom-call(bf16[4,4,128,768]{3,2,1,0:T(8,128)(2,1)} %bitcast.350, bf16[192,2048]{1,0:T(8,128)(2,1)} %reduce-scatter.14.cloned.1.call-done.refs_1_, ...), custom_call_target="tpu_custom_call" | custom-call | bytes 180000000 | tf_op jit(solution)/shard_map/pallas_call | solution.py:210
  1207.8 3.3 convert_bitcast_fusion
  1211.1 3.7 copy.190
  1214.8 3.3 convert_bitcast_fusion.1
  1218.1 3.5 copy.189
  1224.0 3.3 select_bitcast_fusion
  1228.4 23.9 %shard_map.265 = (f32[68,128]{1,0:T(8,128)S(1)}, bf16[512,768]{1,0:T(8,128)(2,1)S(1)}, bf16[1536,512]{1,0:T(8,128)(2,1)S(1)}) custom-call(f32[68,128]{1,0:T(8,128)S(1)} %reshape.596.refs_0_, bf16[512,768]{1,0:T(8,128)(2,1)S(1)} %bitcast_select_fusion.3.refs_1_, bf16[192,2048]{1,0:T(8,128)(2,1)S(1)} %copy-done.22), custom_call_target="tpu_custom_call" | custom-call | bytes 180000000 | tf_op jit(solution)/shard_map/pallas_call | solution.py:210
  1257.3 2.6 copy.188
  (407 shorter events, 119.1 us)
Async XLA Ops:
  7.2 148.8 %all-gather.9.cloned.1.call-start = ((), (), s32[]{:S(2)}) async-start(), calls=%async_computation.8 | async-start | bytes 3932160 | tf_op jit(solution)/shard_map/all_gather | solution.py:1689
  12.1 44.2 %copy-start = (bf16[1,512,1536]{1,2,0:T(8,128)(2,1)}, bf16[1,512,1536]{1,2,0:T(8,128)(2,1)S(1)}, u32[]{:S(2)}) copy-start(bf16[1,512,1536]{1,2,0:T(8,128)(2,1)S(1)} %copy.163) | copy-start | bytes 4718596
  12.2 44.2 %copy-start.12 = (bf16[1,512,256]{2,1,0:T(8,128)(2,1)S(1)}, bf16[1,512,256]{2,1,0:T(8,128)(2,1)}, u32[]{:S(2)}) copy-start(bf16[1,512,256]{2,1,0:T(8,128)(2,1)} %param.23) | copy-start | bytes 786436
  55.5 100.5 %all-gather.7.cloned.1.call-start = ((), (), s32[]{:S(2)}) async-start(), calls=%async_computation.7 | async-start | bytes 3932160 | tf_op jit(solution)/shard_map/all_gather | solution.py:1689
  56.3 321.1 %all-gather.15.cloned.1.call-start = ((), (), s32[]{:S(2)}) async-start(), calls=%async_computation.18 | async-start | bytes 3932160 | tf_op jit(solution)/shard_map/all_gather | solution.py:1706
  60.8 71.7 %copy-start.109 = (s32[2]{0:T(128)S(1)}, s32[2]{0:T(128)}, u32[]{:S(2)}) copy-start(s32[2]{0:T(128)} %param.20) | copy-start | bytes 28
  132.4 268.0 %all-gather.11.cloned.1.call-start = ((), (), s32[]{:S(2)}) async-start(), calls=%async_computation.9 | async-start | bytes 3932160 | tf_op jit(solution)/shard_map/all_gather | solution.py:1689
  145.7 6.9 copy-start.62
  145.7 4.7 copy-start.92
  152.0 74.2 %copy-start.90 = (f32[2,288]{1,0:T(2,128)}, f32[2,288]{1,0:T(2,128)S(1)}, u32[]{:S(2)}) copy-start(f32[2,288]{1,0:T(2,128)S(1)} %multiply_reduce_fusion.9) | copy-start | bytes 6916
  152.5 73.7 %copy-start.93 = (f32[128]{0:T(128)}, f32[128]{0:T(128)S(1)}, u32[]{:S(2)}) copy-start(f32[128]{0:T(128)S(1)} %get-tuple-element.254) | copy-start | bytes 1540
  152.6 73.7 %copy-start.87 = (f32[2,288]{1,0:T(2,128)}, f32[2,288]{1,0:T(2,128)S(1)}, u32[]{:S(2)}) copy-start(f32[2,288]{1,0:T(2,128)S(1)} %fusion.129) | copy-start | bytes 6916
  153.9 243.9 %copy-start.50 = (f32[1,288,64]{2,1,0:T(8,128)}, f32[1,288,64]{2,1,0:T(8,128)S(1)}, u32[]{:S(2)}) copy-start(f32[1,288,64]{2,1,0:T(8,128)S(1)} %get-tuple-element.259) | copy-start | bytes 221188
  154.7 81.4 %copy-start.43 = (f32[2,288,64]{2,1,0:T(8,128)}, f32[2,288,64]{2,1,0:T(8,128)S(1)}, u32[]{:S(2)}) copy-start(f32[2,288,64]{2,1,0:T(8,128)S(1)} %get-tuple-element.243) | copy-start | bytes 442372
  154.7 74.6 %copy-start.110 = (s32[2,9]{1,0:T(2,128)S(1)}, s32[2,9]{1,0:T(2,128)}, u32[]{:S(2)}) copy-start(s32[2,9]{1,0:T(2,128)} %param.19) | copy-start | bytes 220
  228.8 236.8 %all-gather.13.cloned.1.call-start = ((), (), s32[]{:S(2)}) async-start(), calls=%async_computation.10 | async-start | bytes 3932160 | tf_op jit(solution)/shard_map/all_gather | solution.py:1689
  377.1 407.8 %reduce-scatter.16.cloned.1.call-start = ((), (), s32[]{:S(2)}) async-start(), calls=%async_computation.15 | async-start | bytes 3932160 | tf_op jit(solution)/shard_map/reduce_scatter | solution.py:1771
  379.7 5.3 copy-start.104
  389.1 7.5 copy-start.95
  390.2 7.5 copy-start.53
  390.2 7.5 copy-start.56
  390.2 7.5 copy-start.59
  391.1 8.0 copy-start.41
  393.5 5.7 copy-start.98
  463.3 126.5 %copy-start.72 = (bf16[2,288,2,128]{3,2,1,0:T(2,128)(2,1)}, bf16[2,288,2,128]{3,2,1,0:T(2,128)(2,1)S(1)}, u32[]{:S(2)}) copy-start(bf16[2,288,2,128]{3,2,1,0:T(2,128)(2,1)S(1)} %copy.170) | copy-start | bytes 884740
  592.6 8.0 slice-start.2
  604.3 26.9 %copy-start.51 = (f32[1,288,64]{2,1,0:T(8,128)S(1)}, f32[1,288,64]{2,1,0:T(8,128)}, u32[]{:S(2)}) copy-start(f32[1,288,64]{2,1,0:T(8,128)} %copy-done.50) | copy-start | bytes 221188
  604.3 26.9 %copy-start.54 = (f32[1,288,64]{2,1,0:T(8,128)S(1)}, f32[1,288,64]{2,1,0:T(8,128)}, u32[]{:S(2)}) copy-start(f32[1,288,64]{2,1,0:T(8,128)} %copy-done.52) | copy-start | bytes 221188
  604.3 26.9 %copy-start.57 = (f32[1,288,64]{2,1,0:T(8,128)S(1)}, f32[1,288,64]{2,1,0:T(8,128)}, u32[]{:S(2)}) copy-start(f32[1,288,64]{2,1,0:T(8,128)} %copy-done.55) | copy-start | bytes 221188
  604.3 26.9 %copy-start.60 = (f32[1,288,64]{2,1,0:T(8,128)S(1)}, f32[1,288,64]{2,1,0:T(8,128)}, u32[]{:S(2)}) copy-start(f32[1,288,64]{2,1,0:T(8,128)} %copy-done.58) | copy-start | bytes 221188
  604.5 26.9 %copy-start.64 = (f32[2,288,512]{2,1,0:T(8,128)S(1)}, f32[2,288,512]{2,1,0:T(8,128)}, u32[]{:S(2)}) copy-start(f32[2,288,512]{2,1,0:T(8,128)} %copy-done.63) | copy-start | bytes 3538948
  728.8 91.5 %reduce-scatter.14.cloned.1.call-start = ((), (), s32[]{:S(2)}) async-start(), calls=%async_computation.14 | async-start | bytes 3932160 | tf_op jit(solution)/shard_map/reduce_scatter | solution.py:1771
  735.3 132.5 %reduce-scatter.10.cloned.1.call-start = ((), (), s32[]{:S(2)}) async-start(), calls=%async_computation.12 | async-start | bytes 3932160 | tf_op jit(solution)/shard_map/reduce_scatter | solution.py:1771
  741.9 173.5 %reduce-scatter.8.cloned.1.call-start = ((), (), s32[]{:S(2)}) async-start(), calls=%async_computation.11 | async-start | bytes 3932160 | tf_op jit(solution)/shard_map/reduce_scatter | solution.py:1771
  748.2 214.5 %reduce-scatter.12.cloned.1.call-start = ((), (), s32[]{:S(2)}) async-start(), calls=%async_computation.13 | async-start | bytes 3932160 | tf_op jit(solution)/shard_map/reduce_scatter | solution.py:1771
  754.6 467.0 %reduce-scatter.18.cloned.1.call-start = ((), (), s32[]{:S(2)}) async-start(), calls=%async_computation.16 | async-start | bytes 3932160 | tf_op jit(solution)/shard_map/reduce_scatter | solution.py:1775
  762.4 464.9 %reduce-scatter.20.cloned.1.call-start = ((), (), s32[]{:S(2)}) async-start(), calls=%async_computation.17 | async-start | bytes 3932160 | tf_op jit(solution)/shard_map/reduce_scatter | solution.py:1771
  763.7 4.3 copy-start.100
  825.5 266.5 %copy-start.61 = (f32[1,288,64]{2,1,0:T(8,128)S(1)}, f32[1,288,64]{2,1,0:T(8,128)}, u32[]{:S(2)}) copy-start(f32[1,288,64]{2,1,0:T(8,128)} %copy-done.58) | copy-start | bytes 221188
  825.6 266.7 %copy-start.88 = (f32[2,288]{1,0:T(2,128)S(1)}, f32[2,288]{1,0:T(2,128)}, u32[]{:S(2)}) copy-start(f32[2,288]{1,0:T(2,128)} %copy-done.87) | copy-start | bytes 6916
  825.6 266.7 %copy-start.94 = (f32[128]{0:T(128)S(1)}, f32[128]{0:T(128)}, u32[]{:S(2)}) copy-start(f32[128]{0:T(128)} %copy-done.93) | copy-start | bytes 1540
  1092.0 6.2 copy-start.6
  1092.0 6.2 copy-start.8
  1111.6 95.4 %copy-start.99 = (f32[1,2048]{1,0:T(1,128)S(1)}, f32[1,2048]{1,0:T(1,128)}, u32[]{:S(2)}) copy-start(f32[1,2048]{1,0:T(1,128)} %get-tuple-element.106) | copy-start | bytes 24580
  1111.6 95.4 %copy-start.107 = (f32[128]{0:T(128)S(1)}, f32[128]{0:T(128)}, u32[]{:S(2)}) copy-start(f32[128]{0:T(128)} %get-tuple-element.199) | copy-start | bytes 1540
  1111.6 96.2 %copy-start.9 = (bf16[1536,512]{1,0:T(8,128)(2,1)S(1)}, bf16[1536,512]{1,0:T(8,128)(2,1)}, u32[]{:S(2)}) copy-start(bf16[1536,512]{1,0:T(8,128)(2,1)} %copy-done.8) | copy-start | bytes 4718596
  1228.4 23.9 %copy-start.48 = (f32[4,128,768]{2,1,0:T(8,128)S(1)}, f32[4,128,768]{2,1,0:T(8,128)}, u32[]{:S(2)}) copy-start(f32[4,128,768]{2,1,0:T(8,128)} %get-tuple-element.109) | copy-start | bytes 4718596
  1257.3 10.9 copy-start.11
  (84 other events, 187.2 us)
Sparse Core Ops, SparseCore 0:
  55.6 44.3 all-gather.8
  102.4 43.9 all-gather.6
  148.0 95.5 all-gather.14
  245.9 57.6 all-gather.10
  377.2 76.8 all-gather.12
  728.9 44.3 reduce-scatter.15
  776.3 43.9 reduce-scatter.13
  823.8 43.9 reduce-scatter.9
  871.4 43.9 reduce-scatter.7
  918.7 43.9 reduce-scatter.11
  965.0 108.0 reduce-scatter.17
  1076.0 63.0 reduce-scatter.19

commit v9 on v8

--- a/solution.py
+++ b/solution.py
@@ -1831,20 +1831,20 @@
             middle, mlp_in, hidden_bf, _, output_second, grad_mlp,
             grad_gate, grad_up, grad_middle, mlp_gain_second, grad_attn,
         ) = outs
-        unit_second = scatter_units(
-            weight_products(
-                [
-                    (flat(grad_gate), flat(mlp_in)),
-                    (flat(grad_up), flat(mlp_in)),
-                    (flat(hidden_bf), flat(grad_mlp)),
-                ]
-            )
-        )
+        products_second = weight_products(
+            [
+                (flat(grad_gate), flat(mlp_in)),
+                (flat(grad_up), flat(mlp_in)),
+                (flat(hidden_bf), flat(grad_mlp)),
+            ]
+        )
+        unit_second = scatter_units(products_second)
         terms, pairs, head_second = attn_backward(
             grad_attn, saved_second, second_weights, gains[1], slot,
-            lambda whole: kv_scatter(whole, [], 7, []),
+            lambda whole: kv_scatter(tied(whole, *products_second), [], 7, []),
         )
         attn_second = scatter_shards(weight_products(pairs))
+        terms = tied(terms, unit_second[0])
         part = FeedForward(
             terms, own_next, gains[1][0][None], first_weights[2:], False, True,
             {
@@ -1864,12 +1864,15 @@
                 (flat(hidden_first), flat(grad_mlp)),
             ]
         )
+        grad_attn = tied(grad_attn, unit_second[1], *products)
         unit_first = scatter_units(products[:2])
         unit_first += scatter_units([tied(products[2], *unit_first)])
         carried = []
         terms, pairs, head_first = attn_backward(
             grad_attn, saved_first, first_weights, gains[0], slot,
-            lambda whole: kv_scatter(whole, [UnitsHome(unit_second, 1)], 9, carried),
+            lambda whole: kv_scatter(
+                tied(whole, attn_second), [UnitsHome(unit_second, 1)], 9, carried
+            ),
         )
         (home_second,) = carried
         whole = jnp.concatenate(weight_products(pairs), axis=1).reshape(dp_size, 4, -1, q_width + qkv_width)

time: 1280 us -> 1200 us (0.938)
  waiting for transfers between devices: 172 us -> 106 us
  Pallas kernels: 847 us -> 825 us
    reduce_scatter x6, waiting for transfers between devices: 171 us -> 104 us  [scatter_units(): lax.psum_scatter(item, 'tensor', scatter_dimension=0, tiled=True)]
    pallas_call x11, Pallas kernels: 847 us -> 825 us  [fused(): pl.pallas_call(kernel, out_shape=[item[0] for item in outs], in_specs=[it...]
    unnamed x255 -> x259, local copies, waits for them, and re-layouts: 46.7 us -> 49.8 us
  transfers between devices with their start and end apart: 12 -> 12, of which waited for: 4 -> 3; matrix products, arithmetic and copies ran while one was open for 13% -> 15% of each run, Pallas kernels for 43% -> 53%
where the time goes in v9:
time: 1200 us; the launch traced here: 1190 us
  Pallas kernels  825 us (69%)
  waiting for transfers between devices  106 us (9%)
  matrix products  87.9 us (7%)
  local copies, waits for them, and re-layouts  85.1 us (7%)
  other arithmetic  65.8 us (5%)
  between operations  20.1 us (2%)
    pallas_call x11, Pallas kernels, fused(): pl.pallas_call(kernel, out_shape=[item[0] for item in outs], in_specs=[it...  825 us
    reduce_scatter x6, waiting for transfers between devices, scatter_units(): lax.psum_scatter(item, 'tensor', scatter_dimension=0, tiled=True)  104 us
    unnamed x259, local copies, waits for them, and re-layouts  49.8 us
    dot_general x10, matrix products, dot_outer(): return lax.dot_general(left, right, OUTER, preferred_element_type=F32)  38.7 us
  transfers between devices with their start and end apart: 12, of which 3 were waited for; matrix products, arithmetic and copies ran while one was open for 15% of the time, Pallas kernels for 53%

profile of v9, /device:TPU:0, one launch (start us, length us, event | category | flops | bytes accessed | tf_op | source)
XLA Modules:
  0.0 1190.5 jit_solution(1894900779862311723)
XLA Ops:
  12.2 41.5 %shard_map.255 = (bf16[192,2048]{1,0:T(8,128)(2,1)S(1)}, bf16[192,2048]{1,0:T(8,128)(2,1)S(1)}, f32[2,4,10,128]{3,2,1,0:T(8,128)S(1)}) custom-call(bf16[1536,512]{1,0:T(8,128)(2,1)S(1)} %bitcast.323, bf16[1536,512]{1,0:T(8,128)(2,1)S(1)} %bitcast.321, f32[10,128]{1,0:T(8,128)S(1)} %fusion.112.refs_2_), custom_call_target="tpu_custom_call" | custom-call | bytes 135000000 | tf_op jit(solution)/shard_map/pallas_call | solution.py:210
  60.8 68.4 %shard_map.256 = (bf16[2048,512]{1,0:T(8,128)(2,1)S(1)}, bf16[256,2048]{1,0:T(8,128)(2,1)S(1)}, bf16[192,2048]{1,0:T(8,128)(2,1)S(1)}, bf16[768,512]{1,0:T(8,128)(2,1)}) custom-call(bf16[512,512]{1,0:T(8,128)(2,1)S(1)} %bitcast.329, bf16[512,256]{1,0:T(8,128)(2,1)S(1)} %bitcast.341, bf16[512,256]{1,0:T(8,128)(2,1)S(1)} %bitcast.343, ...), custom_call_target="tpu_custom_call" | custom-call | bytes 240000000 | tf_op jit(solution)/shard_map/pallas_call | solution.py:210
  149.2 74.8 %shard_map.257 = (bf16[768,2048]{1,0:T(8,128)(2,1)S(1)}, bf16[192,2048]{1,0:T(8,128)(2,1)S(1)}, bf16[2,4,288,256]{3,2,1,0:T(8,128)(2,1)S(1)}) custom-call(bf16[192,2048]{1,0:T(8,128)(2,1)S(1)} %copy-done.30, bf16[1536,512]{1,0:T(8,128)(2,1)S(1)} %bitcast.324, bf16[2,288,256]{2,1,0:T(8,128)(2,1)S(1)} %pad_maximum_fusion.9.refs_2_), custom_call_target="tpu_custom_call" | custom-call | bytes 120000000 | tf_op jit(solution)/shard_map/pallas_call | solution.py:210
  241.9 2.2 convolution_convert_fusion.3
  244.1 131.5 %shard_map.258 = (bf16[192,2048]{1,0:T(8,128)(2,1)}, bf16[192,2048]{1,0:T(8,128)(2,1)}, f32[72,2048]{1,0:T(8,128)}, bf16[3,192,2048]{2,1,0:T(8,128)(2,1)}, bf16[...) custom-call(bf16[1536,512]{1,0:T(8,128)(2,1)} %bitcast.322, ...), custom_call_target="tpu_custom_call" | custom-call | bytes 270000000 | tf_op jit(solution)/shard_map/pallas_call | solution.py:210
  376.1 2.2 fusion.9
  378.3 2.3 slice.200
  380.6 3.0 slice.188
  383.6 2.3 copy.214
  385.9 3.7 fusion.39
  391.7 2.4 reshape.581
  401.0 53.1 %shard_map.259 = (bf16[768,2048]{1,0:T(8,128)(2,1)S(1)}, bf16[2,4,288,256]{3,2,1,0:T(8,128)(2,1)S(1)}) custom-call(bf16[192,2048]{1,0:T(8,128)(2,1)S(1)} %copy-done.28, bf16[2,288,256]{2,1,0:T(8,128)(2,1)S(1)} %pad_maximum_fusion.11.refs_1_), custom_call_target="tpu_custom_call" | custom-call | bytes 120000000 | tf_op jit(solution)/shard_map/pallas_call | solution.py:210
  454.1 3.8 fusion.152
  461.7 2.2 convolution_convert_fusion.2
  463.9 124.6 %shard_map.260 = (f32[72,2048]{1,0:T(8,128)}, bf16[3,192,2048]{2,1,0:T(8,128)(2,1)}, bf16[3,192,768]{2,1,0:T(8,128)(2,1)}, f32[72,2048]{1,0:T(8,128)}, bf16[2,28...) custom-call(bf16[2,288,2048]{2,1,0:T(8,128)(2,1)} %bitcast.352, ...), custom_call_target="tpu_custom_call" | custom-call | bytes 300000000 | tf_op jit(solution)/shard_map/pallas_call | solution.py:210
  588.5 6.3 bitcast_convert_fusion.5
  594.9 2.7 convolution_convert_fusion.7
  597.7 6.3 bitcast_convert_fusion.4
  604.0 4.0 fusion.3
  608.1 3.5 fusion.5
  617.1 4.1 bitcast_convert_fusion.3
  622.9 26.5 %shard_map.261 = f32[2,288,256]{2,1,0:T(8,128)S(1)} custom-call(bf16[2,4,288,256]{3,2,1,0:T(8,128)(2,1)S(1)} %bitcast.328), custom_call_target="tpu_custom_call" | custom-call | bytes 90000000 | tf_op jit(solution)/shard_map/pallas_call | solution.py:210
  662.9 4.4 convolution_convert_fusion.1
  667.4 109.8 %shard_map.262 = (bf16[3,192,768]{2,1,0:T(8,128)(2,1)}, bf16[3,192,768]{2,1,0:T(8,128)(2,1)}, f32[72,2048]{1,0:T(8,128)}, f32[1,2048]{1,0:T(1,128)}, bf16[2,288,...) custom-call(bf16[2,288,2048]{2,1,0:T(8,128)(2,1)} %bitcast.357, ...), custom_call_target="tpu_custom_call" | custom-call | bytes 270000000 | tf_op jit(solution)/shard_map/pallas_call | solution.py:210
  777.2 6.3 bitcast_convert_fusion.1
  784.6 5.7 bitcast_convert_fusion.2
  791.8 3.5 select_bitcast_fusion.1
  795.9 4.0 bitcast_convert_fusion
  799.9 3.2 convolution_convert_fusion.6
  804.3 4.1 fusion
  815.8 3.4 fusion.45
  819.2 13.8 %reduce-scatter.18.cloned.1.call-done.refs_2_ = bf16[192,2048]{1,0:T(8,128)(2,1)} async-done(((bf16[768,2048]{1,0:T(8,128)(2,1)}), bf16[192,2048]{1,0:T(8,128)(2,1)}) %reduce-scatter.18.cloned.1.call-update) | async-done | bytes 786448 | tf_op jit(solution)/shard_map/reduce_scatter | solution.py:1771
  833.0 47.4 %reduce-scatter.16.cloned.1.call-done.refs_1_ = bf16[192,2048]{1,0:T(8,128)(2,1)} async-done(((bf16[768,2048]{1,0:T(8,128)(2,1)}), bf16[192,2048]{1,0:T(8,128)(2,1)}) %reduce-scatter.16.cloned.1.call-update) | async-done | bytes 786448 | tf_op jit(solution)/shard_map/reduce_scatter | solution.py:1771
  884.4 43.0 %reduce-scatter.12.cloned.1.call-done.refs_2_ = bf16[192,2048]{1,0:T(8,128)(2,1)} async-done(((bf16[768,2048]{1,0:T(8,128)(2,1)}), bf16[192,2048]{1,0:T(8,128)(2,1)}) %reduce-scatter.12.cloned.1.call-update) | async-done | bytes 786448 | tf_op jit(solution)/shard_map/reduce_scatter | solution.py:1771
  929.6 75.4 %shard_map.263 = (bf16[1536,512]{1,0:T(8,128)(2,1)S(1)}, bf16[1536,512]{1,0:T(8,128)(2,1)S(1)}, bf16[1536,512]{1,0:T(8,128)(2,1)S(1)}, f32[2,288,256]{2,1,0:T(8,128)S(1)}) custom-call(bf16[192,2048]{1,0:T(8,128)(2,1)S(1)} %copy-done.21, bf16[192,2048]{1,0:T(8,128)(2,1)S(1)} %copy-done.22, bf16[192,2048]{1,0:T(8,128)(2,1)S(1)} %copy-done.23, ...), custom_call_target="tpu_custom_call" | custom-call | bytes 90000000 | tf_op jit(solution)/shard_map/pallas_call | solution.py:210
  1005.1 2.2 multiply_add_fusion.5
  1013.8 4.6 copy.197
  1018.4 4.0 copy.270
  1022.4 2.8 convolution_convert_fusion
  1025.3 95.3 %shard_map.264 = (f32[4,128,768]{2,1,0:T(8,128)}, bf16[1536,512]{1,0:T(8,128)(2,1)}, bf16[1536,512]{1,0:T(8,128)(2,1)}, f32[1,2048]{1,0:T(1,128)}, bf16[2,288,2048]{2,1,0:T(8,128)(2,1)}) custom-call(bf16[4,4,128,768]{3,2,1,0:T(8,128)(2,1)} %bitcast.350, bf16[192,2048]{1,0:T(8,128)(2,1)} %reduce-scatter.16.cloned.1.call-done.refs_1_, ...), custom_call_target="tpu_custom_call" | custom-call | bytes 180000000 | tf_op jit(solution)/shard_map/pallas_call | solution.py:210
  1121.4 3.3 convert_bitcast_fusion
  1124.7 3.7 copy.202
  1128.4 3.3 convert_bitcast_fusion.1
  1131.6 3.6 copy.201
  1137.4 3.3 select_bitcast_fusion
  1141.8 23.8 %shard_map.265 = (f32[68,128]{1,0:T(8,128)S(1)}, bf16[512,768]{1,0:T(8,128)(2,1)S(1)}, bf16[1536,512]{1,0:T(8,128)(2,1)S(1)}) custom-call(f32[68,128]{1,0:T(8,128)S(1)} %reshape.595.refs_0_, bf16[512,768]{1,0:T(8,128)(2,1)S(1)} %bitcast_select_fusion.3.refs_1_, bf16[192,2048]{1,0:T(8,128)(2,1)S(1)} %copy-done.27), custom_call_target="tpu_custom_call" | custom-call | bytes 180000000 | tf_op jit(solution)/shard_map/pallas_call | solution.py:210
  1170.7 2.6 copy.200
  1179.5 2.0 maximum_convert_fusion
  (413 shorter events, 120.4 us)
Async XLA Ops:
  7.2 140.8 %all-gather.9.cloned.1.call-start = ((), (), s32[]{:S(2)}) async-start(), calls=%async_computation.8 | async-start | bytes 3932160 | tf_op jit(solution)/shard_map/all_gather | solution.py:1689
  12.1 44.2 %copy-start = (bf16[1,512,1536]{1,2,0:T(8,128)(2,1)}, bf16[1,512,1536]{1,2,0:T(8,128)(2,1)S(1)}, u32[]{:S(2)}) copy-start(bf16[1,512,1536]{1,2,0:T(8,128)(2,1)S(1)} %copy.173) | copy-start | bytes 4718596
  12.2 44.2 %copy-start.16 = (bf16[1,512,256]{2,1,0:T(8,128)(2,1)S(1)}, bf16[1,512,256]{2,1,0:T(8,128)(2,1)}, u32[]{:S(2)}) copy-start(bf16[1,512,256]{2,1,0:T(8,128)(2,1)} %param.23) | copy-start | bytes 786436
  55.5 92.5 %all-gather.7.cloned.1.call-start = ((), (), s32[]{:S(2)}) async-start(), calls=%async_computation.7 | async-start | bytes 3932160 | tf_op jit(solution)/shard_map/all_gather | solution.py:1689
  56.3 322.0 %all-gather.15.cloned.1.call-start = ((), (), s32[]{:S(2)}) async-start(), calls=%async_computation.18 | async-start | bytes 3932160 | tf_op jit(solution)/shard_map/all_gather | solution.py:1706
  60.8 71.6 %copy-start.107 = (s32[2]{0:T(128)S(1)}, s32[2]{0:T(128)}, u32[]{:S(2)}) copy-start(s32[2]{0:T(128)} %param.20) | copy-start | bytes 28
  132.4 268.6 %all-gather.11.cloned.1.call-start = ((), (), s32[]{:S(2)}) async-start(), calls=%async_computation.9 | async-start | bytes 3932160 | tf_op jit(solution)/shard_map/all_gather | solution.py:1689
  146.8 251.5 %copy-start.55 = (f32[1,288,64]{2,1,0:T(8,128)}, f32[1,288,64]{2,1,0:T(8,128)S(1)}, u32[]{:S(2)}) copy-start(f32[1,288,64]{2,1,0:T(8,128)S(1)} %get-tuple-element.267) | copy-start | bytes 221188
  226.6 577.8 %copy-start.12 = (bf16[2,4,288,256]{3,2,1,0:T(8,128)(2,1)}, bf16[2,4,288,256]{3,2,1,0:T(8,128)(2,1)S(1)}, u32[]{:S(2)}) copy-start(bf16[2,4,288,256]{3,2,1,0:T(8,128)(2,1)S(1)} %get-tuple-element.78) | copy-start | bytes 3538948
  226.6 237.3 %all-gather.13.cloned.1.call-start = ((), (), s32[]{:S(2)}) async-start(), calls=%async_computation.10 | async-start | bytes 3932160 | tf_op jit(solution)/shard_map/all_gather | solution.py:1689
  228.2 8.4 copy-start.45
  375.6 291.7 %reduce-scatter.8.cloned.1.call-start = ((), (), s32[]{:S(2)}) async-start(), calls=%async_computation.11 | async-start | bytes 3932160 | tf_op jit(solution)/shard_map/reduce_scatter | solution.py:1771
  389.7 7.5 copy-start.95
  390.7 7.5 copy-start.58
  390.7 7.5 copy-start.61
  390.7 7.5 copy-start.64
  391.7 8.0 copy-start.47
  394.0 5.6 copy-start.98
  454.1 149.9 %copy-start.14 = (bf16[2,4,288,256]{3,2,1,0:T(8,128)(2,1)}, bf16[2,4,288,256]{3,2,1,0:T(8,128)(2,1)S(1)}, u32[]{:S(2)}) copy-start(bf16[2,4,288,256]{3,2,1,0:T(8,128)(2,1)S(1)} %get-tuple-element.86) | copy-start | bytes 3538948
  594.8 205.1 %reduce-scatter.10.cloned.1.call-start = ((), (), s32[]{:S(2)}) async-start(), calls=%async_computation.12 | async-start | bytes 3932160 | tf_op jit(solution)/shard_map/reduce_scatter | solution.py:1771
  604.0 210.2 %reduce-scatter.14.cloned.1.call-start = ((), (), s32[]{:S(2)}) async-start(), calls=%async_computation.14 | async-start | bytes 3932160 | tf_op jit(solution)/shard_map/reduce_scatter | solution.py:1775
  604.0 9.8 slice-start.2
  608.0 5.0 copy-start.79
  608.1 5.8 slice-start.3
  621.2 28.3 %copy-start.56 = (f32[1,288,64]{2,1,0:T(8,128)S(1)}, f32[1,288,64]{2,1,0:T(8,128)}, u32[]{:S(2)}) copy-start(f32[1,288,64]{2,1,0:T(8,128)} %copy-done.55) | copy-start | bytes 221188
  621.2 28.3 %copy-start.59 = (f32[1,288,64]{2,1,0:T(8,128)S(1)}, f32[1,288,64]{2,1,0:T(8,128)}, u32[]{:S(2)}) copy-start(f32[1,288,64]{2,1,0:T(8,128)} %copy-done.57) | copy-start | bytes 221188
  621.2 28.3 %copy-start.62 = (f32[1,288,64]{2,1,0:T(8,128)S(1)}, f32[1,288,64]{2,1,0:T(8,128)}, u32[]{:S(2)}) copy-start(f32[1,288,64]{2,1,0:T(8,128)} %copy-done.60) | copy-start | bytes 221188
  621.2 28.3 %copy-start.65 = (f32[1,288,64]{2,1,0:T(8,128)S(1)}, f32[1,288,64]{2,1,0:T(8,128)}, u32[]{:S(2)}) copy-start(f32[1,288,64]{2,1,0:T(8,128)} %copy-done.63) | copy-start | bytes 221188
  622.9 28.3 %copy-start.15 = (bf16[2,4,288,256]{3,2,1,0:T(8,128)(2,1)S(1)}, bf16[2,4,288,256]{3,2,1,0:T(8,128)(2,1)}, u32[]{:S(2)}) copy-start(bf16[2,4,288,256]{3,2,1,0:T(8,128)(2,1)} %copy-done.14) | copy-start | bytes 3538948
  622.9 28.3 %copy-start.37 = (bf16[2,2,288,1152]{3,2,1,0:T(8,128)(2,1)S(1)}, bf16[2,2,288,1152]{3,2,1,0:T(8,128)(2,1)}, u32[]{:S(2)}) copy-start(bf16[2,2,288,1152]{3,2,1,0:T(8,128)(2,1)} %copy-done.36) | copy-start | bytes 7962628
  661.4 171.6 %reduce-scatter.18.cloned.1.call-start = ((), (), s32[]{:S(2)}) async-start(), calls=%async_computation.16 | async-start | bytes 3932160 | tf_op jit(solution)/shard_map/reduce_scatter | solution.py:1771
  783.4 96.9 %reduce-scatter.16.cloned.1.call-start = ((), (), s32[]{:S(2)}) async-start(), calls=%async_computation.15 | async-start | bytes 3932160 | tf_op jit(solution)/shard_map/reduce_scatter | solution.py:1771
  790.3 137.1 %reduce-scatter.12.cloned.1.call-start = ((), (), s32[]{:S(2)}) async-start(), calls=%async_computation.13 | async-start | bytes 3932160 | tf_op jit(solution)/shard_map/reduce_scatter | solution.py:1771
  791.0 349.7 %reduce-scatter.20.cloned.1.call-start = ((), (), s32[]{:S(2)}) async-start(), calls=%async_computation.17 | async-start | bytes 3932160 | tf_op jit(solution)/shard_map/reduce_scatter | solution.py:1771
  803.2 5.3 slice-start
  819.2 62.7 %copy-start.46 = (f32[2,36,2,8,128]{4,3,2,1,0:T(8,128)S(1)}, f32[2,36,2,8,128]{4,3,2,1,0:T(8,128)}, u32[]{:S(2)}) copy-start(f32[2,36,2,8,128]{4,3,2,1,0:T(8,128)} %copy-done.45) | copy-start | bytes 1769476
  819.2 62.7 %copy-start.97 = (f32[128]{0:T(128)S(1)}, f32[128]{0:T(128)}, u32[]{:S(2)}) copy-start(f32[128]{0:T(128)} %get-tuple-element.261) | copy-start | bytes 1540
  881.9 45.5 %copy-start.21 = (bf16[192,2048]{1,0:T(8,128)(2,1)S(1)}, bf16[192,2048]{1,0:T(8,128)(2,1)}, u32[]{:S(2)}) copy-start(bf16[192,2048]{1,0:T(8,128)(2,1)} %reduce-scatter.8.cloned.1.call-done.refs_0_) | copy-start | bytes 2359300
  883.4 44.0 %copy-start.70 = (bf16[2,288,2,128]{3,1,2,0:T(8,128)(2,1)}, bf16[2,288,2,128]{3,1,2,0:T(8,128)(2,1)S(1)}, u32[]{:S(2)}) copy-start(bf16[2,288,2,128]{3,1,2,0:T(8,128)(2,1)S(1)} %fusion.56) | copy-start | bytes 884740
  929.6 77.7 %copy-start.68 = (f32[2,288,512]{2,1,0:T(8,128)S(1)}, f32[2,288,512]{2,1,0:T(8,128)}, u32[]{:S(2)}) copy-start(f32[2,288,512]{2,1,0:T(8,128)} %copy-done.67) | copy-start | bytes 3538948
  929.6 77.7 %copy-start.87 = (f32[2,288]{1,0:T(2,128)S(1)}, f32[2,288]{1,0:T(2,128)}, u32[]{:S(2)}) copy-start(f32[2,288]{1,0:T(2,128)} %copy-done.86) | copy-start | bytes 6916
  929.6 77.7 %copy-start.94 = (f32[128]{0:T(128)S(1)}, f32[128]{0:T(128)}, u32[]{:S(2)}) copy-start(f32[128]{0:T(128)} %copy-done.93) | copy-start | bytes 1540
  1025.3 95.3 %copy-start.99 = (f32[1,2048]{1,0:T(1,128)S(1)}, f32[1,2048]{1,0:T(1,128)}, u32[]{:S(2)}) copy-start(f32[1,2048]{1,0:T(1,128)} %get-tuple-element.116) | copy-start | bytes 24580
  1025.3 95.3 %copy-start.106 = (f32[128]{0:T(128)S(1)}, f32[128]{0:T(128)}, u32[]{:S(2)}) copy-start(f32[128]{0:T(128)} %get-tuple-element.207) | copy-start | bytes 1540
  1025.3 96.0 %copy-start.85 = (f32[1,4352]{1,0:T(1,128)S(1)}, f32[1,4352]{1,0:T(1,128)}, u32[]{:S(2)}) copy-start(f32[1,4352]{1,0:T(1,128)} %stack.36) | copy-start | bytes 52228
  1025.3 96.1 %copy-start.9 = (bf16[1536,512]{1,0:T(8,128)(2,1)S(1)}, bf16[1536,512]{1,0:T(8,128)(2,1)}, u32[]{:S(2)}) copy-start(bf16[1536,512]{1,0:T(8,128)(2,1)} %copy-done.8) | copy-start | bytes 4718596
  1141.8 23.9 %copy-start.53 = (f32[4,128,768]{2,1,0:T(8,128)S(1)}, f32[4,128,768]{2,1,0:T(8,128)}, u32[]{:S(2)}) copy-start(f32[4,128,768]{2,1,0:T(8,128)} %get-tuple-element.119) | copy-start | bytes 4718596
  1170.7 10.9 copy-start.11
  (86 other events, 195.9 us)
Sparse Core Ops, SparseCore 0:
  55.6 44.3 all-gather.8
  102.4 43.9 all-gather.6
  148.0 95.2 all-gather.14
  245.5 59.4 all-gather.10
  375.7 74.5 all-gather.12
  594.9 45.6 reduce-scatter.7
  644.2 60.5 reduce-scatter.9
  707.1 73.2 reduce-scatter.13
  784.0 48.9 reduce-scatter.17
  836.4 43.9 reduce-scatter.15
  883.4 43.9 reduce-scatter.11
  930.2 43.9 reduce-scatter.19

commit v10 on v9

--- a/solution.py
+++ b/solution.py
@@ -1798,15 +1798,15 @@
         terms, saved_first = attn_forward(
             hidden, first_weights, gains[0], slot,
             lambda own: kv_gather(
-                tied(own, *first_weights[2:]), [UnitsSpread(down_rows)] + units_on(0), 3, carried
+                tied(own, *first_weights[2:]), [UnitsSpread(down_rows)] + units_on(0, 1), 3, carried
             ),
         )
-        (down_all,), (gate_rows,) = carried
+        (down_all,), (gate_rows, up_rows) = carried
         first_weights.append(down_all)
         part = FeedForward(
             terms, own_in, gains[0][1][None], first_weights[2:], True, False, {}
         )
-        outs, ((up_rows, down_rows),) = with_cargo(part, units_on(1, 2), everyone, 4, 90, 56)
+        outs, ((down_rows,),) = with_cargo(part, units_on(2), everyone, 4, 90, 56)
         middle_first, mlp_in_first, hidden_first, own_next, output_first, gate_first, up_first = outs
         second_weights = [
             attn_next[:, :own_depth].reshape(depth, -1),
@@ -1843,7 +1843,8 @@
             grad_attn, saved_second, second_weights, gains[1], slot,
             lambda whole: kv_scatter(tied(whole, *products_second), [], 7, []),
         )
-        attn_second = scatter_shards(weight_products(pairs))
+        pairs = weight_products(pairs)
+        attn_second = scatter_shards([tied(pairs[0], unit_second[2]), pairs[1]])
         terms = tied(terms, unit_second[0])
         part = FeedForward(
             terms, own_next, gains[1][0][None], first_weights[2:], False, True,
@@ -1852,7 +1853,9 @@
                 "middle_in": middle_first, "mlp_gain": gains[0][1][None],
             },
         )
-        outs, _ = with_cargo(part, [], everyone, 8, 90, 60)
+        outs, (home_second,) = with_cargo(
+            part, [UnitsHome(unit_second[:1], 1)], everyone, 8, 90, 60
+        )
         (
             grad_gate, grad_up, grad_middle, mlp_gain_first, grad_attn,
             attn_gain_second, incoming_second, grad_mlp,
@@ -1864,17 +1867,15 @@
                 (flat(hidden_first), flat(grad_mlp)),
             ]
         )
-        grad_attn = tied(grad_attn, unit_second[1], *products)
-        unit_first = scatter_units(products[:2])
+        grad_attn = tied(grad_attn, *unit_second[1:], *products)
+        unit_first = scatter_units([tied(item, attn_second) for item in products[:2]])
         unit_first += scatter_units([tied(products[2], *unit_first)])
         carried = []
         terms, pairs, head_first = attn_backward(
             grad_attn, saved_first, first_weights, gains[0], slot,
-            lambda whole: kv_scatter(
-                tied(whole, attn_second), [UnitsHome(unit_second, 1)], 9, carried
-            ),
-        )
-        (home_second,) = carried
+            lambda whole: kv_scatter(whole, [UnitsHome(unit_second[1:], 1)], 9, carried),
+        )
+        home_second += carried[0]
         whole = jnp.concatenate(weight_products(pairs), axis=1).reshape(dp_size, 4, -1, q_width + qkv_width)
         part = LastHub(terms, own_in, gains[0][0][None], grad_middle)
         (attn_gain_first, incoming_first), ((attn_first,), home_first) = with_cargo(

time: 1200 us -> 1190 us (level)
    unnamed x259 -> x305, local copies, waits for them, and re-layouts: 49.8 us -> 54 us
  transfers between devices with their start and end apart: 12 -> 12, of which waited for: 3 -> 3; matrix products, arithmetic and copies ran while one was open for 15% -> 15% of each run, Pallas kernels for 53% -> 54%
where the time goes in v10:
time: 1190 us; the launch traced here: 1180 us
  Pallas kernels  825 us (69%)
  waiting for transfers between devices  97.8 us (8%)
  matrix products  91.6 us (8%)
  local copies, waits for them, and re-layouts  84.6 us (7%)
  other arithmetic  63.8 us (5%)
  between operations  20.3 us (2%)
    pallas_call x11, Pallas kernels, fused(): pl.pallas_call(kernel, out_shape=[item[0] for item in outs], in_specs=[it...  825 us
    reduce_scatter x6, waiting for transfers between devices, scatter_units(): lax.psum_scatter(item, 'tensor', scatter_dimension=0, tiled=True)  96.2 us
    unnamed x305, local copies, waits for them, and re-layouts  54 us
    dot_general x10, matrix products, dot_outer(): return lax.dot_general(left, right, OUTER, preferred_element_type=F32)  40.2 us
  transfers between devices with their start and end apart: 12, of which 3 were waited for; matrix products, arithmetic and copies ran while one was open for 15% of the time, Pallas kernels for 54%

profile of v10, /device:TPU:0, one launch (start us, length us, event | category | flops | bytes accessed | tf_op | source)
XLA Modules:
  0.0 1184.1 jit_solution(17118690539990276477)
XLA Ops:
  12.2 41.5 %shard_map.255 = (bf16[192,2048]{1,0:T(8,128)(2,1)S(1)}, bf16[192,2048]{1,0:T(8,128)(2,1)S(1)}, f32[2,4,10,128]{3,2,1,0:T(8,128)S(1)}) custom-call(bf16[1536,512]{1,0:T(8,128)(2,1)S(1)} %bitcast.321, bf16[1536,512]{1,0:T(8,128)(2,1)S(1)} %bitcast.323, f32[10,128]{1,0:T(8,128)S(1)} %fusion.112.refs_2_), custom_call_target="tpu_custom_call" | custom-call | bytes 135000000 | tf_op jit(solution)/shard_map/pallas_call | solution.py:210
  60.7 68.4 %shard_map.256 = (bf16[2048,512]{1,0:T(8,128)(2,1)S(1)}, bf16[256,2048]{1,0:T(8,128)(2,1)S(1)}, bf16[192,2048]{1,0:T(8,128)(2,1)S(1)}, bf16[768,512]{1,0:T(8,128)(2,1)S(1)}) custom-call(bf16[512,512]{1,0:T(8,128)(2,1)S(1)} %bitcast.328, bf16[512,256]{1,0:T(8,128)(2,1)S(1)} %bitcast.340, bf16[512,256]{1,0:T(8,128)(2,1)S(1)} %bitcast.342, ...), custom_call_target="tpu_custom_call" | custom-call | bytes 240000000 | tf_op jit(solution)/shard_map/pallas_call | solution.py:210
  152.9 93.4 %shard_map.257 = (bf16[768,2048]{1,0:T(8,128)(2,1)S(1)}, bf16[192,2048]{1,0:T(8,128)(2,1)S(1)}, bf16[192,2048]{1,0:T(8,128)(2,1)}, bf16[2,4,288,256]{3,2,1,0:T(8,128)(2,1)S(1)}) custom-call(bf16[192,2048]{1,0:T(8,128)(2,1)S(1)} %copy-done.15, bf16[1536,512]{1,0:T(8,128)(2,1)S(1)} %bitcast.322, bf16[1536,512]{1,0:T(8,128)(2,1)S(1)} %bitcast.324, ...), custom_call_target="tpu_custom_call" | custom-call | bytes 120000000 | tf_op jit(solution)/shard_map/pallas_call | solution.py:210
  267.8 2.2 convolution_convert_fusion.3
  270.0 112.8 %shard_map.258 = (bf16[192,2048]{1,0:T(8,128)(2,1)}, f32[72,2048]{1,0:T(8,128)}, bf16[3,192,2048]{2,1,0:T(8,128)(2,1)}, bf16[3,192,768]{2,1,0:T(8,128)(2,1)}, f3...) custom-call(bf16[1536,512]{1,0:T(8,128)(2,1)} %bitcast.325, ...), custom_call_target="tpu_custom_call" | custom-call | bytes 270000000 | tf_op jit(solution)/shard_map/pallas_call | solution.py:210
  382.9 2.2 fusion.9
  386.4 3.1 slice.188
  390.8 3.7 fusion.39
  402.9 43.9 %shard_map.259 = (bf16[768,2048]{1,0:T(8,128)(2,1)S(1)}, bf16[2,4,288,256]{3,2,1,0:T(8,128)(2,1)S(1)}) custom-call(bf16[192,2048]{1,0:T(8,128)(2,1)S(1)} %copy-done.21, bf16[2,288,256]{2,1,0:T(8,128)(2,1)S(1)} %pad_maximum_fusion.11.refs_1_), custom_call_target="tpu_custom_call" | custom-call | bytes 120000000 | tf_op jit(solution)/shard_map/pallas_call | solution.py:210
  446.8 3.7 fusion.152
  455.0 2.2 convolution_convert_fusion.2
  457.2 125.7 %shard_map.260 = (f32[72,2048]{1,0:T(8,128)}, bf16[3,192,2048]{2,1,0:T(8,128)(2,1)}, bf16[3,192,768]{2,1,0:T(8,128)(2,1)}, f32[72,2048]{1,0:T(8,128)}, bf16[2,28...) custom-call(bf16[2,288,2048]{2,1,0:T(8,128)(2,1)} %bitcast.351, ...), custom_call_target="tpu_custom_call" | custom-call | bytes 300000000 | tf_op jit(solution)/shard_map/pallas_call | solution.py:210
  582.9 6.3 bitcast_convert_fusion.3
  589.2 3.2 convolution_convert_fusion.7
  593.5 6.3 bitcast_convert_fusion.5
  599.8 4.0 fusion.3
  603.8 3.4 fusion.5
  612.8 4.0 bitcast_convert_fusion.4
  618.5 26.1 %shard_map.261 = f32[2,288,256]{2,1,0:T(8,128)S(1)} custom-call(bf16[2,4,288,256]{3,2,1,0:T(8,128)(2,1)S(1)} %bitcast.327), custom_call_target="tpu_custom_call" | custom-call | bytes 90000000 | tf_op jit(solution)/shard_map/pallas_call | solution.py:210
  652.1 3.4 bitcast_convert_fusion.6
  655.4 3.7 pad_maximum_fusion.1
  660.8 4.4 convolution_convert_fusion.1
  665.2 18.3 %reduce-scatter.8.cloned.1.call-done.refs_0_ = bf16[192,2048]{1,0:T(8,128)(2,1)} async-done(((bf16[768,2048]{1,0:T(8,128)(2,1)}), bf16[192,2048]{1,0:T(8,128)(2,1)}) %reduce-scatter.8.cloned.1.call-update) | async-done | bytes 786448 | tf_op jit(solution)/shard_map/reduce_scatter | solution.py:1771
  683.5 136.2 %shard_map.262 = (bf16[1536,512]{1,0:T(8,128)(2,1)}, bf16[3,192,768]{2,1,0:T(8,128)(2,1)}, bf16[3,192,768]{2,1,0:T(8,128)(2,1)}, f32[72,2048]{1,0:T(8,128)}, f32...) custom-call(bf16[192,2048]{1,0:T(8,128)(2,1)} %reduce-scatter.8.clon, ...), custom_call_target="tpu_custom_call" | custom-call | bytes 270000000 | tf_op jit(solution)/shard_map/pallas_call | solution.py:210
  819.7 6.3 bitcast_convert_fusion.2
  827.1 5.8 bitcast_convert_fusion.1
  834.3 3.5 select_bitcast_fusion.1
  838.4 4.1 bitcast_convert_fusion
  842.5 2.5 convolution_convert_fusion.6
  845.1 3.9 fusion
  852.9 2.6 fusion.45
  857.6 30.3 %reduce-scatter.16.cloned.1.call-done.refs_1_ = bf16[192,2048]{1,0:T(8,128)(2,1)} async-done(((bf16[768,2048]{1,0:T(8,128)(2,1)}), bf16[192,2048]{1,0:T(8,128)(2,1)}) %reduce-scatter.16.cloned.1.call-update) | async-done | bytes 786448 | tf_op jit(solution)/shard_map/reduce_scatter | solution.py:1771
  887.9 47.5 %reduce-scatter.18.cloned.1.call-done.refs_2_ = bf16[192,2048]{1,0:T(8,128)(2,1)} async-done(((bf16[768,2048]{1,0:T(8,128)(2,1)}), bf16[192,2048]{1,0:T(8,128)(2,1)}) %reduce-scatter.18.cloned.1.call-update) | async-done | bytes 786448 | tf_op jit(solution)/shard_map/reduce_scatter | solution.py:1771
  936.3 4.0 fusion.27
  941.7 58.4 %shard_map.263 = (bf16[1536,512]{1,0:T(8,128)(2,1)S(1)}, bf16[1536,512]{1,0:T(8,128)(2,1)S(1)}, f32[2,288,256]{2,1,0:T(8,128)S(1)}) custom-call(bf16[192,2048]{1,0:T(8,128)(2,1)S(1)} %copy-done.23, bf16[192,2048]{1,0:T(8,128)(2,1)S(1)} %copy-done.22, bf16[2,4,288,256]{3,2,1,0:T(8,128)(2,1)S(1)} %pad_maximum_fusion.4.refs_2_), custom_call_target="tpu_custom_call" | custom-call | bytes 90000000 | tf_op jit(solution)/shard_map/pallas_call | solution.py:210
  1003.6 2.0 bitcast_convert_fusion.7
  1007.5 4.6 copy.195
  1012.1 4.0 copy.269
  1016.1 2.8 convolution_convert_fusion
  1018.9 95.2 %shard_map.264 = (f32[4,128,768]{2,1,0:T(8,128)}, bf16[1536,512]{1,0:T(8,128)(2,1)}, bf16[1536,512]{1,0:T(8,128)(2,1)}, f32[1,2048]{1,0:T(1,128)}, bf16[2,288,2048]{2,1,0:T(8,128)(2,1)}) custom-call(bf16[4,4,128,768]{3,2,1,0:T(8,128)(2,1)} %bitcast.349, bf16[192,2048]{1,0:T(8,128)(2,1)} %reduce-scatter.16.cloned.1.call-done.refs_1_, ...), custom_call_target="tpu_custom_call" | custom-call | bytes 180000000 | tf_op jit(solution)/shard_map/pallas_call | solution.py:210
  1115.0 3.3 convert_bitcast_fusion
  1118.3 3.7 copy.202
  1121.9 3.3 convert_bitcast_fusion.1
  1125.2 3.6 copy.201
  1131.0 3.3 select_bitcast_fusion
  1135.4 23.8 %shard_map.265 = (f32[68,128]{1,0:T(8,128)S(1)}, bf16[512,768]{1,0:T(8,128)(2,1)S(1)}, bf16[1536,512]{1,0:T(8,128)(2,1)S(1)}) custom-call(f32[68,128]{1,0:T(8,128)S(1)} %reshape.596.refs_0_, bf16[512,768]{1,0:T(8,128)(2,1)S(1)} %bitcast_select_fusion.3.refs_1_, bf16[192,2048]{1,0:T(8,128)(2,1)S(1)} %copy-done.20), custom_call_target="tpu_custom_call" | custom-call | bytes 180000000 | tf_op jit(solution)/shard_map/pallas_call | solution.py:210
  1164.3 2.6 copy.200
  1173.1 2.0 maximum_convert_fusion
  (459 shorter events, 118.7 us)
Async XLA Ops:
  7.2 144.6 %all-gather.9.cloned.1.call-start = ((), (), s32[]{:S(2)}) async-start(), calls=%async_computation.8 | async-start | bytes 3932160 | tf_op jit(solution)/shard_map/all_gather | solution.py:1689
  12.1 44.2 %copy-start.9 = (bf16[1,512,256]{2,1,0:T(8,128)(2,1)S(1)}, bf16[1,512,256]{2,1,0:T(8,128)(2,1)}, u32[]{:S(2)}) copy-start(bf16[1,512,256]{2,1,0:T(8,128)(2,1)} %param.23) | copy-start | bytes 786436
  55.5 96.3 %all-gather.7.cloned.1.call-start = ((), (), s32[]{:S(2)}) async-start(), calls=%async_computation.7 | async-start | bytes 3932160 | tf_op jit(solution)/shard_map/all_gather | solution.py:1689
  56.2 328.8 %all-gather.15.cloned.1.call-start = ((), (), s32[]{:S(2)}) async-start(), calls=%async_computation.18 | async-start | bytes 3932160 | tf_op jit(solution)/shard_map/all_gather | solution.py:1706
  60.7 72.5 %copy-start.130 = (s32[2]{0:T(128)S(1)}, s32[2]{0:T(128)}, u32[]{:S(2)}) copy-start(s32[2]{0:T(128)} %param.20) | copy-start | bytes 28
  133.2 269.7 %all-gather.11.cloned.1.call-start = ((), (), s32[]{:S(2)}) async-start(), calls=%async_computation.9 | async-start | bytes 3932160 | tf_op jit(solution)/shard_map/all_gather | solution.py:1689
  145.9 5.7 copy-start.81
  148.2 112.8 %copy-start.113 = (f32[128]{0:T(128)}, f32[128]{0:T(128)S(1)}, u32[]{:S(2)}) copy-start(f32[128]{0:T(128)S(1)} %get-tuple-element.265) | copy-start | bytes 1540
  148.2 251.7 %copy-start.111 = (f32[128]{0:T(128)}, f32[128]{0:T(128)S(1)}, u32[]{:S(2)}) copy-start(f32[128]{0:T(128)S(1)} %get-tuple-element.264) | copy-start | bytes 1540
  249.9 4.5 copy-start.131
  250.0 207.3 %all-gather.13.cloned.1.call-start = ((), (), s32[]{:S(2)}) async-start(), calls=%async_computation.10 | async-start | bytes 3932160 | tf_op jit(solution)/shard_map/all_gather | solution.py:1689
  253.2 7.8 copy-start.39
  267.8 387.7 %reduce-scatter.12.cloned.1.call-start = ((), (), s32[]{:S(2)}) async-start(), calls=%async_computation.13 | async-start | bytes 3932160 | tf_op jit(solution)/shard_map/reduce_scatter | solution.py:1771
  386.4 4.4 copy-start.122
  395.6 5.5 copy-start.52
  395.6 5.5 copy-start.55
  395.6 5.5 copy-start.58
  395.6 5.5 copy-start.61
  395.7 5.8 copy-start.41
  396.8 4.7 copy-start.115
  589.2 94.3 %reduce-scatter.8.cloned.1.call-start = ((), (), s32[]{:S(2)}) async-start(), calls=%async_computation.11 | async-start | bytes 3932160 | tf_op jit(solution)/shard_map/reduce_scatter | solution.py:1771
  599.7 226.2 %reduce-scatter.14.cloned.1.call-start = ((), (), s32[]{:S(2)}) async-start(), calls=%async_computation.14 | async-start | bytes 3932160 | tf_op jit(solution)/shard_map/reduce_scatter | solution.py:1775
  599.8 9.8 slice-start.2
  603.8 5.0 copy-start.78
  603.8 5.0 copy-start.79
  603.8 5.8 slice-start.3
  618.4 27.4 %copy-start.67 = (f32[2,288,512]{2,1,0:T(8,128)S(1)}, f32[2,288,512]{2,1,0:T(8,128)}, u32[]{:S(2)}) copy-start(f32[2,288,512]{2,1,0:T(8,128)} %copy-done.66) | copy-start | bytes 3538948
  618.4 27.4 %copy-start.97 = (f32[2,288]{1,0:T(2,128)S(1)}, f32[2,288]{1,0:T(2,128)}, u32[]{:S(2)}) copy-start(f32[2,288]{1,0:T(2,128)} %copy-done.96) | copy-start | bytes 6916
  618.4 27.4 %copy-start.112 = (f32[128]{0:T(128)S(1)}, f32[128]{0:T(128)}, u32[]{:S(2)}) copy-start(f32[128]{0:T(128)} %copy-done.111) | copy-start | bytes 1540
  618.5 28.2 %copy-start.30 = (bf16[2,2,288,1152]{3,2,1,0:T(8,128)(2,1)S(1)}, bf16[2,2,288,1152]{3,2,1,0:T(8,128)(2,1)}, u32[]{:S(2)}) copy-start(bf16[2,2,288,1152]{3,2,1,0:T(8,128)(2,1)} %copy-done.29) | copy-start | bytes 7962628
  659.1 183.4 %reduce-scatter.10.cloned.1.call-start = ((), (), s32[]{:S(2)}) async-start(), calls=%async_computation.12 | async-start | bytes 3932160 | tf_op jit(solution)/shard_map/reduce_scatter | solution.py:1771
  659.9 228.0 %reduce-scatter.16.cloned.1.call-start = ((), (), s32[]{:S(2)}) async-start(), calls=%async_computation.15 | async-start | bytes 3932160 | tf_op jit(solution)/shard_map/reduce_scatter | solution.py:1771
  826.0 109.4 %reduce-scatter.18.cloned.1.call-start = ((), (), s32[]{:S(2)}) async-start(), calls=%async_computation.16 | async-start | bytes 3932160 | tf_op jit(solution)/shard_map/reduce_scatter | solution.py:1771
  832.9 301.4 %reduce-scatter.20.cloned.1.call-start = ((), (), s32[]{:S(2)}) async-start(), calls=%async_computation.17 | async-start | bytes 3932160 | tf_op jit(solution)/shard_map/reduce_scatter | solution.py:1771
  856.7 78.8 %copy-start.91 = (f32[2,288,2]{1,2,0:T(2,128)S(1)}, f32[2,288,2]{1,2,0:T(2,128)}, u32[]{:S(2)}) copy-start(f32[2,288,2]{1,2,0:T(2,128)} %copy-done.90) | copy-start | bytes 13828
  940.3 59.9 %copy-start.53 = (f32[1,288,64]{2,1,0:T(8,128)S(1)}, f32[1,288,64]{2,1,0:T(8,128)}, u32[]{:S(2)}) copy-start(f32[1,288,64]{2,1,0:T(8,128)} %copy-done.51) | copy-start | bytes 221188
  940.3 59.9 %copy-start.56 = (f32[1,288,64]{2,1,0:T(8,128)S(1)}, f32[1,288,64]{2,1,0:T(8,128)}, u32[]{:S(2)}) copy-start(f32[1,288,64]{2,1,0:T(8,128)} %copy-done.54) | copy-start | bytes 221188
  940.3 59.9 %copy-start.59 = (f32[1,288,64]{2,1,0:T(8,128)S(1)}, f32[1,288,64]{2,1,0:T(8,128)}, u32[]{:S(2)}) copy-start(f32[1,288,64]{2,1,0:T(8,128)} %copy-done.57) | copy-start | bytes 221188
  940.3 59.9 %copy-start.62 = (f32[1,288,64]{2,1,0:T(8,128)S(1)}, f32[1,288,64]{2,1,0:T(8,128)}, u32[]{:S(2)}) copy-start(f32[1,288,64]{2,1,0:T(8,128)} %copy-done.60) | copy-start | bytes 221188
  941.7 58.7 %copy-start.65 = (f32[2,288,512]{2,1,0:T(8,128)S(1)}, f32[2,288,512]{2,1,0:T(8,128)}, u32[]{:S(2)}) copy-start(f32[2,288,512]{2,1,0:T(8,128)} %copy-done.64) | copy-start | bytes 3538948
  941.7 58.7 %copy-start.95 = (f32[2,288]{1,0:T(2,128)S(1)}, f32[2,288]{1,0:T(2,128)}, u32[]{:S(2)}) copy-start(f32[2,288]{1,0:T(2,128)} %copy-done.94) | copy-start | bytes 6916
  941.7 58.7 %copy-start.110 = (f32[128]{0:T(128)S(1)}, f32[128]{0:T(128)}, u32[]{:S(2)}) copy-start(f32[128]{0:T(128)} %copy-done.109) | copy-start | bytes 1540
  941.7 59.1 %copy-start.101 = (f32[2,288]{1,0:T(2,128)S(1)}, f32[2,288]{1,0:T(2,128)}, u32[]{:S(2)}) copy-start(f32[2,288]{1,0:T(2,128)} %copy-done.100) | copy-start | bytes 6916
  1018.9 95.2 %copy-start.118 = (f32[1,2048]{1,0:T(1,128)S(1)}, f32[1,2048]{1,0:T(1,128)}, u32[]{:S(2)}) copy-start(f32[1,2048]{1,0:T(1,128)} %get-tuple-element.120) | copy-start | bytes 24580
  1018.9 95.2 %copy-start.129 = (f32[128]{0:T(128)S(1)}, f32[128]{0:T(128)}, u32[]{:S(2)}) copy-start(f32[128]{0:T(128)} %get-tuple-element.211) | copy-start | bytes 1540
  1018.9 96.0 %copy-start.89 = (f32[1,4352]{1,0:T(1,128)S(1)}, f32[1,4352]{1,0:T(1,128)}, u32[]{:S(2)}) copy-start(f32[1,4352]{1,0:T(1,128)} %stack.36) | copy-start | bytes 52228
  1135.4 23.9 %copy-start.49 = (f32[4,128,768]{2,1,0:T(8,128)S(1)}, f32[4,128,768]{2,1,0:T(8,128)}, u32[]{:S(2)}) copy-start(f32[4,128,768]{2,1,0:T(8,128)} %get-tuple-element.123) | copy-start | bytes 4718596
  1164.3 10.9 copy-start.6
  (109 other events, 235.9 us)
Sparse Core Ops, SparseCore 0:
  55.6 44.3 all-gather.8
  102.4 44.0 all-gather.6
  148.6 105.1 all-gather.14
  256.1 69.2 all-gather.10
  327.0 56.7 all-gather.12
  589.3 46.6 reduce-scatter.11
  639.5 43.9 reduce-scatter.7
  685.8 88.0 reduce-scatter.13
  777.4 63.0 reduce-scatter.9
  843.9 43.9 reduce-scatter.15
  891.4 43.9 reduce-scatter.17
  938.3 43.9 reduce-scatter.19

commit v11 on v10

--- a/solution.py
+++ b/solution.py
@@ -1212,6 +1212,25 @@
             )
             self.gain_grad[...] += gain_grad
             self.rows_out.begin(chunk, result + self.add[at])
+        self.rows_out.complete(self.gathered)
+
+
+class RowsOut(Staged):
+    def __init__(self, own):
+        rows, depth = own.shape
+        self.rows_out = Gatherer("tensor", rows, depth // 2)
+        super().__init__(
+            {"own": (own, VMEM)},
+            {"gathered": vmem_bf16(2, self.rows_out.size * rows, depth)},
+            {},
+            [self.rows_out],
+        )
+
+    def start(self):
+        for chunk in range(self.rows_out.chunks):
+            self.rows_out.begin(chunk, self.own[rows_at(chunk, self.rows_out.rows)])
+
+    def run(self):
         self.rows_out.complete(self.gathered)
 
 
@@ -1242,14 +1261,18 @@
                 "mlp_in": vmem_bf16(chunks, chunk_rows, depth),
                 "hidden": vmem_bf16(chunks, chunk_rows, units),
                 "own_out": vmem_f32(rows, depth),
-                "out": vmem_bf16(2, tensor_rows, depth),
             }
             self.back = Scatterer("dp", rows, half)
-            self.out_rows = Gatherer("tensor", rows, half)
-            helpers += [self.back, self.out_rows]
+            helpers += [self.back]
             scratch["kept"] = kept
         if forward and not backward:
-            outs |= {"gate": vmem_f32(chunks, chunk_rows, units), "up": vmem_f32(chunks, chunk_rows, units)}
+            outs |= {
+                "out": vmem_bf16(2, tensor_rows, depth),
+                "gate": vmem_f32(chunks, chunk_rows, units),
+                "up": vmem_f32(chunks, chunk_rows, units),
+            }
+            self.out_rows = Gatherer("tensor", rows, half)
+            helpers += [self.out_rows]
         if forward and backward:
             outs["grad_mlp"] = vmem_bf16(chunks, chunk_rows, depth)
             self.grad_in = Gatherer("dp", rows, half)
@@ -1273,12 +1296,9 @@
         if backward and not forward:
             outs |= {
                 "gain_grad": vmem_f32(1, depth),
-                "incoming": vmem_bf16(2, tensor_rows, depth),
+                "grad_own": vmem_f32(rows, depth),
                 "grad_mlp": vmem_bf16(chunks, chunk_rows, depth),
             }
-            scratch["grad_own"] = pltpu.VMEM((rows, depth), F32)
-            self.incoming_rows = Gatherer("tensor", rows, half)
-            helpers += [self.incoming_rows]
         super().__init__(ins, outs, scratch, helpers)
 
     def loads(self):
@@ -1319,7 +1339,6 @@
                 result = (result + self.add[at]).astype(BF16).astype(F32)
                 self.grad_own[at] = result
                 self.spread_in.begin(chunk, result)
-                self.incoming_rows.begin(chunk, result)
         for copy in self.loads():
             copy.wait()
 
@@ -1361,10 +1380,8 @@
         self.hand_back(self.chunks - 1)
         if self.has_backward:
             self.grad_rows.complete(self.grad_attn)
-        if self.has_forward:
+        else:
             self.out_rows.complete(self.out)
-        else:
-            self.incoming_rows.complete(self.incoming)
 
     def hand_back(self, chunk):
         at = rows_at(chunk, self.rows)
@@ -1379,7 +1396,8 @@
         if self.has_forward:
             output = (self.middle[at] + self.back.collect(chunk)).astype(BF16).astype(F32)
             self.own_out[at] = output
-            self.out_rows.begin(chunk, output)
+            if not self.has_backward:
+                self.out_rows.begin(chunk, output)
 
     def unit_tiles(self, body):
         tile = 256
@@ -1443,6 +1461,33 @@
 
         for place in range(self.size):
             scatterer.over(chunk, place).start()
+
+
+def finish_units(first, second, core, tile=256):
+    units, own_depth = first[0].shape
+
+    def kernel(core_ref, *refs):
+        ins, (gate, up, down) = refs[:6], refs[6:]
+        rows = lax.broadcasted_iota(jnp.int32, (own_depth, own_depth), 0)
+        identity = (rows == lax.broadcasted_iota(jnp.int32, rows.shape, 1)).astype(BF16)
+        picked = [
+            jnp.where(core_ref[0] == 0, ins[i][...], ins[3 + i][...]) for i in range(3)
+        ]
+        gate[...] = dot_inner(identity, picked[0])
+        up[...] = dot_inner(identity, picked[1])
+        down[...] = picked[2].astype(F32)
+
+    tall = pl.BlockSpec((tile, own_depth), lambda step: (step, 0))
+    wide = pl.BlockSpec((own_depth, tile), lambda step: (0, step))
+    return pl.pallas_call(
+        kernel,
+        grid=(units // tile,),
+        out_shape=[jax.ShapeDtypeStruct((own_depth, units), F32)] * 2
+        + [jax.ShapeDtypeStruct((units, own_depth), F32)],
+        in_specs=[pl.BlockSpec(memory_space=pltpu.SMEM)] + [tall] * 6,
+        out_specs=[wide, wide, tall],
+        cost_estimate=pl.CostEstimate(flops=0, bytes_accessed=25_000_000, transcendentals=0),
+    )(core.reshape(1), *first, *second)
 
 
 def hub_plain(terms, own_args, body, own_outs, scatter, gathers):
@@ -1787,9 +1832,15 @@
 
         def kv_scatter(whole, cargo, collective_id, carried):
             part = ScatterKV(whole.reshape(trees, dp_size, row_count, 2 * HD))
-            (total,), outs = with_cargo(part, cargo, line, collective_id, 30)
+            (total,), outs = with_cargo(part, cargo, everyone, collective_id, 30)
             carried += outs
             return total
+
+        def in_order(pairs):
+            done = []
+            for left, right in pairs:
+                done += weight_products([(tied(left, *done[-1:]), right)])
+            return done
 
         def flat(array):
             return array.reshape(-1, array.shape[-1])
@@ -1828,20 +1879,21 @@
         )
         outs, _ = with_cargo(part, [], everyone, 6, 100, 60)
         (
-            middle, mlp_in, hidden_bf, _, output_second, grad_mlp,
+            middle, mlp_in, hidden_bf, own_second, grad_mlp,
             grad_gate, grad_up, grad_middle, mlp_gain_second, grad_attn,
         ) = outs
-        products_second = weight_products(
-            [
-                (flat(grad_gate), flat(mlp_in)),
-                (flat(grad_up), flat(mlp_in)),
-                (flat(hidden_bf), flat(grad_mlp)),
-            ]
-        )
-        unit_second = scatter_units(products_second)
+        products = in_order([(flat(grad_gate), flat(mlp_in)), (flat(grad_up), flat(mlp_in))])
+        unit_second = scatter_units(products)
+        carried = []
         terms, pairs, head_second = attn_backward(
             grad_attn, saved_second, second_weights, gains[1], slot,
-            lambda whole: kv_scatter(tied(whole, *products_second), [], 7, []),
+            lambda whole: kv_scatter(
+                tied(whole, *products), [RowsOut(own_second)], 7, carried
+            ),
+        )
+        ((output_second,),) = carried
+        unit_second += scatter_units(
+            weight_products([(tied(flat(hidden_bf), output_second), flat(grad_mlp))])
         )
         pairs = weight_products(pairs)
         attn_second = scatter_shards([tied(pairs[0], unit_second[2]), pairs[1]])
@@ -1853,29 +1905,27 @@
                 "middle_in": middle_first, "mlp_gain": gains[0][1][None],
             },
         )
-        outs, (home_second,) = with_cargo(
-            part, [UnitsHome(unit_second[:1], 1)], everyone, 8, 90, 60
-        )
+        outs, _ = with_cargo(part, [], everyone, 8, 90, 60)
         (
             grad_gate, grad_up, grad_middle, mlp_gain_first, grad_attn,
-            attn_gain_second, incoming_second, grad_mlp,
+            attn_gain_second, own_incoming, grad_mlp,
         ) = outs
-        products = weight_products(
-            [
-                (flat(grad_gate), flat(mlp_in_first)),
-                (flat(grad_up), flat(mlp_in_first)),
-                (flat(hidden_first), flat(grad_mlp)),
-            ]
+        products = in_order(
+            [(flat(grad_gate), flat(mlp_in_first)), (flat(grad_up), flat(mlp_in_first))]
         )
         grad_attn = tied(grad_attn, *unit_second[1:], *products)
-        unit_first = scatter_units([tied(item, attn_second) for item in products[:2]])
-        unit_first += scatter_units([tied(products[2], *unit_first)])
+        unit_first = scatter_units(products)
         carried = []
         terms, pairs, head_first = attn_backward(
             grad_attn, saved_first, first_weights, gains[0], slot,
-            lambda whole: kv_scatter(whole, [UnitsHome(unit_second[1:], 1)], 9, carried),
-        )
-        home_second += carried[0]
+            lambda whole: kv_scatter(
+                whole, [UnitsHome(unit_second, 1), RowsOut(own_incoming)], 9, carried
+            ),
+        )
+        home_second, (incoming_second,) = carried
+        unit_first += scatter_units(
+            weight_products([(tied(flat(hidden_first), incoming_second), flat(grad_mlp))])
+        )
         whole = jnp.concatenate(weight_products(pairs), axis=1).reshape(dp_size, 4, -1, q_width + qkv_width)
         part = LastHub(terms, own_in, gains[0][0][None], grad_middle)
         (attn_gain_first, incoming_first), ((attn_first,), home_first) = with_cargo(
@@ -1908,9 +1958,7 @@
             everyone, True, 11, 60,
         )
         attn_home = (jnp.where(core == 0, mine, arrived), jnp.where(core == 0, arrived, mine))
-        unit_home = [
-            jnp.where(core == 0, first, second) for first, second in zip(home_first + down_home, home_second)
-        ]
+        grad_gate, grad_up, grad_down = finish_units(home_first + down_home, home_second, core)
         gain_total = gain_total.reshape(2, -1)
     else:
         def bring_home(first, second):
@@ -1925,7 +1973,8 @@
 
         attn_home = bring_home(weight_grads[0][0], weight_grads[1][0])
         unit_home = jnp.stack(bring_home(pieces_of(weight_grads[0][1]), pieces_of(weight_grads[1][1])))
-        unit_home = unit_home.transpose(2, 0, 1, 3, 4).reshape(3, own_units, own_depth)
+        unit_home = unit_home.transpose(2, 0, 1, 3, 4).reshape(3, own_units, own_depth).astype(F32)
+        grad_gate, grad_up, grad_down = unit_home[0].T, unit_home[1].T, unit_home[2]
         gain_total = lax.psum(gain_total, ("section", "dp", "tensor"))
 
     def joined(start, width):
@@ -1951,9 +2000,9 @@
         gain_own[2 * depth : 2 * depth + HD][None],
         gain_own[2 * depth + HD :][None],
         mlp_gain_grad[None],
-        unit_home[0].T.astype(F32)[None],
-        unit_home[1].T.astype(F32)[None],
-        unit_home[2].astype(F32)[None],
+        grad_gate[None],
+        grad_up[None],
+        grad_down[None],
     )
 
 

time: 1190 us -> 1080 us (0.908)
  waiting for transfers between devices: 97.8 us -> 2.22 us
  other arithmetic: 63.8 us -> 44.8 us
    reduce_scatter x6, waiting for transfers between devices: 96.2 us -> 0.05 us  [scatter_units(): lax.psum_scatter(item, 'tensor', scatter_dimension=0, tiled=True)]
    pallas_call x11, Pallas kernels: 825 us -> 813 us  [fused(): pl.pallas_call(kernel, out_shape=[item[0] for item in outs], in_specs=[it...]
    unnamed x305 -> x331, local copies, waits for them, and re-layouts: 54 us -> 54.8 us
  transfers between devices with their start and end apart: 12 -> 12, of which waited for: 3 -> 0; matrix products, arithmetic and copies ran while one was open for 15% -> 15% of each run, Pallas kernels for 54% -> 59%
where the time goes in v11:
time: 1080 us; the launch traced here: 1070 us
  Pallas kernels  823 us (76%)
  matrix products  94 us (9%)
  local copies, waits for them, and re-layouts  82.1 us (8%)
  other arithmetic  44.8 us (4%)
  between operations  20.5 us (2%)
    pallas_call x11, Pallas kernels, fused(): pl.pallas_call(kernel, out_shape=[item[0] for item in outs], in_specs=[it...  813 us
    unnamed x331, local copies, waits for them, and re-layouts  54.8 us
    dot_general x10, matrix products, dot_outer(): return lax.dot_general(left, right, OUTER, preferred_element_type=F32)  43.4 us
  transfers between devices with their start and end apart: 12, of which 0 were waited for; matrix products, arithmetic and copies ran while one was open for 15% of the time, Pallas kernels for 59%

profile of v11, /device:TPU:0, one launch (start us, length us, event | category | flops | bytes accessed | tf_op | source)
XLA Modules:
  0.0 1067.8 jit_solution(11792795752689109827)
XLA Ops:
  12.2 41.5 %shard_map.255 = (bf16[192,2048]{1,0:T(8,128)(2,1)S(1)}, bf16[192,2048]{1,0:T(8,128)(2,1)S(1)}, f32[2,4,10,128]{3,2,1,0:T(8,128)S(1)}) custom-call(bf16[1536,512]{1,0:T(8,128)(2,1)S(1)} %bitcast.312, bf16[1536,512]{1,0:T(8,128)(2,1)S(1)} %bitcast.314, f32[10,128]{1,0:T(8,128)S(1)} %fusion.112.refs_2_), custom_call_target="tpu_custom_call" | custom-call | bytes 135000000 | tf_op jit(solution)/shard_map/pallas_call | solution.py:210
  60.7 68.4 %shard_map.256 = (bf16[2048,512]{1,0:T(8,128)(2,1)S(1)}, bf16[256,2048]{1,0:T(8,128)(2,1)S(1)}, bf16[192,2048]{1,0:T(8,128)(2,1)S(1)}, bf16[768,512]{1,0:T(8,128)(2,1)S(1)}) custom-call(bf16[512,512]{1,0:T(8,128)(2,1)S(1)} %bitcast.319, bf16[512,256]{1,0:T(8,128)(2,1)S(1)} %bitcast.331, bf16[512,256]{1,0:T(8,128)(2,1)S(1)} %bitcast.333, ...), custom_call_target="tpu_custom_call" | custom-call | bytes 240000000 | tf_op jit(solution)/shard_map/pallas_call | solution.py:210
  138.4 1.8 constant_dynamic-slice_fusion.3
  140.8 1.9 copy-done.38
  152.9 93.5 %shard_map.257 = (bf16[768,2048]{1,0:T(8,128)(2,1)S(1)}, bf16[192,2048]{1,0:T(8,128)(2,1)S(1)}, bf16[192,2048]{1,0:T(8,128)(2,1)}, bf16[2,4,288,256]{3,2,1,0:T(8,128)(2,1)S(1)}) custom-call(bf16[192,2048]{1,0:T(8,128)(2,1)S(1)} %copy-done.25, bf16[1536,512]{1,0:T(8,128)(2,1)S(1)} %bitcast.313, bf16[1536,512]{1,0:T(8,128)(2,1)S(1)} %bitcast.315, ...), custom_call_target="tpu_custom_call" | custom-call | bytes 120000000 | tf_op jit(solution)/shard_map/pallas_call | solution.py:210
  258.5 1.9 bitcast_convert_fusion.2.refs_6_
  267.8 2.2 convolution_convert_fusion.9
  270.0 112.7 %shard_map.258 = (bf16[192,2048]{1,0:T(8,128)(2,1)}, f32[72,2048]{1,0:T(8,128)}, bf16[3,192,2048]{2,1,0:T(8,128)(2,1)}, bf16[3,192,768]{2,1,0:T(8,128)(2,1)}, f3...) custom-call(bf16[1536,512]{1,0:T(8,128)(2,1)} %bitcast.316, ...), custom_call_target="tpu_custom_call" | custom-call | bytes 270000000 | tf_op jit(solution)/shard_map/pallas_call | solution.py:210
  382.6 2.2 fusion.9
  384.9 2.3 slice.200
  387.1 3.2 slice.188
  390.3 2.3 copy.201
  392.6 3.0 fusion.39
  398.0 1.8 multiply_reduce_fusion.2
  402.6 44.0 %shard_map.259 = (bf16[768,2048]{1,0:T(8,128)(2,1)S(1)}, bf16[2,4,288,256]{3,2,1,0:T(8,128)(2,1)S(1)}) custom-call(bf16[192,2048]{1,0:T(8,128)(2,1)S(1)} %copy-done.31, bf16[2,288,256]{2,1,0:T(8,128)(2,1)S(1)} %pad_maximum_fusion.11.refs_1_), custom_call_target="tpu_custom_call" | custom-call | bytes 120000000 | tf_op jit(solution)/shard_map/pallas_call | solution.py:210
  446.6 3.2 fusion.152
  454.3 2.2 convolution_convert_fusion.8
  456.5 119.8 %shard_map.260 = (f32[72,2048]{1,0:T(8,128)}, bf16[3,192,2048]{2,1,0:T(8,128)(2,1)}, bf16[3,192,768]{2,1,0:T(8,128)(2,1)}, f32[72,2048]{1,0:T(8,128)}, bf16[3,19...) custom-call(bf16[2,288,2048]{2,1,0:T(8,128)(2,1)} %bitcast.340, ...), custom_call_target="tpu_custom_call" | custom-call | bytes 300000000 | tf_op jit(solution)/shard_map/pallas_call | solution.py:210
  576.3 6.3 convolution_convert_fusion.5
  582.8 2.4 convolution_convert_fusion.13
  585.4 4.0 fusion.3
  594.8 4.0 convolution_convert_fusion.4
  600.6 30.9 %shard_map.261 = (bf16[2,288,2048]{2,1,0:T(8,128)(2,1)S(1)}, f32[2,288,256]{2,1,0:T(8,128)S(1)}) custom-call(f32[72,2048]{1,0:T(8,128)S(1)} %copy-done.35, bf16[2,4,288,256]{3,2,1,0:T(8,128)(2,1)S(1)} %bitcast.318), custom_call_target="tpu_custom_call" | custom-call | bytes 90000000 | tf_op jit(solution)/shard_map/pallas_call | solution.py:210
  632.3 6.3 convolution_convert_fusion.3
  641.0 2.6 fusion.46
  648.2 2.8 convolution_convert_fusion.7
  651.1 90.7 %shard_map.262 = (bf16[3,192,768]{2,1,0:T(8,128)(2,1)}, bf16[3,192,768]{2,1,0:T(8,128)(2,1)}, f32[72,2048]{1,0:T(8,128)}, f32[1,2048]{1,0:T(1,128)}, bf16[2,288,...) custom-call(bf16[2,288,2048]{2,1,0:T(8,128)(2,1)} %bitcast.345, ...), custom_call_target="tpu_custom_call" | custom-call | bytes 270000000 | tf_op jit(solution)/shard_map/pallas_call | solution.py:210
  741.8 6.3 convolution_convert_fusion.2
  748.1 6.2 convolution_convert_fusion.1
  755.4 3.9 convolution_convert_fusion.10
  759.3 3.4 bitcast_convert_fusion
  762.6 3.5 pad_maximum_fusion.1
  766.9 4.1 convolution_convert_fusion.12
  772.7 4.1 fusion
  776.8 3.4 fusion.2
  783.3 2.1 copy.183
  785.5 4.2 fusion.27
  791.3 80.3 %shard_map.263 = (bf16[1536,512]{1,0:T(8,128)(2,1)S(1)}, bf16[1536,512]{1,0:T(8,128)(2,1)S(1)}, bf16[1536,512]{1,0:T(8,128)(2,1)S(1)}, bf16[2,288,2048]{2,1,0:T(8,128)(2,1)S(1)}, f32[2,288,256]{2,1,0:T(8,128)S(1)}) custom-call(bf16[192,2048]{1,0:T(8,128)(2,1)S(1)} %copy-done.32, bf16[192,2048]{1,0:T(8,128)(2,1)S(1)} %copy-done.34, ...), custom_call_target="tpu_custom_call" | custom-call | bytes 90000000 | tf_op jit(solution)/shard_map/pallas_call | solution.py:210
  877.4 4.0 convolution_convert_fusion
  882.7 3.5 select_bitcast_fusion.1
  893.9 2.0 bitcast_convert_fusion.1
  896.2 2.8 copy.185
  899.0 4.0 copy.257
  903.0 2.8 convolution_convert_fusion.6
  905.8 107.5 %shard_map.264 = (f32[4,128,768]{2,1,0:T(8,128)}, bf16[1536,512]{1,0:T(8,128)(2,1)}, bf16[1536,512]{1,0:T(8,128)(2,1)}, f32[1,2048]{1,0:T(1,128)}, bf16[2,288,2048]{2,1,0:T(8,128)(2,1)}) custom-call(bf16[4,4,128,768]{3,2,1,0:T(8,128)(2,1)} %bitcast.338, bf16[192,2048]{1,0:T(8,128)(2,1)} %reduce-scatter.14.cloned.1.call-done.refs_1_, ...), custom_call_target="tpu_custom_call" | custom-call | bytes 180000000 | tf_op jit(solution)/shard_map/pallas_call | solution.py:210
  1014.2 1.9 bitcast_select_fusion.3.refs_1_
  1017.3 23.8 %shard_map.265 = (f32[68,128]{1,0:T(8,128)S(1)}, bf16[512,768]{1,0:T(8,128)(2,1)S(1)}, bf16[1536,512]{1,0:T(8,128)(2,1)S(1)}) custom-call(f32[68,128]{1,0:T(8,128)S(1)} %reshape.626.refs_0_, bf16[512,768]{1,0:T(8,128)(2,1)S(1)} %bitcast_select_fusion.3.refs_1_, bf16[192,2048]{1,0:T(8,128)(2,1)S(1)} %copy-done.28), custom_call_target="tpu_custom_call" | custom-call | bytes 180000000 | tf_op jit(solution)/shard_map/pallas_call | solution.py:210
  1051.3 9.5 shard_map.266
  (482 shorter events, 106.3 us)
Async XLA Ops:
  7.2 144.5 %all-gather.9.cloned.1.call-start = ((), (), s32[]{:S(2)}) async-start(), calls=%async_computation.8 | async-start | bytes 3932160 | tf_op jit(solution)/shard_map/all_gather | solution.py:1734
  12.1 44.2 %copy-start.16 = (bf16[1,512,256]{2,1,0:T(8,128)(2,1)S(1)}, bf16[1,512,256]{2,1,0:T(8,128)(2,1)}, u32[]{:S(2)}) copy-start(bf16[1,512,256]{2,1,0:T(8,128)(2,1)} %param.23) | copy-start | bytes 786436
  55.5 96.2 %all-gather.7.cloned.1.call-start = ((), (), s32[]{:S(2)}) async-start(), calls=%async_computation.7 | async-start | bytes 3932160 | tf_op jit(solution)/shard_map/all_gather | solution.py:1734
  56.2 328.6 %all-gather.15.cloned.1.call-start = ((), (), s32[]{:S(2)}) async-start(), calls=%async_computation.18 | async-start | bytes 3932160 | tf_op jit(solution)/shard_map/all_gather | solution.py:1751
  60.7 72.5 %copy-start.148 = (s32[2]{0:T(128)S(1)}, s32[2]{0:T(128)}, u32[]{:S(2)}) copy-start(s32[2]{0:T(128)} %param.20) | copy-start | bytes 28
  133.2 269.4 %all-gather.11.cloned.1.call-start = ((), (), s32[]{:S(2)}) async-start(), calls=%async_computation.9 | async-start | bytes 3932160 | tf_op jit(solution)/shard_map/all_gather | solution.py:1734
  145.8 5.7 copy-start.100
  148.2 112.2 %copy-start.132 = (f32[128]{0:T(128)}, f32[128]{0:T(128)S(1)}, u32[]{:S(2)}) copy-start(f32[128]{0:T(128)S(1)} %get-tuple-element.279) | copy-start | bytes 1540
  249.9 4.0 copy-start.149
  250.0 206.5 %all-gather.13.cloned.1.call-start = ((), (), s32[]{:S(2)}) async-start(), calls=%async_computation.10 | async-start | bytes 3932160 | tf_op jit(solution)/shard_map/all_gather | solution.py:1734
  250.9 141.8 %copy-start.140 = (f32[1,4,4,128]{3,1,2,0:T(4,128)}, f32[1,4,4,128]{3,1,2,0:T(4,128)S(1)}, u32[]{:S(2)}) copy-start(f32[1,4,4,128]{3,1,2,0:T(4,128)S(1)} %copy.209) | copy-start | bytes 24580
  252.6 7.8 copy-start.53
  267.7 383.3 %reduce-scatter.8.cloned.1.call-start = ((), (), s32[]{:S(2)}) async-start(), calls=%async_computation.11 | async-start | bytes 3932160 | tf_op jit(solution)/shard_map/reduce_scatter | solution.py:1816
  387.1 5.5 copy-start.51
  396.7 4.2 copy-start.66
  396.7 4.2 copy-start.70
  396.7 4.2 copy-start.74
  396.7 4.2 copy-start.78
  396.9 4.5 copy-start.55
  446.6 138.8 %copy-start.14 = (bf16[2,4,288,256]{3,2,1,0:T(8,128)(2,1)}, bf16[2,4,288,256]{3,2,1,0:T(8,128)(2,1)S(1)}, u32[]{:S(2)}) copy-start(bf16[2,4,288,256]{3,2,1,0:T(8,128)(2,1)S(1)} %get-tuple-element.95) | copy-start | bytes 3538948
  582.6 180.0 %reduce-scatter.12.cloned.1.call-start = ((), (), s32[]{:S(2)}) async-start(), calls=%async_computation.13 | async-start | bytes 3932160 | tf_op jit(solution)/shard_map/reduce_scatter | solution.py:1816
  585.4 4.0 slice-start
  585.4 4.0 slice-start.1
  638.6 128.3 %reduce-scatter.10.cloned.1.call-start = ((), (), s32[]{:S(2)}) async-start(), calls=%async_computation.12 | async-start | bytes 3932160 | tf_op jit(solution)/shard_map/reduce_scatter | solution.py:1816
  639.4 266.4 %reduce-scatter.16.cloned.1.call-start = ((), (), s32[]{:S(2)}) async-start(), calls=%async_computation.15 | async-start | bytes 3932160 | tf_op jit(solution)/shard_map/reduce_scatter | solution.py:1816
  639.6 4.0 copy-start.58
  639.6 4.0 copy-start.61
  646.6 4.4 copy-start.106
  754.4 151.4 %reduce-scatter.14.cloned.1.call-start = ((), (), s32[]{:S(2)}) async-start(), calls=%async_computation.14 | async-start | bytes 3932160 | tf_op jit(solution)/shard_map/reduce_scatter | solution.py:1816
  755.0 259.2 %reduce-scatter.18.cloned.1.call-start = ((), (), s32[]{:S(2)}) async-start(), calls=%async_computation.16 | async-start | bytes 3932160 | tf_op jit(solution)/shard_map/reduce_scatter | solution.py:1820
  755.3 3.9 copy-start.141
  755.3 3.9 copy-start.145
  766.2 250.0 %reduce-scatter.20.cloned.1.call-start = ((), (), s32[]{:S(2)}) async-start(), calls=%async_computation.17 | async-start | bytes 3932160 | tf_op jit(solution)/shard_map/reduce_scatter | solution.py:1816
  766.9 5.8 copy-start.13
  776.8 4.9 copy-start.95
  776.8 4.9 copy-start.97
  785.5 4.2 copy-start.88
  785.5 4.4 copy-start.36
  789.8 87.6 %copy-start.153 = (bf16[3,192,2048]{2,1,0:T(8,128)(2,1)S(1)}, bf16[3,192,2048]{2,1,0:T(8,128)(2,1)}, u32[]{:S(2)}) copy-start(bf16[3,192,2048]{2,1,0:T(8,128)(2,1)} %get-tuple-element.135) | copy-start | bytes 7077892
  789.8 87.5 %copy-start.155 = (bf16[3,192,768]{2,1,0:T(8,128)(2,1)S(1)}, bf16[3,192,768]{2,1,0:T(8,128)(2,1)}, u32[]{:S(2)}) copy-start(bf16[3,192,768]{2,1,0:T(8,128)(2,1)} %get-tuple-element.133) | copy-start | bytes 2654212
  882.7 4.2 copy-start.43
  899.0 4.0 copy-start.39
  899.0 4.0 copy-start.105
  899.0 4.0 copy-start.109
  905.8 107.5 %copy-start.136 = (f32[1,2048]{1,0:T(1,128)S(1)}, f32[1,2048]{1,0:T(1,128)}, u32[]{:S(2)}) copy-start(f32[1,2048]{1,0:T(1,128)} %get-tuple-element.128) | copy-start | bytes 24580
  905.8 108.2 %copy-start.112 = (f32[1,4352]{1,0:T(1,128)S(1)}, f32[1,4352]{1,0:T(1,128)}, u32[]{:S(2)}) copy-start(f32[1,4352]{1,0:T(1,128)} %stack.36) | copy-start | bytes 52228
  1014.2 26.9 %copy-start.63 = (f32[4,128,768]{2,1,0:T(8,128)S(1)}, f32[4,128,768]{2,1,0:T(8,128)}, u32[]{:S(2)}) copy-start(f32[4,128,768]{2,1,0:T(8,128)} %get-tuple-element.132) | copy-start | bytes 4718596
  1014.2 26.9 %copy-start.81 = (bf16[512,768]{1,0:T(8,128)(2,1)S(1)}, bf16[512,768]{1,0:T(8,128)(2,1)}, u32[]{:S(2)}) copy-start(bf16[512,768]{1,0:T(8,128)(2,1)} %reduce-scatter.18.cloned.1.call-done) | copy-start | bytes 2359300
  (123 other events, 226.1 us)
Sparse Core Ops, SparseCore 0:
  55.6 44.3 all-gather.8
  102.4 43.9 all-gather.6
  148.6 105.1 all-gather.14
  256.0 69.2 all-gather.10
  327.0 56.7 all-gather.12
  582.7 58.9 reduce-scatter.7
  644.7 56.5 reduce-scatter.11
  704.8 53.6 reduce-scatter.9
  761.5 52.1 reduce-scatter.15
  816.5 47.0 reduce-scatter.13
  865.9 69.7 reduce-scatter.17
  939.2 45.7 reduce-scatter.19

commit v12 on v11

--- a/solution.py
+++ b/solution.py
@@ -182,7 +182,7 @@
         pass
 
 
-def fused(parts, axes, across, collective_id, cost_us, vmem=40):
+def fused(parts, axes, across, collective_id, cost_us, vmem):
     counts = [(len(part.ins), len(part.outs), len(part.scratch)) for part in parts]
 
     def kernel(*refs):
@@ -715,31 +715,38 @@
 
 
 class ScatterKV(Part):
-    def __init__(self, whole):
+    def __init__(self, whole, place_first=False, kept_as=F32):
+        self.place_first = place_first
         trees, size, rows, width = whole.shape
+        if place_first:
+            trees, size = size, trees
         self.trees, self.size = trees, size
         self.sides = [(0, 1, 3), (3, 2, 0)] if size == 4 else []
         self.ins = [(whole, VMEM)]
-        self.outs = [(jax.ShapeDtypeStruct((trees, rows, width), F32), VMEM)]
+        self.outs = [(jax.ShapeDtypeStruct((trees, rows, width), kept_as), VMEM)]
         self.scratch = [
+            pltpu.VMEM((rows, width), F32),
             pltpu.VMEM((size, trees, rows, width), BF16), pltpu.VMEM((trees, rows, width), BF16),
             SEM((size, trees)), SEM((size, trees)), SEM((trees,)), SEM((trees,)),
         ]
 
     def bind(self, ins, outs, scratch):
         (self.terms,), (self.out,) = ins, outs
-        self.boxes, self.joint, self.send, self.recv, self.join_send, self.join_recv = scratch
+        self.total, self.boxes, self.joint, self.send, self.recv, self.join_send, self.join_recv = scratch
         self.me = lax.axis_index("dp")
+
+    def term(self, tree, place):
+        return self.terms.at[place, tree] if self.place_first else self.terms.at[tree, place]
 
     def copy(self, place, slot, tree):
         return remote(
-            self.terms.at[tree, place], self.boxes.at[slot, tree], self.send.at[place, tree],
+            self.term(tree, place), self.boxes.at[slot, tree], self.send.at[place, tree],
             self.recv.at[slot, tree], {"dp": place},
         )
 
     def by_way(self, via, target, tree):
         return remote(
-            self.terms.at[tree, target], self.joint.at[tree], self.join_send.at[tree],
+            self.term(tree, target), self.joint.at[tree], self.join_send.at[tree],
             self.join_recv.at[tree], {"dp": via},
         )
 
@@ -781,17 +788,19 @@
                 @pl.when(self.me == via)
                 def _():
                     self.by_way(via, target, tree).wait_recv()
-                    both = self.joint[tree].astype(F32) + self.terms[tree, target].astype(F32)
+                    both = self.joint[tree].astype(F32) + self.term(tree, target)[...].astype(F32)
                     self.joint[tree] = both.astype(BF16)
                     self.joined(via, target, tree).start()
 
         for tree in range(self.trees):
-            self.out[tree] = self.terms[tree, self.me].astype(F32)
+            self.total[...] = self.term(tree, self.me)[...].astype(F32)
             for place in line_order(self.size):
                 @pl.when(self.expected(place))
                 def _():
                     self.copy(place, place, tree).wait_recv()
-                    self.out[tree] += self.boxes[place, tree].astype(F32)
+                    self.total[...] += self.boxes[place, tree].astype(F32)
+
+            self.out[tree] = self.total[...].astype(self.out.dtype)
 
     def finish(self):
         for tree in range(self.trees):
@@ -1181,13 +1190,16 @@
 
 
 class LastHub(Staged):
-    def __init__(self, terms, values, gain, add):
+    def __init__(self, terms, values, gain, add, other):
         rows, depth = values.shape
         half = depth // 2
         self.rows_in = RowScatterer("tensor", rows, half)
         self.rows_out = Gatherer("tensor", rows, half)
         super().__init__(
-            {"terms": (terms, VMEM), "values": (values, VMEM), "gain": (gain, VMEM), "add": (add, VMEM)},
+            {
+                "terms": (terms, VMEM), "values": (values, VMEM), "gain": (gain, VMEM),
+                "add": (add, VMEM), "other": (other, VMEM),
+            },
             {
                 "gain_grad": vmem_f32(1, depth),
                 "gathered": vmem_bf16(2, self.rows_out.size * rows, depth),
@@ -1214,13 +1226,18 @@
             self.rows_out.begin(chunk, result + self.add[at])
         self.rows_out.complete(self.gathered)
 
+        @pl.when(lax.axis_index("section") == 1)
+        def _():
+            self.gathered[...] = self.other[...]
+
 
 class RowsOut(Staged):
-    def __init__(self, own):
+    def __init__(self, own, other=None):
         rows, depth = own.shape
         self.rows_out = Gatherer("tensor", rows, depth // 2)
+        self.has_other = other is not None
         super().__init__(
-            {"own": (own, VMEM)},
+            {"own": (own, VMEM)} | ({"other": (other, VMEM)} if self.has_other else {}),
             {"gathered": vmem_bf16(2, self.rows_out.size * rows, depth)},
             {},
             [self.rows_out],
@@ -1232,6 +1249,10 @@
 
     def run(self):
         self.rows_out.complete(self.gathered)
+        if self.has_other:
+            @pl.when(lax.axis_index("section") == 0)
+            def _():
+                self.gathered[...] = self.other[...]
 
 
 class FeedForward(Staged):
@@ -1268,8 +1289,8 @@
         if forward and not backward:
             outs |= {
                 "out": vmem_bf16(2, tensor_rows, depth),
-                "gate": vmem_f32(chunks, chunk_rows, units),
-                "up": vmem_f32(chunks, chunk_rows, units),
+                "gate": vmem_bf16(chunks, chunk_rows, units),
+                "up": vmem_bf16(chunks, chunk_rows, units),
             }
             self.out_rows = Gatherer("tensor", rows, half)
             helpers += [self.out_rows]
@@ -1411,8 +1432,8 @@
             rows = self.mlp_in[chunk]
             gate = dot_inner(rows, self.w_gate[at, :])
             up = dot_inner(rows, self.w_up[at, :])
-            self.gate[chunk, :, at] = gate
-            self.up[chunk, :, at] = up
+            self.gate[chunk, :, at] = gate.astype(self.gate.dtype)
+            self.up[chunk, :, at] = up.astype(self.up.dtype)
             self.hidden[chunk, :, at] = (gate * jax.nn.sigmoid(gate) * up).astype(BF16)
 
         self.unit_tiles(tile)
@@ -1423,7 +1444,7 @@
     def backward_chunk(self, chunk):
         def tile(at):
             grad_hidden = dot_inner(self.grad_mlp[chunk], self.w_down[at, :])
-            gate, up = self.gate[chunk, :, at], self.up[chunk, :, at]
+            gate, up = self.gate[chunk, :, at].astype(F32), self.up[chunk, :, at].astype(F32)
             share = jax.nn.sigmoid(gate)
             act = gate * share
             self.grad_up[chunk, :, at] = (grad_hidden * act).astype(BF16)
@@ -1463,31 +1484,69 @@
             scatterer.over(chunk, place).start()
 
 
-def finish_units(first, second, core, tile=256):
+def finish_weights(first, second, attn_first, attn_second, arrived, widths, core, rows_out, tile=256):
     units, own_depth = first[0].shape
+    q_width, k_width, _, _ = widths
+    starts = [0, q_width, q_width + k_width, 0]
+    steps = units // tile
+    count = len(rows_out)
+
+    def transposed(block):
+        size = block.shape[1]
+        rows = lax.broadcasted_iota(jnp.int32, (size, size), 0)
+        identity = (rows == lax.broadcasted_iota(jnp.int32, rows.shape, 1)).astype(BF16)
+        return dot_inner(identity, block)
 
     def kernel(core_ref, *refs):
-        ins, (gate, up, down) = refs[:6], refs[6:]
-        rows = lax.broadcasted_iota(jnp.int32, (own_depth, own_depth), 0)
-        identity = (rows == lax.broadcasted_iota(jnp.int32, rows.shape, 1)).astype(BF16)
-        picked = [
-            jnp.where(core_ref[0] == 0, ins[i][...], ins[3 + i][...]) for i in range(3)
-        ]
-        gate[...] = dot_inner(identity, picked[0])
-        up[...] = dot_inner(identity, picked[1])
+        ins, passed_in = refs[:12], refs[12 : 12 + count]
+        (gate, up, down), attn_outs = refs[12 + count : 15 + count], refs[15 + count : 19 + count]
+        for src, dst in zip(passed_in, refs[19 + count :]):
+            dst[...] = src[...]
+
+        on_first = core_ref[0] == 0
+        picked = [jnp.where(on_first, ins[i][...], ins[3 + i][...]) for i in range(3)]
+        gate[...] = transposed(picked[0])
+        up[...] = transposed(picked[1])
         down[...] = picked[2].astype(F32)
+
+        @pl.when(pl.program_id(0) == 0)
+        def _():
+            for index, (out, start, width) in enumerate(zip(attn_outs, starts, widths)):
+                at = pl.ds(start, width)
+                mine, other, came = (ins[6 + 2 * i + index // 3][:, at] for i in range(3))
+                halves = [jnp.where(on_first, mine, came), jnp.where(on_first, came, other)]
+                for half, values in enumerate(halves):
+                    if index == 3:
+                        out[pl.ds(half * width, width)] = transposed(values)
+                    else:
+                        out[:, pl.ds(half * width, width)] = values.astype(F32)
+
+    def whole(shape):
+        return pl.BlockSpec(shape, lambda step: (0, 0))
 
     tall = pl.BlockSpec((tile, own_depth), lambda step: (step, 0))
     wide = pl.BlockSpec((own_depth, tile), lambda step: (0, step))
+    attn_ins = [*attn_first, *attn_second, *arrived]
+    flat_rows = [item.reshape(-1, item.shape[-1]) for item in rows_out]
+    passed = [
+        pl.BlockSpec((item.shape[0] // steps, item.shape[1]), lambda step: (step, 0))
+        for item in flat_rows
+    ]
+    attn_shapes = [(own_depth, 2 * width) for width in widths[:3]] + [(2 * q_width, own_depth)]
+    shapes = [(own_depth, units)] * 2 + [(units, own_depth)] + attn_shapes
     return pl.pallas_call(
         kernel,
-        grid=(units // tile,),
-        out_shape=[jax.ShapeDtypeStruct((own_depth, units), F32)] * 2
-        + [jax.ShapeDtypeStruct((units, own_depth), F32)],
-        in_specs=[pl.BlockSpec(memory_space=pltpu.SMEM)] + [tall] * 6,
-        out_specs=[wide, wide, tall],
+        grid=(steps,),
+        out_shape=[jax.ShapeDtypeStruct(shape, F32) for shape in shapes]
+        + [jax.ShapeDtypeStruct(item.shape, item.dtype) for item in flat_rows],
+        in_specs=[pl.BlockSpec(memory_space=pltpu.SMEM)]
+        + [tall] * 6
+        + [whole(item.shape) for item in attn_ins]
+        + passed,
+        out_specs=[wide, wide, tall] + [whole(shape) for shape in attn_shapes] + passed,
         cost_estimate=pl.CostEstimate(flops=0, bytes_accessed=25_000_000, transcendentals=0),
-    )(core.reshape(1), *first, *second)
+        compiler_params=pltpu.CompilerParams(vmem_limit_bytes=60 << 20),
+    )(core.reshape(1), *first, *second, *attn_ins, *flat_rows)
 
 
 def hub_plain(terms, own_args, body, own_outs, scatter, gathers):
@@ -1510,7 +1569,7 @@
     return [cell.value for cell in cells] + gathered
 
 
-def with_cargo(part, cargo, axes, collective_id, cost_us, vmem=40):
+def with_cargo(part, cargo, axes, collective_id, cost_us, vmem):
     outs = fused(cargo + [part], axes, bool(cargo), collective_id, cost_us, vmem)
     return outs[-1], outs[:-1]
 
@@ -1740,15 +1799,14 @@
         line = ["section", "dp"]
         everyone = ["section", "dp", "tensor"]
         (gate_rows, up_rows), (gains_all,) = fused(
-            [UnitsOut(unit_mats[:2], 0), SharedRows(gains_own.reshape(-1, 128))], line, True, 1, 45
+            [UnitsOut(unit_mats[:2], 0), SharedRows(gains_own.reshape(-1, 128))], line, True, 1, 45, 40
         )
         shards = AttnShards(w_query[0], w_key[0], w_value[0], w_out[0])
         shards.arrays[0] = tied(shards.arrays[0], gate_rows)
         (w_qkv, w_heads), (down_rows,), (attn_shard,) = fused(
-            [AttnOut(shards, 0), UnitsOut(unit_mats[2:], 0), HalfOver(shards)], line, True, 2, 80
+            [AttnOut(shards, 0), UnitsOut(unit_mats[2:], 0), HalfOver(shards)], line, True, 2, 80, 40
         )
         first_weights = [w_qkv, w_heads, spread_units(gate_rows), spread_units(up_rows)]
-        attn_next = lax.all_gather(attn_shard, "dp", axis=0)
     else:
         gains_all = lax.all_gather(gains_own, ("section", "dp"))
         attn_halves = jnp.stack(
@@ -1826,13 +1884,13 @@
             return [UnitsOut([unit_mats[i] for i in which], 1)]
 
         def kv_gather(own, cargo, collective_id, carried):
-            (whole,), outs = with_cargo(GatherKV(own), cargo, everyone, collective_id, 40)
+            (whole,), outs = with_cargo(GatherKV(own), cargo, everyone, collective_id, 40, 40)
             carried += outs
             return whole.reshape(trees, -1, 2 * HD)
 
         def kv_scatter(whole, cargo, collective_id, carried):
             part = ScatterKV(whole.reshape(trees, dp_size, row_count, 2 * HD))
-            (total,), outs = with_cargo(part, cargo, everyone, collective_id, 30)
+            (total,), outs = with_cargo(part, cargo, everyone, collective_id, 30, 40)
             carried += outs
             return total
 
@@ -1849,16 +1907,17 @@
         terms, saved_first = attn_forward(
             hidden, first_weights, gains[0], slot,
             lambda own: kv_gather(
-                tied(own, *first_weights[2:]), [UnitsSpread(down_rows)] + units_on(0, 1), 3, carried
+                tied(own, *first_weights[2:]), [UnitsSpread(down_rows)] + units_on(0, 1, 2), 3, carried
             ),
         )
-        (down_all,), (gate_rows, up_rows) = carried
+        (down_all,), (gate_rows, up_rows, down_rows) = carried
         first_weights.append(down_all)
         part = FeedForward(
             terms, own_in, gains[0][1][None], first_weights[2:], True, False, {}
         )
-        outs, ((down_rows,),) = with_cargo(part, units_on(2), everyone, 4, 90, 56)
+        outs, ((down_next,),) = with_cargo(part, [UnitsSpread(down_rows)], everyone, 4, 90, 56)
         middle_first, mlp_in_first, hidden_first, own_next, output_first, gate_first, up_first = outs
+        attn_next = lax.all_gather(tied(attn_shard, gate_rows), "dp", axis=0)
         second_weights = [
             attn_next[:, :own_depth].reshape(depth, -1),
             attn_next[:, own_depth:].transpose(1, 0, 2).reshape(q_width, depth),
@@ -1867,12 +1926,9 @@
         carried = []
         terms, saved_second = attn_forward(
             output_first, second_weights, gains[1], slot,
-            lambda own: kv_gather(
-                tied(own, second_weights[2]), [UnitsSpread(down_rows)], 5, carried
-            ),
-        )
-        ((down_all,),) = carried
-        second_weights.append(down_all)
+            lambda own: kv_gather(tied(own, second_weights[2]), [], 5, carried),
+        )
+        second_weights.append(down_next)
         part = FeedForward(
             terms, own_next, gains[1][1][None], second_weights[2:], True, True,
             {"grad_own": grad_own},
@@ -1888,15 +1944,15 @@
         terms, pairs, head_second = attn_backward(
             grad_attn, saved_second, second_weights, gains[1], slot,
             lambda whole: kv_scatter(
-                tied(whole, *products), [RowsOut(own_second)], 7, carried
+                tied(whole, *products), [RowsOut(own_second, output_first)], 7, carried
             ),
         )
-        ((output_second,),) = carried
+        ((layer_out,),) = carried
         unit_second += scatter_units(
-            weight_products([(tied(flat(hidden_bf), output_second), flat(grad_mlp))])
+            weight_products([(tied(flat(hidden_bf), layer_out), flat(grad_mlp))])
         )
         pairs = weight_products(pairs)
-        attn_second = scatter_shards([tied(pairs[0], unit_second[2]), pairs[1]])
+        attn_second = scatter_shards([tied(pairs[0], unit_second[1]), pairs[1]])
         terms = tied(terms, unit_second[0])
         part = FeedForward(
             terms, own_next, gains[1][0][None], first_weights[2:], False, True,
@@ -1926,16 +1982,16 @@
         unit_first += scatter_units(
             weight_products([(tied(flat(hidden_first), incoming_second), flat(grad_mlp))])
         )
-        whole = jnp.concatenate(weight_products(pairs), axis=1).reshape(dp_size, 4, -1, q_width + qkv_width)
-        part = LastHub(terms, own_in, gains[0][0][None], grad_middle)
-        (attn_gain_first, incoming_first), ((attn_first,), home_first) = with_cargo(
-            part, [ScatterKV(whole.transpose(1, 0, 2, 3)), UnitsHome(unit_first[:2], 0)], everyone,
-            10, 60, 56,
-        )
-        attn_first = attn_first.reshape(own_depth, -1).astype(BF16)
-        outputs = [output_first, output_second]
-        grads = [incoming_first, incoming_second]
-        weight_grads = [(attn_first, None), (attn_second, None)]
+        parts = [
+            ScatterKV(item.reshape(dp_size, 4, own_depth // 4, -1), True, BF16)
+            for item in weight_products(pairs)
+        ]
+        part = LastHub(terms, own_in, gains[0][0][None], grad_middle, incoming_second)
+        (attn_gain_first, input_grad), (*attn_first, home_first) = with_cargo(
+            part, parts + [UnitsHome(unit_first[:2], 0)], everyone, 10, 60, 56
+        )
+        attn_first = [item.reshape(own_depth, -1) for (item,) in attn_first]
+        attn_second = [attn_second[:, :qkv_width], attn_second[:, qkv_width:]]
         gain_grads = [
             jnp.concatenate([attn_gain_first[0], mlp_gain_first[0], *head_first]),
             jnp.concatenate([attn_gain_second[0], mlp_gain_second[0], *head_second]),
@@ -1944,6 +2000,8 @@
         outputs, grads, products, gain_grads = plain_layers(
             hidden, own_in, grad_own, both_weights, gains, slot, shared_kv
         )
+        layer_out = jnp.where(core == 0, *outputs)
+        input_grad = jnp.where(core == 0, *grads)
         weight_grads = []
         for pairs in products:
             whole = weight_products(pairs)
@@ -1951,14 +2009,21 @@
 
     gain_total = jnp.stack(gain_grads)
     if fast:
-        mine = jnp.where(core == 0, weight_grads[0][0], weight_grads[1][0])
-        other = jnp.where(core == 0, weight_grads[1][0], weight_grads[0][0])
-        (gain_total,), (arrived,), down_home = fused(
-            [TotalOverAll(gain_total.reshape(-1, 128)), Swap(other), UnitsHome(unit_first[2:], 0)],
-            everyone, True, 11, 60,
-        )
-        attn_home = (jnp.where(core == 0, mine, arrived), jnp.where(core == 0, arrived, mine))
-        grad_gate, grad_up, grad_down = finish_units(home_first + down_home, home_second, core)
+        others = [
+            Swap(jnp.where(core == 0, second, first))
+            for first, second in zip(attn_first, attn_second)
+        ]
+        (gain_total,), *arrived, down_home = fused(
+            [TotalOverAll(gain_total.reshape(-1, 128)), *others, UnitsHome(unit_first[2:], 0)],
+            everyone, True, 11, 60, 40,
+        )
+        grad_gate, grad_up, grad_down, *attn_grads, layer_out, input_grad = finish_weights(
+            home_first + down_home, home_second, attn_first, attn_second,
+            [item for (item,) in arrived], (q_width, k_width, k_width, q_width), core,
+            (layer_out, input_grad),
+        )
+        layer_out = layer_out.reshape(trees, row_count, depth)
+        input_grad = input_grad.reshape(trees, row_count, depth)
         gain_total = gain_total.reshape(2, -1)
     else:
         def bring_home(first, second):
@@ -1977,11 +2042,16 @@
         grad_gate, grad_up, grad_down = unit_home[0].T, unit_home[1].T, unit_home[2]
         gain_total = lax.psum(gain_total, ("section", "dp", "tensor"))
 
-    def joined(start, width):
-        parts = [half[:, start : start + width] for half in attn_home]
-        if shared_kv and start in (q_width, q_width + k_width):
-            return parts[0].astype(F32)
-        return jnp.concatenate(parts, axis=1).astype(F32)
+        def joined(start, width):
+            parts = [half[:, start : start + width] for half in attn_home]
+            if shared_kv and start in (q_width, q_width + k_width):
+                return parts[0].astype(F32)
+            return jnp.concatenate(parts, axis=1).astype(F32)
+
+        attn_grads = [
+            joined(0, q_width), joined(q_width, k_width), joined(q_width + k_width, k_width),
+            joined(qkv_width, q_width).T,
+        ]
 
     gain_own = pick(gain_total, core)
     share_width = attn_gain.shape[1]
@@ -1990,13 +2060,10 @@
         gain_own, depth + data_index * share_width, share_width, 0
     )
     return (
-        jnp.where(core == 0, outputs[0], outputs[1])[None],
-        jnp.where(core == 0, grads[0], grads[1])[None],
+        layer_out[None],
+        input_grad[None],
         attn_gain_grad[None],
-        joined(0, q_width)[None],
-        joined(q_width, k_width)[None],
-        joined(q_width + k_width, k_width)[None],
-        joined(qkv_width, q_width).T[None],
+        *(item[None] for item in attn_grads),
         gain_own[2 * depth : 2 * depth + HD][None],
         gain_own[2 * depth + HD :][None],
         mlp_gain_grad[None],

time: 1080 us -> 1040 us (0.963)
  Pallas kernels: 823 us -> 797 us
    pallas_call x11, Pallas kernels: 813 us -> 782 us  [fused(): pl.pallas_call(kernel, out_shape=[item[0] for item in outs], in_specs=[it...]
    unnamed x331 -> x312, local copies, waits for them, and re-layouts: 54.8 us -> 54.2 us
  transfers between devices with their start and end apart: 12 -> 12, of which waited for: 0 -> 1; matrix products, arithmetic and copies ran while one was open for 15% -> 15% of each run, Pallas kernels for 59% -> 51%
where the time goes in v12:
time: 1040 us
  Pallas kernels  797 us (77%)
  matrix products  95.2 us (9%)
  local copies, waits for them, and re-layouts  75.5 us (7%)
  other arithmetic  43.3 us (4%)
  between operations  20.5 us (2%)
    pallas_call x11, Pallas kernels, fused(): pl.pallas_call(kernel, out_shape=[item[0] for item in outs], in_specs=[it...  782 us
    unnamed x312, local copies, waits for them, and re-layouts  54.2 us
    dot_general x10, matrix products, dot_outer(): return lax.dot_general(left, right, OUTER, preferred_element_type=F32)  45.7 us
  transfers between devices with their start and end apart: 12, of which 1 were waited for; matrix products, arithmetic and copies ran while one was open for 15% of the time, Pallas kernels for 51%

profile of v12, /device:TPU:0, one launch (start us, length us, event | category | flops | bytes accessed | tf_op | source)
XLA Modules:
  0.0 1035.8 jit_solution(11701785533510096761)
XLA Ops:
  8.6 1.7 copy.150
  10.4 1.7 copy.151
  12.2 41.5 %shard_map.255 = (bf16[192,2048]{1,0:T(8,128)(2,1)S(1)}, bf16[192,2048]{1,0:T(8,128)(2,1)S(1)}, f32[2,4,10,128]{3,2,1,0:T(8,128)S(1)}) custom-call(bf16[1536,512]{1,0:T(8,128)(2,1)S(1)} %bitcast.295, bf16[1536,512]{1,0:T(8,128)(2,1)S(1)} %bitcast.297, f32[10,128]{1,0:T(8,128)S(1)} %fusion.112.refs_2_), custom_call_target="tpu_custom_call" | custom-call | bytes 135000000 | tf_op jit(solution)/shard_map/pallas_call | solution.py:210
  66.2 68.4 %shard_map.256 = (bf16[2048,512]{1,0:T(8,128)(2,1)S(1)}, bf16[256,2048]{1,0:T(8,128)(2,1)S(1)}, bf16[192,2048]{1,0:T(8,128)(2,1)S(1)}, bf16[768,512]{1,0:T(8,128)(2,1)S(1)}) custom-call(bf16[512,512]{1,0:T(8,128)(2,1)S(1)} %bitcast.307, bf16[512,256]{1,0:T(8,128)(2,1)S(1)} %bitcast.315, bf16[512,256]{1,0:T(8,128)(2,1)S(1)} %bitcast.317, ...), custom_call_target="tpu_custom_call" | custom-call | bytes 240000000 | tf_op jit(solution)/shard_map/pallas_call | solution.py:210
  149.0 65.5 %shard_map.257 = (bf16[768,2048]{1,0:T(8,128)(2,1)S(1)}, bf16[192,2048]{1,0:T(8,128)(2,1)S(1)}, bf16[192,2048]{1,0:T(8,128)(2,1)}, bf16[192,2048]{1,0:T(8,128)(2,1)S(1)}, bf16[2,4,288,256]{3,2,1,0:T(8,128)(2,1)S(1)}) custom-call(bf16[192,2048]{1,0:T(8,128)(2,1)S(1)} %copy-done.34, bf16[1536,512]{1,0:T(8,128)(2,1)S(1)} %bitcast.296, ...), custom_call_target="tpu_custom_call" | custom-call | bytes 120000000 | tf_op jit(solution)/shard_map/pallas_call | solution.py:210
  227.7 1.9 bitcast_convert_fusion.2.refs_6_
  237.1 2.2 convolution_convert_fusion.9
  239.3 123.7 %shard_map.258 = (bf16[768,2048]{1,0:T(8,128)(2,1)}, f32[72,2048]{1,0:T(8,128)}, bf16[3,192,2048]{2,1,0:T(8,128)(2,1)}, bf16[3,192,768]{2,1,0:T(8,128)(2,1)}, f3...) custom-call(bf16[192,2048]{1,0:T(8,128)(2,1)} %copy-done.24, ...), custom_call_target="tpu_custom_call" | custom-call | bytes 270000000 | tf_op jit(solution)/shard_map/pallas_call | solution.py:210
  363.1 2.2 fusion.9
  366.6 3.2 slice.164
  371.2 3.1 fusion.39
  377.5 29.1 %shard_map.259 = bf16[2,4,288,256]{3,2,1,0:T(8,128)(2,1)S(1)} custom-call(bf16[2,288,256]{2,1,0:T(8,128)(2,1)S(1)} %copy-done.16), custom_call_target="tpu_custom_call" | custom-call | bytes 120000000 | tf_op jit(solution)/shard_map/pallas_call | solution.py:210
  406.6 2.2 fusion.144
  408.8 2.2 reshape.533
  411.0 2.5 multiply_reduce_fusion.2
  424.7 2.2 convolution_convert_fusion.8
  426.9 120.1 %shard_map.260 = (f32[72,2048]{1,0:T(8,128)}, bf16[3,192,2048]{2,1,0:T(8,128)(2,1)}, bf16[3,192,768]{2,1,0:T(8,128)(2,1)}, f32[72,2048]{1,0:T(8,128)}, bf16[3,19...) custom-call(bf16[2,288,2048]{2,1,0:T(8,128)(2,1)} %bitcast.322, ...), custom_call_target="tpu_custom_call" | custom-call | bytes 300000000 | tf_op jit(solution)/shard_map/pallas_call | solution.py:210
  547.0 6.3 convolution_convert_fusion.5
  553.3 6.3 convolution_convert_fusion.4
  559.9 3.7 convolution_convert_fusion.13
  563.6 1.7 reshape.537
  566.2 4.6 fusion.3
  576.7 2.4 copy.164
  581.5 29.9 %shard_map.261 = (bf16[2,288,2048]{2,1,0:T(8,128)(2,1)S(1)}, f32[2,288,256]{2,1,0:T(8,128)S(1)}) custom-call(f32[72,2048]{1,0:T(8,128)S(1)} %copy-done.36, bf16[2,288,2048]{2,1,0:T(8,128)(2,1)S(1)} %copy-done.1, bf16[2,4,288,256]{3,2,1,0:T(8,128)(2,1)S(1)} %bitcast.305), custom_call_target="tpu_custom_call" | custom-call | bytes 90000000 | tf_op jit(solution)/shard_map/pallas_call | solution.py:210
  613.7 4.1 convolution_convert_fusion.3
  619.8 2.6 fusion.46
  627.5 2.8 convolution_convert_fusion.7
  630.3 82.1 %shard_map.262 = (bf16[3,192,768]{2,1,0:T(8,128)(2,1)}, bf16[3,192,768]{2,1,0:T(8,128)(2,1)}, f32[72,2048]{1,0:T(8,128)}, f32[1,2048]{1,0:T(1,128)}, bf16[2,288,...) custom-call(bf16[2,288,2048]{2,1,0:T(8,128)(2,1)} %bitcast.331, ...), custom_call_target="tpu_custom_call" | custom-call | bytes 270000000 | tf_op jit(solution)/shard_map/pallas_call | solution.py:210
  712.4 6.3 convolution_convert_fusion.2
  718.6 6.3 convolution_convert_fusion.1
  725.9 3.7 convolution_convert_fusion.10
  729.7 3.3 bitcast_convert_fusion
  733.0 3.8 pad_maximum_fusion
  738.1 2.6 convolution_convert_fusion.12
  740.7 4.0 fusion
  744.7 3.3 fusion.2
  750.7 4.1 fusion.27
  756.4 78.2 %shard_map.263 = (bf16[1536,512]{1,0:T(8,128)(2,1)S(1)}, bf16[1536,512]{1,0:T(8,128)(2,1)S(1)}, bf16[1536,512]{1,0:T(8,128)(2,1)S(1)}, bf16[2,288,2048]{2,1,0:T(8,128)(2,1)S(1)}, f32[2,288,256]{2,1,0:T(8,128)S(1)}) custom-call(bf16[192,2048]{1,0:T(8,128)(2,1)S(1)} %copy-done.30, bf16[192,2048]{1,0:T(8,128)(2,1)S(1)} %copy-done.31, ...), custom_call_target="tpu_custom_call" | custom-call | bytes 90000000 | tf_op jit(solution)/shard_map/pallas_call | solution.py:210
  839.6 4.1 convolution_convert_fusion
  845.0 2.6 fusion.45
  852.1 2.1 convolution_convert_fusion.11
  854.2 2.8 convolution_convert_fusion.6
  857.0 3.4 bitcast_convert_fusion.1
  860.4 119.6 %shard_map.264 = (bf16[4,128,512]{2,1,0:T(8,128)(2,1)}, bf16[4,128,256]{2,1,0:T(8,128)(2,1)}, bf16[1536,512]{1,0:T(8,128)(2,1)}, bf16[1536,512]{1,0:T(8,128)(2,1...) custom-call(bf16[4,4,128,512]{3,2,1,0:T(8,128)(2,1)} %bitcast.337, bf16[4,4,128,256]{3,2,1,0:T(8,128)(2,1)} %bitcast.343, ...), custom_call_target="tpu_custom_call" | custom-call | bytes 180000000 | tf_op jit(solution)/shard_map/pallas_call | solution.py:210
  980.8 1.8 fusion.146
  982.6 2.1 fusion.147
  985.9 23.8 %shard_map.265 = (f32[68,128]{1,0:T(8,128)S(1)}, bf16[512,512]{1,0:T(8,128)(2,1)S(1)}, bf16[512,256]{1,0:T(8,128)(2,1)S(1)}, bf16[1536,512]{1,0:T(8,128)(2,1)S(1)}) custom-call(f32[68,128]{1,0:T(8,128)S(1)} %reshape.554.refs_0_, bf16[512,512]{1,0:T(8,128)(2,1)S(1)} %get-tuple-element.200.refs_1_, bf16[512,256]{1,0:T(8,128)(2,1)S(1)} %get-tuple-element.198.refs_2_, ...), custom_call_target="tpu_custom_call" | custom-call | bytes 180000000 | tf_op jit(solution)/shard_map/pallas_call | solution.py:210
  1013.7 14.7 %shard_map.266 = (f32[512,1536]{1,0:T(8,128)}, f32[512,1536]{1,0:T(8,128)}, f32[1536,512]{1,0:T(8,128)}, f32[512,512]{1,0:T(8,128)}, f32[512,256]{1,0:T(8,128)},...) custom-call(s32[1]{0:T(128)} %bitcast.core_ref, ...), custom_call_target="tpu_custom_call" | custom-call | bytes 25000000 | tf_op jit(solution)/shard_map/pallas_call | solution.py:1537
  (450 shorter events, 103.0 us)
Async XLA Ops:
  7.2 138.5 %all-gather.9.cloned.1.call-start = ((), (), s32[]{:S(2)}) async-start(), calls=%async_computation.8 | async-start | bytes 3932160 | tf_op jit(solution)/shard_map/all_gather | solution.py:1793
  12.1 44.2 %copy-start.139 = (s32[2]{0:T(128)S(1)}, s32[2]{0:T(128)}, u32[]{:S(2)}) copy-start(s32[2]{0:T(128)} %param.20) | copy-start | bytes 28
  12.2 49.3 %copy-start.17 = (bf16[1,512,256]{2,1,0:T(8,128)(2,1)S(1)}, bf16[1,512,256]{2,1,0:T(8,128)(2,1)}, u32[]{:S(2)}) copy-start(bf16[1,512,256]{2,1,0:T(8,128)(2,1)} %param.23) | copy-start | bytes 786436
  55.5 90.9 %all-gather.7.cloned.1.call-start = ((), (), s32[]{:S(2)}) async-start(), calls=%async_computation.7 | async-start | bytes 3932160 | tf_op jit(solution)/shard_map/all_gather | solution.py:1793
  56.3 309.0 %all-gather.15.cloned.1.call-start = ((), (), s32[]{:S(2)}) async-start(), calls=%async_computation.18 | async-start | bytes 3932160 | tf_op jit(solution)/shard_map/all_gather | solution.py:1920
  60.1 76.5 %copy-start.129 = (f32[1,4,4,128]{3,1,2,0:T(4,128)}, f32[1,4,4,128]{3,1,2,0:T(4,128)S(1)}, u32[]{:S(2)}) copy-start(f32[1,4,4,128]{3,1,2,0:T(4,128)S(1)} %copy.190) | copy-start | bytes 24580
  66.2 68.4 %copy-start.78 = (bf16[2,288,2048]{2,1,0:T(8,128)(2,1)S(1)}, bf16[2,288,2048]{2,1,0:T(8,128)(2,1)}, u32[]{:S(2)}) copy-start(bf16[2,288,2048]{2,1,0:T(8,128)(2,1)} %param.16) | copy-start | bytes 7077892
  139.9 5.6 copy-start.94
  142.2 87.4 %copy-start.123 = (f32[128]{0:T(128)}, f32[128]{0:T(128)S(1)}, u32[]{:S(2)}) copy-start(f32[128]{0:T(128)S(1)} %get-tuple-element.211) | copy-start | bytes 1540
  142.2 232.3 %copy-start.121 = (f32[128]{0:T(128)}, f32[128]{0:T(128)S(1)}, u32[]{:S(2)}) copy-start(f32[128]{0:T(128)S(1)} %get-tuple-element.210) | copy-start | bytes 1540
  218.9 4.8 copy-start.140
  218.9 157.6 %all-gather.11.cloned.1.call-start = ((), (), s32[]{:S(2)}) async-start(), calls=%async_computation.9 | async-start | bytes 3932160 | tf_op jit(solution)/shard_map/all_gather | solution.py:1793
  219.5 207.4 %all-gather.13.cloned.1.call-start = ((), (), s32[]{:S(2)}) async-start(), calls=%async_computation.10 | async-start | bytes 3932160 | tf_op jit(solution)/shard_map/all_gather | solution.py:1793
  220.7 150.4 %copy-start.131 = (f32[1,4,4,128]{3,1,2,0:T(4,128)}, f32[1,4,4,128]{3,1,2,0:T(4,128)S(1)}, u32[]{:S(2)}) copy-start(f32[1,4,4,128]{3,1,2,0:T(4,128)S(1)} %copy.193) | copy-start | bytes 24580
  222.5 7.1 copy-start.51
  223.7 4.0 copy-start.100
  237.1 393.3 %reduce-scatter.8.cloned.1.call-start = ((), (), s32[]{:S(2)}) async-start(), calls=%async_computation.11 | async-start | bytes 3932160 | tf_op jit(solution)/shard_map/reduce_scatter | solution.py:1874
  365.3 5.9 copy-start.135
  366.6 4.5 copy-start.1
  371.1 4.3 copy-start.62
  371.1 4.3 copy-start.65
  371.2 4.3 copy-start.68
  371.2 4.3 copy-start.71
  415.2 3.4 copy-start.93
  553.2 179.8 %reduce-scatter.10.cloned.1.call-start = ((), (), s32[]{:S(2)}) async-start(), calls=%async_computation.12 | async-start | bytes 3932160 | tf_op jit(solution)/shard_map/reduce_scatter | solution.py:1874
  559.6 178.0 %reduce-scatter.12.cloned.1.call-start = ((), (), s32[]{:S(2)}) async-start(), calls=%async_computation.13 | async-start | bytes 3932160 | tf_op jit(solution)/shard_map/reduce_scatter | solution.py:1874
  565.3 5.5 slice-start
  566.2 4.6 slice-start.1
  581.5 32.2 %copy-start.145 = (bf16[3,192,2048]{2,1,0:T(8,128)(2,1)S(1)}, bf16[3,192,2048]{2,1,0:T(8,128)(2,1)}, u32[]{:S(2)}) copy-start(bf16[3,192,2048]{2,1,0:T(8,128)(2,1)} %get-tuple-element.124) | copy-start | bytes 7077892
  581.5 32.2 %copy-start.147 = (bf16[3,192,768]{2,1,0:T(8,128)(2,1)S(1)}, bf16[3,192,768]{2,1,0:T(8,128)(2,1)}, u32[]{:S(2)}) copy-start(bf16[3,192,768]{2,1,0:T(8,128)(2,1)} %get-tuple-element.121) | copy-start | bytes 2654212
  617.9 242.5 %reduce-scatter.16.cloned.1.call-start = ((), (), s32[]{:S(2)}) async-start(), calls=%async_computation.15 | async-start | bytes 3932160 | tf_op jit(solution)/shard_map/reduce_scatter | solution.py:1874
  618.4 4.0 copy-start.55
  618.4 4.0 copy-start.58
  724.9 135.5 %reduce-scatter.14.cloned.1.call-start = ((), (), s32[]{:S(2)}) async-start(), calls=%async_computation.14 | async-start | bytes 3932160 | tf_op jit(solution)/shard_map/reduce_scatter | solution.py:1874
  725.5 255.3 %reduce-scatter.18.cloned.1.call-start = ((), (), s32[]{:S(2)}) async-start(), calls=%async_computation.16 | async-start | bytes 3932160 | tf_op jit(solution)/shard_map/reduce_scatter | solution.py:1878
  725.9 3.8 copy-start.97
  725.9 3.8 copy-start.99
  725.9 3.8 copy-start.132
  725.9 3.8 copy-start.136
  736.8 247.9 %reduce-scatter.20.cloned.1.call-start = ((), (), s32[]{:S(2)}) async-start(), calls=%async_computation.17 | async-start | bytes 3932160 | tf_op jit(solution)/shard_map/reduce_scatter | solution.py:1874
  744.7 4.9 copy-start.85
  744.7 4.9 copy-start.87
  750.7 4.3 copy-start.35
  755.0 84.6 %copy-start.144 = (bf16[3,192,2048]{2,1,0:T(8,128)(2,1)S(1)}, bf16[3,192,2048]{2,1,0:T(8,128)(2,1)}, u32[]{:S(2)}) copy-start(bf16[3,192,2048]{2,1,0:T(8,128)(2,1)} %get-tuple-element.145) | copy-start | bytes 7077892
  755.0 84.6 %copy-start.146 = (bf16[3,192,768]{2,1,0:T(8,128)(2,1)S(1)}, bf16[3,192,768]{2,1,0:T(8,128)(2,1)}, u32[]{:S(2)}) copy-start(bf16[3,192,768]{2,1,0:T(8,128)(2,1)} %get-tuple-element.143) | copy-start | bytes 2654212
  843.7 3.9 copy-start.56
  843.7 3.9 copy-start.59
  860.4 119.6 %copy-start.127 = (f32[1,2048]{1,0:T(1,128)S(1)}, f32[1,2048]{1,0:T(1,128)}, u32[]{:S(2)}) copy-start(f32[1,2048]{1,0:T(1,128)} %get-tuple-element.137) | copy-start | bytes 24580
  (114 other events, 179.6 us)
Sparse Core Ops, SparseCore 0:
  55.6 44.3 all-gather.8
  102.4 43.9 all-gather.6
  219.1 77.2 all-gather.14
  298.7 51.0 all-gather.10
  351.4 44.0 all-gather.12
  553.4 57.3 reduce-scatter.7
  614.3 47.7 reduce-scatter.9
  665.1 50.9 reduce-scatter.11
  725.0 56.4 reduce-scatter.15
  784.9 44.6 reduce-scatter.13
  832.5 81.3 reduce-scatter.17
  916.7 46.8 reduce-scatter.19

commit v13 on v12

--- a/solution.py
+++ b/solution.py
@@ -178,6 +178,12 @@
     def run(self):
         pass
 
+    def pass_on(self):
+        pass
+
+    def late(self):
+        pass
+
     def finish(self):
         pass
 
@@ -202,6 +208,10 @@
             part.start()
         for part in reversed(parts):
             part.run()
+        for part in reversed(parts):
+            part.pass_on()
+        for part in reversed(parts):
+            part.late()
         for part in parts:
             part.finish()
 
@@ -440,12 +450,12 @@
                 self.copy(other, place, core, me).wait_send()
 
 
-def far_pair(place, me):
-    return (place + me == 3) & ((place == 0) | (place == 3))
+def passed_on(place, me):
+    return ((place == 3) & (me <= 1)) | ((place == 0) & (me >= 2))
 
 
 def line_relays(size):
-    return [(2, 0, 3), (1, 3, 0)] if size == 4 else []
+    return [(2, 1, 3, 0), (2, 0, 3, 1), (1, 2, 0, 0), (1, 3, 0, 1)] if size == 4 else []
 
 
 def line_order(size):
@@ -501,7 +511,7 @@
         ]
         self.scratch = [
             SEM((self.count,)), SEM((2, self.size, self.count)), SEM((self.size, self.count)),
-            SEM((self.count,)),
+            SEM((self.count, 2)),
         ]
 
     def bind(self, ins, outs, scratch):
@@ -520,10 +530,11 @@
             {"section": core, "dp": place},
         )
 
-    def relay(self, source, target, index):
+    def relay(self, source, target, turn, index):
         block = self.lands(index, source)
         return remote(
-            block, block, self.relay_send.at[index], self.recv.at[source, index], {"dp": target}
+            block, block, self.relay_send.at[index, turn], self.recv.at[source, index],
+            {"dp": target},
         )
 
     def local(self, index):
@@ -538,7 +549,7 @@
                 for place in range(self.size):
                     sent = (place != self.me) | (core != self.layer)
                     if self.size == 4:
-                        sent = sent & jnp.logical_not(far_pair(place, self.me))
+                        sent = sent & jnp.logical_not(passed_on(place, self.me))
                     yield core, place, index, sent
 
     def start(self):
@@ -559,11 +570,11 @@
                 def _():
                     self.copy(0, 0, place, index).wait_recv()
 
-                for via, source, target in line_relays(self.size):
+                for via, source, target, turn in line_relays(self.size):
                     if source == place:
                         @pl.when(self.me == via)
                         def _():
-                            self.relay(source, target, index).start()
+                            self.relay(source, target, turn, index).start()
 
     def finish(self):
         @pl.when(self.core == self.layer)
@@ -576,11 +587,11 @@
             for index in range(self.count):
                 self.local(index).wait()
 
-        for via, source, target in line_relays(self.size):
+        for via, source, target, turn in line_relays(self.size):
             @pl.when(self.me == via)
             def _():
                 for index in range(self.count):
-                    self.relay(source, target, index).wait_send()
+                    self.relay(source, target, turn, index).wait_send()
 
 
 class HalfOver(Part):
@@ -653,7 +664,7 @@
         self.trees, self.size = trees, lax.axis_size("dp")
         self.ins = [(own, VMEM)]
         self.outs = [(jax.ShapeDtypeStruct((trees, self.size, rows, width), BF16), VMEM)]
-        self.scratch = [SEM((self.size, trees)), SEM((self.size, trees)), SEM((trees,))]
+        self.scratch = [SEM((self.size, trees)), SEM((self.size, trees)), SEM((trees, 2))]
 
     def bind(self, ins, outs, scratch):
         (self.own,), (self.out,) = ins, outs
@@ -666,9 +677,9 @@
             self.recv.at[slot, tree], {"dp": place},
         )
 
-    def relay(self, source, target, tree):
+    def relay(self, source, target, turn, tree):
         return remote(
-            self.out.at[tree, source], self.out.at[tree, source], self.relay_send.at[tree],
+            self.out.at[tree, source], self.out.at[tree, source], self.relay_send.at[tree, turn],
             self.recv.at[source, tree], {"dp": target},
         )
 
@@ -677,7 +688,7 @@
             for place in range(self.size):
                 sent = place != self.me
                 if self.size == 4:
-                    sent = sent & jnp.logical_not(far_pair(place, self.me))
+                    sent = sent & jnp.logical_not(passed_on(place, self.me))
                 yield place, tree, sent
 
     def start(self):
@@ -695,11 +706,11 @@
                 def _():
                     self.copy(place, place, tree).wait_recv()
 
-                for via, source, target in line_relays(self.size):
+                for via, source, target, turn in line_relays(self.size):
                     if source == place:
                         @pl.when(self.me == via)
                         def _():
-                            self.relay(source, target, tree).start()
+                            self.relay(source, target, turn, tree).start()
 
     def finish(self):
         for place, tree, sent in self.targets():
@@ -707,27 +718,30 @@
             def _():
                 self.copy(place, self.me, tree).wait_send()
 
-        for via, source, target in line_relays(self.size):
+        for via, source, target, turn in line_relays(self.size):
             @pl.when(self.me == via)
             def _():
                 for tree in range(self.trees):
-                    self.relay(source, target, tree).wait_send()
+                    self.relay(source, target, turn, tree).wait_send()
 
 
 class ScatterKV(Part):
-    def __init__(self, whole, place_first=False, kept_as=F32):
+    def __init__(self, whole, place_first=False, kept_as=F32, far_only=False):
         self.place_first = place_first
         trees, size, rows, width = whole.shape
         if place_first:
             trees, size = size, trees
         self.trees, self.size = trees, size
-        self.sides = [(0, 1, 3), (3, 2, 0)] if size == 4 else []
+        self.sides = [(0, 1, 2, 0), (0, 1, 3, 1), (3, 2, 1, 0), (3, 2, 0, 1)] if size == 4 else []
+        if far_only:
+            self.sides = self.sides[1::2]
         self.ins = [(whole, VMEM)]
         self.outs = [(jax.ShapeDtypeStruct((trees, rows, width), kept_as), VMEM)]
         self.scratch = [
             pltpu.VMEM((rows, width), F32),
-            pltpu.VMEM((size, trees, rows, width), BF16), pltpu.VMEM((trees, rows, width), BF16),
-            SEM((size, trees)), SEM((size, trees)), SEM((trees,)), SEM((trees,)),
+            pltpu.VMEM((size, trees, rows, width), BF16),
+            pltpu.VMEM((2, trees, rows, width), BF16),
+            SEM((size, trees)), SEM((size, trees)), SEM((2, trees)), SEM((2, trees)),
         ]
 
     def bind(self, ins, outs, scratch):
@@ -744,54 +758,56 @@
             self.recv.at[slot, tree], {"dp": place},
         )
 
-    def by_way(self, via, target, tree):
+    def by_way(self, via, target, turn, tree):
         return remote(
-            self.term(tree, target), self.joint.at[tree], self.join_send.at[tree],
-            self.join_recv.at[tree], {"dp": via},
-        )
-
-    def joined(self, via, target, tree):
+            self.term(tree, target), self.joint.at[turn, tree], self.join_send.at[turn, tree],
+            self.join_recv.at[turn, tree], {"dp": via},
+        )
+
+    def joined(self, via, target, turn, tree):
         return remote(
-            self.joint.at[tree], self.boxes.at[via, tree], self.send.at[target, tree],
+            self.joint.at[turn, tree], self.boxes.at[via, tree], self.send.at[target, tree],
             self.recv.at[via, tree], {"dp": target},
         )
 
     def plain(self, place):
         ok = place != self.me
-        for source, via, target in self.sides:
+        for source, via, target, turn in self.sides:
             if place == target:
                 ok = ok & (self.me != source) & (self.me != via)
         return ok
 
     def expected(self, place):
         ok = place != self.me
-        for source, via, target in self.sides:
+        for source, via, target, turn in self.sides:
             if place == source:
                 ok = ok & (self.me != target)
         return ok
 
     def start(self):
         for tree in range(self.trees):
-            for source, via, target in self.sides:
+            for source, via, target, turn in self.sides:
                 @pl.when(self.me == source)
                 def _():
-                    self.by_way(via, target, tree).start()
+                    self.by_way(via, target, turn, tree).start()
 
             for place in range(self.size):
                 @pl.when(self.plain(place))
                 def _():
                     self.copy(place, self.me, tree).start()
 
-    def run(self):
+    def pass_on(self):
         for tree in range(self.trees):
-            for source, via, target in self.sides:
+            for source, via, target, turn in self.sides:
                 @pl.when(self.me == via)
                 def _():
-                    self.by_way(via, target, tree).wait_recv()
-                    both = self.joint[tree].astype(F32) + self.term(tree, target)[...].astype(F32)
-                    self.joint[tree] = both.astype(BF16)
-                    self.joined(via, target, tree).start()
-
+                    self.by_way(via, target, turn, tree).wait_recv()
+                    both = self.joint[turn, tree].astype(F32)
+                    both += self.term(tree, target)[...].astype(F32)
+                    self.joint[turn, tree] = both.astype(BF16)
+                    self.joined(via, target, turn, tree).start()
+
+    def late(self):
         for tree in range(self.trees):
             self.total[...] = self.term(tree, self.me)[...].astype(F32)
             for place in line_order(self.size):
@@ -809,14 +825,14 @@
                 def _():
                     self.copy(place, self.me, tree).wait_send()
 
-            for source, via, target in self.sides:
+            for source, via, target, turn in self.sides:
                 @pl.when(self.me == source)
                 def _():
-                    self.by_way(via, target, tree).wait_send()
+                    self.by_way(via, target, turn, tree).wait_send()
 
                 @pl.when(self.me == via)
                 def _():
-                    self.joined(via, target, tree).wait_send()
+                    self.joined(via, target, turn, tree).wait_send()
 
 
 class TotalOverAll(Part):
@@ -867,7 +883,7 @@
         self.chunks = chunks = chunk_count(rows)
         self.rows = rows // chunks
         self.scratch = [pltpu.VMEM((2, chunks, size, 2 * self.rows, half), BF16)]
-        self.scratch += [SEM((chunks, size))] * 4 + [SEM((chunks,))]
+        self.scratch += [SEM((chunks, size))] * 4 + [SEM((chunks, 2))]
 
     def bind(self, refs):
         self.board, self.send, self.recv, self.sib_send, self.sib_recv, self.relay_send = refs
@@ -880,7 +896,7 @@
     def direct(self, place):
         sent = place != self.me
         if self.relays:
-            sent = sent & jnp.logical_not(far_pair(place, self.me))
+            sent = sent & jnp.logical_not(passed_on(place, self.me))
         return sent
 
     def spread(self, chunk, place, slot):
@@ -889,10 +905,10 @@
             block, block, self.send.at[chunk, place], self.recv.at[chunk, slot], {self.axis: place}
         )
 
-    def passed(self, chunk, source, target):
+    def passed(self, chunk, source, target, turn):
         block = self.board.at[self.core, chunk, source]
         return remote(
-            block, block, self.relay_send.at[chunk], self.recv.at[chunk, source],
+            block, block, self.relay_send.at[chunk, turn], self.recv.at[chunk, source],
             {self.axis: target},
         )
 
@@ -920,11 +936,11 @@
             def _():
                 self.spread(chunk, place, place).wait_recv()
 
-            for via, source, target in self.relays:
+            for via, source, target, turn in self.relays:
                 if source == place:
                     @pl.when(self.me == via)
                     def _():
-                        self.passed(chunk, source, target).start()
+                        self.passed(chunk, source, target, turn).start()
 
             @pl.when(place != self.me)
             def _():
@@ -984,10 +1000,10 @@
 
                 self.over(self.core, chunk, place).wait_send()
 
-            for via, source, target in self.relays:
+            for via, source, target, turn in self.relays:
                 @pl.when(self.me == via)
                 def _():
-                    self.passed(chunk, source, target).wait_send()
+                    self.passed(chunk, source, target, turn).wait_send()
 
 
 class Scatterer:
@@ -1224,6 +1240,8 @@
             )
             self.gain_grad[...] += gain_grad
             self.rows_out.begin(chunk, result + self.add[at])
+
+    def late(self):
         self.rows_out.complete(self.gathered)
 
         @pl.when(lax.axis_index("section") == 1)
@@ -1247,7 +1265,7 @@
         for chunk in range(self.rows_out.chunks):
             self.rows_out.begin(chunk, self.own[rows_at(chunk, self.rows_out.rows)])
 
-    def run(self):
+    def late(self):
         self.rows_out.complete(self.gathered)
         if self.has_other:
             @pl.when(lax.axis_index("section") == 0)
@@ -1961,7 +1979,9 @@
                 "middle_in": middle_first, "mlp_gain": gains[0][1][None],
             },
         )
-        outs, _ = with_cargo(part, [], everyone, 8, 90, 60)
+        outs, (home_second,) = with_cargo(
+            part, [UnitsHome(unit_second[:1], 1)], everyone, 8, 90, 60
+        )
         (
             grad_gate, grad_up, grad_middle, mlp_gain_first, grad_attn,
             attn_gain_second, own_incoming, grad_mlp,
@@ -1970,25 +1990,26 @@
             [(flat(grad_gate), flat(mlp_in_first)), (flat(grad_up), flat(mlp_in_first))]
         )
         grad_attn = tied(grad_attn, *unit_second[1:], *products)
-        unit_first = scatter_units(products)
+        unit_first = scatter_units([products[0], tied(products[1], attn_second)])
         carried = []
         terms, pairs, head_first = attn_backward(
             grad_attn, saved_first, first_weights, gains[0], slot,
             lambda whole: kv_scatter(
-                whole, [UnitsHome(unit_second, 1), RowsOut(own_incoming)], 9, carried
+                whole, [UnitsHome(unit_second[1:], 1), RowsOut(own_incoming)], 9, carried
             ),
         )
-        home_second, (incoming_second,) = carried
+        home_second += carried[0]
+        (incoming_second,) = carried[1]
         unit_first += scatter_units(
             weight_products([(tied(flat(hidden_first), incoming_second), flat(grad_mlp))])
         )
         parts = [
-            ScatterKV(item.reshape(dp_size, 4, own_depth // 4, -1), True, BF16)
+            ScatterKV(item.reshape(dp_size, 4, own_depth // 4, -1), True, BF16, True)
             for item in weight_products(pairs)
         ]
         part = LastHub(terms, own_in, gains[0][0][None], grad_middle, incoming_second)
         (attn_gain_first, input_grad), (*attn_first, home_first) = with_cargo(
-            part, parts + [UnitsHome(unit_first[:2], 0)], everyone, 10, 60, 56
+            part, parts + [UnitsHome(unit_first[:1], 0)], everyone, 10, 60, 56
         )
         attn_first = [item.reshape(own_depth, -1) for (item,) in attn_first]
         attn_second = [attn_second[:, :qkv_width], attn_second[:, qkv_width:]]
@@ -2014,7 +2035,7 @@
             for first, second in zip(attn_first, attn_second)
         ]
         (gain_total,), *arrived, down_home = fused(
-            [TotalOverAll(gain_total.reshape(-1, 128)), *others, UnitsHome(unit_first[2:], 0)],
+            [TotalOverAll(gain_total.reshape(-1, 128)), *others, UnitsHome(unit_first[1:], 0)],
             everyone, True, 11, 60, 40,
         )
         grad_gate, grad_up, grad_down, *attn_grads, layer_out, input_grad = finish_weights(

time: 1040 us -> 1020 us (0.981)
  Pallas kernels: 797 us -> 765 us
  waiting for transfers between devices: 2.73 us -> 19 us
    pallas_call x11, Pallas kernels: 782 us -> 750 us  [fused(): pl.pallas_call(kernel, out_shape=[item[0] for item in outs], in_specs=[it...]
    reduce_scatter x6, waiting for transfers between devices: 0.03 us -> 16.7 us  [scatter_units(): lax.psum_scatter(item, 'tensor', scatter_dimension=0, tiled=True)]
    unnamed x312 -> x314, local copies, waits for them, and re-layouts: 54.2 us -> 53.6 us
  transfers between devices with their start and end apart: 12 -> 12, of which waited for: 1 -> 2; matrix products, arithmetic and copies ran while one was open for 15% -> 14% of each run, Pallas kernels for 51% -> 48%
where the time goes in v13:
time: 1020 us
  Pallas kernels  765 us (75%)
  matrix products  89.2 us (9%)
  local copies, waits for them, and re-layouts  76.2 us (7%)
  other arithmetic  46.4 us (5%)
  between operations  20.5 us (2%)
  waiting for transfers between devices  19 us (2%)
    pallas_call x11, Pallas kernels, fused(): pl.pallas_call(kernel, out_shape=[item[0] for item in outs], in_specs=[it...  750 us
    unnamed x314, local copies, waits for them, and re-layouts  53.6 us
    dot_general x10, matrix products, dot_outer(): return lax.dot_general(left, right, OUTER, preferred_element_type=F32)  42.3 us
  transfers between devices with their start and end apart: 12, of which 2 were waited for; matrix products, arithmetic and copies ran while one was open for 14% of the time, Pallas kernels for 48%

profile of v13, /device:TPU:0, one launch (start us, length us, event | category | flops | bytes accessed | tf_op | source)
XLA Modules:
  0.0 1018.3 jit_solution(8615593755139699532)
XLA Ops:
  8.6 1.7 copy.150
  10.4 1.7 copy.151
  12.2 41.5 %shard_map.255 = (bf16[192,2048]{1,0:T(8,128)(2,1)S(1)}, bf16[192,2048]{1,0:T(8,128)(2,1)S(1)}, f32[2,4,10,128]{3,2,1,0:T(8,128)S(1)}) custom-call(bf16[1536,512]{1,0:T(8,128)(2,1)S(1)} %bitcast.295, bf16[1536,512]{1,0:T(8,128)(2,1)S(1)} %bitcast.297, f32[10,128]{1,0:T(8,128)S(1)} %fusion.112.refs_2_), custom_call_target="tpu_custom_call" | custom-call | bytes 135000000 | tf_op jit(solution)/shard_map/pallas_call | solution.py:220
  66.1 69.1 %shard_map.256 = (bf16[2048,512]{1,0:T(8,128)(2,1)S(1)}, bf16[256,2048]{1,0:T(8,128)(2,1)S(1)}, bf16[192,2048]{1,0:T(8,128)(2,1)S(1)}, bf16[768,512]{1,0:T(8,128)(2,1)S(1)}) custom-call(bf16[512,512]{1,0:T(8,128)(2,1)S(1)} %bitcast.307, bf16[512,256]{1,0:T(8,128)(2,1)S(1)} %bitcast.315, bf16[512,256]{1,0:T(8,128)(2,1)S(1)} %bitcast.317, ...), custom_call_target="tpu_custom_call" | custom-call | bytes 240000000 | tf_op jit(solution)/shard_map/pallas_call | solution.py:220
  149.0 59.4 %shard_map.257 = (bf16[768,2048]{1,0:T(8,128)(2,1)S(1)}, bf16[192,2048]{1,0:T(8,128)(2,1)S(1)}, bf16[192,2048]{1,0:T(8,128)(2,1)}, bf16[192,2048]{1,0:T(8,128)(2,1)S(1)}, bf16[2,4,288,256]{3,2,1,0:T(8,128)(2,1)S(1)}) custom-call(bf16[192,2048]{1,0:T(8,128)(2,1)S(1)} %copy-done.33, bf16[1536,512]{1,0:T(8,128)(2,1)S(1)} %bitcast.296, ...), custom_call_target="tpu_custom_call" | custom-call | bytes 120000000 | tf_op jit(solution)/shard_map/pallas_call | solution.py:220
  221.7 2.0 bitcast_convert_fusion.2.refs_6_
  231.2 2.2 convolution_convert_fusion.9
  233.3 126.6 %shard_map.258 = (bf16[768,2048]{1,0:T(8,128)(2,1)}, f32[72,2048]{1,0:T(8,128)}, bf16[3,192,2048]{2,1,0:T(8,128)(2,1)}, bf16[3,192,768]{2,1,0:T(8,128)(2,1)}, f3...) custom-call(bf16[192,2048]{1,0:T(8,128)(2,1)} %copy-done.23, ...), custom_call_target="tpu_custom_call" | custom-call | bytes 270000000 | tf_op jit(solution)/shard_map/pallas_call | solution.py:220
  360.0 2.2 fusion.9
  363.5 3.2 slice.164
  368.1 3.1 fusion.39
  374.4 26.0 %shard_map.259 = bf16[2,4,288,256]{3,2,1,0:T(8,128)(2,1)S(1)} custom-call(bf16[2,288,256]{2,1,0:T(8,128)(2,1)S(1)} %copy-done.16), custom_call_target="tpu_custom_call" | custom-call | bytes 120000000 | tf_op jit(solution)/shard_map/pallas_call | solution.py:220
  400.4 2.2 fusion.144
  402.6 2.2 reshape.533
  404.8 2.5 multiply_reduce_fusion.2
  418.5 2.2 convolution_convert_fusion.8
  420.7 118.3 %shard_map.260 = (f32[72,2048]{1,0:T(8,128)}, bf16[3,192,2048]{2,1,0:T(8,128)(2,1)}, bf16[3,192,768]{2,1,0:T(8,128)(2,1)}, f32[72,2048]{1,0:T(8,128)}, bf16[3,19...) custom-call(bf16[2,288,2048]{2,1,0:T(8,128)(2,1)} %bitcast.322, ...), custom_call_target="tpu_custom_call" | custom-call | bytes 300000000 | tf_op jit(solution)/shard_map/pallas_call | solution.py:220
  539.0 6.3 convolution_convert_fusion.5
  545.2 6.3 convolution_convert_fusion.4
  552.7 3.4 convolution_convert_fusion.13
  556.1 1.8 reshape.539
  558.9 4.4 fusion.3
  569.4 2.4 copy.164
  574.1 28.3 %shard_map.261 = (bf16[2,288,2048]{2,1,0:T(8,128)(2,1)S(1)}, f32[2,288,256]{2,1,0:T(8,128)S(1)}) custom-call(f32[72,2048]{1,0:T(8,128)S(1)} %copy-done.35, bf16[2,288,2048]{2,1,0:T(8,128)(2,1)S(1)} %copy-done.1, bf16[2,4,288,256]{3,2,1,0:T(8,128)(2,1)S(1)} %bitcast.305), custom_call_target="tpu_custom_call" | custom-call | bytes 90000000 | tf_op jit(solution)/shard_map/pallas_call | solution.py:220
  604.6 4.0 convolution_convert_fusion.3
  611.7 1.9 multiply_reduce_fusion.4
  618.2 2.0 convolution_convert_fusion.10
  620.3 3.3 bitcast_convert_fusion
  623.6 3.8 pad_maximum_fusion
  629.1 2.8 convolution_convert_fusion.7
  631.9 15.2 %reduce-scatter.8.cloned.1.call-done.refs_0_ = bf16[192,2048]{1,0:T(8,128)(2,1)} async-done(((bf16[768,2048]{1,0:T(8,128)(2,1)}), bf16[192,2048]{1,0:T(8,128)(2,1)}) %reduce-scatter.8.cloned.1.call-update) | async-done | bytes 786448 | tf_op jit(solution)/shard_map/reduce_scatter | solution.py:1892
  647.1 100.0 %shard_map.262 = (bf16[1536,512]{1,0:T(8,128)(2,1)}, bf16[3,192,768]{2,1,0:T(8,128)(2,1)}, bf16[3,192,768]{2,1,0:T(8,128)(2,1)}, f32[72,2048]{1,0:T(8,128)}, f32...) custom-call(bf16[192,2048]{1,0:T(8,128)(2,1)} %reduce-scatter.8.clon, ...), custom_call_target="tpu_custom_call" | custom-call | bytes 270000000 | tf_op jit(solution)/shard_map/pallas_call | solution.py:220
  747.2 5.2 convolution_convert_fusion.2
  753.6 5.8 convolution_convert_fusion.1
  759.4 2.6 convolution_convert_fusion.12
  762.0 3.8 fusion
  765.9 3.3 fusion.2
  771.8 4.0 fusion.27
  777.3 55.3 %shard_map.263 = (bf16[1536,512]{1,0:T(8,128)(2,1)S(1)}, bf16[1536,512]{1,0:T(8,128)(2,1)S(1)}, bf16[2,288,2048]{2,1,0:T(8,128)(2,1)S(1)}, f32[2,288,256]{2,1,0:T(8,128)S(1)}) custom-call(bf16[192,2048]{1,0:T(8,128)(2,1)S(1)} %copy-done.28, bf16[192,2048]{1,0:T(8,128)(2,1)S(1)} %copy-done.31, f32[72,2048]{1,0:T(8,128)S(1)} %copy-done.34, ...), custom_call_target="tpu_custom_call" | custom-call | bytes 90000000 | tf_op jit(solution)/shard_map/pallas_call | solution.py:220
  836.3 4.0 convolution_convert_fusion
  841.7 2.6 fusion.45
  848.8 2.0 convolution_convert_fusion.11
  850.8 2.8 convolution_convert_fusion.6
  853.7 3.3 bitcast_convert_fusion.1
  857.0 84.1 %shard_map.264 = (bf16[4,128,512]{2,1,0:T(8,128)(2,1)}, bf16[4,128,256]{2,1,0:T(8,128)(2,1)}, bf16[1536,512]{1,0:T(8,128)(2,1)}, f32[1,2048]{1,0:T(1,128)}, bf16[2,288,2048]{2,1,0:T(8,128)(2,1)}) custom-call(bf16[4,4,128,512]{3,2,1,0:T(8,128)(2,1)} %bitcast.337, bf16[4,4,128,256]{3,2,1,0:T(8,128)(2,1)} %bitcast.343, ...), custom_call_target="tpu_custom_call" | custom-call | bytes 180000000 | tf_op jit(solution)/shard_map/pallas_call | solution.py:220
  943.6 1.9 fusion.147
  949.3 41.7 %shard_map.265 = (f32[68,128]{1,0:T(8,128)S(1)}, bf16[512,512]{1,0:T(8,128)(2,1)S(1)}, bf16[512,256]{1,0:T(8,128)(2,1)S(1)}, bf16[1536,512]{1,0:T(8,128)(2,1)S(1)}, bf16[1536,512]{1,0:T(8,128)(2,1)S(1)}) custom-call(f32[68,128]{1,0:T(8,128)S(1)} %reshape.554.refs_0_, bf16[512,512]{1,0:T(8,128)(2,1)S(1)} %get-tuple-element.202.refs_1_, ...), custom_call_target="tpu_custom_call" | custom-call | bytes 180000000 | tf_op jit(solution)/shard_map/pallas_call | solution.py:220
  996.3 14.7 %shard_map.266 = (f32[512,1536]{1,0:T(8,128)}, f32[512,1536]{1,0:T(8,128)}, f32[1536,512]{1,0:T(8,128)}, f32[512,512]{1,0:T(8,128)}, f32[512,256]{1,0:T(8,128)},...) custom-call(s32[1]{0:T(128)} %bitcast.core_ref, ...), custom_call_target="tpu_custom_call" | custom-call | bytes 25000000 | tf_op jit(solution)/shard_map/pallas_call | solution.py:1555
  (452 shorter events, 108.6 us)
Async XLA Ops:
  7.2 139.2 %all-gather.9.cloned.1.call-start = ((), (), s32[]{:S(2)}) async-start(), calls=%async_computation.8 | async-start | bytes 3932160 | tf_op jit(solution)/shard_map/all_gather | solution.py:1811
  12.1 44.2 %copy-start.137 = (s32[2]{0:T(128)S(1)}, s32[2]{0:T(128)}, u32[]{:S(2)}) copy-start(s32[2]{0:T(128)} %param.20) | copy-start | bytes 28
  12.2 49.3 %copy-start.17 = (bf16[1,512,256]{2,1,0:T(8,128)(2,1)S(1)}, bf16[1,512,256]{2,1,0:T(8,128)(2,1)}, u32[]{:S(2)}) copy-start(bf16[1,512,256]{2,1,0:T(8,128)(2,1)} %param.23) | copy-start | bytes 786436
  55.5 90.9 %all-gather.7.cloned.1.call-start = ((), (), s32[]{:S(2)}) async-start(), calls=%async_computation.7 | async-start | bytes 3932160 | tf_op jit(solution)/shard_map/all_gather | solution.py:1811
  56.3 306.0 %all-gather.15.cloned.1.call-start = ((), (), s32[]{:S(2)}) async-start(), calls=%async_computation.18 | async-start | bytes 3932160 | tf_op jit(solution)/shard_map/all_gather | solution.py:1938
  60.1 77.2 %copy-start.128 = (f32[1,4,4,128]{3,1,2,0:T(4,128)}, f32[1,4,4,128]{3,1,2,0:T(4,128)S(1)}, u32[]{:S(2)}) copy-start(f32[1,4,4,128]{3,1,2,0:T(4,128)S(1)} %copy.190) | copy-start | bytes 24580
  66.1 69.1 %copy-start.77 = (bf16[2,288,2048]{2,1,0:T(8,128)(2,1)S(1)}, bf16[2,288,2048]{2,1,0:T(8,128)(2,1)}, u32[]{:S(2)}) copy-start(bf16[2,288,2048]{2,1,0:T(8,128)(2,1)} %param.16) | copy-start | bytes 7077892
  137.4 3.2 copy-start.117
  140.6 5.6 copy-start.94
  143.0 80.7 %copy-start.122 = (f32[128]{0:T(128)}, f32[128]{0:T(128)S(1)}, u32[]{:S(2)}) copy-start(f32[128]{0:T(128)S(1)} %get-tuple-element.213) | copy-start | bytes 1540
  143.0 228.5 %copy-start.120 = (f32[128]{0:T(128)}, f32[128]{0:T(128)S(1)}, u32[]{:S(2)}) copy-start(f32[128]{0:T(128)S(1)} %get-tuple-element.212) | copy-start | bytes 1540
  212.9 4.9 copy-start.138
  213.0 160.5 %all-gather.11.cloned.1.call-start = ((), (), s32[]{:S(2)}) async-start(), calls=%async_computation.9 | async-start | bytes 3932160 | tf_op jit(solution)/shard_map/all_gather | solution.py:1811
  213.5 207.2 %all-gather.13.cloned.1.call-start = ((), (), s32[]{:S(2)}) async-start(), calls=%async_computation.10 | async-start | bytes 3932160 | tf_op jit(solution)/shard_map/all_gather | solution.py:1811
  214.7 153.3 %copy-start.130 = (f32[1,4,4,128]{3,1,2,0:T(4,128)}, f32[1,4,4,128]{3,1,2,0:T(4,128)S(1)}, u32[]{:S(2)}) copy-start(f32[1,4,4,128]{3,1,2,0:T(4,128)S(1)} %copy.193) | copy-start | bytes 24580
  216.5 7.2 copy-start.51
  217.7 4.0 copy-start.98
  220.6 3.3 copy-start.95
  231.1 392.5 %reduce-scatter.10.cloned.1.call-start = ((), (), s32[]{:S(2)}) async-start(), calls=%async_computation.12 | async-start | bytes 3932160 | tf_op jit(solution)/shard_map/reduce_scatter | solution.py:1892
  362.2 5.9 copy-start.134
  363.5 4.5 copy-start.1
  368.0 4.3 copy-start.62
  368.1 4.3 copy-start.65
  368.1 4.3 copy-start.68
  368.1 4.3 copy-start.71
  409.0 3.4 copy-start.93
  551.5 95.6 %reduce-scatter.8.cloned.1.call-start = ((), (), s32[]{:S(2)}) async-start(), calls=%async_computation.11 | async-start | bytes 3932160 | tf_op jit(solution)/shard_map/reduce_scatter | solution.py:1892
  552.3 207.1 %reduce-scatter.12.cloned.1.call-start = ((), (), s32[]{:S(2)}) async-start(), calls=%async_computation.13 | async-start | bytes 3932160 | tf_op jit(solution)/shard_map/reduce_scatter | solution.py:1892
  558.0 5.3 slice-start
  558.9 4.4 slice-start.1
  574.1 30.5 %copy-start.145 = (bf16[3,192,2048]{2,1,0:T(8,128)(2,1)S(1)}, bf16[3,192,2048]{2,1,0:T(8,128)(2,1)}, u32[]{:S(2)}) copy-start(bf16[3,192,2048]{2,1,0:T(8,128)(2,1)} %get-tuple-element.125) | copy-start | bytes 7077892
  574.1 30.5 %copy-start.147 = (bf16[3,192,768]{2,1,0:T(8,128)(2,1)S(1)}, bf16[3,192,768]{2,1,0:T(8,128)(2,1)}, u32[]{:S(2)}) copy-start(bf16[3,192,768]{2,1,0:T(8,128)(2,1)} %get-tuple-element.122) | copy-start | bytes 2654212
  608.6 232.1 %reduce-scatter.16.cloned.1.call-start = ((), (), s32[]{:S(2)}) async-start(), calls=%async_computation.15 | async-start | bytes 3932160 | tf_op jit(solution)/shard_map/reduce_scatter | solution.py:1896
  608.8 4.7 copy-start.44
  610.1 10.2 copy-start.96
  627.4 229.6 %reduce-scatter.14.cloned.1.call-start = ((), (), s32[]{:S(2)}) async-start(), calls=%async_computation.14 | async-start | bytes 3932160 | tf_op jit(solution)/shard_map/reduce_scatter | solution.py:1892
  647.1 100.0 %copy-start.141 = (bf16[3,192,2048]{2,1,0:T(8,128)(2,1)S(1)}, bf16[3,192,2048]{2,1,0:T(8,128)(2,1)}, u32[]{:S(2)}) copy-start(bf16[3,192,2048]{2,1,0:T(8,128)(2,1)} %get-tuple-element.127) | copy-start | bytes 7077892
  752.4 193.2 %reduce-scatter.20.cloned.1.call-start = ((), (), s32[]{:S(2)}) async-start(), calls=%async_computation.17 | async-start | bytes 3932160 | tf_op jit(solution)/shard_map/reduce_scatter | solution.py:1892
  753.6 5.8 copy-start.21
  765.8 4.8 copy-start.84
  765.8 4.8 copy-start.86
  775.8 60.6 %copy-start.144 = (bf16[3,192,2048]{2,1,0:T(8,128)(2,1)S(1)}, bf16[3,192,2048]{2,1,0:T(8,128)(2,1)}, u32[]{:S(2)}) copy-start(bf16[3,192,2048]{2,1,0:T(8,128)(2,1)} %get-tuple-element.146) | copy-start | bytes 7077892
  775.8 60.5 %copy-start.146 = (bf16[3,192,768]{2,1,0:T(8,128)(2,1)S(1)}, bf16[3,192,768]{2,1,0:T(8,128)(2,1)}, u32[]{:S(2)}) copy-start(bf16[3,192,768]{2,1,0:T(8,128)(2,1)} %get-tuple-element.144) | copy-start | bytes 2654212
  840.4 106.6 %reduce-scatter.18.cloned.1.call-start = ((), (), s32[]{:S(2)}) async-start(), calls=%async_computation.16 | async-start | bytes 3932160 | tf_op jit(solution)/shard_map/reduce_scatter | solution.py:1892
  841.0 3.3 copy-start.56
  841.0 3.3 copy-start.59
  857.0 84.1 %copy-start.126 = (f32[1,2048]{1,0:T(1,128)S(1)}, f32[1,2048]{1,0:T(1,128)}, u32[]{:S(2)}) copy-start(f32[1,2048]{1,0:T(1,128)} %get-tuple-element.137) | copy-start | bytes 24580
  857.0 85.0 %copy-start.91 = (bf16[512,768]{1,0:T(8,128)(2,1)S(1)}, bf16[512,768]{1,0:T(8,128)(2,1)}, u32[]{:S(2)}) copy-start(bf16[512,768]{1,0:T(8,128)(2,1)} %reduce-scatter.16.cloned.1.call-done) | copy-start | bytes 2359300
  (115 other events, 183.8 us)
Sparse Core Ops, SparseCore 0:
  55.6 44.3 all-gather.8
  102.4 43.9 all-gather.6
  213.1 77.5 all-gather.14
  292.9 47.1 all-gather.10
  341.8 47.5 all-gather.12
  551.6 49.4 reduce-scatter.9
  604.1 42.9 reduce-scatter.7
  650.7 52.8 reduce-scatter.11
  706.5 64.6 reduce-scatter.15
  774.6 55.4 reduce-scatter.13
  840.5 60.0 reduce-scatter.19
  903.4 43.5 reduce-scatter.17

commit v14 on v13

--- a/solution.py
+++ b/solution.py
@@ -1817,12 +1817,12 @@
         line = ["section", "dp"]
         everyone = ["section", "dp", "tensor"]
         (gate_rows, up_rows), (gains_all,) = fused(
-            [UnitsOut(unit_mats[:2], 0), SharedRows(gains_own.reshape(-1, 128))], line, True, 1, 45, 40
+            [UnitsOut(unit_mats[:2], 0), SharedRows(gains_own.reshape(-1, 128))], line, True, 1, 45, 60
         )
         shards = AttnShards(w_query[0], w_key[0], w_value[0], w_out[0])
         shards.arrays[0] = tied(shards.arrays[0], gate_rows)
         (w_qkv, w_heads), (down_rows,), (attn_shard,) = fused(
-            [AttnOut(shards, 0), UnitsOut(unit_mats[2:], 0), HalfOver(shards)], line, True, 2, 80, 40
+            [AttnOut(shards, 0), UnitsOut(unit_mats[2:], 0), HalfOver(shards)], line, True, 2, 80, 60
         )
         first_weights = [w_qkv, w_heads, spread_units(gate_rows), spread_units(up_rows)]
     else:
@@ -1933,7 +1933,7 @@
         part = FeedForward(
             terms, own_in, gains[0][1][None], first_weights[2:], True, False, {}
         )
-        outs, ((down_next,),) = with_cargo(part, [UnitsSpread(down_rows)], everyone, 4, 90, 56)
+        outs, ((down_next,),) = with_cargo(part, [UnitsSpread(down_rows)], everyone, 4, 90, 60)
         middle_first, mlp_in_first, hidden_first, own_next, output_first, gate_first, up_first = outs
         attn_next = lax.all_gather(tied(attn_shard, gate_rows), "dp", axis=0)
         second_weights = [
@@ -2009,7 +2009,7 @@
         ]
         part = LastHub(terms, own_in, gains[0][0][None], grad_middle, incoming_second)
         (attn_gain_first, input_grad), (*attn_first, home_first) = with_cargo(
-            part, parts + [UnitsHome(unit_first[:1], 0)], everyone, 10, 60, 56
+            part, parts + [UnitsHome(unit_first[:1], 0)], everyone, 10, 60, 60
         )
         attn_first = [item.reshape(own_depth, -1) for (item,) in attn_first]
         attn_second = [attn_second[:, :qkv_width], attn_second[:, qkv_width:]]
@@ -2036,7 +2036,7 @@
         ]
         (gain_total,), *arrived, down_home = fused(
             [TotalOverAll(gain_total.reshape(-1, 128)), *others, UnitsHome(unit_first[1:], 0)],
-            everyone, True, 11, 60, 40,
+            everyone, True, 11, 60, 60,
         )
         grad_gate, grad_up, grad_down, *attn_grads, layer_out, input_grad = finish_weights(
             home_first + down_home, home_second, attn_first, attn_second,

time: 1020 us -> 1020 us (level)
    unnamed x314 -> x288, local copies, waits for them, and re-layouts: 53.6 us -> 41.6 us
  transfers between devices with their start and end apart: 12 -> 12, of which waited for: 2 -> 3; matrix products, arithmetic and copies ran while one was open for 14% -> 15% of each run, Pallas kernels for 48% -> 48%
where the time goes in v14:
time: 1020 us; the launch traced here: 1010 us
  Pallas kernels  768 us (75%)
  matrix products  89.1 us (9%)
  local copies, waits for them, and re-layouts  66.3 us (6%)
  other arithmetic  47.3 us (5%)
  waiting for transfers between devices  20.5 us (2%)
  between operations  20.4 us (2%)
    pallas_call x11, Pallas kernels, fused(): pl.pallas_call(kernel, out_shape=[item[0] for item in outs], in_specs=[it...  754 us
    dot_general x10, matrix products, dot_outer(): return lax.dot_general(left, right, OUTER, preferred_element_type=F32)  42.2 us
    unnamed x288, local copies, waits for them, and re-layouts  41.6 us
  transfers between devices with their start and end apart: 12, of which 3 were waited for; matrix products, arithmetic and copies ran while one was open for 15% of the time, Pallas kernels for 48%

profile of v14, /device:TPU:0, one launch (start us, length us, event | category | flops | bytes accessed | tf_op | source)
XLA Modules:
  0.0 1013.9 jit_solution(9487810658432500370)
XLA Ops:
  8.7 2.6 copy.150
  13.5 43.0 %shard_map.255 = (bf16[192,2048]{1,0:T(8,128)(2,1)}, bf16[192,2048]{1,0:T(8,128)(2,1)}, f32[2,4,10,128]{3,2,1,0:T(8,128)}) custom-call(bf16[1536,512]{1,0:T(8,128)(2,1)} %bitcast.295, bf16[1536,512]{1,0:T(8,128)(2,1)} %bitcast.297, f32[10,128]{1,0:T(8,128)} %fusion.112.refs_2_), custom_call_target="tpu_custom_call" | custom-call | bytes 135000000 | tf_op jit(solution)/shard_map/pallas_call | solution.py:220
  63.4 69.6 %shard_map.256 = (bf16[2048,512]{1,0:T(8,128)(2,1)}, bf16[256,2048]{1,0:T(8,128)(2,1)}, bf16[192,2048]{1,0:T(8,128)(2,1)}, bf16[768,512]{1,0:T(8,128)(2,1)}) custom-call(bf16[512,512]{1,0:T(8,128)(2,1)} %bitcast.326, bf16[512,256]{1,0:T(8,128)(2,1)} %bitcast.339, bf16[512,256]{1,0:T(8,128)(2,1)} %bitcast.341, bf16[512,512]{1,0:T(8,128)(2,1)} %bitcast.328, ...), custom_call_target="tpu_custom_call" | custom-call | bytes 240000000 | tf_op jit(solution)/shard_map/pallas_call | solution.py:220
  133.8 1.9 copy-done.131
  144.6 2.3 all-gather.7.cloned.1.call-done.refs_4_
  149.5 59.4 %shard_map.257 = (bf16[768,2048]{1,0:T(8,128)(2,1)S(1)}, bf16[192,2048]{1,0:T(8,128)(2,1)S(1)}, bf16[192,2048]{1,0:T(8,128)(2,1)}, bf16[192,2048]{1,0:T(8,128)(2,1)S(1)}, bf16[2,4,288,256]{3,2,1,0:T(8,128)(2,1)S(1)}) custom-call(bf16[192,2048]{1,0:T(8,128)(2,1)S(1)} %copy-done.19, bf16[1536,512]{1,0:T(8,128)(2,1)S(1)} %bitcast.296, ...), custom_call_target="tpu_custom_call" | custom-call | bytes 120000000 | tf_op jit(solution)/shard_map/pallas_call | solution.py:220
  222.3 1.9 bitcast_convert_fusion.2.refs_6_
  231.0 2.2 convolution_convert_fusion.9
  233.2 126.4 %shard_map.258 = (bf16[768,2048]{1,0:T(8,128)(2,1)}, f32[72,2048]{1,0:T(8,128)}, bf16[3,192,2048]{2,1,0:T(8,128)(2,1)}, bf16[3,192,768]{2,1,0:T(8,128)(2,1)}, f3...) custom-call(bf16[192,2048]{1,0:T(8,128)(2,1)} %copy-done.15, ...), custom_call_target="tpu_custom_call" | custom-call | bytes 270000000 | tf_op jit(solution)/shard_map/pallas_call | solution.py:220
  359.7 2.2 fusion.9
  363.2 3.2 slice.164
  367.8 3.1 fusion.39
  374.1 26.0 %shard_map.259 = bf16[2,4,288,256]{3,2,1,0:T(8,128)(2,1)S(1)} custom-call(bf16[2,288,256]{2,1,0:T(8,128)(2,1)S(1)} %copy-done.13), custom_call_target="tpu_custom_call" | custom-call | bytes 120000000 | tf_op jit(solution)/shard_map/pallas_call | solution.py:220
  400.1 2.2 fusion.144
  402.3 2.2 reshape.533
  404.5 2.5 multiply_reduce_fusion.2
  418.1 2.2 convolution_convert_fusion.8
  420.4 118.1 %shard_map.260 = (f32[72,2048]{1,0:T(8,128)}, bf16[3,192,2048]{2,1,0:T(8,128)(2,1)}, bf16[3,192,768]{2,1,0:T(8,128)(2,1)}, f32[72,2048]{1,0:T(8,128)}, bf16[3,19...) custom-call(bf16[2,288,2048]{2,1,0:T(8,128)(2,1)} %bitcast.314, ...), custom_call_target="tpu_custom_call" | custom-call | bytes 300000000 | tf_op jit(solution)/shard_map/pallas_call | solution.py:220
  538.5 6.3 convolution_convert_fusion.5
  544.7 6.3 convolution_convert_fusion.4
  552.2 3.4 convolution_convert_fusion.13
  558.4 4.4 fusion.3
  568.8 2.4 copy.164
  573.5 28.3 %shard_map.261 = (bf16[2,288,2048]{2,1,0:T(8,128)(2,1)S(1)}, f32[2,288,256]{2,1,0:T(8,128)S(1)}) custom-call(f32[72,2048]{1,0:T(8,128)S(1)} %copy-done.21, bf16[2,288,2048]{2,1,0:T(8,128)(2,1)S(1)} %copy-done.3, bf16[2,4,288,256]{3,2,1,0:T(8,128)(2,1)S(1)} %bitcast.305), custom_call_target="tpu_custom_call" | custom-call | bytes 90000000 | tf_op jit(solution)/shard_map/pallas_call | solution.py:220
  604.1 4.0 convolution_convert_fusion.3
  611.2 1.9 multiply_reduce_fusion.4
  617.7 2.0 convolution_convert_fusion.10
  619.8 3.3 bitcast_convert_fusion
  623.1 3.8 pad_maximum_fusion
  628.6 2.8 convolution_convert_fusion.7
  631.4 15.3 %reduce-scatter.8.cloned.1.call-done.refs_0_ = bf16[192,2048]{1,0:T(8,128)(2,1)} async-done(((bf16[768,2048]{1,0:T(8,128)(2,1)}), bf16[192,2048]{1,0:T(8,128)(2,1)}) %reduce-scatter.8.cloned.1.call-update) | async-done | bytes 786448 | tf_op jit(solution)/shard_map/reduce_scatter | solution.py:1892
  646.6 100.0 %shard_map.262 = (bf16[1536,512]{1,0:T(8,128)(2,1)}, bf16[3,192,768]{2,1,0:T(8,128)(2,1)}, bf16[3,192,768]{2,1,0:T(8,128)(2,1)}, f32[72,2048]{1,0:T(8,128)}, f32...) custom-call(bf16[192,2048]{1,0:T(8,128)(2,1)} %reduce-scatter.8.clon, ...), custom_call_target="tpu_custom_call" | custom-call | bytes 270000000 | tf_op jit(solution)/shard_map/pallas_call | solution.py:220
  746.7 5.2 convolution_convert_fusion.2
  753.1 5.8 convolution_convert_fusion.1
  758.9 2.6 convolution_convert_fusion.12
  761.6 3.8 fusion
  765.4 3.3 fusion.2
  771.3 4.0 fusion.27
  776.8 55.3 %shard_map.263 = (bf16[1536,512]{1,0:T(8,128)(2,1)S(1)}, bf16[1536,512]{1,0:T(8,128)(2,1)S(1)}, bf16[2,288,2048]{2,1,0:T(8,128)(2,1)S(1)}, f32[2,288,256]{2,1,0:T(8,128)S(1)}) custom-call(bf16[192,2048]{1,0:T(8,128)(2,1)S(1)} %copy-done.17, bf16[192,2048]{1,0:T(8,128)(2,1)S(1)} %copy-done.18, f32[72,2048]{1,0:T(8,128)S(1)} %copy-done.20, ...), custom_call_target="tpu_custom_call" | custom-call | bytes 90000000 | tf_op jit(solution)/shard_map/pallas_call | solution.py:220
  835.8 4.0 convolution_convert_fusion
  841.2 2.6 fusion.45
  848.2 2.0 convolution_convert_fusion.11
  850.3 2.8 convolution_convert_fusion.6
  853.1 3.3 bitcast_convert_fusion.1
  856.5 84.1 %shard_map.264 = (bf16[4,128,512]{2,1,0:T(8,128)(2,1)}, bf16[4,128,256]{2,1,0:T(8,128)(2,1)}, bf16[1536,512]{1,0:T(8,128)(2,1)}, f32[1,2048]{1,0:T(1,128)}, bf16[2,288,2048]{2,1,0:T(8,128)(2,1)}) custom-call(bf16[4,4,128,512]{3,2,1,0:T(8,128)(2,1)} %bitcast.333, bf16[4,4,128,256]{3,2,1,0:T(8,128)(2,1)} %bitcast.343, ...), custom_call_target="tpu_custom_call" | custom-call | bytes 180000000 | tf_op jit(solution)/shard_map/pallas_call | solution.py:220
  943.8 2.1 fusion.147
  946.5 43.3 %shard_map.265 = (f32[68,128]{1,0:T(8,128)}, bf16[512,512]{1,0:T(8,128)(2,1)}, bf16[512,256]{1,0:T(8,128)(2,1)}, bf16[1536,512]{1,0:T(8,128)(2,1)}, bf16[1536,512]{1,0:T(8,128)(2,1)}) custom-call(f32[68,128]{1,0:T(8,128)} %reshape.554.refs_0_, bf16[512,512]{1,0:T(8,128)(2,1)} %get-tuple-element.202.refs_1_, bf16[512,256]{1,0:T(8,128)(2,1)} %get-tuple-element.200.refs_2_, ...), custom_call_target="tpu_custom_call" | custom-call | bytes 180000000 | tf_op jit(solution)/shard_map/pallas_call | solution.py:220
  991.9 14.7 %shard_map.266 = (f32[512,1536]{1,0:T(8,128)}, f32[512,1536]{1,0:T(8,128)}, f32[1536,512]{1,0:T(8,128)}, f32[512,512]{1,0:T(8,128)}, f32[512,256]{1,0:T(8,128)},...) custom-call(s32[1]{0:T(128)} %bitcast.core_ref, ...), custom_call_target="tpu_custom_call" | custom-call | bytes 25000000 | tf_op jit(solution)/shard_map/pallas_call | solution.py:1555
  (426 shorter events, 99.4 us)
Async XLA Ops:
  7.2 4.2 copy-start.63
  7.2 137.4 %all-gather.9.cloned.1.call-start = ((), (), s32[]{:S(2)}) async-start(), calls=%async_computation.8 | async-start | bytes 3932160 | tf_op jit(solution)/shard_map/all_gather | solution.py:1811
  13.5 43.9 %copy-start.122 = (s32[2]{0:T(128)S(1)}, s32[2]{0:T(128)}, u32[]{:S(2)}) copy-start(s32[2]{0:T(128)} %param.20) | copy-start | bytes 28
  56.6 90.4 %all-gather.7.cloned.1.call-start = ((), (), s32[]{:S(2)}) async-start(), calls=%async_computation.7 | async-start | bytes 3932160 | tf_op jit(solution)/shard_map/all_gather | solution.py:1811
  57.3 304.6 %all-gather.15.cloned.1.call-start = ((), (), s32[]{:S(2)}) async-start(), calls=%async_computation.18 | async-start | bytes 3932160 | tf_op jit(solution)/shard_map/all_gather | solution.py:1938
  62.1 71.7 %copy-start.113 = (f32[1,4,4,128]{3,1,2,0:T(4,128)}, f32[1,4,4,128]{3,1,2,0:T(4,128)S(1)}, u32[]{:S(2)}) copy-start(f32[1,4,4,128]{3,1,2,0:T(4,128)S(1)} %copy.190) | copy-start | bytes 24580
  63.4 69.6 %copy-start.59 = (bf16[2,288,2048]{2,1,0:T(8,128)(2,1)S(1)}, bf16[2,288,2048]{2,1,0:T(8,128)(2,1)}, u32[]{:S(2)}) copy-start(bf16[2,288,2048]{2,1,0:T(8,128)(2,1)} %param.16) | copy-start | bytes 7077892
  133.2 3.9 copy-start.27
  133.2 3.9 copy-start.30
  138.1 8.9 copy-start
  138.1 8.9 copy-start.1
  138.8 5.6 copy-start.79
  140.6 3.8 copy-start.92
  141.2 83.0 %copy-start.107 = (f32[128]{0:T(128)}, f32[128]{0:T(128)S(1)}, u32[]{:S(2)}) copy-start(f32[128]{0:T(128)S(1)} %get-tuple-element.213) | copy-start | bytes 1540
  141.2 230.0 %copy-start.105 = (f32[128]{0:T(128)}, f32[128]{0:T(128)S(1)}, u32[]{:S(2)}) copy-start(f32[128]{0:T(128)S(1)} %get-tuple-element.212) | copy-start | bytes 1540
  213.5 4.9 copy-start.123
  213.5 159.6 %all-gather.11.cloned.1.call-start = ((), (), s32[]{:S(2)}) async-start(), calls=%async_computation.9 | async-start | bytes 3932160 | tf_op jit(solution)/shard_map/all_gather | solution.py:1811
  214.1 206.3 %all-gather.13.cloned.1.call-start = ((), (), s32[]{:S(2)}) async-start(), calls=%async_computation.10 | async-start | bytes 3932160 | tf_op jit(solution)/shard_map/all_gather | solution.py:1811
  215.3 152.4 %copy-start.115 = (f32[1,4,4,128]{3,1,2,0:T(4,128)}, f32[1,4,4,128]{3,1,2,0:T(4,128)S(1)}, u32[]{:S(2)}) copy-start(f32[1,4,4,128]{3,1,2,0:T(4,128)S(1)} %copy.193) | copy-start | bytes 24580
  217.1 7.1 copy-start.33
  218.3 4.0 copy-start.83
  231.0 392.1 %reduce-scatter.10.cloned.1.call-start = ((), (), s32[]{:S(2)}) async-start(), calls=%async_computation.12 | async-start | bytes 3932160 | tf_op jit(solution)/shard_map/reduce_scatter | solution.py:1892
  361.9 5.9 copy-start.119
  363.2 4.5 copy-start.3
  367.7 4.2 copy-start.44
  367.8 4.2 copy-start.47
  367.8 4.2 copy-start.50
  367.8 4.2 copy-start.53
  551.0 95.6 %reduce-scatter.8.cloned.1.call-start = ((), (), s32[]{:S(2)}) async-start(), calls=%async_computation.11 | async-start | bytes 3932160 | tf_op jit(solution)/shard_map/reduce_scatter | solution.py:1892
  551.8 207.1 %reduce-scatter.12.cloned.1.call-start = ((), (), s32[]{:S(2)}) async-start(), calls=%async_computation.13 | async-start | bytes 3932160 | tf_op jit(solution)/shard_map/reduce_scatter | solution.py:1892
  557.5 5.3 slice-start
  558.4 4.4 slice-start.1
  573.5 30.6 %copy-start.130 = (bf16[3,192,2048]{2,1,0:T(8,128)(2,1)S(1)}, bf16[3,192,2048]{2,1,0:T(8,128)(2,1)}, u32[]{:S(2)}) copy-start(bf16[3,192,2048]{2,1,0:T(8,128)(2,1)} %get-tuple-element.125) | copy-start | bytes 7077892
  573.5 30.6 %copy-start.134 = (bf16[3,192,768]{2,1,0:T(8,128)(2,1)S(1)}, bf16[3,192,768]{2,1,0:T(8,128)(2,1)}, u32[]{:S(2)}) copy-start(bf16[3,192,768]{2,1,0:T(8,128)(2,1)} %get-tuple-element.122) | copy-start | bytes 2654212
  608.1 232.1 %reduce-scatter.16.cloned.1.call-start = ((), (), s32[]{:S(2)}) async-start(), calls=%async_computation.15 | async-start | bytes 3932160 | tf_op jit(solution)/shard_map/reduce_scatter | solution.py:1896
  608.4 4.7 copy-start.26
  609.6 10.2 %copy-start.81 = (bf16[2,288,128]{2,1,0:T(8,128)(2,1)}, bf16[2,288,128]{2,1,0:T(8,128)(2,1)S(1)}, u32[]{:S(2)}) copy-start(bf16[2,288,128]{2,1,0:T(8,128)(2,1)S(1)} %slice.239) | copy-start | bytes 442372
  626.9 229.5 %reduce-scatter.14.cloned.1.call-start = ((), (), s32[]{:S(2)}) async-start(), calls=%async_computation.14 | async-start | bytes 3932160 | tf_op jit(solution)/shard_map/reduce_scatter | solution.py:1892
  646.6 100.1 %copy-start.126 = (bf16[3,192,2048]{2,1,0:T(8,128)(2,1)S(1)}, bf16[3,192,2048]{2,1,0:T(8,128)(2,1)}, u32[]{:S(2)}) copy-start(bf16[3,192,2048]{2,1,0:T(8,128)(2,1)} %get-tuple-element.127) | copy-start | bytes 7077892
  751.9 194.0 %reduce-scatter.20.cloned.1.call-start = ((), (), s32[]{:S(2)}) async-start(), calls=%async_computation.17 | async-start | bytes 3932160 | tf_op jit(solution)/shard_map/reduce_scatter | solution.py:1892
  753.1 5.8 copy-start.75
  765.4 4.8 copy-start.67
  765.4 4.8 copy-start.69
  775.3 60.5 %copy-start.129 = (bf16[3,192,2048]{2,1,0:T(8,128)(2,1)S(1)}, bf16[3,192,2048]{2,1,0:T(8,128)(2,1)}, u32[]{:S(2)}) copy-start(bf16[3,192,2048]{2,1,0:T(8,128)(2,1)} %get-tuple-element.146) | copy-start | bytes 7077892
  775.3 60.5 %copy-start.133 = (bf16[3,192,768]{2,1,0:T(8,128)(2,1)S(1)}, bf16[3,192,768]{2,1,0:T(8,128)(2,1)}, u32[]{:S(2)}) copy-start(bf16[3,192,768]{2,1,0:T(8,128)(2,1)} %get-tuple-element.144) | copy-start | bytes 2654212
  839.9 106.6 %reduce-scatter.18.cloned.1.call-start = ((), (), s32[]{:S(2)}) async-start(), calls=%async_computation.16 | async-start | bytes 3932160 | tf_op jit(solution)/shard_map/reduce_scatter | solution.py:1892
  856.5 84.1 %copy-start.111 = (f32[1,2048]{1,0:T(1,128)S(1)}, f32[1,2048]{1,0:T(1,128)}, u32[]{:S(2)}) copy-start(f32[1,2048]{1,0:T(1,128)} %get-tuple-element.137) | copy-start | bytes 24580
  856.5 85.6 %copy-start.76 = (bf16[512,768]{1,0:T(8,128)(2,1)S(1)}, bf16[512,768]{1,0:T(8,128)(2,1)}, u32[]{:S(2)}) copy-start(bf16[512,768]{1,0:T(8,128)(2,1)} %reduce-scatter.16.cloned.1.call-done) | copy-start | bytes 2359300
  (102 other events, 179.9 us)
Sparse Core Ops, SparseCore 0:
  56.7 44.3 all-gather.8
  102.9 43.9 all-gather.6
  213.6 77.5 all-gather.14
  293.5 47.8 all-gather.10
  343.0 47.1 all-gather.12
  551.2 49.4 reduce-scatter.9
  603.6 43.0 reduce-scatter.7
  650.2 52.8 reduce-scatter.11
  706.0 64.6 reduce-scatter.15
  774.1 55.4 reduce-scatter.13
  840.0 60.0 reduce-scatter.19
  902.9 43.5 reduce-scatter.17

commit v15 on v14

--- a/solution.py
+++ b/solution.py
@@ -126,7 +126,7 @@
 
 
 MESH = pl.DeviceIdType.MESH
-CHUNK = 256
+CHUNK = 512
 SEM = pltpu.SemaphoreType.DMA
 VMEM = pl.BlockSpec(memory_space=pltpu.VMEM)
 HBM = pl.BlockSpec(memory_space=pl.ANY)

time: 1020 us -> 1020 us (level)
  no operation moved by 1% of the time
where the time goes in v15:
time: 1020 us; the launch traced here: 1010 us
  Pallas kernels  763 us (75%)
  matrix products  89.3 us (9%)
  local copies, waits for them, and re-layouts  66.2 us (6%)
  other arithmetic  47.2 us (5%)
  between operations  20.1 us (2%)
  waiting for transfers between devices  20 us (2%)
    pallas_call x11, Pallas kernels, fused(): pl.pallas_call(kernel, out_shape=[item[0] for item in outs], in_specs=[it...  748 us
    dot_general x10, matrix products, dot_outer(): return lax.dot_general(left, right, OUTER, preferred_element_type=F32)  42.3 us
    unnamed x288, local copies, waits for them, and re-layouts  41.6 us
  transfers between devices with their start and end apart: 12, of which 3 were waited for; matrix products, arithmetic and copies ran while one was open for 15% of the time, Pallas kernels for 48%

profile of v15, /device:TPU:0, one launch (start us, length us, event | category | flops | bytes accessed | tf_op | source)
XLA Modules:
  0.0 1007.8 jit_solution(7162050971703598368)
XLA Ops:
  8.7 2.6 copy.150
  13.5 43.0 %shard_map.255 = (bf16[192,2048]{1,0:T(8,128)(2,1)}, bf16[192,2048]{1,0:T(8,128)(2,1)}, f32[2,4,10,128]{3,2,1,0:T(8,128)}) custom-call(bf16[1536,512]{1,0:T(8,128)(2,1)} %bitcast.295, bf16[1536,512]{1,0:T(8,128)(2,1)} %bitcast.297, f32[10,128]{1,0:T(8,128)} %fusion.112.refs_2_), custom_call_target="tpu_custom_call" | custom-call | bytes 135000000 | tf_op jit(solution)/shard_map/pallas_call | solution.py:220
  63.4 69.6 %shard_map.256 = (bf16[2048,512]{1,0:T(8,128)(2,1)}, bf16[256,2048]{1,0:T(8,128)(2,1)}, bf16[192,2048]{1,0:T(8,128)(2,1)}, bf16[768,512]{1,0:T(8,128)(2,1)}) custom-call(bf16[512,512]{1,0:T(8,128)(2,1)} %bitcast.326, bf16[512,256]{1,0:T(8,128)(2,1)} %bitcast.339, bf16[512,256]{1,0:T(8,128)(2,1)} %bitcast.341, bf16[512,512]{1,0:T(8,128)(2,1)} %bitcast.328, ...), custom_call_target="tpu_custom_call" | custom-call | bytes 240000000 | tf_op jit(solution)/shard_map/pallas_call | solution.py:220
  133.8 1.9 copy-done.131
  144.6 2.3 all-gather.7.cloned.1.call-done.refs_4_
  149.5 59.4 %shard_map.257 = (bf16[768,2048]{1,0:T(8,128)(2,1)S(1)}, bf16[192,2048]{1,0:T(8,128)(2,1)S(1)}, bf16[192,2048]{1,0:T(8,128)(2,1)}, bf16[192,2048]{1,0:T(8,128)(2,1)S(1)}, bf16[2,4,288,256]{3,2,1,0:T(8,128)(2,1)S(1)}) custom-call(bf16[192,2048]{1,0:T(8,128)(2,1)S(1)} %copy-done.19, bf16[1536,512]{1,0:T(8,128)(2,1)S(1)} %bitcast.296, ...), custom_call_target="tpu_custom_call" | custom-call | bytes 120000000 | tf_op jit(solution)/shard_map/pallas_call | solution.py:220
  222.3 1.9 bitcast_convert_fusion.2.refs_6_
  231.0 2.2 convolution_convert_fusion.9
  233.2 125.1 %shard_map.258 = (bf16[768,2048]{1,0:T(8,128)(2,1)}, f32[72,2048]{1,0:T(8,128)}, bf16[3,192,2048]{2,1,0:T(8,128)(2,1)}, bf16[3,192,768]{2,1,0:T(8,128)(2,1)}, f3...) custom-call(bf16[192,2048]{1,0:T(8,128)(2,1)} %copy-done.15, ...), custom_call_target="tpu_custom_call" | custom-call | bytes 270000000 | tf_op jit(solution)/shard_map/pallas_call | solution.py:220
  358.4 2.2 fusion.9
  361.9 3.2 slice.164
  366.5 3.1 fusion.39
  372.8 26.1 %shard_map.259 = bf16[2,4,288,256]{3,2,1,0:T(8,128)(2,1)S(1)} custom-call(bf16[2,288,256]{2,1,0:T(8,128)(2,1)S(1)} %copy-done.13), custom_call_target="tpu_custom_call" | custom-call | bytes 120000000 | tf_op jit(solution)/shard_map/pallas_call | solution.py:220
  398.9 2.2 fusion.144
  401.0 2.2 reshape.533
  403.2 2.5 multiply_reduce_fusion.2
  416.9 2.2 convolution_convert_fusion.8
  419.1 115.0 %shard_map.260 = (f32[72,2048]{1,0:T(8,128)}, bf16[3,192,2048]{2,1,0:T(8,128)(2,1)}, bf16[3,192,768]{2,1,0:T(8,128)(2,1)}, f32[72,2048]{1,0:T(8,128)}, bf16[3,19...) custom-call(bf16[2,288,2048]{2,1,0:T(8,128)(2,1)} %bitcast.314, ...), custom_call_target="tpu_custom_call" | custom-call | bytes 300000000 | tf_op jit(solution)/shard_map/pallas_call | solution.py:220
  534.1 6.2 convolution_convert_fusion.5
  540.3 6.3 convolution_convert_fusion.4
  547.8 3.4 convolution_convert_fusion.13
  553.9 4.4 fusion.3
  564.3 2.4 copy.164
  569.1 28.2 %shard_map.261 = (bf16[2,288,2048]{2,1,0:T(8,128)(2,1)S(1)}, f32[2,288,256]{2,1,0:T(8,128)S(1)}) custom-call(f32[72,2048]{1,0:T(8,128)S(1)} %copy-done.21, bf16[2,288,2048]{2,1,0:T(8,128)(2,1)S(1)} %copy-done.3, bf16[2,4,288,256]{3,2,1,0:T(8,128)(2,1)S(1)} %bitcast.305), custom_call_target="tpu_custom_call" | custom-call | bytes 90000000 | tf_op jit(solution)/shard_map/pallas_call | solution.py:220
  599.6 4.0 convolution_convert_fusion.3
  606.5 1.9 multiply_reduce_fusion.4
  613.1 2.0 convolution_convert_fusion.10
  615.2 3.3 bitcast_convert_fusion
  618.5 3.8 pad_maximum_fusion
  623.9 2.8 convolution_convert_fusion.7
  626.8 14.9 %reduce-scatter.8.cloned.1.call-done.refs_0_ = bf16[192,2048]{1,0:T(8,128)(2,1)} async-done(((bf16[768,2048]{1,0:T(8,128)(2,1)}), bf16[192,2048]{1,0:T(8,128)(2,1)}) %reduce-scatter.8.cloned.1.call-update) | async-done | bytes 786448 | tf_op jit(solution)/shard_map/reduce_scatter | solution.py:1892
  641.6 98.7 %shard_map.262 = (bf16[1536,512]{1,0:T(8,128)(2,1)}, bf16[3,192,768]{2,1,0:T(8,128)(2,1)}, bf16[3,192,768]{2,1,0:T(8,128)(2,1)}, f32[72,2048]{1,0:T(8,128)}, f32...) custom-call(bf16[192,2048]{1,0:T(8,128)(2,1)} %reduce-scatter.8.clon, ...), custom_call_target="tpu_custom_call" | custom-call | bytes 270000000 | tf_op jit(solution)/shard_map/pallas_call | solution.py:220
  740.4 5.2 convolution_convert_fusion.2
  746.8 5.8 convolution_convert_fusion.1
  752.6 2.6 convolution_convert_fusion.12
  755.3 3.8 fusion
  759.1 3.3 fusion.2
  765.0 4.0 fusion.27
  770.6 55.7 %shard_map.263 = (bf16[1536,512]{1,0:T(8,128)(2,1)S(1)}, bf16[1536,512]{1,0:T(8,128)(2,1)S(1)}, bf16[2,288,2048]{2,1,0:T(8,128)(2,1)S(1)}, f32[2,288,256]{2,1,0:T(8,128)S(1)}) custom-call(bf16[192,2048]{1,0:T(8,128)(2,1)S(1)} %copy-done.17, bf16[192,2048]{1,0:T(8,128)(2,1)S(1)} %copy-done.18, f32[72,2048]{1,0:T(8,128)S(1)} %copy-done.20, ...), custom_call_target="tpu_custom_call" | custom-call | bytes 90000000 | tf_op jit(solution)/shard_map/pallas_call | solution.py:220
  830.0 4.0 convolution_convert_fusion
  835.3 2.6 fusion.45
  842.4 2.0 convolution_convert_fusion.11
  844.5 2.8 convolution_convert_fusion.6
  847.3 3.3 bitcast_convert_fusion.1
  850.6 84.1 %shard_map.264 = (bf16[4,128,512]{2,1,0:T(8,128)(2,1)}, bf16[4,128,256]{2,1,0:T(8,128)(2,1)}, bf16[1536,512]{1,0:T(8,128)(2,1)}, f32[1,2048]{1,0:T(1,128)}, bf16[2,288,2048]{2,1,0:T(8,128)(2,1)}) custom-call(bf16[4,4,128,512]{3,2,1,0:T(8,128)(2,1)} %bitcast.333, bf16[4,4,128,256]{3,2,1,0:T(8,128)(2,1)} %bitcast.343, ...), custom_call_target="tpu_custom_call" | custom-call | bytes 180000000 | tf_op jit(solution)/shard_map/pallas_call | solution.py:220
  937.9 2.1 fusion.147
  940.6 43.3 %shard_map.265 = (f32[68,128]{1,0:T(8,128)}, bf16[512,512]{1,0:T(8,128)(2,1)}, bf16[512,256]{1,0:T(8,128)(2,1)}, bf16[1536,512]{1,0:T(8,128)(2,1)}, bf16[1536,512]{1,0:T(8,128)(2,1)}) custom-call(f32[68,128]{1,0:T(8,128)} %reshape.554.refs_0_, bf16[512,512]{1,0:T(8,128)(2,1)} %get-tuple-element.202.refs_1_, bf16[512,256]{1,0:T(8,128)(2,1)} %get-tuple-element.200.refs_2_, ...), custom_call_target="tpu_custom_call" | custom-call | bytes 180000000 | tf_op jit(solution)/shard_map/pallas_call | solution.py:220
  986.0 14.7 %shard_map.266 = (f32[512,1536]{1,0:T(8,128)}, f32[512,1536]{1,0:T(8,128)}, f32[1536,512]{1,0:T(8,128)}, f32[512,512]{1,0:T(8,128)}, f32[512,256]{1,0:T(8,128)},...) custom-call(s32[1]{0:T(128)} %bitcast.core_ref, ...), custom_call_target="tpu_custom_call" | custom-call | bytes 25000000 | tf_op jit(solution)/shard_map/pallas_call | solution.py:1555
  (426 shorter events, 99.3 us)
Async XLA Ops:
  7.2 4.2 copy-start.63
  7.2 137.4 %all-gather.9.cloned.1.call-start = ((), (), s32[]{:S(2)}) async-start(), calls=%async_computation.8 | async-start | bytes 3932160 | tf_op jit(solution)/shard_map/all_gather | solution.py:1811
  13.5 43.9 %copy-start.122 = (s32[2]{0:T(128)S(1)}, s32[2]{0:T(128)}, u32[]{:S(2)}) copy-start(s32[2]{0:T(128)} %param.20) | copy-start | bytes 28
  56.6 90.4 %all-gather.7.cloned.1.call-start = ((), (), s32[]{:S(2)}) async-start(), calls=%async_computation.7 | async-start | bytes 3932160 | tf_op jit(solution)/shard_map/all_gather | solution.py:1811
  57.3 303.3 %all-gather.15.cloned.1.call-start = ((), (), s32[]{:S(2)}) async-start(), calls=%async_computation.18 | async-start | bytes 3932160 | tf_op jit(solution)/shard_map/all_gather | solution.py:1938
  62.1 71.7 %copy-start.113 = (f32[1,4,4,128]{3,1,2,0:T(4,128)}, f32[1,4,4,128]{3,1,2,0:T(4,128)S(1)}, u32[]{:S(2)}) copy-start(f32[1,4,4,128]{3,1,2,0:T(4,128)S(1)} %copy.190) | copy-start | bytes 24580
  63.4 69.6 %copy-start.59 = (bf16[2,288,2048]{2,1,0:T(8,128)(2,1)S(1)}, bf16[2,288,2048]{2,1,0:T(8,128)(2,1)}, u32[]{:S(2)}) copy-start(bf16[2,288,2048]{2,1,0:T(8,128)(2,1)} %param.16) | copy-start | bytes 7077892
  133.2 3.9 copy-start.27
  133.2 3.9 copy-start.30
  138.1 8.9 copy-start
  138.1 8.9 copy-start.1
  138.8 5.6 copy-start.79
  140.6 3.8 copy-start.92
  141.2 83.0 %copy-start.107 = (f32[128]{0:T(128)}, f32[128]{0:T(128)S(1)}, u32[]{:S(2)}) copy-start(f32[128]{0:T(128)S(1)} %get-tuple-element.213) | copy-start | bytes 1540
  141.2 228.7 %copy-start.105 = (f32[128]{0:T(128)}, f32[128]{0:T(128)S(1)}, u32[]{:S(2)}) copy-start(f32[128]{0:T(128)S(1)} %get-tuple-element.212) | copy-start | bytes 1540
  213.5 4.9 copy-start.123
  213.5 158.3 %all-gather.11.cloned.1.call-start = ((), (), s32[]{:S(2)}) async-start(), calls=%async_computation.9 | async-start | bytes 3932160 | tf_op jit(solution)/shard_map/all_gather | solution.py:1811
  214.1 205.0 %all-gather.13.cloned.1.call-start = ((), (), s32[]{:S(2)}) async-start(), calls=%async_computation.10 | async-start | bytes 3932160 | tf_op jit(solution)/shard_map/all_gather | solution.py:1811
  215.3 151.1 %copy-start.115 = (f32[1,4,4,128]{3,1,2,0:T(4,128)}, f32[1,4,4,128]{3,1,2,0:T(4,128)S(1)}, u32[]{:S(2)}) copy-start(f32[1,4,4,128]{3,1,2,0:T(4,128)S(1)} %copy.193) | copy-start | bytes 24580
  217.1 7.1 copy-start.33
  218.3 4.0 copy-start.83
  231.0 387.5 %reduce-scatter.10.cloned.1.call-start = ((), (), s32[]{:S(2)}) async-start(), calls=%async_computation.12 | async-start | bytes 3932160 | tf_op jit(solution)/shard_map/reduce_scatter | solution.py:1892
  360.6 5.9 copy-start.119
  361.9 4.5 copy-start.3
  366.4 4.2 copy-start.44
  366.4 4.2 copy-start.47
  366.5 4.2 copy-start.50
  366.5 4.2 copy-start.53
  546.6 95.0 %reduce-scatter.8.cloned.1.call-start = ((), (), s32[]{:S(2)}) async-start(), calls=%async_computation.11 | async-start | bytes 3932160 | tf_op jit(solution)/shard_map/reduce_scatter | solution.py:1892
  547.4 205.3 %reduce-scatter.12.cloned.1.call-start = ((), (), s32[]{:S(2)}) async-start(), calls=%async_computation.13 | async-start | bytes 3932160 | tf_op jit(solution)/shard_map/reduce_scatter | solution.py:1892
  553.0 5.3 slice-start
  553.9 4.4 slice-start.1
  569.1 30.5 %copy-start.130 = (bf16[3,192,2048]{2,1,0:T(8,128)(2,1)S(1)}, bf16[3,192,2048]{2,1,0:T(8,128)(2,1)}, u32[]{:S(2)}) copy-start(bf16[3,192,2048]{2,1,0:T(8,128)(2,1)} %get-tuple-element.125) | copy-start | bytes 7077892
  569.1 30.5 %copy-start.134 = (bf16[3,192,768]{2,1,0:T(8,128)(2,1)S(1)}, bf16[3,192,768]{2,1,0:T(8,128)(2,1)}, u32[]{:S(2)}) copy-start(bf16[3,192,768]{2,1,0:T(8,128)(2,1)} %get-tuple-element.122) | copy-start | bytes 2654212
  603.6 230.9 %reduce-scatter.16.cloned.1.call-start = ((), (), s32[]{:S(2)}) async-start(), calls=%async_computation.15 | async-start | bytes 3932160 | tf_op jit(solution)/shard_map/reduce_scatter | solution.py:1896
  603.8 4.6 copy-start.26
  605.0 10.1 %copy-start.81 = (bf16[2,288,128]{2,1,0:T(8,128)(2,1)}, bf16[2,288,128]{2,1,0:T(8,128)(2,1)S(1)}, u32[]{:S(2)}) copy-start(bf16[2,288,128]{2,1,0:T(8,128)(2,1)S(1)} %slice.239) | copy-start | bytes 442372
  622.3 228.3 %reduce-scatter.14.cloned.1.call-start = ((), (), s32[]{:S(2)}) async-start(), calls=%async_computation.14 | async-start | bytes 3932160 | tf_op jit(solution)/shard_map/reduce_scatter | solution.py:1892
  641.6 98.8 %copy-start.126 = (bf16[3,192,2048]{2,1,0:T(8,128)(2,1)S(1)}, bf16[3,192,2048]{2,1,0:T(8,128)(2,1)}, u32[]{:S(2)}) copy-start(bf16[3,192,2048]{2,1,0:T(8,128)(2,1)} %get-tuple-element.127) | copy-start | bytes 7077892
  745.6 194.4 %reduce-scatter.20.cloned.1.call-start = ((), (), s32[]{:S(2)}) async-start(), calls=%async_computation.17 | async-start | bytes 3932160 | tf_op jit(solution)/shard_map/reduce_scatter | solution.py:1892
  746.8 5.9 copy-start.75
  759.1 4.8 copy-start.67
  759.1 4.8 copy-start.69
  769.1 60.9 %copy-start.129 = (bf16[3,192,2048]{2,1,0:T(8,128)(2,1)S(1)}, bf16[3,192,2048]{2,1,0:T(8,128)(2,1)}, u32[]{:S(2)}) copy-start(bf16[3,192,2048]{2,1,0:T(8,128)(2,1)} %get-tuple-element.146) | copy-start | bytes 7077892
  769.1 60.9 %copy-start.133 = (bf16[3,192,768]{2,1,0:T(8,128)(2,1)S(1)}, bf16[3,192,768]{2,1,0:T(8,128)(2,1)}, u32[]{:S(2)}) copy-start(bf16[3,192,768]{2,1,0:T(8,128)(2,1)} %get-tuple-element.144) | copy-start | bytes 2654212
  834.0 106.6 %reduce-scatter.18.cloned.1.call-start = ((), (), s32[]{:S(2)}) async-start(), calls=%async_computation.16 | async-start | bytes 3932160 | tf_op jit(solution)/shard_map/reduce_scatter | solution.py:1892
  850.6 84.1 %copy-start.111 = (f32[1,2048]{1,0:T(1,128)S(1)}, f32[1,2048]{1,0:T(1,128)}, u32[]{:S(2)}) copy-start(f32[1,2048]{1,0:T(1,128)} %get-tuple-element.137) | copy-start | bytes 24580
  850.6 85.5 %copy-start.76 = (bf16[512,768]{1,0:T(8,128)(2,1)S(1)}, bf16[512,768]{1,0:T(8,128)(2,1)}, u32[]{:S(2)}) copy-start(bf16[512,768]{1,0:T(8,128)(2,1)} %reduce-scatter.16.cloned.1.call-done) | copy-start | bytes 2359300
  (102 other events, 180.2 us)
Sparse Core Ops, SparseCore 0:
  56.7 44.3 all-gather.8
  102.9 43.9 all-gather.6
  213.6 77.5 all-gather.14
  293.5 50.5 all-gather.10
  345.7 44.4 all-gather.12
  546.7 49.3 reduce-scatter.9
  599.1 42.4 reduce-scatter.7
  645.2 52.6 reduce-scatter.11
  700.8 63.9 reduce-scatter.15
  768.2 55.5 reduce-scatter.13
  834.1 60.3 reduce-scatter.19
  897.4 43.1 reduce-scatter.17
